TPU v7x, 128 devices: a whole 4x4x4 slice. The times are simulated.
128 devices in a mesh: gx: 16 (over y, z), gy: 8 (over x, core).
Axes of the slice: x: 4, y: 4, z: 4, core: 2. Of those that a mesh axis runs over, the one named last changes fastest.
Arguments:
- fluid_vel: float32 [3, 128, 128, 256], P(None, 'gx', 'gy'), may hold values from -6 to 6
- part_pos: float32 [32768, 3, 128], P(('gx', 'gy')), may hold values from 0 to 1
- part_vel: float32 [32768, 3, 128], P(('gx', 'gy')), may hold values from -6 to 6
- brick_owner: int32 [32768, 1], P(('gx', 'gy')), may hold values from 0 to 127; in each aligned block of 256 rows (0 to 255, 256 to 511, ...) at most 4 rows name the same one
- brick_local: int32 [32768], P(('gx', 'gy')), may hold values from 0 to 255
- cell_in_brick: int32 [32768, 128], P(('gx', 'gy')), may hold values from 0 to 127
- pair_self: int32 [2, 65536], P(None, ('gx', 'gy')), may hold values from 0 to 255
- pair_other: int32 [2, 65536], P(None, ('gx', 'gy')), may hold values from 0 to 287
- halo_list: int32 [4096], P(('gx', 'gy')), may hold values from 0 to 255
Outputs:
- fluid_new: float32 [3, 128, 128, 256], P(None, 'gx', 'gy')
- pos_out: float32 [32768, 3, 128], P(('gx', 'gy'))
- vel_out: float32 [32768, 3, 128], P(('gx', 'gy'))
Inputs may be any that keep to these rules, and one draw needn't show every extreme that they name: `brick_owner`: within the 256 blocks of one device (aligned blocks of rows), no tile is named more than 4 times, a bound that some block reaches.
All inputs are finite; a program needn't handle non-finite values.
Results may differ from a plain program's by a relative error of at most 0.0001.
Values sent between devices are 32-bit elements; how exact they have to be, the bound alone decides.
No kernel may reach another device: no remote copies, remote signals or barrier semaphores. Data moves between devices by JAX's collectives and lax.ppermute only.
A program may use at most 64 MiB of HBM per device.

v0:
```python
import jax
import jax.numpy as jnp
from jax import lax
from jax.sharding import PartitionSpec as P

SUBSTEPS = 2
BRICK_X = 2
BRICK_Y = 4
BRICK_Z = 16


def padded_2(cells, sides, width, closed):
    for axis, dim in sides:
        count = lax.axis_size(axis)
        ends = count if closed else count - 1
        head = lax.slice_in_dim(cells, 0, width, axis=dim)
        tail = lax.slice_in_dim(cells, cells.shape[dim] - width, cells.shape[dim], axis=dim)
        cells = jnp.concatenate(
            [
                lax.ppermute(tail, axis, [(i, (i + 1) % count) for i in range(ends)]),
                cells,
                lax.ppermute(head, axis, [((i + 1) % count, i) for i in range(ends)]),
            ],
            axis=dim,
        )
    return cells


def pair_force(xa, xb):
    dist2 = 0.0025 + (xa[:, 0, :, None] - xb[:, 0, None, :]) ** 2
    dist2 = dist2 + (xa[:, 1, :, None] - xb[:, 1, None, :]) ** 2
    dist2 = dist2 + (xa[:, 2, :, None] - xb[:, 2, None, :]) ** 2
    dist = jnp.sqrt(dist2)
    coef = 10.0 * jnp.maximum(0.25 - dist, 0.0) / dist
    total = jnp.sum(coef, axis=2)
    pulled = jnp.einsum("gij,gcj->gci", coef, xb, precision=lax.Precision.HIGHEST)
    return xa * total[:, None, :] - pulled


def grid_bricks(grid):
    comps, sizex, sizey, sizez = grid.shape
    parts = grid.reshape(
        comps, sizex // BRICK_X, BRICK_X, sizey // BRICK_Y, BRICK_Y, sizez // BRICK_Z, BRICK_Z
    )
    parts = jnp.transpose(parts, (1, 3, 5, 0, 2, 4, 6))
    return parts.reshape(-1, comps, BRICK_X * BRICK_Y * BRICK_Z)


def brick_grid(bricks, sizex, sizey, sizez):
    comps = bricks.shape[1]
    parts = bricks.reshape(
        sizex // BRICK_X, sizey // BRICK_Y, sizez // BRICK_Z, comps, BRICK_X, BRICK_Y, BRICK_Z
    )
    parts = jnp.transpose(parts, (3, 0, 4, 1, 5, 2, 6))
    return parts.reshape(comps, sizex, sizey, sizez)


def per_device(
    fluid_vel,
    part_pos,
    part_vel,
    brick_owner,
    brick_local,
    cell_in_brick,
    pair_self,
    pair_other,
    halo_list,
):
    rows_x = lax.axis_size("gx")
    rows_y = lax.axis_size("gy")
    tiles = rows_x * rows_y
    blocks = part_pos.shape[0]
    per_brick = BRICK_X * BRICK_Y * BRICK_Z
    capacity = max(3, 2 * blocks // tiles)
    slots = tiles * capacity
    sizex = fluid_vel.shape[1]
    sizey = fluid_vel.shape[2]
    sizez = fluid_vel.shape[3]
    bricks = sizex // BRICK_X * (sizey // BRICK_Y) * (sizez // BRICK_Z)
    loads = jnp.concatenate([jnp.ones((blocks, 1, per_brick), jnp.float32), part_vel], axis=1)
    bunch = min(32, blocks)
    cells_iota = jnp.arange(per_brick, dtype=jnp.int32)
    cell_groups = cell_in_brick.reshape(blocks // bunch, bunch, per_brick)

    def histogram(item):
        load_part, cell_part = item
        onehot = (cell_part[:, :, None] == cells_iota[None, None, :]).astype(jnp.float32)
        return jnp.einsum("qki,qic->qkc", load_part, onehot, precision=lax.Precision.HIGHEST)

    deposit = lax.map(histogram, (loads.reshape(blocks // bunch, bunch, 4, per_brick), cell_groups))
    deposit = deposit.reshape(blocks, 4, per_brick)
    target = brick_owner[:, 0]
    chosen = (target[:, None] == jnp.arange(tiles, dtype=jnp.int32)[None, :]).astype(jnp.float32)
    block_iota = jnp.arange(blocks, dtype=jnp.int32)
    earlier = (block_iota[:, None] > block_iota[None, :]).astype(jnp.float32)
    before = jnp.dot(earlier, chosen, precision=lax.Precision.HIGHEST)
    rank = jnp.sum(before * chosen, axis=1).astype(jnp.int32)
    slot = target * capacity + rank
    placing = (jnp.arange(slots, dtype=jnp.int32)[:, None] == slot[None, :]).astype(jnp.float32)
    send_ids = jnp.dot(
        placing, brick_local.astype(jnp.float32), precision=lax.Precision.HIGHEST
    ).astype(jnp.int32)
    send_dep = jnp.dot(
        placing, deposit.reshape(blocks, 4 * per_brick), precision=lax.Precision.HIGHEST
    ).reshape(slots, 4, per_brick)
    got_ids, got_dep = (
        lax.all_to_all(send_ids, ("gx", "gy"), split_axis=0, concat_axis=0, tiled=True),
        lax.all_to_all(send_dep, ("gx", "gy"), split_axis=0, concat_axis=0, tiled=True),
    )
    gathering = (jnp.arange(bricks, dtype=jnp.int32)[:, None] == got_ids[None, :]).astype(
        jnp.float32
    )
    summed = jnp.dot(
        gathering, got_dep.reshape(slots, 4 * per_brick), precision=lax.Precision.HIGHEST
    )
    dep_grid = brick_grid(summed.reshape(bricks, 4, per_brick), sizex, sizey, sizez)
    count = dep_grid[0]
    momentum = dep_grid[1:]
    solid = 0.5 * count
    voids = 1.0 - 0.6 * solid / (1.0 + solid)
    beta = (1.0 - voids) / (voids * voids)
    padded = padded_2(fluid_vel, (("gx", 1), ("gy", 2)), 1, False)
    padded = jnp.pad(padded, ((0, 0), (0, 0), (0, 0), (1, 1)))
    beside = padded[:, 2:, 1:-1, 1:-1] + padded[:, :-2, 1:-1, 1:-1]
    beside = beside + padded[:, 1:-1, 2:, 1:-1] + padded[:, 1:-1, :-2, 1:-1]
    beside = beside + padded[:, 1:-1, 1:-1, 2:] + padded[:, 1:-1, 1:-1, :-2]
    lap = beside - 6.0 * fluid_vel
    fluid_new = fluid_vel + 0.1 * lap + 0.15 * beta[None] * (momentum - count[None] * fluid_vel)
    table = grid_bricks(jnp.concatenate([fluid_new, beta[None]], axis=0))
    answer = table[got_ids]
    back = lax.all_to_all(answer, ("gx", "gy"), split_axis=0, concat_axis=0, tiled=True)
    mine = back[slot]

    def pick_cells(item):
        fluid_part, cell_part = item
        onehot = (cell_part[:, :, None] == cells_iota[None, None, :]).astype(jnp.float32)
        return jnp.einsum("qkc,qic->qki", fluid_part, onehot, precision=lax.Precision.HIGHEST)

    local_fluid = lax.map(
        pick_cells, (mine.reshape(blocks // bunch, bunch, 4, per_brick), cell_groups)
    )
    local_fluid = local_fluid.reshape(blocks, 4, per_brick)
    flow = local_fluid[:, :3, :]
    drift = 2.0 * local_fluid[:, 3:4, :]
    down = jnp.array([0.0, 0.0, -1.0], jnp.float32)[None, :, None]
    width = halo_list.shape[0] // 2
    pair_count = pair_self.shape[1]
    group = min(64, pair_count)
    position = part_pos
    velocity = part_vel
    for step in range(SUBSTEPS):
        outgoing = position[halo_list]
        rims = padded_2(outgoing, (("gx", 0),), width, True)
        extended = jnp.concatenate([position, rims[:width], rims[3 * width :]], axis=0)
        firsts = pair_self[step]
        seconds = pair_other[step]

        def one_group(pair):
            return pair_force(extended[pair[0]], extended[pair[1]])

        forces = lax.map(one_group, (firsts.reshape(-1, group), seconds.reshape(-1, group)))
        forces = forces.reshape(pair_count, 3 * per_brick)
        members = (firsts[None, :] == block_iota[:, None]).astype(jnp.float32)
        push = jnp.dot(members, forces, precision=lax.Precision.HIGHEST).reshape(
            blocks, 3, per_brick
        )
        velocity = velocity + 0.1 * (push + drift * (flow - velocity) + down)
        position = position + 0.1 * velocity
    return (fluid_new, position, velocity)


def solution(mesh):
    in_specs = (
        P(None, "gx", "gy", None),
        P(("gx", "gy"), None, None),
        P(("gx", "gy"), None, None),
        P(("gx", "gy"), None),
        P(("gx", "gy")),
        P(("gx", "gy"), None),
        P(None, ("gx", "gy")),
        P(None, ("gx", "gy")),
        P(("gx", "gy")),
    )
    out_specs = (
        P(None, "gx", "gy", None),
        P(("gx", "gy"), None, None),
        P(("gx", "gy"), None, None),
    )
    return jax.shard_map(
        per_device, mesh=mesh, in_specs=in_specs, out_specs=out_specs, check_vma=False
    )
```

profile of v0, /device:TPU:0, one launch (start us, length us, event | category | flops | bytes accessed | tf_op | source)
XLA Modules:
  0.0 458.4 jit_solution(11579686951144017939)
XLA Ops:
  1.5 3.9 collective-permute-start.1
  10.1 11.8 %all-to-all-start = ((s32[128,4,1]{1,2,0:T(1,128)}), s32[128,4,1]{1,2,0:T(1,128)S(1)}, u32[]{:S(2)}, u32[]{:S(2)}) async-start(s32[128,4,1]{1,2,0:T(1,128)} %bitcast.25), calls=%async_computation | async-start | bytes 131072 | tf_op jit(solution)/shard_map/all_to_all | solution.py:107
  23.4 17.7 %while.44 = (s32[]{:T(128)}, f32[8,32,4,128]{3,2,1,0:T(4,128)S(1)}, f32[8,32,4,128]{3,2,1,0:T(4,128)S(1)}, s32[8,32,128]{2,1,0:T(8,128)}, s32[]{:T(128)}) while((s32[]{:T(128)}, f32[8,32,4,128]{3,2,1,0:T(4,128)S(1)}, f32[8,32,4,128]{3,2,1,0:T(4,128)S(1)}, s32[8,32,128]{2,1,0:T(8,128)}, s32[]{:T(128)}) %tuple.124), condition=%wide.region_2.3_spmd.clone, body=%wide.region_1.2_spmd.clone.sunk | while | flops 25690112 | bytes 181313 | solution.py:90
  44.9 9.8 %all-to-all-start.1 = ((f32[512,4,128]{2,1,0:T(4,128)}), f32[512,4,128]{2,1,0:T(4,128)S(1)}, u32[]{:S(2)}, u32[]{:S(2)}) async-start(f32[512,4,128]{2,1,0:T(4,128)} %copy.60), calls=%async_computation.1 | async-start | bytes 2097152 | tf_op jit(solution)/shard_map/all_to_all | solution.py:108
  56.6 4.3 collective-permute-start.5
  63.4 4.4 collective-permute-done.4
  69.3 3.2 collective-permute-start.3
  75.5 3.5 convolution_bitcast_fusion
  82.5 2.5 squeeze.36
  86.6 1.9 copy.63
  88.5 2.8 slice.128
  91.3 3.3 fusion.64
  94.6 1.9 concatenate.41
  98.3 3.0 maximum_bitcast_fusion
  101.4 4.2 reshape.265
  106.0 2.6 gather_fusion.5
  108.6 12.8 %all-to-all-start.2 = ((f32[512,4,128]{2,1,0:T(4,128)}), f32[512,4,128]{2,1,0:T(4,128)}, u32[]{:S(2)}, u32[]{:S(2)}) async-start(f32[512,4,128]{2,1,0:T(4,128)} %gather_fusion.5), calls=%async_computation.2 | async-start | bytes 2097152 | tf_op jit(solution)/shard_map/all_to_all | solution.py:131
  121.6 154.5 %while.42 = (s32[]{:T(128)}, f32[8,64,3,128]{3,2,1,0:T(4,128)S(1)}, s32[8,64]{1,0:T(8,128)S(1)}, f32[288,3,128]{2,1,0:T(4,128)}, s32[8,64]{1,0:T(8,128)S(1)}, /*index=5*/s32[]{:T(128)}) while((s32[]{:T(128)}, f32[8,64,3,128]{3,2,1,0:T(4,128)S(1)}, s32[8,64]{1,0:T(8,128)S(1)}, f32[288,3,128]{2,1,0:T(4,128)}, s32[8,64]{1,0:T(8,128)S(1)}, ...), condition=%wide.region_5.6_spmd, body=%wide.region_3.5_spmd.sunk | while | flops 66103680 | bytes 1648717 | solution.py:161
  125.2 5.3 %fusion.111 = f32[64,128]{1,0:T(8,128)S(1)} fusion(f32[64,128]{1,0:T(8,128)S(1)} %bitcast.224, f32[64,128]{1,0:T(8,128)S(1)} %bitcast.236, f32[64,128]{1,0:T(8,128)S(1)} %bitcast.226, f32[64,128]{1,0:T(8,128)S(1)} %bitcast.238, f32[64,128]{1,0:T(8,128)S(1)} %bitcast.222, f32[64,128]{1,0:T(8,128)S(1)} %bitcast.234), kind=kLoop, calls=%fused_computation.12.clone.1 | loop fusion | flops 14671872 | bytes 229376 | tf_op jit(solution)/shard_map/while/body/eval_jaxpr/reduce_sum | solution.py:35
  130.5 10.3 %fusion.112 = f32[8,64,3,128]{3,2,1,0:T(4,128)S(1)} fusion(f32[8,64,3,128]{3,2,1,0:T(4,128)S(1)} %get-tuple-element.418, s32[]{:T(128)} %get-tuple-element.417, f32[64,3,128]{2,1,0:T(4,128)S(1)} %gather_fusion, f32[64,128]{1,0:T(8,128)S(1)} %bitcast.225, f32[64,128]{1,0:T(8,128)S(1)} %bitcast.237, f32[64,128]{1,0:T(8,128)S(1)} %bitcast.227, ...), kind=kOutput, calls=%fused_computation.15.clone.1 | convolution fusion | flops 51429376 | bytes 622596 | tf_op jit(solution)/shard_map/while/body/eval_jaxpr/gij,gcj->gci/dot_general | solution.py:36
  144.5 5.3 %fusion.111 = f32[64,128]{1,0:T(8,128)S(1)} fusion(f32[64,128]{1,0:T(8,128)S(1)} %bitcast.224, f32[64,128]{1,0:T(8,128)S(1)} %bitcast.236, f32[64,128]{1,0:T(8,128)S(1)} %bitcast.226, f32[64,128]{1,0:T(8,128)S(1)} %bitcast.238, f32[64,128]{1,0:T(8,128)S(1)} %bitcast.222, f32[64,128]{1,0:T(8,128)S(1)} %bitcast.234), kind=kLoop, calls=%fused_computation.12.clone.1 | loop fusion | flops 14671872 | bytes 229376 | tf_op jit(solution)/shard_map/while/body/eval_jaxpr/reduce_sum | solution.py:35
  149.8 10.3 %fusion.112 = f32[8,64,3,128]{3,2,1,0:T(4,128)S(1)} fusion(f32[8,64,3,128]{3,2,1,0:T(4,128)S(1)} %get-tuple-element.418, s32[]{:T(128)} %get-tuple-element.417, f32[64,3,128]{2,1,0:T(4,128)S(1)} %gather_fusion, f32[64,128]{1,0:T(8,128)S(1)} %bitcast.225, f32[64,128]{1,0:T(8,128)S(1)} %bitcast.237, f32[64,128]{1,0:T(8,128)S(1)} %bitcast.227, ...), kind=kOutput, calls=%fused_computation.15.clone.1 | convolution fusion | flops 51429376 | bytes 622596 | tf_op jit(solution)/shard_map/while/body/eval_jaxpr/gij,gcj->gci/dot_general | solution.py:36
  163.8 5.3 %fusion.111 = f32[64,128]{1,0:T(8,128)S(1)} fusion(f32[64,128]{1,0:T(8,128)S(1)} %bitcast.224, f32[64,128]{1,0:T(8,128)S(1)} %bitcast.236, f32[64,128]{1,0:T(8,128)S(1)} %bitcast.226, f32[64,128]{1,0:T(8,128)S(1)} %bitcast.238, f32[64,128]{1,0:T(8,128)S(1)} %bitcast.222, f32[64,128]{1,0:T(8,128)S(1)} %bitcast.234), kind=kLoop, calls=%fused_computation.12.clone.1 | loop fusion | flops 14671872 | bytes 229376 | tf_op jit(solution)/shard_map/while/body/eval_jaxpr/reduce_sum | solution.py:35
  169.2 10.3 %fusion.112 = f32[8,64,3,128]{3,2,1,0:T(4,128)S(1)} fusion(f32[8,64,3,128]{3,2,1,0:T(4,128)S(1)} %get-tuple-element.418, s32[]{:T(128)} %get-tuple-element.417, f32[64,3,128]{2,1,0:T(4,128)S(1)} %gather_fusion, f32[64,128]{1,0:T(8,128)S(1)} %bitcast.225, f32[64,128]{1,0:T(8,128)S(1)} %bitcast.237, f32[64,128]{1,0:T(8,128)S(1)} %bitcast.227, ...), kind=kOutput, calls=%fused_computation.15.clone.1 | convolution fusion | flops 51429376 | bytes 622596 | tf_op jit(solution)/shard_map/while/body/eval_jaxpr/gij,gcj->gci/dot_general | solution.py:36
  183.2 5.3 %fusion.111 = f32[64,128]{1,0:T(8,128)S(1)} fusion(f32[64,128]{1,0:T(8,128)S(1)} %bitcast.224, f32[64,128]{1,0:T(8,128)S(1)} %bitcast.236, f32[64,128]{1,0:T(8,128)S(1)} %bitcast.226, f32[64,128]{1,0:T(8,128)S(1)} %bitcast.238, f32[64,128]{1,0:T(8,128)S(1)} %bitcast.222, f32[64,128]{1,0:T(8,128)S(1)} %bitcast.234), kind=kLoop, calls=%fused_computation.12.clone.1 | loop fusion | flops 14671872 | bytes 229376 | tf_op jit(solution)/shard_map/while/body/eval_jaxpr/reduce_sum | solution.py:35
  188.5 10.3 %fusion.112 = f32[8,64,3,128]{3,2,1,0:T(4,128)S(1)} fusion(f32[8,64,3,128]{3,2,1,0:T(4,128)S(1)} %get-tuple-element.418, s32[]{:T(128)} %get-tuple-element.417, f32[64,3,128]{2,1,0:T(4,128)S(1)} %gather_fusion, f32[64,128]{1,0:T(8,128)S(1)} %bitcast.225, f32[64,128]{1,0:T(8,128)S(1)} %bitcast.237, f32[64,128]{1,0:T(8,128)S(1)} %bitcast.227, ...), kind=kOutput, calls=%fused_computation.15.clone.1 | convolution fusion | flops 51429376 | bytes 622596 | tf_op jit(solution)/shard_map/while/body/eval_jaxpr/gij,gcj->gci/dot_general | solution.py:36
  202.5 5.3 %fusion.111 = f32[64,128]{1,0:T(8,128)S(1)} fusion(f32[64,128]{1,0:T(8,128)S(1)} %bitcast.224, f32[64,128]{1,0:T(8,128)S(1)} %bitcast.236, f32[64,128]{1,0:T(8,128)S(1)} %bitcast.226, f32[64,128]{1,0:T(8,128)S(1)} %bitcast.238, f32[64,128]{1,0:T(8,128)S(1)} %bitcast.222, f32[64,128]{1,0:T(8,128)S(1)} %bitcast.234), kind=kLoop, calls=%fused_computation.12.clone.1 | loop fusion | flops 14671872 | bytes 229376 | tf_op jit(solution)/shard_map/while/body/eval_jaxpr/reduce_sum | solution.py:35
  207.8 10.3 %fusion.112 = f32[8,64,3,128]{3,2,1,0:T(4,128)S(1)} fusion(f32[8,64,3,128]{3,2,1,0:T(4,128)S(1)} %get-tuple-element.418, s32[]{:T(128)} %get-tuple-element.417, f32[64,3,128]{2,1,0:T(4,128)S(1)} %gather_fusion, f32[64,128]{1,0:T(8,128)S(1)} %bitcast.225, f32[64,128]{1,0:T(8,128)S(1)} %bitcast.237, f32[64,128]{1,0:T(8,128)S(1)} %bitcast.227, ...), kind=kOutput, calls=%fused_computation.15.clone.1 | convolution fusion | flops 51429376 | bytes 622596 | tf_op jit(solution)/shard_map/while/body/eval_jaxpr/gij,gcj->gci/dot_general | solution.py:36
  221.8 5.3 %fusion.111 = f32[64,128]{1,0:T(8,128)S(1)} fusion(f32[64,128]{1,0:T(8,128)S(1)} %bitcast.224, f32[64,128]{1,0:T(8,128)S(1)} %bitcast.236, f32[64,128]{1,0:T(8,128)S(1)} %bitcast.226, f32[64,128]{1,0:T(8,128)S(1)} %bitcast.238, f32[64,128]{1,0:T(8,128)S(1)} %bitcast.222, f32[64,128]{1,0:T(8,128)S(1)} %bitcast.234), kind=kLoop, calls=%fused_computation.12.clone.1 | loop fusion | flops 14671872 | bytes 229376 | tf_op jit(solution)/shard_map/while/body/eval_jaxpr/reduce_sum | solution.py:35
  227.1 10.3 %fusion.112 = f32[8,64,3,128]{3,2,1,0:T(4,128)S(1)} fusion(f32[8,64,3,128]{3,2,1,0:T(4,128)S(1)} %get-tuple-element.418, s32[]{:T(128)} %get-tuple-element.417, f32[64,3,128]{2,1,0:T(4,128)S(1)} %gather_fusion, f32[64,128]{1,0:T(8,128)S(1)} %bitcast.225, f32[64,128]{1,0:T(8,128)S(1)} %bitcast.237, f32[64,128]{1,0:T(8,128)S(1)} %bitcast.227, ...), kind=kOutput, calls=%fused_computation.15.clone.1 | convolution fusion | flops 51429376 | bytes 622596 | tf_op jit(solution)/shard_map/while/body/eval_jaxpr/gij,gcj->gci/dot_general | solution.py:36
  241.1 5.3 %fusion.111 = f32[64,128]{1,0:T(8,128)S(1)} fusion(f32[64,128]{1,0:T(8,128)S(1)} %bitcast.224, f32[64,128]{1,0:T(8,128)S(1)} %bitcast.236, f32[64,128]{1,0:T(8,128)S(1)} %bitcast.226, f32[64,128]{1,0:T(8,128)S(1)} %bitcast.238, f32[64,128]{1,0:T(8,128)S(1)} %bitcast.222, f32[64,128]{1,0:T(8,128)S(1)} %bitcast.234), kind=kLoop, calls=%fused_computation.12.clone.1 | loop fusion | flops 14671872 | bytes 229376 | tf_op jit(solution)/shard_map/while/body/eval_jaxpr/reduce_sum | solution.py:35
  246.4 10.3 %fusion.112 = f32[8,64,3,128]{3,2,1,0:T(4,128)S(1)} fusion(f32[8,64,3,128]{3,2,1,0:T(4,128)S(1)} %get-tuple-element.418, s32[]{:T(128)} %get-tuple-element.417, f32[64,3,128]{2,1,0:T(4,128)S(1)} %gather_fusion, f32[64,128]{1,0:T(8,128)S(1)} %bitcast.225, f32[64,128]{1,0:T(8,128)S(1)} %bitcast.237, f32[64,128]{1,0:T(8,128)S(1)} %bitcast.227, ...), kind=kOutput, calls=%fused_computation.15.clone.1 | convolution fusion | flops 51429376 | bytes 622596 | tf_op jit(solution)/shard_map/while/body/eval_jaxpr/gij,gcj->gci/dot_general | solution.py:36
  260.4 5.3 %fusion.111 = f32[64,128]{1,0:T(8,128)S(1)} fusion(f32[64,128]{1,0:T(8,128)S(1)} %bitcast.224, f32[64,128]{1,0:T(8,128)S(1)} %bitcast.236, f32[64,128]{1,0:T(8,128)S(1)} %bitcast.226, f32[64,128]{1,0:T(8,128)S(1)} %bitcast.238, f32[64,128]{1,0:T(8,128)S(1)} %bitcast.222, f32[64,128]{1,0:T(8,128)S(1)} %bitcast.234), kind=kLoop, calls=%fused_computation.12.clone.1 | loop fusion | flops 14671872 | bytes 229376 | tf_op jit(solution)/shard_map/while/body/eval_jaxpr/reduce_sum | solution.py:35
  265.7 10.3 %fusion.112 = f32[8,64,3,128]{3,2,1,0:T(4,128)S(1)} fusion(f32[8,64,3,128]{3,2,1,0:T(4,128)S(1)} %get-tuple-element.418, s32[]{:T(128)} %get-tuple-element.417, f32[64,3,128]{2,1,0:T(4,128)S(1)} %gather_fusion, f32[64,128]{1,0:T(8,128)S(1)} %bitcast.225, f32[64,128]{1,0:T(8,128)S(1)} %bitcast.237, f32[64,128]{1,0:T(8,128)S(1)} %bitcast.227, ...), kind=kOutput, calls=%fused_computation.15.clone.1 | convolution fusion | flops 51429376 | bytes 622596 | tf_op jit(solution)/shard_map/while/body/eval_jaxpr/gij,gcj->gci/dot_general | solution.py:36
  276.5 2.4 gather_fusion.6
  278.9 26.9 %while.45 = (s32[]{:T(128)}, f32[8,32,4,128]{3,1,0,2:T(8,128)}, f32[8,32,4,128]{3,2,1,0:T(4,128)S(1)}, s32[8,32,128]{2,1,0:T(8,128)}, s32[]{:T(128)}) while((s32[]{:T(128)}, f32[8,32,4,128]{3,1,0,2:T(8,128)}, f32[8,32,4,128]{3,2,1,0:T(4,128)S(1)}, s32[8,32,128]{2,1,0:T(8,128)}, s32[]{:T(128)}) %tuple.125), condition=%wide.region_7.8_spmd.clone, body=%wide.region_6.7_spmd.clone.sunk | while | flops 25690112 | bytes 311877 | solution.py:139
  279.6 2.0 fusion.122
  283.0 2.0 fusion.122
  286.3 2.0 fusion.122
  289.7 2.0 fusion.122
  293.0 2.0 fusion.122
  296.4 2.0 fusion.122
  299.7 2.0 fusion.122
  303.1 2.0 fusion.122
  306.7 2.5 multiply_add_fusion.1
  311.0 4.6 %collective-permute-start.7 = (f32[16,3,128]{2,0,1:T(8,128)S(1)}, f32[16,3,128]{2,0,1:T(8,128)S(1)}, u32[]{:S(2)}, u32[]{:S(2)}) collective-permute-start(f32[16,3,128]{2,0,1:T(8,128)S(1)} %copy.82), channel_id=1, source_target_pairs={{8,0},{16,8},{24,16},{32,24},{40,32},{48,40},{56,48},{64,56},{72,6... | collective-permute-start | bytes 73736 | tf_op jit(solution)/shard_map/ppermute | solution.py:22
  317.9 137.5 %while.43 = (s32[]{:T(128)}, f32[8,64,3,128]{3,2,1,0:T(4,128)S(1)}, s32[8,64]{1,0:T(8,128)S(1)}, f32[288,3,128]{2,1,0:T(4,128)S(1)}, s32[8,64]{1,0:T(8,128)S(1)}, /*index=5*/s32[]{:T(128)}) while((s32[]{:T(128)}, f32[8,64,3,128]{3,2,1,0:T(4,128)S(1)}, s32[8,64]{1,0:T(8,128)S(1)}, f32[288,3,128]{2,1,0:T(4,128)S(1)}, s32[8,64]{1,0:T(8,128)S(1)}, ...), condition=%wide.region_10.11_spmd, body=%wide.region_8.10_spmd.sunk | while | flops 66103680 | bytes 1648717 | solution.py:161
  319.5 5.3 %fusion.117 = f32[64,128]{1,0:T(8,128)S(1)} fusion(f32[64,128]{1,0:T(8,128)S(1)} %bitcast.230, f32[64,128]{1,0:T(8,128)S(1)} %bitcast.242, f32[64,128]{1,0:T(8,128)S(1)} %bitcast.232, f32[64,128]{1,0:T(8,128)S(1)} %bitcast.244, f32[64,128]{1,0:T(8,128)S(1)} %bitcast.228, f32[64,128]{1,0:T(8,128)S(1)} %bitcast.240), kind=kLoop, calls=%fused_computation.32.clone.1 | loop fusion | flops 14671872 | bytes 229376 | tf_op jit(solution)/shard_map/while/body/eval_jaxpr/reduce_sum | solution.py:35
  324.8 10.3 %fusion.118 = f32[8,64,3,128]{3,2,1,0:T(4,128)S(1)} fusion(f32[8,64,3,128]{3,2,1,0:T(4,128)S(1)} %get-tuple-element.436, s32[]{:T(128)} %get-tuple-element.435, f32[64,3,128]{2,1,0:T(4,128)S(1)} %gather_fusion.2, f32[64,128]{1,0:T(8,128)S(1)} %bitcast.231, f32[64,128]{1,0:T(8,128)S(1)} %bitcast.243, f32[64,128]{1,0:T(8,128)S(1)} %bitcast.233, ...), kind=kOutput, calls=%fused_computation.35.clone.1 | convolution fusion | flops 51429376 | bytes 622596 | tf_op jit(solution)/shard_map/while/body/eval_jaxpr/gij,gcj->gci/dot_general | solution.py:36
  336.7 5.3 %fusion.117 = f32[64,128]{1,0:T(8,128)S(1)} fusion(f32[64,128]{1,0:T(8,128)S(1)} %bitcast.230, f32[64,128]{1,0:T(8,128)S(1)} %bitcast.242, f32[64,128]{1,0:T(8,128)S(1)} %bitcast.232, f32[64,128]{1,0:T(8,128)S(1)} %bitcast.244, f32[64,128]{1,0:T(8,128)S(1)} %bitcast.228, f32[64,128]{1,0:T(8,128)S(1)} %bitcast.240), kind=kLoop, calls=%fused_computation.32.clone.1 | loop fusion | flops 14671872 | bytes 229376 | tf_op jit(solution)/shard_map/while/body/eval_jaxpr/reduce_sum | solution.py:35
  342.0 10.3 %fusion.118 = f32[8,64,3,128]{3,2,1,0:T(4,128)S(1)} fusion(f32[8,64,3,128]{3,2,1,0:T(4,128)S(1)} %get-tuple-element.436, s32[]{:T(128)} %get-tuple-element.435, f32[64,3,128]{2,1,0:T(4,128)S(1)} %gather_fusion.2, f32[64,128]{1,0:T(8,128)S(1)} %bitcast.231, f32[64,128]{1,0:T(8,128)S(1)} %bitcast.243, f32[64,128]{1,0:T(8,128)S(1)} %bitcast.233, ...), kind=kOutput, calls=%fused_computation.35.clone.1 | convolution fusion | flops 51429376 | bytes 622596 | tf_op jit(solution)/shard_map/while/body/eval_jaxpr/gij,gcj->gci/dot_general | solution.py:36
  353.9 5.3 %fusion.117 = f32[64,128]{1,0:T(8,128)S(1)} fusion(f32[64,128]{1,0:T(8,128)S(1)} %bitcast.230, f32[64,128]{1,0:T(8,128)S(1)} %bitcast.242, f32[64,128]{1,0:T(8,128)S(1)} %bitcast.232, f32[64,128]{1,0:T(8,128)S(1)} %bitcast.244, f32[64,128]{1,0:T(8,128)S(1)} %bitcast.228, f32[64,128]{1,0:T(8,128)S(1)} %bitcast.240), kind=kLoop, calls=%fused_computation.32.clone.1 | loop fusion | flops 14671872 | bytes 229376 | tf_op jit(solution)/shard_map/while/body/eval_jaxpr/reduce_sum | solution.py:35
  359.2 10.3 %fusion.118 = f32[8,64,3,128]{3,2,1,0:T(4,128)S(1)} fusion(f32[8,64,3,128]{3,2,1,0:T(4,128)S(1)} %get-tuple-element.436, s32[]{:T(128)} %get-tuple-element.435, f32[64,3,128]{2,1,0:T(4,128)S(1)} %gather_fusion.2, f32[64,128]{1,0:T(8,128)S(1)} %bitcast.231, f32[64,128]{1,0:T(8,128)S(1)} %bitcast.243, f32[64,128]{1,0:T(8,128)S(1)} %bitcast.233, ...), kind=kOutput, calls=%fused_computation.35.clone.1 | convolution fusion | flops 51429376 | bytes 622596 | tf_op jit(solution)/shard_map/while/body/eval_jaxpr/gij,gcj->gci/dot_general | solution.py:36
  371.0 5.3 %fusion.117 = f32[64,128]{1,0:T(8,128)S(1)} fusion(f32[64,128]{1,0:T(8,128)S(1)} %bitcast.230, f32[64,128]{1,0:T(8,128)S(1)} %bitcast.242, f32[64,128]{1,0:T(8,128)S(1)} %bitcast.232, f32[64,128]{1,0:T(8,128)S(1)} %bitcast.244, f32[64,128]{1,0:T(8,128)S(1)} %bitcast.228, f32[64,128]{1,0:T(8,128)S(1)} %bitcast.240), kind=kLoop, calls=%fused_computation.32.clone.1 | loop fusion | flops 14671872 | bytes 229376 | tf_op jit(solution)/shard_map/while/body/eval_jaxpr/reduce_sum | solution.py:35
  376.4 10.3 %fusion.118 = f32[8,64,3,128]{3,2,1,0:T(4,128)S(1)} fusion(f32[8,64,3,128]{3,2,1,0:T(4,128)S(1)} %get-tuple-element.436, s32[]{:T(128)} %get-tuple-element.435, f32[64,3,128]{2,1,0:T(4,128)S(1)} %gather_fusion.2, f32[64,128]{1,0:T(8,128)S(1)} %bitcast.231, f32[64,128]{1,0:T(8,128)S(1)} %bitcast.243, f32[64,128]{1,0:T(8,128)S(1)} %bitcast.233, ...), kind=kOutput, calls=%fused_computation.35.clone.1 | convolution fusion | flops 51429376 | bytes 622596 | tf_op jit(solution)/shard_map/while/body/eval_jaxpr/gij,gcj->gci/dot_general | solution.py:36
  388.2 5.3 %fusion.117 = f32[64,128]{1,0:T(8,128)S(1)} fusion(f32[64,128]{1,0:T(8,128)S(1)} %bitcast.230, f32[64,128]{1,0:T(8,128)S(1)} %bitcast.242, f32[64,128]{1,0:T(8,128)S(1)} %bitcast.232, f32[64,128]{1,0:T(8,128)S(1)} %bitcast.244, f32[64,128]{1,0:T(8,128)S(1)} %bitcast.228, f32[64,128]{1,0:T(8,128)S(1)} %bitcast.240), kind=kLoop, calls=%fused_computation.32.clone.1 | loop fusion | flops 14671872 | bytes 229376 | tf_op jit(solution)/shard_map/while/body/eval_jaxpr/reduce_sum | solution.py:35
  393.5 10.3 %fusion.118 = f32[8,64,3,128]{3,2,1,0:T(4,128)S(1)} fusion(f32[8,64,3,128]{3,2,1,0:T(4,128)S(1)} %get-tuple-element.436, s32[]{:T(128)} %get-tuple-element.435, f32[64,3,128]{2,1,0:T(4,128)S(1)} %gather_fusion.2, f32[64,128]{1,0:T(8,128)S(1)} %bitcast.231, f32[64,128]{1,0:T(8,128)S(1)} %bitcast.243, f32[64,128]{1,0:T(8,128)S(1)} %bitcast.233, ...), kind=kOutput, calls=%fused_computation.35.clone.1 | convolution fusion | flops 51429376 | bytes 622596 | tf_op jit(solution)/shard_map/while/body/eval_jaxpr/gij,gcj->gci/dot_general | solution.py:36
  405.4 5.3 %fusion.117 = f32[64,128]{1,0:T(8,128)S(1)} fusion(f32[64,128]{1,0:T(8,128)S(1)} %bitcast.230, f32[64,128]{1,0:T(8,128)S(1)} %bitcast.242, f32[64,128]{1,0:T(8,128)S(1)} %bitcast.232, f32[64,128]{1,0:T(8,128)S(1)} %bitcast.244, f32[64,128]{1,0:T(8,128)S(1)} %bitcast.228, f32[64,128]{1,0:T(8,128)S(1)} %bitcast.240), kind=kLoop, calls=%fused_computation.32.clone.1 | loop fusion | flops 14671872 | bytes 229376 | tf_op jit(solution)/shard_map/while/body/eval_jaxpr/reduce_sum | solution.py:35
  410.7 10.3 %fusion.118 = f32[8,64,3,128]{3,2,1,0:T(4,128)S(1)} fusion(f32[8,64,3,128]{3,2,1,0:T(4,128)S(1)} %get-tuple-element.436, s32[]{:T(128)} %get-tuple-element.435, f32[64,3,128]{2,1,0:T(4,128)S(1)} %gather_fusion.2, f32[64,128]{1,0:T(8,128)S(1)} %bitcast.231, f32[64,128]{1,0:T(8,128)S(1)} %bitcast.243, f32[64,128]{1,0:T(8,128)S(1)} %bitcast.233, ...), kind=kOutput, calls=%fused_computation.35.clone.1 | convolution fusion | flops 51429376 | bytes 622596 | tf_op jit(solution)/shard_map/while/body/eval_jaxpr/gij,gcj->gci/dot_general | solution.py:36
  422.6 5.3 %fusion.117 = f32[64,128]{1,0:T(8,128)S(1)} fusion(f32[64,128]{1,0:T(8,128)S(1)} %bitcast.230, f32[64,128]{1,0:T(8,128)S(1)} %bitcast.242, f32[64,128]{1,0:T(8,128)S(1)} %bitcast.232, f32[64,128]{1,0:T(8,128)S(1)} %bitcast.244, f32[64,128]{1,0:T(8,128)S(1)} %bitcast.228, f32[64,128]{1,0:T(8,128)S(1)} %bitcast.240), kind=kLoop, calls=%fused_computation.32.clone.1 | loop fusion | flops 14671872 | bytes 229376 | tf_op jit(solution)/shard_map/while/body/eval_jaxpr/reduce_sum | solution.py:35
  427.9 10.3 %fusion.118 = f32[8,64,3,128]{3,2,1,0:T(4,128)S(1)} fusion(f32[8,64,3,128]{3,2,1,0:T(4,128)S(1)} %get-tuple-element.436, s32[]{:T(128)} %get-tuple-element.435, f32[64,3,128]{2,1,0:T(4,128)S(1)} %gather_fusion.2, f32[64,128]{1,0:T(8,128)S(1)} %bitcast.231, f32[64,128]{1,0:T(8,128)S(1)} %bitcast.243, f32[64,128]{1,0:T(8,128)S(1)} %bitcast.233, ...), kind=kOutput, calls=%fused_computation.35.clone.1 | convolution fusion | flops 51429376 | bytes 622596 | tf_op jit(solution)/shard_map/while/body/eval_jaxpr/gij,gcj->gci/dot_general | solution.py:36
  439.8 5.3 %fusion.117 = f32[64,128]{1,0:T(8,128)S(1)} fusion(f32[64,128]{1,0:T(8,128)S(1)} %bitcast.230, f32[64,128]{1,0:T(8,128)S(1)} %bitcast.242, f32[64,128]{1,0:T(8,128)S(1)} %bitcast.232, f32[64,128]{1,0:T(8,128)S(1)} %bitcast.244, f32[64,128]{1,0:T(8,128)S(1)} %bitcast.228, f32[64,128]{1,0:T(8,128)S(1)} %bitcast.240), kind=kLoop, calls=%fused_computation.32.clone.1 | loop fusion | flops 14671872 | bytes 229376 | tf_op jit(solution)/shard_map/while/body/eval_jaxpr/reduce_sum | solution.py:35
  445.1 10.3 %fusion.118 = f32[8,64,3,128]{3,2,1,0:T(4,128)S(1)} fusion(f32[8,64,3,128]{3,2,1,0:T(4,128)S(1)} %get-tuple-element.436, s32[]{:T(128)} %get-tuple-element.435, f32[64,3,128]{2,1,0:T(4,128)S(1)} %gather_fusion.2, f32[64,128]{1,0:T(8,128)S(1)} %bitcast.231, f32[64,128]{1,0:T(8,128)S(1)} %bitcast.243, f32[64,128]{1,0:T(8,128)S(1)} %bitcast.233, ...), kind=kOutput, calls=%fused_computation.35.clone.1 | convolution fusion | flops 51429376 | bytes 622596 | tf_op jit(solution)/shard_map/while/body/eval_jaxpr/gij,gcj->gci/dot_general | solution.py:36
  455.8 2.6 multiply_add_fusion
  (265 shorter events, 101.6 us)
Async XLA Ops:
  1.5 66.3 %collective-permute-start.1 = (f32[3,1,16,256]{3,2,1,0:T(8,128)S(1)}, f32[3,1,16,256]{3,2,1,0:T(8,128)S(1)}, u32[]{:S(2)}, u32[]{:S(2)}) collective-permute-start(f32[3,1,16,256]{3,2,1,0:T(8,128)S(1)} %get-tuple-element.220), channel_id=1, source_target_pairs={{0,8},{8,16},{16,24},{24,32},{32,40},{40,48},{48,56},{56,64},{64,7... | collective-permute-start | bytes 147464 | tf_op jit(solution)/shard_map/ppermute | solution.py:20
  5.4 62.5 %collective-permute-start = (f32[3,1,16,256]{3,2,1,0:T(8,128)S(1)}, f32[3,1,16,256]{3,2,1,0:T(8,128)S(1)}, u32[]{:S(2)}, u32[]{:S(2)}) collective-permute-start(f32[3,1,16,256]{3,2,1,0:T(8,128)S(1)} %get-tuple-element.219), channel_id=1, source_target_pairs={{8,0},{16,8},{24,16},{32,24},{40,32},{48,40},{56,48},{64,56},{72,6... | collective-permute-start | bytes 147464 | tf_op jit(solution)/shard_map/ppermute | solution.py:22
  10.1 34.8 %all-to-all-start = ((s32[128,4,1]{1,2,0:T(1,128)}), s32[128,4,1]{1,2,0:T(1,128)S(1)}, u32[]{:S(2)}, u32[]{:S(2)}) async-start(s32[128,4,1]{1,2,0:T(1,128)} %bitcast.25), calls=%async_computation | async-start | bytes 131072 | tf_op jit(solution)/shard_map/all_to_all | solution.py:107
  23.2 18.8 %copy-start.20 = (s32[32]{0:T(128)S(1)}, s32[32]{0:T(128)}, u32[]{:S(2)}) copy-start(s32[32]{0:T(128)} %param.26) | copy-start | bytes 388
  23.2 18.8 %copy-start.18 = (s32[256,1]{0,1:T(1,128)S(1)}, s32[256,1]{0,1:T(1,128)}, u32[]{:S(2)}) copy-start(s32[256,1]{0,1:T(1,128)} %param.21) | copy-start | bytes 3076
  23.2 18.8 %copy-start.16 = (s32[2,512]{1,0:T(2,128)S(1)}, s32[2,512]{1,0:T(2,128)}, u32[]{:S(2)}) copy-start(s32[2,512]{1,0:T(2,128)} %param.25) | copy-start | bytes 12292
  23.2 18.8 %copy-start.17 = (s32[2,512]{1,0:T(2,128)S(1)}, s32[2,512]{1,0:T(2,128)}, u32[]{:S(2)}) copy-start(s32[2,512]{1,0:T(2,128)} %param.24) | copy-start | bytes 12292
  41.1 13.8 %copy-start.1 = (f32[256,3,128]{2,0,1:T(8,128)S(1)}, f32[256,3,128]{2,0,1:T(8,128)}, u32[]{:S(2)}) copy-start(f32[256,3,128]{2,0,1:T(8,128)} %param.19) | copy-start | bytes 1179652
  41.3 26.5 %copy-start.4 = (f32[3,8,16,256]{3,2,1,0:T(8,128)S(1)}, f32[3,8,16,256]{3,2,1,0:T(8,128)}, u32[]{:S(2)}) copy-start(f32[3,8,16,256]{3,2,1,0:T(8,128)} %param.18) | copy-start | bytes 1179652
  44.9 30.2 %all-to-all-start.1 = ((f32[512,4,128]{2,1,0:T(4,128)}), f32[512,4,128]{2,1,0:T(4,128)S(1)}, u32[]{:S(2)}, u32[]{:S(2)}) async-start(f32[512,4,128]{2,1,0:T(4,128)} %copy.60), calls=%async_computation.1 | async-start | bytes 2097152 | tf_op jit(solution)/shard_map/all_to_all | solution.py:108
  54.8 7.0 %copy-start.15 = (s32[1024]{0:T(1024)}, s32[1024]{0:T(1024)S(1)}, u32[]{:S(2)}) copy-start(s32[1024]{0:T(1024)S(1)} %get-tuple-element.236) | copy-start | bytes 12292
  55.5 12.2 %collective-permute-start.4 = (f32[16,3,128]{2,0,1:T(8,128)S(1)}, f32[16,3,128]{2,0,1:T(8,128)S(1)}, u32[]{:S(2)}, u32[]{:S(2)}) collective-permute-start(f32[16,3,128]{2,0,1:T(8,128)S(1)} %get-tuple-element.223), channel_id=1, source_target_pairs={{0,8},{8,16},{16,24},{24,32},{32,40},{40,48},{48,56},{56,64},{64,7... | collective-permute-start | bytes 73736 | tf_op jit(solution)/shard_map/ppermute | solution.py:20
  56.6 11.1 %collective-permute-start.5 = (f32[16,3,128]{2,0,1:T(8,128)S(1)}, f32[16,3,128]{2,0,1:T(8,128)S(1)}, u32[]{:S(2)}, u32[]{:S(2)}) collective-permute-start(f32[16,3,128]{2,0,1:T(8,128)S(1)} %get-tuple-element.224), channel_id=1, source_target_pairs={{8,0},{16,8},{24,16},{32,24},{40,32},{48,40},{56,48},{64,56},{72,6... | collective-permute-start | bytes 73736 | tf_op jit(solution)/shard_map/ppermute | solution.py:22
  67.8 7.4 %copy-start.8 = (f32[3,1,16,256]{3,2,1,0:T(8,128)}, f32[3,1,16,256]{3,2,1,0:T(8,128)S(1)}, u32[]{:S(2)}) copy-start(f32[3,1,16,256]{3,2,1,0:T(8,128)S(1)} %collective-permute-done.1) | copy-start | bytes 147460
  67.9 7.3 %copy-start.9 = (f32[3,1,16,256]{3,2,1,0:T(8,128)}, f32[3,1,16,256]{3,2,1,0:T(8,128)S(1)}, u32[]{:S(2)}) copy-start(f32[3,1,16,256]{3,2,1,0:T(8,128)S(1)} %collective-permute-done) | copy-start | bytes 147460
  67.9 11.2 %copy-start.3 = (f32[3,10,16,256]{3,2,1,0:T(8,128)}, f32[3,10,16,256]{3,2,1,0:T(8,128)S(1)}, u32[]{:S(2)}) copy-start(f32[3,10,16,256]{3,2,1,0:T(8,128)S(1)} %constant_dynamic-update-slice_fusion) | copy-start | bytes 1474564
  68.0 5.5 %collective-permute-start.2 = (f32[3,10,1,256]{3,2,1,0:T(1,128)S(1)}, f32[3,10,1,256]{3,2,1,0:T(1,128)S(1)}, u32[]{:S(2)}, u32[]{:S(2)}) collective-permute-start(f32[3,10,1,256]{3,2,1,0:T(1,128)S(1)} %get-tuple-element.218), channel_id=1, source_target_pairs={{1,0},{2,1},{3,2},{4,3},{5,4},{6,5},{7,6},{9,8},{10,9},{11,10},{12... | collective-permute-start | bytes 92168 | tf_op jit(solution)/shard_map/ppermute | solution.py:22
  69.3 4.2 collective-permute-start.3
  73.5 1.7 copy-start.10
  73.5 1.7 copy-start.11
  79.1 2.3 copy-start
  81.4 5.2 %slice-start = ((f32[4,4,2,4,4,16,16]{6,5,4,2,0,3,1:T(8,128)}), f32[3,4,2,4,4,16,16]{6,5,4,2,0,3,1:T(8,128)S(1)}, s32[]{:S(2)}) async-start(f32[4,4,2,4,4,16,16]{6,5,4,2,0,3,1:T(8,128)} %copy-done), calls=%async_computation.3 | async-start | bytes 6291456 | tf_op jit(solution)/shard_map/slice | solution.py:118
  96.5 1.4 copy-start.2
  108.6 167.9 %all-to-all-start.2 = ((f32[512,4,128]{2,1,0:T(4,128)}), f32[512,4,128]{2,1,0:T(4,128)}, u32[]{:S(2)}, u32[]{:S(2)}) async-start(f32[512,4,128]{2,1,0:T(4,128)} %gather_fusion.5), calls=%async_computation.2 | async-start | bytes 2097152 | tf_op jit(solution)/shard_map/all_to_all | solution.py:131
  276.1 30.6 %copy-start.14 = (s32[1,512]{1,0:T(1,128)S(1)}, s32[1,512]{1,0:T(1,128)}, u32[]{:S(2)}) copy-start(s32[1,512]{1,0:T(1,128)} %get-tuple-element.231) | copy-start | bytes 6148
  276.1 30.6 %copy-start.19 = (f32[3]{0:T(128)S(1)}, f32[3]{0:T(128)}, u32[]{:S(2)}) copy-start(f32[3]{0:T(128)} %constant.102.clone) | copy-start | bytes 40
  276.2 30.5 %copy-start.5 = (f32[256,3,128]{2,0,1:T(8,128)S(1)}, f32[256,3,128]{2,0,1:T(8,128)}, u32[]{:S(2)}) copy-start(f32[256,3,128]{2,0,1:T(8,128)} %param.20) | copy-start | bytes 1179652
  278.9 36.8 %copy-start.12 = (s32[512]{0:T(512)S(1)}, s32[512]{0:T(512)}, u32[]{:S(2)}) copy-start(s32[512]{0:T(512)} %get-tuple-element.234) | copy-start | bytes 6148
  306.7 11.3 %copy-start.7 = (f32[256,128]{1,0:T(8,128)}, f32[256,128]{1,0:T(8,128)S(1)}, u32[]{:S(2)}) copy-start(f32[256,128]{1,0:T(8,128)S(1)} %fusion.74) | copy-start | bytes 393220
  310.2 7.2 %collective-permute-start.6 = (f32[16,3,128]{2,0,1:T(8,128)S(1)}, f32[16,3,128]{2,0,1:T(8,128)S(1)}, u32[]{:S(2)}, u32[]{:S(2)}) collective-permute-start(f32[16,3,128]{2,0,1:T(8,128)S(1)} %copy.81), channel_id=1, source_target_pairs={{0,8},{8,16},{16,24},{24,32},{32,40},{40,48},{48,56},{56,64},{64,7... | collective-permute-start | bytes 73736 | tf_op jit(solution)/shard_map/ppermute | solution.py:20
  311.0 6.4 %collective-permute-start.7 = (f32[16,3,128]{2,0,1:T(8,128)S(1)}, f32[16,3,128]{2,0,1:T(8,128)S(1)}, u32[]{:S(2)}, u32[]{:S(2)}) collective-permute-start(f32[16,3,128]{2,0,1:T(8,128)S(1)} %copy.82), channel_id=1, source_target_pairs={{8,0},{16,8},{24,16},{32,24},{40,32},{48,40},{56,48},{64,56},{72,6... | collective-permute-start | bytes 73736 | tf_op jit(solution)/shard_map/ppermute | solution.py:22
  317.9 137.9 %copy-start.6 = (f32[256,3,128]{2,0,1:T(8,128)S(1)}, f32[256,3,128]{2,0,1:T(8,128)}, u32[]{:S(2)}) copy-start(f32[256,3,128]{2,0,1:T(8,128)} %get-tuple-element.228) | copy-start | bytes 1179652
  317.9 137.9 %copy-start.13 = (s32[1,512]{1,0:T(1,128)S(1)}, s32[1,512]{1,0:T(1,128)}, u32[]{:S(2)}) copy-start(s32[1,512]{1,0:T(1,128)} %get-tuple-element.232) | copy-start | bytes 6148
where the time goes:
time: 461 us; the launch traced here: 458 us
  matrix products  204 us (44%)
  other arithmetic  101 us (22%)
  local copies, waits for them, and re-layouts  90.1 us (20%)
  starting transfers between devices  54.9 us (12%)
  waiting for transfers between devices  6.03 us (1%)
    dot_general x16, matrix products, pair_force(): jnp.einsum('gij,gcj->gci', coef, xb, precision=lax.Precision.HIGHEST)  165 us
    reduce_sum x16, other arithmetic, pair_force(): total = jnp.sum(coef, axis=2)  84.8 us
    gather x32, local copies, waits for them, and re-layouts, one_group(): return pair_force(extended[pair[0]], extended[pair[1]])  38 us
    dot_general x8, matrix products, pick_cells(): jnp.einsum('qkc,qic->qki', fluid_part, onehot, precision=lax.Precision.HI...  15.8 us
    all_to_all x1, starting transfers between devices, per_device(): lax.all_to_all(answer, ('gx', 'gy'), split_axis=0, concat_axis=0, tiled=T...  12.8 us
    all_to_all x1, starting transfers between devices, per_device(): lax.all_to_all(send_ids, ('gx', 'gy'), split_axis=0, concat_axis=0, tiled...  11.8 us
    dot_general x8, matrix products, histogram(): jnp.einsum('qki,qic->qkc', load_part, onehot, precision=lax.Precision.HIG...  11.7 us
    ppermute x4, starting transfers between devices, padded_2(): lax.ppermute(head, axis, [((i + 1) % count, i) for i in range(ends)])  11.4 us
  transfers between devices with their start and end apart: 11, of which 2 were waited for; matrix products, arithmetic and copies ran while one was open for 41% of the time, Pallas kernels for 0%

commit v1 on v0

v1 whole, which is shorter than its diff:
```python
import functools

import jax
import jax.numpy as jnp
from jax import lax
from jax.experimental import pallas as pl
from jax.experimental.pallas import tpu as pltpu
from jax.sharding import PartitionSpec as P

F32 = jnp.float32
BF16 = jnp.bfloat16
CAP = 4
EPS2 = 0.0025
VMEM = pl.BlockSpec(memory_space=pltpu.VMEM)
SMEM = pl.BlockSpec(memory_space=pltpu.SMEM)
PARAMS = dict(vmem_limit_bytes=48 * 1024 * 1024)


def split2(x):
    hi = x.astype(BF16)
    return hi, (x - hi.astype(F32)).astype(BF16)


def onehot_cells(row):
    cells = lax.broadcasted_iota(jnp.int32, (128, 128), 0)
    return (cells == jnp.broadcast_to(row, (128, 128))).astype(F32).astype(BF16)


def dot(a, b, dims=((1,), (0,))):
    return lax.dot_general(a, b, (dims, ((), ())), preferred_element_type=F32)


def pack_rows(halo, pos, out, first, half):
    for j in range(16):
        q = halo[half * 16 + j]
        for m in range(3):
            out[pl.ds(first + m * 16 + j, 1), :] = pos[m, pl.ds(q, 1), :]


def faces_kernel(halo, fv, pos, down_out, up_out, left_out, right_out):
    sx = fv.shape[1]
    for out, x, half in ((down_out, 0, 0), (up_out, sx - 1, 1)):
        for m in range(3):
            for h in range(2):
                out[(m * 2 + h) * 16 : (m * 2 + h + 1) * 16, :] = fv[m, x, :, h * 128 : (h + 1) * 128]
        pack_rows(halo, pos, out, 96, half)
    for out, y in ((left_out, 0), (right_out, fv.shape[2] - 1)):
        for m in range(3):
            out[m, :, :] = fv[m, :, y, :]


def deposit_kernel(owner, local, cell, vel, out, slot_out, taken):
    blocks = cell.shape[0]
    lanes = lax.broadcasted_iota(jnp.int32, (4, 128), 1)
    rows4 = lax.broadcasted_iota(jnp.int32, (4, 128), 0)
    mark = (lanes == 127) & (rows4 == 0)
    out[...] = jnp.broadcast_to(jnp.where(mark, -1.0, 0.0).astype(F32)[None], out.shape)

    def clear(t, c):
        taken[t] = 0
        return c

    lax.fori_loop(0, taken.shape[0], clear, 0, unroll=8)
    r8 = lax.broadcasted_iota(jnp.int32, (8, 128), 0)

    def group(g, c):
        base = pl.multiple_of(g * 8, 8)
        cells8 = cell[pl.ds(base, 8), :]
        v = [vel[m, pl.ds(base, 8), :] for m in range(3)]
        for k in range(8):
            q = base + k
            hot = onehot_cells(cells8[k : k + 1, :])
            rows = [jnp.broadcast_to(v[m][k : k + 1, :], (8, 128)) for m in range(3)]
            load = jnp.where(r8 == 1, rows[0], jnp.where(r8 == 2, rows[1], rows[2]))
            load = jnp.where(r8 == 0, 1.0, jnp.where(r8 < 4, load, 0.0))
            hi = load.astype(BF16).astype(F32)
            lhs = jnp.concatenate([hi, load - hi], axis=0).astype(BF16)
            both = dot(lhs, hot, ((1,), (1,)))
            both = both[0:8] + both[8:16]
            tile = owner[q]
            rank = taken[tile]
            taken[tile] = rank + 1
            slot = tile * CAP + rank
            slot_out[q] = slot
            ident = jnp.full((4, 128), local[q], jnp.int32).astype(F32)
            out[slot] = jnp.where(mark, ident, both[0:4])
        return c

    lax.fori_loop(0, blocks // 8, group, 0)


def swap_groups(v):
    row = lax.broadcasted_iota(jnp.int32, v.shape, 1)
    grp = lax.broadcasted_iota(jnp.int32, v.shape, 2) // 16
    for s in range(3):
        step = 1 << s
        ra, gb = (row >> s) & 1, (grp >> s) & 1
        up = pltpu.roll(pltpu.roll(v, 8 - step, 1), 16 * step, 2)
        dn = pltpu.roll(pltpu.roll(v, step, 1), 128 - 16 * step, 2)
        v = jnp.where(ra == gb, v, jnp.where(ra < gb, up, dn))
    return v


def fluid_kernel(xlo_on, recv, fv, from_low, from_high, from_left, from_right, fluid, answer, grid):
    sx, sy, sz = fv.shape[1:]
    slots = recv.shape[0] // 4
    bricks = sx // 2 * (sy // 4) * (sz // 16)
    count = recv[pl.ds(0, slots, stride=4), :]
    lane = lax.broadcasted_iota(jnp.int32, (slots, 128), 1)
    ident = count[:, 127:128]
    ident_row = count.T[127:128, :]
    wide = lax.broadcasted_iota(jnp.int32, (slots, bricks), 1).astype(F32)
    by_slot = (wide == jnp.broadcast_to(ident, (slots, bricks))).astype(F32).astype(BF16)
    tall = lax.broadcasted_iota(jnp.int32, (bricks, slots), 0).astype(F32)
    by_brick = (tall == jnp.broadcast_to(ident_row, (bricks, slots))).astype(F32).astype(BF16)
    parts = [jnp.where(lane == 127, 1.0, count).astype(BF16)]
    for m in range(3):
        parts += list(split2(recv[pl.ds(m + 1, slots, stride=4), :]))
    summed = dot(by_brick, jnp.concatenate(parts, axis=1))
    cnt = summed[:, 0:128]
    momentum = [summed[:, (1 + 2 * m) * 128 : (2 + 2 * m) * 128] + summed[:, (2 + 2 * m) * 128 : (3 + 2 * m) * 128] for m in range(3)]
    last = lax.broadcasted_iota(jnp.int32, (bricks, 128), 1) == 127
    others = jnp.sum(jnp.where(last, 0.0, cnt), axis=1, keepdims=True)
    cnt = jnp.where(last, 128.0 * cnt - others, cnt)
    solid = 0.5 * cnt
    voids = 1.0 - 0.6 * solid / (1.0 + solid)
    beta = (1.0 - voids) / (voids * voids)
    scale = 0.15 * beta
    sources = [scale * momentum[m] for m in range(3)] + [scale * cnt]
    for c in range(4):
        moved = swap_groups(sources[c].reshape(bricks // 8, 8, 128))
        for bx in range(sx // 2):
            for by in range(sy // 4):
                for h in range(2):
                    v = moved[(bx * 4 + by) * 2 + h]
                    for x in range(2):
                        grid[c, bx * 2 + x, by * 4 : by * 4 + 4, h * 128 : h * 128 + 128] = v[x * 4 : x * 4 + 4, :]
    yrow = lax.broadcasted_iota(jnp.int32, (sy, sz), 0)
    zlane = lax.broadcasted_iota(jnp.int32, (sy, sz), 1)
    low_on = (xlo_on[0]).astype(F32)
    high_on = (xlo_on[1]).astype(F32)
    for m in range(3):
        low = jnp.concatenate([from_low[(m * 2 + h) * 16 : (m * 2 + h + 1) * 16, :] for h in range(2)], axis=1) * low_on
        high = jnp.concatenate([from_high[(m * 2 + h) * 16 : (m * 2 + h + 1) * 16, :] for h in range(2)], axis=1) * high_on
        for x in range(sx):
            f = fv[m, x]
            beside = (fv[m, x + 1] if x < sx - 1 else high) + (fv[m, x - 1] if x > 0 else low)
            right = jnp.broadcast_to(from_right[m, x : x + 1, :], (sy, sz))
            left = jnp.broadcast_to(from_left[m, x : x + 1, :], (sy, sz))
            beside = beside + jnp.where(yrow == sy - 1, right, pltpu.roll(f, sy - 1, 0))
            beside = beside + jnp.where(yrow == 0, left, pltpu.roll(f, 1, 0))
            beside = beside + jnp.where(zlane == sz - 1, 0.0, pltpu.roll(f, sz - 1, 1))
            beside = beside + jnp.where(zlane == 0, 0.0, pltpu.roll(f, 1, 1))
            fluid[m, x] = f + 0.1 * (beside - 6.0 * f) + (grid[m, x] - grid[3, x] * f)
    table = []
    for m in range(3):
        tiles = []
        for bx in range(sx // 2):
            for by in range(sy // 4):
                for h in range(2):
                    tiles.append(
                        jnp.concatenate(
                            [fluid[m, bx * 2 + x, by * 4 : by * 4 + 4, h * 128 : h * 128 + 128] for x in range(2)],
                            axis=0,
                        )
                    )
        v = swap_groups(jnp.stack(tiles, axis=0)).reshape(bricks, 128)
        table += list(split2(v))
    table += list(split2(beta))
    found = dot(by_slot, jnp.concatenate(table, axis=1))
    for c in range(4):
        answer[pl.ds(c, slots, stride=4), :] = (
            found[:, 2 * c * 128 : (2 * c + 1) * 128] + found[:, (2 * c + 1) * 128 : (2 * c + 2) * 128]
        )


def feature_rows(x):
    hi, lo, both = [], [], []
    for m in range(3):
        u = x[m] - 0.5
        h = u.astype(BF16).astype(F32)
        l = (u - h).astype(BF16).astype(F32)
        hi.append(h)
        lo.append(l)
        both.append(h + l)
    return hi, lo, both, both[0] * both[0] + both[1] * both[1] + both[2] * both[2]


def split3(n):
    a = n.astype(BF16).astype(F32)
    b = (n - a).astype(BF16).astype(F32)
    return a, b, n - a - b


def push_loop(step, first, second, pos, low, high, push, feat_b, feat_a, base_a):
    blocks = pos.shape[1]
    one = jnp.ones((8, 128), F32)
    zero = jnp.zeros((8, 128), F32)

    def put(ref, rows, stride, q0, feats):
        for k, v in enumerate(feats):
            ref[pl.ds(q0 * stride + k, 8, stride=stride), :] = v

    def own(g, c):
        q0 = pl.multiple_of(g * 8, 8)
        hi, lo, both, norm = feature_rows([pos[m, pl.ds(q0, 8), :] for m in range(3)])
        n = split3(norm)
        put(feat_b, 16, 16, q0, hi + [one, n[0], n[1], n[2], one] + lo + [zero, one, zero, zero, zero])
        n = split3(norm + EPS2)
        h2, l2 = [-2.0 * v for v in hi], [-2.0 * v for v in lo]
        put(
            feat_a, 32, 32, q0,
            h2 + [n[0], one, one, one, n[1]] + h2 + [zero, n[2], zero, zero, zero]
            + l2 + [zero] * 5 + l2 + [zero] * 5,
        )
        put(base_a, 8, 8, q0, both + [zero] * 5)
        return c

    lax.fori_loop(0, blocks // 8, own, 0)
    for i, (ref, at) in enumerate((low, high)):
        for g in range(2):
            hi, lo, _, norm = feature_rows([ref[at + m * 16 + g * 8 : at + m * 16 + g * 8 + 8, :] for m in range(3)])
            n = split3(norm)
            put(feat_b, 16, 16, blocks + i * 16 + g * 8, hi + [one, n[0], n[1], n[2], one] + lo + [zero, one, zero, zero, zero])
    push[...] = jnp.zeros(push.shape, F32)

    def one_pair(p):
        a = first[step, p]
        b = second[step, p]
        fb = feat_b[pl.ds(pl.multiple_of(b * 16, 16), 16), :]
        ga = feat_a[pl.ds(pl.multiple_of(a * 32, 32), 32), :].astype(BF16)
        fbt = jnp.concatenate([fb, fb], axis=0).T.astype(BF16)
        r2 = dot(fbt, ga)
        w = jnp.maximum(lax.rsqrt(jnp.maximum(r2, EPS2)) - 4.0, 0.0)
        hi, lo = split2(w)
        lhs = fb.astype(BF16)
        res = dot(lhs, hi) + dot(lhs, lo)
        res = res[0:8] + res[8:16]
        ua = base_a[pl.ds(pl.multiple_of(a * 8, 8), 8), :]
        return a, ua * jnp.broadcast_to(res[3:4], (8, 128)) - res

    unroll = 4

    def pairs(g, c):
        done = [one_pair(g * unroll + k) for k in range(unroll)]
        for a, f in done:
            rows = pl.ds(pl.multiple_of(a * 8, 8), 8)
            push[rows, :] = push[rows, :] + f
        return c

    lax.fori_loop(0, first.shape[1] // unroll, pairs, 0)


def push_kernel(first, second, pos, low, high, push, feat_b, feat_a, base_a):
    push_loop(0, first, second, pos, (low, 96), (high, 96), push, feat_b, feat_a, base_a)


def advance(pos, vel, push, flow, pos_out, vel_out):
    blocks = pos.shape[1]
    drift = 2.0 * flow[pl.ds(3, blocks, stride=8), :]
    for m in range(3):
        v = vel[m]
        force = 2.5 * push[pl.ds(m, blocks, stride=8), :] + drift * (flow[pl.ds(m, blocks, stride=8), :] - v)
        if m == 2:
            force = force - 1.0
        v = v + 0.1 * force
        vel_out[m] = v
        pos_out[m] = pos[m] + 0.1 * v


def pick_kernel(slot, halo, back, cell, pos, vel, push, flow, pos_out, vel_out, down_out, up_out):
    def group(g, c):
        base = pl.multiple_of(g * 8, 8)
        cells8 = cell[pl.ds(base, 8), :]
        for k in range(8):
            q = base + k
            hot = onehot_cells(cells8[k : k + 1, :])
            v = back[slot[q]]
            v = jnp.concatenate([v, v], axis=0)
            hi = v.astype(BF16).astype(F32)
            lhs = jnp.concatenate([hi, v - hi], axis=0).astype(BF16)
            both = dot(lhs, hot)
            flow[pl.ds(pl.multiple_of(q * 8, 8), 8), :] = both[0:8] + both[8:16]
        return c

    lax.fori_loop(0, cell.shape[0] // 8, group, 0)
    advance(pos, vel, push, flow, pos_out, vel_out)
    pack_rows(halo, pos_out, down_out, 0, 0)
    pack_rows(halo, pos_out, up_out, 0, 1)


def last_kernel(first, second, pos, vel, low, high, flow, pos_out, vel_out, push, feat_b, feat_a, base_a):
    push_loop(1, first, second, pos, (low, 0), (high, 0), push, feat_b, feat_a, base_a)
    advance(pos, vel, push, flow, pos_out, vel_out)


def call(kernel, in_specs, out_shape, out_specs, scratch=(), cost=None):
    return pl.pallas_call(
        kernel,
        in_specs=in_specs,
        out_shape=out_shape,
        out_specs=out_specs,
        scratch_shapes=list(scratch),
        compiler_params=pltpu.CompilerParams(**PARAMS),
        cost_estimate=cost,
    )


def shape(*dims, dtype=F32):
    return jax.ShapeDtypeStruct(dims, dtype)


def per_device(
    fluid_vel,
    part_pos,
    part_vel,
    brick_owner,
    brick_local,
    cell_in_brick,
    pair_self,
    pair_other,
    halo_list,
):
    nx, ny = lax.axis_size("gx"), lax.axis_size("gy")
    tiles = nx * ny
    blocks = part_pos.shape[0]
    slots = tiles * CAP
    sx, sy, sz = fluid_vel.shape[1:]
    pos = jnp.transpose(part_pos, (1, 0, 2))
    vel = jnp.transpose(part_vel, (1, 0, 2))

    down, up, left, right = call(
        faces_kernel,
        [SMEM, VMEM, VMEM],
        [shape(144, 128), shape(144, 128), shape(3, sx, sz), shape(3, sx, sz)],
        [VMEM] * 4,
    )(halo_list, fluid_vel, pos)
    fwd = [(i, (i + 1) % nx) for i in range(nx)]
    bwd = [((i + 1) % nx, i) for i in range(nx)]
    from_low = lax.ppermute(up, "gx", fwd)
    from_high = lax.ppermute(down, "gx", bwd)
    from_left = lax.ppermute(right, "gy", [(i, i + 1) for i in range(ny - 1)])
    from_right = lax.ppermute(left, "gy", [(i + 1, i) for i in range(ny - 1)])

    send, slot = call(
        deposit_kernel,
        [SMEM, SMEM, VMEM, VMEM],
        [shape(slots, 4, 128), shape(blocks, dtype=jnp.int32)],
        [VMEM, SMEM],
        [pltpu.SMEM((tiles,), jnp.int32)],
    )(brick_owner[:, 0], brick_local, cell_in_brick, vel)
    recv = lax.all_to_all(send.reshape(slots * 4, 128), ("gx", "gy"), split_axis=0, concat_axis=0, tiled=True)

    pair_scratch = [
        pltpu.VMEM(((blocks + 32) * 16, 128), F32),
        pltpu.VMEM((blocks * 32, 128), F32),
        pltpu.VMEM((blocks * 8, 128), F32),
    ]
    push = call(
        push_kernel,
        [SMEM, SMEM, VMEM, VMEM, VMEM],
        shape(blocks * 8, 128),
        VMEM,
        pair_scratch,
        pl.CostEstimate(flops=20_000_000_000, bytes_accessed=2_000_000, transcendentals=8_000_000),
    )(pair_self, pair_other, pos, from_low, from_high)

    me = lax.axis_index("gx")
    ends = jnp.stack([me > 0, me < nx - 1]).astype(jnp.int32)
    fluid, answer = call(
        fluid_kernel,
        [SMEM] + [VMEM] * 6,
        [shape(3, sx, sy, sz), shape(slots * 4, 128)],
        [VMEM] * 2,
        [pltpu.VMEM((4, sx, sy, sz), F32)],
    )(ends, recv, fluid_vel, from_low, from_high, from_left, from_right)
    back = lax.all_to_all(answer, ("gx", "gy"), split_axis=0, concat_axis=0, tiled=True)

    flow, pos, vel, down, up = call(
        pick_kernel,
        [SMEM, SMEM] + [VMEM] * 5,
        [shape(blocks * 8, 128), shape(3, blocks, 128), shape(3, blocks, 128), shape(48, 128), shape(48, 128)],
        [VMEM] * 5,
    )(slot, halo_list, back.reshape(slots, 4, 128), cell_in_brick, pos, vel, push)
    low = lax.ppermute(up, "gx", fwd)
    high = lax.ppermute(down, "gx", bwd)
    pos, vel = call(
        last_kernel,
        [SMEM, SMEM] + [VMEM] * 5,
        [shape(3, blocks, 128), shape(3, blocks, 128)],
        [VMEM] * 2,
        [pltpu.VMEM((blocks * 8, 128), F32)] + pair_scratch,
    )(pair_self, pair_other, pos, vel, low, high, flow)
    return fluid, jnp.transpose(pos, (1, 0, 2)), jnp.transpose(vel, (1, 0, 2))


def solution(mesh):
    in_specs = (
        P(None, "gx", "gy", None),
        P(("gx", "gy"), None, None),
        P(("gx", "gy"), None, None),
        P(("gx", "gy"), None),
        P(("gx", "gy")),
        P(("gx", "gy"), None),
        P(None, ("gx", "gy")),
        P(None, ("gx", "gy")),
        P(("gx", "gy")),
    )
    out_specs = (
        P(None, "gx", "gy", None),
        P(("gx", "gy"), None, None),
        P(("gx", "gy"), None, None),
    )
    return jax.shard_map(
        per_device, mesh=mesh, in_specs=in_specs, out_specs=out_specs, check_vma=False
    )
```

time: 461 us -> 223 us (0.48)
  matrix products: 204 us -> 0 us
  Pallas kernels: 0 us -> 176 us
  other arithmetic: 101 us -> 0.07 us
  local copies, waits for them, and re-layouts: 90.1 us -> 3.24 us
  starting transfers between devices: 54.9 us -> 30.7 us
  waiting for transfers between devices: 6.03 us -> 11.2 us
    dot_general x38 -> x0, matrix products: 204 us -> none  [the longest x16 165 us: pair_force(): jnp.einsum('gij,gcj->gci', coef, xb, precision=lax.Precision.HIGHEST)]
    pallas_call x0 -> x6, Pallas kernels: none -> 176 us  [the longest x1 77.7 us: per_device(): call(last_kernel, [SMEM, SMEM] + [VMEM] * 5, [shape(3, blocks, 128), shap...]
    reduce_sum x16 -> x0, other arithmetic: 84.8 us -> none  [pair_force(): total = jnp.sum(coef, axis=2)]
    gather x36 -> x0, local copies, waits for them, and re-layouts: 44.4 us -> none  [the longest x32 38 us: one_group(): return pair_force(extended[pair[0]], extended[pair[1]])]
    eq x17 -> x0, local copies, waits for them, and re-layouts: 11.6 us -> none  [the longest x8 5.79 us: histogram(): cell_part[:, :, None] == cells_iota[None, None, :]]
    all_to_all x2 -> x1, starting transfers between devices: 21.5 us -> 11.1 us  [per_device(): lax.all_to_all(send.reshape(slots * 4, 128), ('gx', 'gy'), split_axis=0,...]
    slice x42 -> x0, local copies, waits for them, and re-layouts: 10.1 us -> none  [the longest x4 4.67 us: per_device(): momentum = dep_grid[1:]]
    all_to_all x1, starting transfers between devices: 12.8 us -> 5.46 us  [per_device(): lax.all_to_all(answer, ('gx', 'gy'), split_axis=0, concat_axis=0, tiled=T...]
  transfers between devices with their start and end apart: 11 -> 8, of which waited for: 2 -> 3; matrix products, arithmetic and copies ran while one was open for 41% -> 0% of each run, Pallas kernels for 0% -> 35%
where the time goes in v1:
time: 223 us; the launch traced here: 222 us
  Pallas kernels  176 us (79%)
  starting transfers between devices  30.7 us (14%)
  waiting for transfers between devices  11.2 us (5%)
  local copies, waits for them, and re-layouts  3.24 us (1%)
    pallas_call x1, Pallas kernels, per_device(): call(last_kernel, [SMEM, SMEM] + [VMEM] * 5, [shape(3, blocks, 128), shap...  77.7 us
    pallas_call x1, Pallas kernels, per_device(): call(push_kernel, [SMEM, SMEM, VMEM, VMEM, VMEM], shape(blocks * 8, 128),...  76.2 us
    all_to_all x1, starting transfers between devices, per_device(): lax.all_to_all(send.reshape(slots * 4, 128), ('gx', 'gy'), split_axis=0,...  11.1 us
    pallas_call x1, Pallas kernels, per_device(): call(deposit_kernel, [SMEM, SMEM, VMEM, VMEM], [shape(slots, 4, 128), sha...  9.98 us
    pallas_call x1, Pallas kernels, per_device(): call(pick_kernel, [SMEM, SMEM] + [VMEM] * 5, [shape(blocks * 8, 128), sha...  7.85 us
    ppermute x1, waiting for transfers between devices, per_device(): from_low = lax.ppermute(up, 'gx', fwd)  7.07 us
    all_to_all x1, starting transfers between devices, per_device(): lax.all_to_all(answer, ('gx', 'gy'), split_axis=0, concat_axis=0, tiled=T...  5.46 us
  transfers between devices with their start and end apart: 8, of which 3 were waited for; matrix products, arithmetic and copies ran while one was open for 0% of the time, Pallas kernels for 35%

profile of v1, /device:TPU:0, one launch (start us, length us, event | category | flops | bytes accessed | tf_op | source)
XLA Modules:
  0.0 222.4 jit_solution(16265364237164504977)
XLA Ops:
  0.6 0.0 copy-start.10
  0.6 0.0 copy-start.9
  0.7 0.7 copy-done.10
  1.3 0.0 copy-done.9
  1.3 0.0 copy-start
  1.3 1.0 copy-done
  2.3 0.0 copy-start.4
  2.3 0.9 copy-done.4
  3.2 10.0 %shard_map.112 = (f32[512,4,128]{2,1,0:T(4,128)}, s32[256]{0:T(256)S(1)}) custom-call(s32[256]{0:T(256)S(1)} %bitcast.18, s32[256]{0:T(256)S(1)} %copy-done.10, s32[256,128]{1,0:T(8,128)S(1)} %copy-done.4, f32[3,256,128]{2,1,0:T(8,128)S(1)} %bitcast.13), custom_call_target="tpu_custom_call" | custom-call | tf_op jit(solution)/shard_map/pallas_call | solution.py:345
  13.2 0.0 copy-start.2
  13.2 0.0 copy-start.3
  13.2 11.1 %all-to-all-start = ((f32[128,16,128]{2,1,0:T(8,128)}), f32[128,16,128]{2,1,0:T(8,128)S(1)}, u32[]{:S(2)}, u32[]{:S(2)}) async-start(f32[128,16,128]{2,1,0:T(8,128)} %bitcast.4), calls=%async_computation | async-start | bytes 2097152 | tf_op jit(solution)/shard_map/all_to_all | solution.py:352
  24.4 0.0 copy-start.8
  24.4 0.0 copy-done.2
  24.4 0.0 copy-done.3
  24.4 0.6 copy-done.8
  25.1 0.6 shard_map.113
  25.7 1.3 collective-permute-start.2
  27.0 1.3 collective-permute-start.3
  28.3 1.9 collective-permute-start
  30.2 4.1 %collective-permute-start.1 = (f32[144,128]{1,0:T(8,128)S(1)}, f32[144,128]{1,0:T(8,128)S(1)}, u32[]{:S(2)}, u32[]{:S(2)}) collective-permute-start(f32[144,128]{1,0:T(8,128)S(1)} %get-tuple-element.20), channel_id=1, source_target_pairs={{8,0},{16,8},{24,16},{32,24},{40,32},{48,40},{56,48},{64,56},{72,6... | collective-permute-start | bytes 221192 | tf_op jit(solution)/shard_map/ppermute | solution.py:341
  34.3 0.1 add_convert_fusion.xlo_on
  34.4 0.0 collective-permute-done.2.from_left
  34.4 0.0 collective-permute-done.3.from_right
  34.4 7.1 %collective-permute-done.from_low.low = f32[144,128]{1,0:T(8,128)S(1)} collective-permute-done((f32[144,128]{1,0:T(8,128)S(1)}, f32[144,128]{1,0:T(8,128)S(1)}, u32[]{:S(2)}, u32[]{:S(2)}) %collective-permute-start) | collective-permute-done | bytes 73760 | tf_op jit(solution)/shard_map/ppermute | solution.py:340
  41.5 0.0 collective-permute-done.1.from_high.high
  41.5 2.3 %all-to-all-done = f32[128,16,128]{2,1,0:T(8,128)S(1)} async-done(((f32[128,16,128]{2,1,0:T(8,128)}), f32[128,16,128]{2,1,0:T(8,128)S(1)}, u32[]{:S(2)}, u32[]{:S(2)}) %all-to-all-start) | async-done | bytes 1048608 | tf_op jit(solution)/shard_map/all_to_all | solution.py:352
  43.8 4.0 %shard_map.114 = (f32[3,8,16,256]{3,2,1,0:T(8,128)}, f32[2048,128]{1,0:T(8,128)}) custom-call(s32[2]{0:T(128)S(1)} %add_convert_fusion.xlo_on, f32[2048,128]{1,0:T(8,128)S(1)} %bitcast.11, f32[3,8,16,256]{3,2,1,0:T(8,128)S(1)} %copy-done.3, f32[144,128]{1,0:T(8,128)S(1)} %collective-permute-done.from_low.low, ...), custom_call_target="tpu_custom_call" | custom-call | tf_op jit(solution)/shard_map/pallas_call | solution.py:370
  47.8 0.0 copy-start.6
  47.8 0.0 copy-start.7
  47.8 5.5 %all-to-all-start.1 = ((f32[128,16,128]{2,1,0:T(8,128)}), f32[128,16,128]{2,1,0:T(8,128)S(1)}, u32[]{:S(2)}, u32[]{:S(2)}) async-start(f32[128,16,128]{2,1,0:T(8,128)} %bitcast.7), calls=%async_computation.1 | async-start | bytes 2097152 | tf_op jit(solution)/shard_map/all_to_all | solution.py:377
  53.3 0.0 copy-done.6
  53.3 0.0 copy-done.7
  53.3 0.0 copy-start.1
  53.3 0.0 copy-start.5
  53.3 76.2 %shard_map.115.push = f32[2048,128]{1,0:T(8,128)S(1)} custom-call(s32[2,512]{1,0:T(2,128)S(1)} %copy-done.6, s32[2,512]{1,0:T(2,128)S(1)} %copy-done.7, f32[3,256,128]{2,1,0:T(8,128)S(1)} %bitcast.16, f32[144,128]{1,0:T(8,128)S(1)} %collective-permute-done.from_low.low, f32[144,128]{1,0:T(8,128)S(1)} %collective-permute-done.1.from_high.high), custom_call_target="tpu_custom_call" | custom-call | flops 20000000000 | bytes 2000000 | tf_op jit(solution)/shard_map/pallas_call | solution.py:359
  129.5 0.0 all-to-all-done.1
  129.6 0.0 copy-done.1
  129.6 0.0 copy-done.5
  129.6 7.9 %shard_map.116 = (f32[2048,128]{1,0:T(8,128)S(1)}, f32[3,256,128]{2,1,0:T(8,128)S(1)}, f32[3,256,128]{2,1,0:T(8,128)S(1)}, f32[48,128]{1,0:T(8,128)S(1)}, f32[48,128]{1,0:T(8,128)S(1)}) custom-call(s32[256]{0:T(256)S(1)} %get-tuple-element.24.slot, s32[32]{0:T(128)S(1)} %copy-done.8, f32[512,4,128]{2,1,0:T(4,128)S(1)} %bitcast.12, s32[256,128]{1,0:T(8,128)S(1)} %copy-done.5, ...), custom_call_target="tpu_custom_call" | custom-call | tf_op jit(solution)/shard_map/pallas_call | solution.py:379
  137.4 1.1 collective-permute-start.4
  138.6 4.3 %collective-permute-start.5 = (f32[48,128]{1,0:T(8,128)S(1)}, f32[48,128]{1,0:T(8,128)S(1)}, u32[]{:S(2)}, u32[]{:S(2)}) collective-permute-start(f32[48,128]{1,0:T(8,128)S(1)} %get-tuple-element.29), channel_id=1, source_target_pairs={{8,0},{16,8},{24,16},{32,24},{40,32},{48,40},{56,48},{64,56},{72,6... | collective-permute-start | bytes 73736 | tf_op jit(solution)/shard_map/ppermute | solution.py:386
  142.9 1.8 collective-permute-done.4.low
  144.7 0.0 collective-permute-done.5.high
  144.7 77.7 %shard_map.117 = (f32[3,256,128]{2,1,0:T(8,128)}, f32[3,256,128]{2,1,0:T(8,128)}) custom-call(s32[2,512]{1,0:T(2,128)S(1)} %copy-done.6, s32[2,512]{1,0:T(2,128)S(1)} %copy-done.7, f32[3,256,128]{2,1,0:T(8,128)S(1)} %get-tuple-element.26.pos, f32[3,256,128]{2,1,0:T(8,128)S(1)} %get-tuple-element.27.vel, f32[48,128]{1,0:T(8,128)S(1)} %collective-permute-done.4.low, ...), custom_call_target="tpu_custom_call" | custom-call | tf_op jit(solution)/shard_map/pallas_call | solution.py:387
Async XLA Ops:
  0.6 0.7 copy-start.10
  0.6 0.7 copy-start.9
  1.3 1.0 copy-start
  2.3 0.9 copy-start.4
  13.2 11.2 %copy-start.2 = (f32[256,3,128]{2,0,1:T(8,128)S(1)}, f32[256,3,128]{2,0,1:T(8,128)}, u32[]{:S(2)}) copy-start(f32[256,3,128]{2,0,1:T(8,128)} %param.10) | copy-start | bytes 1179652
  13.2 11.2 %copy-start.3 = (f32[3,8,16,256]{3,2,1,0:T(8,128)S(1)}, f32[3,8,16,256]{3,2,1,0:T(8,128)}, u32[]{:S(2)}) copy-start(f32[3,8,16,256]{3,2,1,0:T(8,128)} %fv.3) | copy-start | bytes 1179652
  13.2 30.6 %all-to-all-start = ((f32[128,16,128]{2,1,0:T(8,128)}), f32[128,16,128]{2,1,0:T(8,128)S(1)}, u32[]{:S(2)}, u32[]{:S(2)}) async-start(f32[128,16,128]{2,1,0:T(8,128)} %bitcast.4), calls=%async_computation | async-start | bytes 2097152 | tf_op jit(solution)/shard_map/all_to_all | solution.py:352
  24.4 0.7 copy-start.8
  25.7 8.7 %collective-permute-start.2 = (f32[3,8,256]{2,1,0:T(8,128)S(1)}, f32[3,8,256]{2,1,0:T(8,128)S(1)}, u32[]{:S(2)}, u32[]{:S(2)}) collective-permute-start(f32[3,8,256]{2,1,0:T(8,128)S(1)} %get-tuple-element.21), channel_id=1, source_target_pairs={{0,1},{1,2},{2,3},{3,4},{4,5},{5,6},{6,7},{8,9},{9,10},{10,11},{11... | collective-permute-start | bytes 73736 | tf_op jit(solution)/shard_map/ppermute | solution.py:342
  27.0 7.4 %collective-permute-start.3 = (f32[3,8,256]{2,1,0:T(8,128)S(1)}, f32[3,8,256]{2,1,0:T(8,128)S(1)}, u32[]{:S(2)}, u32[]{:S(2)}) collective-permute-start(f32[3,8,256]{2,1,0:T(8,128)S(1)} %get-tuple-element.22), channel_id=1, source_target_pairs={{1,0},{2,1},{3,2},{4,3},{5,4},{6,5},{7,6},{9,8},{10,9},{11,10},{12... | collective-permute-start | bytes 73736 | tf_op jit(solution)/shard_map/ppermute | solution.py:343
  28.3 13.1 %collective-permute-start = (f32[144,128]{1,0:T(8,128)S(1)}, f32[144,128]{1,0:T(8,128)S(1)}, u32[]{:S(2)}, u32[]{:S(2)}) collective-permute-start(f32[144,128]{1,0:T(8,128)S(1)} %get-tuple-element.19), channel_id=1, source_target_pairs={{0,8},{8,16},{16,24},{24,32},{32,40},{40,48},{48,56},{56,64},{64,7... | collective-permute-start | bytes 221192 | tf_op jit(solution)/shard_map/ppermute | solution.py:340
  30.2 11.3 %collective-permute-start.1 = (f32[144,128]{1,0:T(8,128)S(1)}, f32[144,128]{1,0:T(8,128)S(1)}, u32[]{:S(2)}, u32[]{:S(2)}) collective-permute-start(f32[144,128]{1,0:T(8,128)S(1)} %get-tuple-element.20), channel_id=1, source_target_pairs={{8,0},{16,8},{24,16},{32,24},{40,32},{48,40},{56,48},{64,56},{72,6... | collective-permute-start | bytes 221192 | tf_op jit(solution)/shard_map/ppermute | solution.py:341
  47.8 5.5 %copy-start.6 = (s32[2,512]{1,0:T(2,128)S(1)}, s32[2,512]{1,0:T(2,128)}, u32[]{:S(2)}) copy-start(s32[2,512]{1,0:T(2,128)} %first.3) | copy-start | bytes 12292
  47.8 5.5 %copy-start.7 = (s32[2,512]{1,0:T(2,128)S(1)}, s32[2,512]{1,0:T(2,128)}, u32[]{:S(2)}) copy-start(s32[2,512]{1,0:T(2,128)} %second.3) | copy-start | bytes 12292
  47.8 81.8 %all-to-all-start.1 = ((f32[128,16,128]{2,1,0:T(8,128)}), f32[128,16,128]{2,1,0:T(8,128)S(1)}, u32[]{:S(2)}, u32[]{:S(2)}) async-start(f32[128,16,128]{2,1,0:T(8,128)} %bitcast.7), calls=%async_computation.1 | async-start | bytes 2097152 | tf_op jit(solution)/shard_map/all_to_all | solution.py:377
  53.3 76.3 %copy-start.1 = (f32[256,3,128]{2,0,1:T(8,128)S(1)}, f32[256,3,128]{2,0,1:T(8,128)}, u32[]{:S(2)}) copy-start(f32[256,3,128]{2,0,1:T(8,128)} %param.11) | copy-start | bytes 1179652
  53.3 76.3 %copy-start.5 = (s32[256,128]{1,0:T(8,128)S(1)}, s32[256,128]{1,0:T(8,128)}, u32[]{:S(2)}) copy-start(s32[256,128]{1,0:T(8,128)} %cell.3) | copy-start | bytes 393220
  137.4 7.2 %collective-permute-start.4 = (f32[48,128]{1,0:T(8,128)S(1)}, f32[48,128]{1,0:T(8,128)S(1)}, u32[]{:S(2)}, u32[]{:S(2)}) collective-permute-start(f32[48,128]{1,0:T(8,128)S(1)} %get-tuple-element.28), channel_id=1, source_target_pairs={{0,8},{8,16},{16,24},{24,32},{32,40},{40,48},{48,56},{56,64},{64,7... | collective-permute-start | bytes 73736 | tf_op jit(solution)/shard_map/ppermute | solution.py:385
  138.6 6.1 %collective-permute-start.5 = (f32[48,128]{1,0:T(8,128)S(1)}, f32[48,128]{1,0:T(8,128)S(1)}, u32[]{:S(2)}, u32[]{:S(2)}) collective-permute-start(f32[48,128]{1,0:T(8,128)S(1)} %get-tuple-element.29), channel_id=1, source_target_pairs={{8,0},{16,8},{24,16},{32,24},{40,32},{48,40},{56,48},{64,56},{72,6... | collective-permute-start | bytes 73736 | tf_op jit(solution)/shard_map/ppermute | solution.py:386

commit v2 on v1

--- a/solution.py
+++ b/solution.py
@@ -9,6 +9,8 @@
 
 F32 = jnp.float32
 BF16 = jnp.bfloat16
+PAIR_GROUP = 64
+BLOCK_GROUP = 32
 CAP = 4
 EPS2 = 0.0025
 VMEM = pl.BlockSpec(memory_space=pltpu.VMEM)
@@ -49,11 +51,12 @@
             out[m, :, :] = fv[m, :, y, :]
 
 
-def deposit_kernel(owner, local, cell, vel, out, slot_out, taken):
+def deposit_kernel(owner, local, cell, vel, after, out, slot_out, done, taken):
     blocks = cell.shape[0]
     lanes = lax.broadcasted_iota(jnp.int32, (4, 128), 1)
     rows4 = lax.broadcasted_iota(jnp.int32, (4, 128), 0)
     mark = (lanes == 127) & (rows4 == 0)
+    done[...] = jnp.zeros(done.shape, F32)
     out[...] = jnp.broadcast_to(jnp.where(mark, -1.0, 0.0).astype(F32)[None], out.shape)
 
     def clear(t, c):
@@ -64,12 +67,12 @@
     r8 = lax.broadcasted_iota(jnp.int32, (8, 128), 0)
 
     def group(g, c):
-        base = pl.multiple_of(g * 8, 8)
-        cells8 = cell[pl.ds(base, 8), :]
-        v = [vel[m, pl.ds(base, 8), :] for m in range(3)]
-        for k in range(8):
+        base = pl.multiple_of(g * BLOCK_GROUP, BLOCK_GROUP)
+        cells = cell[pl.ds(base, BLOCK_GROUP), :]
+        v = [vel[m, pl.ds(base, BLOCK_GROUP), :] for m in range(3)]
+        for k in range(BLOCK_GROUP):
             q = base + k
-            hot = onehot_cells(cells8[k : k + 1, :])
+            hot = onehot_cells(cells[k : k + 1, :])
             rows = [jnp.broadcast_to(v[m][k : k + 1, :], (8, 128)) for m in range(3)]
             load = jnp.where(r8 == 1, rows[0], jnp.where(r8 == 2, rows[1], rows[2]))
             load = jnp.where(r8 == 0, 1.0, jnp.where(r8 < 4, load, 0.0))
@@ -86,7 +89,7 @@
             out[slot] = jnp.where(mark, ident, both[0:4])
         return c
 
-    lax.fori_loop(0, blocks // 8, group, 0)
+    lax.fori_loop(0, blocks // BLOCK_GROUP, group, 0)
 
 
 def swap_groups(v):
@@ -101,7 +104,7 @@
     return v
 
 
-def fluid_kernel(xlo_on, recv, fv, from_low, from_high, from_left, from_right, fluid, answer, grid):
+def fluid_kernel(xlo_on, recv, fv, from_low, from_high, from_left, from_right, after, fluid, answer, done, grid):
     sx, sy, sz = fv.shape[1:]
     slots = recv.shape[0] // 4
     bricks = sx // 2 * (sy // 4) * (sz // 16)
@@ -172,6 +175,7 @@
         answer[pl.ds(c, slots, stride=4), :] = (
             found[:, 2 * c * 128 : (2 * c + 1) * 128] + found[:, (2 * c + 1) * 128 : (2 * c + 2) * 128]
         )
+    done[...] = jnp.zeros(done.shape, F32)
 
 
 def feature_rows(x):
@@ -192,67 +196,63 @@
     return a, b, n - a - b
 
 
-def push_loop(step, first, second, pos, low, high, push, feat_b, feat_a, base_a):
+def push_loop(step, begin, end, first, second, pos, low, high, push, feat_b, feat_a):
     blocks = pos.shape[1]
     one = jnp.ones((8, 128), F32)
     zero = jnp.zeros((8, 128), F32)
 
-    def put(ref, rows, stride, q0, feats):
+    def put(ref, q0, feats):
         for k, v in enumerate(feats):
-            ref[pl.ds(q0 * stride + k, 8, stride=stride), :] = v
+            ref[pl.ds(q0 * 16 + k, 8, stride=16), :] = v
 
     def own(g, c):
         q0 = pl.multiple_of(g * 8, 8)
         hi, lo, both, norm = feature_rows([pos[m, pl.ds(q0, 8), :] for m in range(3)])
         n = split3(norm)
-        put(feat_b, 16, 16, q0, hi + [one, n[0], n[1], n[2], one] + lo + [zero, one, zero, zero, zero])
+        put(feat_b, q0, hi + [one, n[0], n[1], n[2], one] + lo + [one, zero, zero, zero, zero])
         n = split3(norm + EPS2)
         h2, l2 = [-2.0 * v for v in hi], [-2.0 * v for v in lo]
-        put(
-            feat_a, 32, 32, q0,
-            h2 + [n[0], one, one, one, n[1]] + h2 + [zero, n[2], zero, zero, zero]
-            + l2 + [zero] * 5 + l2 + [zero] * 5,
-        )
-        put(base_a, 8, 8, q0, both + [zero] * 5)
+        put(feat_a, q0, h2 + [n[0], one, one, one, n[1]] + l2 + [n[2], zero, zero, zero, zero])
         return c
 
-    lax.fori_loop(0, blocks // 8, own, 0)
+    lax.fori_loop(0, blocks // 8, own, 0, unroll=2)
     for i, (ref, at) in enumerate((low, high)):
         for g in range(2):
             hi, lo, _, norm = feature_rows([ref[at + m * 16 + g * 8 : at + m * 16 + g * 8 + 8, :] for m in range(3)])
             n = split3(norm)
-            put(feat_b, 16, 16, blocks + i * 16 + g * 8, hi + [one, n[0], n[1], n[2], one] + lo + [zero, one, zero, zero, zero])
+            put(feat_b, blocks + i * 16 + g * 8, hi + [one, n[0], n[1], n[2], one] + lo + [one, zero, zero, zero, zero])
     push[...] = jnp.zeros(push.shape, F32)
+    top = lax.broadcasted_iota(jnp.int32, (8, 128), 0) < 3
 
     def one_pair(p):
         a = first[step, p]
         b = second[step, p]
         fb = feat_b[pl.ds(pl.multiple_of(b * 16, 16), 16), :]
-        ga = feat_a[pl.ds(pl.multiple_of(a * 32, 32), 32), :].astype(BF16)
+        fa = feat_a[pl.ds(pl.multiple_of(a * 16, 16), 16), :]
+        x, y = fa[0:8], fa[8:16]
+        z = jnp.where(top, y, 0.0)
+        ga = jnp.concatenate([x, jnp.where(top, x, y), z, z], axis=0).astype(BF16)
         fbt = jnp.concatenate([fb, fb], axis=0).T.astype(BF16)
         r2 = dot(fbt, ga)
         w = jnp.maximum(lax.rsqrt(jnp.maximum(r2, EPS2)) - 4.0, 0.0)
-        hi, lo = split2(w)
         lhs = fb.astype(BF16)
-        res = dot(lhs, hi) + dot(lhs, lo)
-        res = res[0:8] + res[8:16]
-        ua = base_a[pl.ds(pl.multiple_of(a * 8, 8), 8), :]
-        return a, ua * jnp.broadcast_to(res[3:4], (8, 128)) - res
-
-    unroll = 4
+        res = dot(jnp.concatenate([lhs, lhs], axis=1), jnp.concatenate(split2(w), axis=0))
+        total = jnp.broadcast_to(res[3:4], (8, 128))
+        return a, (-0.5) * (x + z) * total - (res[0:8] + res[8:16])
 
     def pairs(g, c):
-        done = [one_pair(g * unroll + k) for k in range(unroll)]
+        done = [one_pair(g * PAIR_GROUP + k) for k in range(PAIR_GROUP)]
         for a, f in done:
             rows = pl.ds(pl.multiple_of(a * 8, 8), 8)
             push[rows, :] = push[rows, :] + f
         return c
 
-    lax.fori_loop(0, first.shape[1] // unroll, pairs, 0)
-
-
-def push_kernel(first, second, pos, low, high, push, feat_b, feat_a, base_a):
-    push_loop(0, first, second, pos, (low, 96), (high, 96), push, feat_b, feat_a, base_a)
+    lax.fori_loop(begin // PAIR_GROUP, end // PAIR_GROUP, pairs, 0)
+
+
+def push_kernel(begin, end, first, second, pos, low, high, after, push, done, feat_b, feat_a):
+    push_loop(0, begin, end, first, second, pos, (low, 96), (high, 96), push, feat_b, feat_a)
+    done[...] = jnp.zeros(done.shape, F32)
 
 
 def advance(pos, vel, push, flow, pos_out, vel_out):
@@ -260,7 +260,8 @@
     drift = 2.0 * flow[pl.ds(3, blocks, stride=8), :]
     for m in range(3):
         v = vel[m]
-        force = 2.5 * push[pl.ds(m, blocks, stride=8), :] + drift * (flow[pl.ds(m, blocks, stride=8), :] - v)
+        total = sum(part[pl.ds(m, blocks, stride=8), :] for part in push)
+        force = 2.5 * total + drift * (flow[pl.ds(m, blocks, stride=8), :] - v)
         if m == 2:
             force = force - 1.0
         v = v + 0.1 * force
@@ -268,33 +269,53 @@
         pos_out[m] = pos[m] + 0.1 * v
 
 
-def pick_kernel(slot, halo, back, cell, pos, vel, push, flow, pos_out, vel_out, down_out, up_out):
+def pick(hot, v):
+    v = jnp.concatenate([v, v], axis=0)
+    hi = v.astype(BF16).astype(F32)
+    both = dot(jnp.concatenate([hi, v - hi], axis=0).astype(BF16), hot)
+    return both[0:8] + both[8:16]
+
+
+def listed_kernel(slot, halo, back, cell, pos, vel, push_a, push_b, down_out, up_out):
+    r8 = lax.broadcasted_iota(jnp.int32, (8, 128), 0)
+
+    def tile(ref, q):
+        rows = [jnp.broadcast_to(ref[m, pl.ds(q, 1), :], (8, 128)) for m in range(3)]
+        return jnp.where(r8 == 0, rows[0], jnp.where(r8 == 1, rows[1], rows[2]))
+
+    for half, out in ((0, down_out), (1, up_out)):
+        for j in range(16):
+            q = halo[half * 16 + j]
+            flow = pick(onehot_cells(cell[pl.ds(q, 1), :]), back[slot[q]])
+            v = tile(vel, q)
+            rows = pl.ds(pl.multiple_of(q * 8, 8), 8)
+            drift = 2.0 * jnp.broadcast_to(flow[3:4], (8, 128))
+            force = 2.5 * (push_a[rows, :] + push_b[rows, :]) + drift * (flow - v)
+            v = v + 0.1 * jnp.where(r8 == 2, force - 1.0, force)
+            x = tile(pos, q) + 0.1 * v
+            for m in range(3):
+                out[m * 16 + j : m * 16 + j + 1, :] = x[m : m + 1, :]
+
+
+def pick_kernel(slot, back, cell, pos, vel, push_a, push_b, after, flow, pos_out, vel_out):
     def group(g, c):
-        base = pl.multiple_of(g * 8, 8)
-        cells8 = cell[pl.ds(base, 8), :]
-        for k in range(8):
+        base = pl.multiple_of(g * BLOCK_GROUP, BLOCK_GROUP)
+        cells = cell[pl.ds(base, BLOCK_GROUP), :]
+        for k in range(BLOCK_GROUP):
             q = base + k
-            hot = onehot_cells(cells8[k : k + 1, :])
-            v = back[slot[q]]
-            v = jnp.concatenate([v, v], axis=0)
-            hi = v.astype(BF16).astype(F32)
-            lhs = jnp.concatenate([hi, v - hi], axis=0).astype(BF16)
-            both = dot(lhs, hot)
-            flow[pl.ds(pl.multiple_of(q * 8, 8), 8), :] = both[0:8] + both[8:16]
+            flow[pl.ds(pl.multiple_of(q * 8, 8), 8), :] = pick(onehot_cells(cells[k : k + 1, :]), back[slot[q]])
         return c
 
-    lax.fori_loop(0, cell.shape[0] // 8, group, 0)
-    advance(pos, vel, push, flow, pos_out, vel_out)
-    pack_rows(halo, pos_out, down_out, 0, 0)
-    pack_rows(halo, pos_out, up_out, 0, 1)
-
-
-def last_kernel(first, second, pos, vel, low, high, flow, pos_out, vel_out, push, feat_b, feat_a, base_a):
-    push_loop(1, first, second, pos, (low, 0), (high, 0), push, feat_b, feat_a, base_a)
-    advance(pos, vel, push, flow, pos_out, vel_out)
-
-
-def call(kernel, in_specs, out_shape, out_specs, scratch=(), cost=None):
+    lax.fori_loop(0, cell.shape[0] // BLOCK_GROUP, group, 0)
+    advance(pos, vel, (push_a, push_b), flow, pos_out, vel_out)
+
+
+def last_kernel(first, second, pos, vel, low, high, flow, pos_out, vel_out, push, feat_b, feat_a):
+    push_loop(1, 0, first.shape[1], first, second, pos, (low, 0), (high, 0), push, feat_b, feat_a)
+    advance(pos, vel, (push,), flow, pos_out, vel_out)
+
+
+def call(kernel, in_specs, out_shape, out_specs, scratch=(), micros=1):
     return pl.pallas_call(
         kernel,
         in_specs=in_specs,
@@ -302,7 +323,7 @@
         out_specs=out_specs,
         scratch_shapes=list(scratch),
         compiler_params=pltpu.CompilerParams(**PARAMS),
-        cost_estimate=cost,
+        cost_estimate=pl.CostEstimate(flops=micros * 1_000_000_000, bytes_accessed=micros * 3_000_000, transcendentals=0),
     )
 
 
@@ -342,54 +363,68 @@
     from_left = lax.ppermute(right, "gy", [(i, i + 1) for i in range(ny - 1)])
     from_right = lax.ppermute(left, "gy", [(i + 1, i) for i in range(ny - 1)])
 
-    send, slot = call(
+    send, slot, placed = call(
         deposit_kernel,
-        [SMEM, SMEM, VMEM, VMEM],
-        [shape(slots, 4, 128), shape(blocks, dtype=jnp.int32)],
-        [VMEM, SMEM],
+        [SMEM, SMEM, VMEM, VMEM, VMEM],
+        [shape(slots, 4, 128), shape(blocks, dtype=jnp.int32), shape(8, 128)],
+        [VMEM, SMEM, VMEM],
         [pltpu.SMEM((tiles,), jnp.int32)],
-    )(brick_owner[:, 0], brick_local, cell_in_brick, vel)
+        7,
+    )(brick_owner[:, 0], brick_local, cell_in_brick, vel, down)
     recv = lax.all_to_all(send.reshape(slots * 4, 128), ("gx", "gy"), split_axis=0, concat_axis=0, tiled=True)
 
-    pair_scratch = [
-        pltpu.VMEM(((blocks + 32) * 16, 128), F32),
-        pltpu.VMEM((blocks * 32, 128), F32),
-        pltpu.VMEM((blocks * 8, 128), F32),
-    ]
-    push = call(
-        push_kernel,
-        [SMEM, SMEM, VMEM, VMEM, VMEM],
-        shape(blocks * 8, 128),
-        VMEM,
-        pair_scratch,
-        pl.CostEstimate(flops=20_000_000_000, bytes_accessed=2_000_000, transcendentals=8_000_000),
-    )(pair_self, pair_other, pos, from_low, from_high)
-
+    pairs = pair_self.shape[1]
+    pair_scratch = [pltpu.VMEM(((blocks + 32) * 16, 128), F32), pltpu.VMEM((blocks * 16, 128), F32)]
+
+    def push(begin, end, after):
+        return call(
+            functools.partial(push_kernel, begin, end),
+            [SMEM, SMEM, VMEM, VMEM, VMEM, VMEM],
+            [shape(blocks * 8, 128), shape(8, 128)],
+            [VMEM, VMEM],
+            pair_scratch,
+            8,
+        )(pair_self, pair_other, pos, from_low, from_high, after)
+
+    push_a, done_a = push(0, pairs // 2, placed)
     me = lax.axis_index("gx")
     ends = jnp.stack([me > 0, me < nx - 1]).astype(jnp.int32)
-    fluid, answer = call(
+    fluid, answer, stepped = call(
         fluid_kernel,
-        [SMEM] + [VMEM] * 6,
-        [shape(3, sx, sy, sz), shape(slots * 4, 128)],
+        [SMEM] + [VMEM] * 7,
+        [shape(3, sx, sy, sz), shape(slots * 4, 128), shape(8, 128)],
+        [VMEM] * 3,
+        [pltpu.VMEM((4, sx, sy, sz), F32)],
+        4,
+    )(ends, recv, fluid_vel, from_low, from_high, from_left, from_right, done_a)
+    back = lax.all_to_all(answer, ("gx", "gy"), split_axis=0, concat_axis=0, tiled=True).reshape(slots, 4, 128)
+    push_b, _ = push(pairs // 2, pairs, stepped)
+
+    down, up = call(
+        listed_kernel,
+        [SMEM, SMEM] + [VMEM] * 6,
+        [shape(48, 128), shape(48, 128)],
         [VMEM] * 2,
-        [pltpu.VMEM((4, sx, sy, sz), F32)],
-    )(ends, recv, fluid_vel, from_low, from_high, from_left, from_right)
-    back = lax.all_to_all(answer, ("gx", "gy"), split_axis=0, concat_axis=0, tiled=True)
-
-    flow, pos, vel, down, up = call(
-        pick_kernel,
-        [SMEM, SMEM] + [VMEM] * 5,
-        [shape(blocks * 8, 128), shape(3, blocks, 128), shape(3, blocks, 128), shape(48, 128), shape(48, 128)],
-        [VMEM] * 5,
-    )(slot, halo_list, back.reshape(slots, 4, 128), cell_in_brick, pos, vel, push)
+        (),
+        2,
+    )(slot, halo_list, back, cell_in_brick, pos, vel, push_a, push_b)
     low = lax.ppermute(up, "gx", fwd)
     high = lax.ppermute(down, "gx", bwd)
+    flow, pos, vel = call(
+        pick_kernel,
+        [SMEM] + [VMEM] * 7,
+        [shape(blocks * 8, 128), shape(3, blocks, 128), shape(3, blocks, 128)],
+        [VMEM] * 3,
+        (),
+        6,
+    )(slot, back, cell_in_brick, pos, vel, push_a, push_b, down)
     pos, vel = call(
         last_kernel,
         [SMEM, SMEM] + [VMEM] * 5,
         [shape(3, blocks, 128), shape(3, blocks, 128)],
         [VMEM] * 2,
         [pltpu.VMEM((blocks * 8, 128), F32)] + pair_scratch,
+        15,
     )(pair_self, pair_other, pos, vel, low, high, flow)
     return fluid, jnp.transpose(pos, (1, 0, 2)), jnp.transpose(vel, (1, 0, 2))
 

time: 223 us -> 107 us (0.48)
  Pallas kernels: 176 us -> 47.9 us
  waiting for transfers between devices: 11.2 us -> 20.3 us
  local copies, waits for them, and re-layouts: 3.24 us -> 7.8 us
    pallas_call x4 -> x6, Pallas kernels: 98.1 us -> 32.3 us  [the longest x2 16.3 us: push(): call(functools.partial(push_kernel, begin, end), [SMEM, SMEM, VMEM, VMEM,...]
    pallas_call x1, Pallas kernels: 77.7 us -> 14.9 us  [per_device(): call(last_kernel, [SMEM, SMEM] + [VMEM] * 5, [shape(3, blocks, 128), shap...]
    all_to_all x1, waiting for transfers between devices: 0.01 us -> 9.76 us  [per_device(): lax.all_to_all(answer, ('gx', 'gy'), split_axis=0, concat_axis=0, tiled=T...]
    unnamed x22 -> x32, local copies, waits for them, and re-layouts: 3.24 us -> 7.8 us
    ppermute x1, waiting for transfers between devices: 7.07 us -> 10.5 us  [per_device(): from_low = lax.ppermute(up, 'gx', fwd)]
    all_to_all x1, waiting for transfers between devices: 2.32 us -> 0.01 us  [per_device(): lax.all_to_all(send.reshape(slots * 4, 128), ('gx', 'gy'), split_axis=0,...]
  transfers between devices with their start and end apart: 8 -> 8, of which waited for: 3 -> 2; matrix products, arithmetic and copies ran while one was open for 0% -> 0% of each run, Pallas kernels for 35% -> 19%
where the time goes in v2:
time: 107 us
  Pallas kernels  47.9 us (45%)
  starting transfers between devices  30.2 us (28%)
  waiting for transfers between devices  20.3 us (19%)
  local copies, waits for them, and re-layouts  7.8 us (7%)
    pallas_call x2, Pallas kernels, push(): call(functools.partial(push_kernel, begin, end), [SMEM, SMEM, VMEM, VMEM,...  16.3 us
    pallas_call x1, Pallas kernels, per_device(): call(last_kernel, [SMEM, SMEM] + [VMEM] * 5, [shape(3, blocks, 128), shap...  14.9 us
    all_to_all x1, starting transfers between devices, per_device(): lax.all_to_all(send.reshape(slots * 4, 128), ('gx', 'gy'), split_axis=0,...  11.1 us
    ppermute x1, waiting for transfers between devices, per_device(): from_low = lax.ppermute(up, 'gx', fwd)  10.5 us
    all_to_all x1, waiting for transfers between devices, per_device(): lax.all_to_all(answer, ('gx', 'gy'), split_axis=0, concat_axis=0, tiled=T...  9.76 us
    unnamed x32, local copies, waits for them, and re-layouts  7.8 us
    pallas_call x1, Pallas kernels, per_device(): call(deposit_kernel, [SMEM, SMEM, VMEM, VMEM, VMEM], [shape(slots, 4, 128...  7.13 us
    all_to_all x1, starting transfers between devices, per_device(): lax.all_to_all(answer, ('gx', 'gy'), split_axis=0, concat_axis=0, tiled=T...  5.25 us
  transfers between devices with their start and end apart: 8, of which 2 were waited for; matrix products, arithmetic and copies ran while one was open for 0% of the time, Pallas kernels for 19%

profile of v2, /device:TPU:0, one launch (start us, length us, event | category | flops | bytes accessed | tf_op | source)
XLA Modules:
  0.0 107.0 jit_solution(7021073220010838260)
XLA Ops:
  0.6 0.0 copy-start.10
  0.6 0.6 copy-done.10
  1.3 0.0 copy-start
  1.3 1.0 copy-done
  2.3 0.0 copy-start.3
  2.3 1.0 copy-done.3
  3.3 0.0 copy-start.2
  3.3 0.0 copy-start.5
  3.3 0.0 copy-start.9
  3.3 0.6 shard_map.112
  3.9 0.0 copy-start.8
  3.9 0.4 copy-done.2
  4.3 0.0 copy-done.5
  4.3 0.0 copy-done.9
  4.3 0.3 copy-done.8
  4.6 7.1 %shard_map.113 = (f32[512,4,128]{2,1,0:T(4,128)}, s32[256]{0:T(256)S(1)}, f32[8,128]{1,0:T(8,128)S(1)}) custom-call(s32[256]{0:T(256)S(1)} %bitcast.22, s32[256]{0:T(256)S(1)} %copy-done.9, s32[256,128]{1,0:T(8,128)S(1)} %copy-done.5, f32[3,256,128]{2,1,0:T(8,128)S(1)} %bitcast.14, f32[144,128]{1,0:T(8,128)S(1)} %get-tuple-element.23.after), custom_call_target="tpu_custom_call" | custom-call | flops 7000000000 | bytes 21000000 | tf_op jit(solution)/shard_map/pallas_call | solution.py:366
  11.8 0.0 copy-start.4
  11.8 11.1 %all-to-all-start = ((f32[128,16,128]{2,1,0:T(8,128)}), f32[128,16,128]{2,1,0:T(8,128)S(1)}, u32[]{:S(2)}, u32[]{:S(2)}) async-start(f32[128,16,128]{2,1,0:T(8,128)} %bitcast.5), calls=%async_computation | async-start | bytes 2097152 | tf_op jit(solution)/shard_map/all_to_all | solution.py:374
  22.9 5.2 %collective-permute-start.1 = (f32[144,128]{1,0:T(8,128)S(1)}, f32[144,128]{1,0:T(8,128)S(1)}, u32[]{:S(2)}, u32[]{:S(2)}) collective-permute-start(f32[144,128]{1,0:T(8,128)S(1)} %get-tuple-element.23.after), channel_id=1, source_target_pairs={{8,0},{16,8},{24,16},{32,24},{40,32},{48,40},{56,48},{64,56},{72,6... | collective-permute-start | bytes 221192 | tf_op jit(solution)/shard_map/ppermute | solution.py:362
  28.2 1.8 %collective-permute-start.2 = (f32[3,8,256]{2,1,0:T(8,128)S(1)}, f32[3,8,256]{2,1,0:T(8,128)S(1)}, u32[]{:S(2)}, u32[]{:S(2)}) collective-permute-start(f32[3,8,256]{2,1,0:T(8,128)S(1)} %get-tuple-element.26), channel_id=1, source_target_pairs={{0,1},{1,2},{2,3},{3,4},{4,5},{5,6},{6,7},{8,9},{9,10},{10,11},{11... | collective-permute-start | bytes 73736 | tf_op jit(solution)/shard_map/ppermute | solution.py:363
  29.9 1.3 %collective-permute-start.3 = (f32[3,8,256]{2,1,0:T(8,128)S(1)}, f32[3,8,256]{2,1,0:T(8,128)S(1)}, u32[]{:S(2)}, u32[]{:S(2)}) collective-permute-start(f32[3,8,256]{2,1,0:T(8,128)S(1)} %get-tuple-element.27), channel_id=1, source_target_pairs={{1,0},{2,1},{3,2},{4,3},{5,4},{6,5},{7,6},{9,8},{10,9},{11,10},{12... | collective-permute-start | bytes 73736 | tf_op jit(solution)/shard_map/ppermute | solution.py:364
  31.2 0.1 collective-permute-start
  31.3 0.0 copy-start.7
  31.3 0.0 copy-start.6
  31.3 0.1 add_convert_fusion.xlo_on
  31.4 10.5 %collective-permute-done.low.from_low = f32[144,128]{1,0:T(8,128)S(1)} collective-permute-done((f32[144,128]{1,0:T(8,128)S(1)}, f32[144,128]{1,0:T(8,128)S(1)}, u32[]{:S(2)}, u32[]{:S(2)}) %collective-permute-start) | collective-permute-done | bytes 73760 | tf_op jit(solution)/shard_map/ppermute | solution.py:361
  42.0 0.0 collective-permute-done.1.high.from_high
  42.0 0.0 copy-done.4
  42.0 0.0 copy-done.7
  42.0 0.0 copy-done.6
  42.0 0.0 copy-start.1
  42.0 7.9 %shard_map.114 = (f32[2048,128]{1,0:T(8,128)S(1)}, f32[8,128]{1,0:T(8,128)S(1)}) custom-call(s32[2,512]{1,0:T(2,128)S(1)} %copy-done.6, s32[2,512]{1,0:T(2,128)S(1)} %copy-done.7, f32[3,256,128]{2,1,0:T(8,128)S(1)} %bitcast.18, f32[144,128]{1,0:T(8,128)S(1)} %collective-permute-done.low.from_low, f32[144,128]{1,0:T(8,128)S(1)} %collective-permute-done.1.high.from_high, ...), custom_call_target="tpu_custom_call" | custom-call | flops 8000000000 | bytes 24000000 | tf_op jit(solution)/shard_map/pallas_call | solution.py:380
  49.9 0.0 copy-start.11
  49.9 1.0 copy-done.11
  50.8 0.0 collective-permute-done.2.from_left
  50.8 0.0 collective-permute-done.3.from_right
  50.8 0.0 all-to-all-done
  50.8 0.0 copy-done.1
  50.9 3.9 %shard_map.115 = (f32[3,8,16,256]{3,2,1,0:T(8,128)}, f32[2048,128]{1,0:T(8,128)}, f32[8,128]{1,0:T(8,128)S(1)}) custom-call(s32[2]{0:T(128)S(1)} %add_convert_fusion.xlo_on, f32[2048,128]{1,0:T(8,128)S(1)} %bitcast.11, f32[3,8,16,256]{3,2,1,0:T(8,128)S(1)} %copy-done.1, f32[144,128]{1,0:T(8,128)S(1)} %collective-permute-done.low.from_low, ...), custom_call_target="tpu_custom_call" | custom-call | flops 4000000000 | bytes 12000000 | tf_op jit(solution)/shard_map/pallas_call | solution.py:392
  54.8 5.3 %all-to-all-start.1 = ((f32[128,16,128]{2,1,0:T(8,128)}), f32[128,16,128]{2,1,0:T(8,128)S(1)}, u32[]{:S(2)}, u32[]{:S(2)}) async-start(f32[128,16,128]{2,1,0:T(8,128)} %bitcast.7), calls=%async_computation.1 | async-start | bytes 2097152 | tf_op jit(solution)/shard_map/all_to_all | solution.py:400
  60.1 8.4 %shard_map.116 = (f32[2048,128]{1,0:T(8,128)S(1)}, f32[8,128]{1,0:T(8,128)}) custom-call(s32[2,512]{1,0:T(2,128)S(1)} %copy-done.6, s32[2,512]{1,0:T(2,128)S(1)} %copy-done.7, f32[3,256,128]{2,1,0:T(8,128)S(1)} %bitcast.19, f32[144,128]{1,0:T(8,128)S(1)} %collective-permute-done.low.from_low, f32[144,128]{1,0:T(8,128)S(1)} %collective-permute-done.1.high.from_high, ...), custom_call_target="tpu_custom_call" | custom-call | flops 8000000000 | bytes 24000000 | tf_op jit(solution)/shard_map/pallas_call | solution.py:380
  68.5 0.0 copy-start.14
  68.5 1.0 copy-done.14
  69.5 9.8 %all-to-all-done.1 = f32[128,16,128]{2,1,0:T(8,128)S(1)} async-done(((f32[128,16,128]{2,1,0:T(8,128)}), f32[128,16,128]{2,1,0:T(8,128)S(1)}, u32[]{:S(2)}, u32[]{:S(2)}) %all-to-all-start.1) | async-done | bytes 1048608 | tf_op jit(solution)/shard_map/all_to_all | solution.py:400
  79.2 0.0 copy-start.12
  79.2 1.2 %copy-done.12 = f32[2048,128]{1,0:T(8,128)S(1)} copy-done((f32[2048,128]{1,0:T(8,128)S(1)}, f32[2048,128]{1,0:T(8,128)}, u32[]{:S(2)}) %copy-start.12) | copy-done | bytes 1048600
  80.4 0.0 copy-start.15
  80.4 1.2 %copy-done.15 = f32[2048,128]{1,0:T(8,128)S(1)} copy-done((f32[2048,128]{1,0:T(8,128)S(1)}, f32[2048,128]{1,0:T(8,128)}, u32[]{:S(2)}) %copy-start.15) | copy-done | bytes 1048600
  81.7 0.0 copy-start.13
  81.7 1.0 shard_map.117
  82.6 0.5 collective-permute-start.4
  83.1 4.9 %collective-permute-start.5 = (f32[48,128]{1,0:T(8,128)S(1)}, f32[48,128]{1,0:T(8,128)S(1)}, u32[]{:S(2)}, u32[]{:S(2)}) collective-permute-start(f32[48,128]{1,0:T(8,128)S(1)} %get-tuple-element.36.after), channel_id=1, source_target_pairs={{8,0},{16,8},{24,16},{32,24},{40,32},{48,40},{56,48},{64,56},{72,6... | collective-permute-start | bytes 73736 | tf_op jit(solution)/shard_map/ppermute | solution.py:412
  88.0 0.0 copy-done.13
  88.0 4.0 %shard_map.118 = (f32[2048,128]{1,0:T(8,128)S(1)}, f32[3,256,128]{2,1,0:T(8,128)S(1)}, f32[3,256,128]{2,1,0:T(8,128)S(1)}) custom-call(s32[256]{0:T(256)S(1)} %get-tuple-element.31.slot, f32[512,4,128]{2,1,0:T(4,128)S(1)} %bitcast.13, s32[256,128]{1,0:T(8,128)S(1)} %copy-done.5, f32[3,256,128]{2,1,0:T(8,128)S(1)} %bitcast.21, f32[3,256,128]{2,1,0:T(8,128)S(1)} %bitcast.16, ...), custom_call_target="tpu_custom_call" | custom-call | flops 6000000000 | bytes 18000000 | tf_op jit(solution)/shard_map/pallas_call | solution.py:413
  92.1 0.0 collective-permute-done.4.low
  92.1 0.0 collective-permute-done.5.high
  92.1 14.9 %shard_map.119 = (f32[3,256,128]{2,1,0:T(8,128)}, f32[3,256,128]{2,1,0:T(8,128)}) custom-call(s32[2,512]{1,0:T(2,128)S(1)} %copy-done.6, s32[2,512]{1,0:T(2,128)S(1)} %copy-done.7, f32[3,256,128]{2,1,0:T(8,128)S(1)} %get-tuple-element.37.pos, f32[3,256,128]{2,1,0:T(8,128)S(1)} %get-tuple-element.38.vel, f32[48,128]{1,0:T(8,128)S(1)} %collective-permute-done.4.low, ...), custom_call_target="tpu_custom_call" | custom-call | flops 15000000512 | bytes 45000000 | tf_op jit(solution)/shard_map/pallas_call | solution.py:421
Async XLA Ops:
  0.6 0.7 copy-start.10
  1.3 1.0 copy-start
  2.3 1.0 copy-start.3
  3.3 1.0 copy-start.2
  3.3 1.0 copy-start.5
  3.3 1.0 copy-start.9
  3.9 0.7 copy-start.8
  11.8 30.2 %copy-start.4 = (f32[256,3,128]{2,0,1:T(8,128)S(1)}, f32[256,3,128]{2,0,1:T(8,128)}, u32[]{:S(2)}) copy-start(f32[256,3,128]{2,0,1:T(8,128)} %param.10) | copy-start | bytes 1179652
  11.8 39.1 %all-to-all-start = ((f32[128,16,128]{2,1,0:T(8,128)}), f32[128,16,128]{2,1,0:T(8,128)S(1)}, u32[]{:S(2)}, u32[]{:S(2)}) async-start(f32[128,16,128]{2,1,0:T(8,128)} %bitcast.5), calls=%async_computation | async-start | bytes 2097152 | tf_op jit(solution)/shard_map/all_to_all | solution.py:374
  22.9 19.0 %collective-permute-start.1 = (f32[144,128]{1,0:T(8,128)S(1)}, f32[144,128]{1,0:T(8,128)S(1)}, u32[]{:S(2)}, u32[]{:S(2)}) collective-permute-start(f32[144,128]{1,0:T(8,128)S(1)} %get-tuple-element.23.after), channel_id=1, source_target_pairs={{8,0},{16,8},{24,16},{32,24},{40,32},{48,40},{56,48},{64,56},{72,6... | collective-permute-start | bytes 221192 | tf_op jit(solution)/shard_map/ppermute | solution.py:362
  28.2 22.7 %collective-permute-start.2 = (f32[3,8,256]{2,1,0:T(8,128)S(1)}, f32[3,8,256]{2,1,0:T(8,128)S(1)}, u32[]{:S(2)}, u32[]{:S(2)}) collective-permute-start(f32[3,8,256]{2,1,0:T(8,128)S(1)} %get-tuple-element.26), channel_id=1, source_target_pairs={{0,1},{1,2},{2,3},{3,4},{4,5},{5,6},{6,7},{8,9},{9,10},{10,11},{11... | collective-permute-start | bytes 73736 | tf_op jit(solution)/shard_map/ppermute | solution.py:363
  29.9 20.9 %collective-permute-start.3 = (f32[3,8,256]{2,1,0:T(8,128)S(1)}, f32[3,8,256]{2,1,0:T(8,128)S(1)}, u32[]{:S(2)}, u32[]{:S(2)}) collective-permute-start(f32[3,8,256]{2,1,0:T(8,128)S(1)} %get-tuple-element.27), channel_id=1, source_target_pairs={{1,0},{2,1},{3,2},{4,3},{5,4},{6,5},{7,6},{9,8},{10,9},{11,10},{12... | collective-permute-start | bytes 73736 | tf_op jit(solution)/shard_map/ppermute | solution.py:364
  31.2 10.7 %collective-permute-start = (f32[144,128]{1,0:T(8,128)S(1)}, f32[144,128]{1,0:T(8,128)S(1)}, u32[]{:S(2)}, u32[]{:S(2)}) collective-permute-start(f32[144,128]{1,0:T(8,128)S(1)} %get-tuple-element.25), channel_id=1, source_target_pairs={{0,8},{8,16},{16,24},{24,32},{32,40},{40,48},{48,56},{56,64},{64,7... | collective-permute-start | bytes 221192 | tf_op jit(solution)/shard_map/ppermute | solution.py:361
  31.3 10.6 %copy-start.7 = (s32[2,512]{1,0:T(2,128)S(1)}, s32[2,512]{1,0:T(2,128)}, u32[]{:S(2)}) copy-start(s32[2,512]{1,0:T(2,128)} %second.5) | copy-start | bytes 12292
  31.3 10.6 %copy-start.6 = (s32[2,512]{1,0:T(2,128)S(1)}, s32[2,512]{1,0:T(2,128)}, u32[]{:S(2)}) copy-start(s32[2,512]{1,0:T(2,128)} %first.5) | copy-start | bytes 12292
  42.0 8.9 %copy-start.1 = (f32[3,8,16,256]{3,2,1,0:T(8,128)S(1)}, f32[3,8,16,256]{3,2,1,0:T(8,128)}, u32[]{:S(2)}) copy-start(f32[3,8,16,256]{3,2,1,0:T(8,128)} %fv.3) | copy-start | bytes 1179652
  49.9 1.0 copy-start.11
  54.8 24.4 %all-to-all-start.1 = ((f32[128,16,128]{2,1,0:T(8,128)}), f32[128,16,128]{2,1,0:T(8,128)S(1)}, u32[]{:S(2)}, u32[]{:S(2)}) async-start(f32[128,16,128]{2,1,0:T(8,128)} %bitcast.7), calls=%async_computation.1 | async-start | bytes 2097152 | tf_op jit(solution)/shard_map/all_to_all | solution.py:400
  68.5 1.0 copy-start.14
  79.2 1.2 %copy-start.12 = (f32[2048,128]{1,0:T(8,128)S(1)}, f32[2048,128]{1,0:T(8,128)}, u32[]{:S(2)}) copy-start(f32[2048,128]{1,0:T(8,128)} %copy-done.11) | copy-start | bytes 3145732
  80.4 1.2 %copy-start.15 = (f32[2048,128]{1,0:T(8,128)S(1)}, f32[2048,128]{1,0:T(8,128)}, u32[]{:S(2)}) copy-start(f32[2048,128]{1,0:T(8,128)} %copy-done.14) | copy-start | bytes 3145732
  81.7 6.4 %copy-start.13 = (f32[2048,128]{1,0:T(8,128)S(1)}, f32[2048,128]{1,0:T(8,128)}, u32[]{:S(2)}) copy-start(f32[2048,128]{1,0:T(8,128)} %copy-done.11) | copy-start | bytes 3145732
  82.6 9.5 %collective-permute-start.4 = (f32[48,128]{1,0:T(8,128)S(1)}, f32[48,128]{1,0:T(8,128)S(1)}, u32[]{:S(2)}, u32[]{:S(2)}) collective-permute-start(f32[48,128]{1,0:T(8,128)S(1)} %get-tuple-element.39), channel_id=1, source_target_pairs={{0,8},{8,16},{16,24},{24,32},{32,40},{40,48},{48,56},{56,64},{64,7... | collective-permute-start | bytes 73736 | tf_op jit(solution)/shard_map/ppermute | solution.py:411
  83.1 9.0 %collective-permute-start.5 = (f32[48,128]{1,0:T(8,128)S(1)}, f32[48,128]{1,0:T(8,128)S(1)}, u32[]{:S(2)}, u32[]{:S(2)}) collective-permute-start(f32[48,128]{1,0:T(8,128)S(1)} %get-tuple-element.36.after), channel_id=1, source_target_pairs={{8,0},{16,8},{24,16},{32,24},{40,32},{48,40},{56,48},{64,56},{72,6... | collective-permute-start | bytes 73736 | tf_op jit(solution)/shard_map/ppermute | solution.py:412

commit v3 on v2

--- a/solution.py
+++ b/solution.py
@@ -9,13 +9,13 @@
 
 F32 = jnp.float32
 BF16 = jnp.bfloat16
-PAIR_GROUP = 64
+PAIR_GROUP = 128
 BLOCK_GROUP = 32
 CAP = 4
 EPS2 = 0.0025
 VMEM = pl.BlockSpec(memory_space=pltpu.VMEM)
 SMEM = pl.BlockSpec(memory_space=pltpu.SMEM)
-PARAMS = dict(vmem_limit_bytes=48 * 1024 * 1024)
+PARAMS = dict(vmem_limit_bytes=20 * 1024 * 1024)
 
 
 def split2(x):
@@ -39,7 +39,7 @@
             out[pl.ds(first + m * 16 + j, 1), :] = pos[m, pl.ds(q, 1), :]
 
 
-def faces_kernel(halo, fv, pos, down_out, up_out, left_out, right_out):
+def faces_kernel(halo, fv, pos, after, down_out, up_out, left_out, right_out):
     sx = fv.shape[1]
     for out, x, half in ((down_out, 0, 0), (up_out, sx - 1, 1)):
         for m in range(3):
@@ -51,7 +51,7 @@
             out[m, :, :] = fv[m, :, y, :]
 
 
-def deposit_kernel(owner, local, cell, vel, after, out, slot_out, done, taken):
+def deposit_kernel(owner, local, cell, vel, out, slot_out, done, taken):
     blocks = cell.shape[0]
     lanes = lax.broadcasted_iota(jnp.int32, (4, 128), 1)
     rows4 = lax.broadcasted_iota(jnp.int32, (4, 128), 0)
@@ -104,7 +104,28 @@
     return v
 
 
-def fluid_kernel(xlo_on, recv, fv, from_low, from_high, from_left, from_right, after, fluid, answer, done, grid):
+def spread_kernel(inside, fv, from_low, from_high, from_left, from_right, out):
+    sx, sy, sz = fv.shape[1:]
+    yrow = lax.broadcasted_iota(jnp.int32, (sy, sz), 0)
+    zlane = lax.broadcasted_iota(jnp.int32, (sy, sz), 1)
+    low_on = (inside[0]).astype(F32)
+    high_on = (inside[1]).astype(F32)
+    for m in range(3):
+        low = jnp.concatenate([from_low[(m * 2 + h) * 16 : (m * 2 + h + 1) * 16, :] for h in range(2)], axis=1) * low_on
+        high = jnp.concatenate([from_high[(m * 2 + h) * 16 : (m * 2 + h + 1) * 16, :] for h in range(2)], axis=1) * high_on
+        for x in range(sx):
+            f = fv[m, x]
+            beside = (fv[m, x + 1] if x < sx - 1 else high) + (fv[m, x - 1] if x > 0 else low)
+            right = jnp.broadcast_to(from_right[m, x : x + 1, :], (sy, sz))
+            left = jnp.broadcast_to(from_left[m, x : x + 1, :], (sy, sz))
+            beside = beside + jnp.where(yrow == sy - 1, right, pltpu.roll(f, sy - 1, 0))
+            beside = beside + jnp.where(yrow == 0, left, pltpu.roll(f, 1, 0))
+            beside = beside + jnp.where(zlane == sz - 1, 0.0, pltpu.roll(f, sz - 1, 1))
+            beside = beside + jnp.where(zlane == 0, 0.0, pltpu.roll(f, 1, 1))
+            out[m, x] = f + 0.1 * (beside - 6.0 * f)
+
+
+def fluid_kernel(recv, fv, spread, fluid, answer, done, grid):
     sx, sy, sz = fv.shape[1:]
     slots = recv.shape[0] // 4
     bricks = sx // 2 * (sy // 4) * (sz // 16)
@@ -138,23 +159,9 @@
                     v = moved[(bx * 4 + by) * 2 + h]
                     for x in range(2):
                         grid[c, bx * 2 + x, by * 4 : by * 4 + 4, h * 128 : h * 128 + 128] = v[x * 4 : x * 4 + 4, :]
-    yrow = lax.broadcasted_iota(jnp.int32, (sy, sz), 0)
-    zlane = lax.broadcasted_iota(jnp.int32, (sy, sz), 1)
-    low_on = (xlo_on[0]).astype(F32)
-    high_on = (xlo_on[1]).astype(F32)
-    for m in range(3):
-        low = jnp.concatenate([from_low[(m * 2 + h) * 16 : (m * 2 + h + 1) * 16, :] for h in range(2)], axis=1) * low_on
-        high = jnp.concatenate([from_high[(m * 2 + h) * 16 : (m * 2 + h + 1) * 16, :] for h in range(2)], axis=1) * high_on
+    for m in range(3):
         for x in range(sx):
-            f = fv[m, x]
-            beside = (fv[m, x + 1] if x < sx - 1 else high) + (fv[m, x - 1] if x > 0 else low)
-            right = jnp.broadcast_to(from_right[m, x : x + 1, :], (sy, sz))
-            left = jnp.broadcast_to(from_left[m, x : x + 1, :], (sy, sz))
-            beside = beside + jnp.where(yrow == sy - 1, right, pltpu.roll(f, sy - 1, 0))
-            beside = beside + jnp.where(yrow == 0, left, pltpu.roll(f, 1, 0))
-            beside = beside + jnp.where(zlane == sz - 1, 0.0, pltpu.roll(f, sz - 1, 1))
-            beside = beside + jnp.where(zlane == 0, 0.0, pltpu.roll(f, 1, 1))
-            fluid[m, x] = f + 0.1 * (beside - 6.0 * f) + (grid[m, x] - grid[3, x] * f)
+            fluid[m, x] = spread[m, x] + (grid[m, x] - grid[3, x] * fv[m, x])
     table = []
     for m in range(3):
         tiles = []
@@ -196,7 +203,7 @@
     return a, b, n - a - b
 
 
-def push_loop(step, begin, end, first, second, pos, low, high, push, feat_b, feat_a):
+def push_loop(step, first, second, pos, low, high, push, feat_b, feat_a):
     blocks = pos.shape[1]
     one = jnp.ones((8, 128), F32)
     zero = jnp.zeros((8, 128), F32)
@@ -232,10 +239,9 @@
         x, y = fa[0:8], fa[8:16]
         z = jnp.where(top, y, 0.0)
         ga = jnp.concatenate([x, jnp.where(top, x, y), z, z], axis=0).astype(BF16)
-        fbt = jnp.concatenate([fb, fb], axis=0).T.astype(BF16)
-        r2 = dot(fbt, ga)
+        lhs = fb.astype(BF16)
+        r2 = dot(jnp.concatenate([lhs, lhs], axis=0), ga, ((0,), (0,)))
         w = jnp.maximum(lax.rsqrt(jnp.maximum(r2, EPS2)) - 4.0, 0.0)
-        lhs = fb.astype(BF16)
         res = dot(jnp.concatenate([lhs, lhs], axis=1), jnp.concatenate(split2(w), axis=0))
         total = jnp.broadcast_to(res[3:4], (8, 128))
         return a, (-0.5) * (x + z) * total - (res[0:8] + res[8:16])
@@ -247,12 +253,11 @@
             push[rows, :] = push[rows, :] + f
         return c
 
-    lax.fori_loop(begin // PAIR_GROUP, end // PAIR_GROUP, pairs, 0)
-
-
-def push_kernel(begin, end, first, second, pos, low, high, after, push, done, feat_b, feat_a):
-    push_loop(0, begin, end, first, second, pos, (low, 96), (high, 96), push, feat_b, feat_a)
-    done[...] = jnp.zeros(done.shape, F32)
+    lax.fori_loop(0, first.shape[1] // PAIR_GROUP, pairs, 0)
+
+
+def push_kernel(first, second, pos, low, high, after, push, feat_b, feat_a):
+    push_loop(0, first, second, pos, (low, 96), (high, 96), push, feat_b, feat_a)
 
 
 def advance(pos, vel, push, flow, pos_out, vel_out):
@@ -260,8 +265,7 @@
     drift = 2.0 * flow[pl.ds(3, blocks, stride=8), :]
     for m in range(3):
         v = vel[m]
-        total = sum(part[pl.ds(m, blocks, stride=8), :] for part in push)
-        force = 2.5 * total + drift * (flow[pl.ds(m, blocks, stride=8), :] - v)
+        force = 2.5 * push[pl.ds(m, blocks, stride=8), :] + drift * (flow[pl.ds(m, blocks, stride=8), :] - v)
         if m == 2:
             force = force - 1.0
         v = v + 0.1 * force
@@ -276,7 +280,7 @@
     return both[0:8] + both[8:16]
 
 
-def listed_kernel(slot, halo, back, cell, pos, vel, push_a, push_b, down_out, up_out):
+def listed_kernel(slot, halo, back, cell, pos, vel, push, down_out, up_out):
     r8 = lax.broadcasted_iota(jnp.int32, (8, 128), 0)
 
     def tile(ref, q):
@@ -290,14 +294,14 @@
             v = tile(vel, q)
             rows = pl.ds(pl.multiple_of(q * 8, 8), 8)
             drift = 2.0 * jnp.broadcast_to(flow[3:4], (8, 128))
-            force = 2.5 * (push_a[rows, :] + push_b[rows, :]) + drift * (flow - v)
+            force = 2.5 * push[rows, :] + drift * (flow - v)
             v = v + 0.1 * jnp.where(r8 == 2, force - 1.0, force)
             x = tile(pos, q) + 0.1 * v
             for m in range(3):
                 out[m * 16 + j : m * 16 + j + 1, :] = x[m : m + 1, :]
 
 
-def pick_kernel(slot, back, cell, pos, vel, push_a, push_b, after, flow, pos_out, vel_out):
+def pick_kernel(slot, back, cell, pos, vel, push, after, flow, pos_out, vel_out):
     def group(g, c):
         base = pl.multiple_of(g * BLOCK_GROUP, BLOCK_GROUP)
         cells = cell[pl.ds(base, BLOCK_GROUP), :]
@@ -307,12 +311,12 @@
         return c
 
     lax.fori_loop(0, cell.shape[0] // BLOCK_GROUP, group, 0)
-    advance(pos, vel, (push_a, push_b), flow, pos_out, vel_out)
+    advance(pos, vel, push, flow, pos_out, vel_out)
 
 
 def last_kernel(first, second, pos, vel, low, high, flow, pos_out, vel_out, push, feat_b, feat_a):
-    push_loop(1, 0, first.shape[1], first, second, pos, (low, 0), (high, 0), push, feat_b, feat_a)
-    advance(pos, vel, (push,), flow, pos_out, vel_out)
+    push_loop(1, first, second, pos, (low, 0), (high, 0), push, feat_b, feat_a)
+    advance(pos, vel, push, flow, pos_out, vel_out)
 
 
 def call(kernel, in_specs, out_shape, out_specs, scratch=(), micros=1):
@@ -350,12 +354,21 @@
     pos = jnp.transpose(part_pos, (1, 0, 2))
     vel = jnp.transpose(part_vel, (1, 0, 2))
 
+    send, slot, placed = call(
+        deposit_kernel,
+        [SMEM, SMEM, VMEM, VMEM],
+        [shape(slots, 4, 128), shape(blocks, dtype=jnp.int32), shape(8, 128)],
+        [VMEM, SMEM, VMEM],
+        [pltpu.SMEM((tiles,), jnp.int32)],
+        7,
+    )(brick_owner[:, 0], brick_local, cell_in_brick, vel)
+    recv = lax.all_to_all(send.reshape(slots * 4, 128), ("gx", "gy"), split_axis=0, concat_axis=0, tiled=True)
     down, up, left, right = call(
         faces_kernel,
-        [SMEM, VMEM, VMEM],
+        [SMEM, VMEM, VMEM, VMEM],
         [shape(144, 128), shape(144, 128), shape(3, sx, sz), shape(3, sx, sz)],
         [VMEM] * 4,
-    )(halo_list, fluid_vel, pos)
+    )(halo_list, fluid_vel, pos, placed)
     fwd = [(i, (i + 1) % nx) for i in range(nx)]
     bwd = [((i + 1) % nx, i) for i in range(nx)]
     from_low = lax.ppermute(up, "gx", fwd)
@@ -363,61 +376,53 @@
     from_left = lax.ppermute(right, "gy", [(i, i + 1) for i in range(ny - 1)])
     from_right = lax.ppermute(left, "gy", [(i + 1, i) for i in range(ny - 1)])
 
-    send, slot, placed = call(
-        deposit_kernel,
-        [SMEM, SMEM, VMEM, VMEM, VMEM],
-        [shape(slots, 4, 128), shape(blocks, dtype=jnp.int32), shape(8, 128)],
-        [VMEM, SMEM, VMEM],
-        [pltpu.SMEM((tiles,), jnp.int32)],
-        7,
-    )(brick_owner[:, 0], brick_local, cell_in_brick, vel, down)
-    recv = lax.all_to_all(send.reshape(slots * 4, 128), ("gx", "gy"), split_axis=0, concat_axis=0, tiled=True)
-
-    pairs = pair_self.shape[1]
+
     pair_scratch = [pltpu.VMEM(((blocks + 32) * 16, 128), F32), pltpu.VMEM((blocks * 16, 128), F32)]
 
-    def push(begin, end, after):
-        return call(
-            functools.partial(push_kernel, begin, end),
-            [SMEM, SMEM, VMEM, VMEM, VMEM, VMEM],
-            [shape(blocks * 8, 128), shape(8, 128)],
-            [VMEM, VMEM],
-            pair_scratch,
-            8,
-        )(pair_self, pair_other, pos, from_low, from_high, after)
-
-    push_a, done_a = push(0, pairs // 2, placed)
     me = lax.axis_index("gx")
     ends = jnp.stack([me > 0, me < nx - 1]).astype(jnp.int32)
+    spread = call(
+        spread_kernel,
+        [SMEM] + [VMEM] * 5,
+        shape(3, sx, sy, sz),
+        VMEM,
+    )(ends, fluid_vel, from_low, from_high, from_left, from_right)
     fluid, answer, stepped = call(
         fluid_kernel,
-        [SMEM] + [VMEM] * 7,
+        [VMEM] * 3,
         [shape(3, sx, sy, sz), shape(slots * 4, 128), shape(8, 128)],
         [VMEM] * 3,
         [pltpu.VMEM((4, sx, sy, sz), F32)],
         4,
-    )(ends, recv, fluid_vel, from_low, from_high, from_left, from_right, done_a)
+    )(recv, fluid_vel, spread)
     back = lax.all_to_all(answer, ("gx", "gy"), split_axis=0, concat_axis=0, tiled=True).reshape(slots, 4, 128)
-    push_b, _ = push(pairs // 2, pairs, stepped)
+    push = call(
+        push_kernel,
+        [SMEM, SMEM, VMEM, VMEM, VMEM, VMEM],
+        shape(blocks * 8, 128),
+        VMEM,
+        pair_scratch,
+        14,
+    )(pair_self, pair_other, pos, from_low, from_high, stepped)
 
     down, up = call(
         listed_kernel,
-        [SMEM, SMEM] + [VMEM] * 6,
+        [SMEM, SMEM] + [VMEM] * 5,
         [shape(48, 128), shape(48, 128)],
         [VMEM] * 2,
         (),
         2,
-    )(slot, halo_list, back, cell_in_brick, pos, vel, push_a, push_b)
+    )(slot, halo_list, back, cell_in_brick, pos, vel, push)
     low = lax.ppermute(up, "gx", fwd)
     high = lax.ppermute(down, "gx", bwd)
     flow, pos, vel = call(
         pick_kernel,
-        [SMEM] + [VMEM] * 7,
+        [SMEM] + [VMEM] * 6,
         [shape(blocks * 8, 128), shape(3, blocks, 128), shape(3, blocks, 128)],
         [VMEM] * 3,
         (),
         6,
-    )(slot, back, cell_in_brick, pos, vel, push_a, push_b, down)
+    )(slot, back, cell_in_brick, pos, vel, push, down)
     pos, vel = call(
         last_kernel,
         [SMEM, SMEM] + [VMEM] * 5,

time: 107 us -> 93.6 us (0.87)
  Pallas kernels: 47.9 us -> 41.9 us
  waiting for transfers between devices: 20.3 us -> 15.7 us
  local copies, waits for them, and re-layouts: 7.8 us -> 3.24 us
  starting transfers between devices: 30.2 us -> 31.5 us
    unnamed x32 -> x22, local copies, waits for them, and re-layouts: 7.8 us -> 3.24 us
    pallas_call x7, Pallas kernels: 33 us -> 28.7 us  [the longest x1 12 us: per_device(): call(push_kernel, [SMEM, SMEM, VMEM, VMEM, VMEM, VMEM], shape(blocks * 8,...]
    ppermute x1, waiting for transfers between devices: 10.5 us -> 7.07 us  [per_device(): from_low = lax.ppermute(up, 'gx', fwd)]
    all_to_all x1, waiting for transfers between devices: 9.76 us -> 7.13 us  [per_device(): lax.all_to_all(answer, ('gx', 'gy'), split_axis=0, concat_axis=0, tiled=T...]
    ppermute x1, starting transfers between devices: 0.08 us -> 1.86 us  [per_device(): from_low = lax.ppermute(up, 'gx', fwd)]
    pallas_call x1, Pallas kernels: 14.9 us -> 13.1 us  [per_device(): call(last_kernel, [SMEM, SMEM] + [VMEM] * 5, [shape(3, blocks, 128), shap...]
    all_to_all x1, waiting for transfers between devices: 0.01 us -> 1.49 us  [per_device(): lax.all_to_all(send.reshape(slots * 4, 128), ('gx', 'gy'), split_axis=0,...]
  transfers between devices with their start and end apart: 8 -> 8, of which waited for: 2 -> 3; matrix products, arithmetic and copies ran while one was open for 0% -> 0% of each run, Pallas kernels for 19% -> 19%
where the time goes in v3:
time: 93.6 us; the launch traced here: 93.2 us
  Pallas kernels  41.9 us (45%)
  starting transfers between devices  31.5 us (34%)
  waiting for transfers between devices  15.7 us (17%)
  local copies, waits for them, and re-layouts  3.24 us (3%)
    pallas_call x1, Pallas kernels, per_device(): call(last_kernel, [SMEM, SMEM] + [VMEM] * 5, [shape(3, blocks, 128), shap...  13.1 us
    pallas_call x1, Pallas kernels, per_device(): call(push_kernel, [SMEM, SMEM, VMEM, VMEM, VMEM, VMEM], shape(blocks * 8,...  12 us
    all_to_all x1, starting transfers between devices, per_device(): lax.all_to_all(send.reshape(slots * 4, 128), ('gx', 'gy'), split_axis=0,...  11.1 us
    pallas_call x1, Pallas kernels, per_device(): call(deposit_kernel, [SMEM, SMEM, VMEM, VMEM], [shape(slots, 4, 128), sha...  7.18 us
    all_to_all x1, waiting for transfers between devices, per_device(): lax.all_to_all(answer, ('gx', 'gy'), split_axis=0, concat_axis=0, tiled=T...  7.13 us
    ppermute x1, waiting for transfers between devices, per_device(): from_low = lax.ppermute(up, 'gx', fwd)  7.07 us
    all_to_all x1, starting transfers between devices, per_device(): lax.all_to_all(answer, ('gx', 'gy'), split_axis=0, concat_axis=0, tiled=T...  6.31 us
    ppermute x1, starting transfers between devices, per_device(): high = lax.ppermute(down, 'gx', bwd)  4.95 us
  transfers between devices with their start and end apart: 8, of which 3 were waited for; matrix products, arithmetic and copies ran while one was open for 0% of the time, Pallas kernels for 19%

profile of v3, /device:TPU:0, one launch (start us, length us, event | category | flops | bytes accessed | tf_op | source)
XLA Modules:
  0.0 93.2 jit_solution(10770300421961498567)
XLA Ops:
  0.6 0.0 copy-start.9
  0.6 0.0 copy-start.8
  0.7 0.7 copy-done.9
  1.3 0.0 copy-done.8
  1.3 0.0 copy-start.1
  1.3 1.0 %copy-done.1 = f32[256,3,128]{2,0,1:T(8,128)S(1)} copy-done((f32[256,3,128]{2,0,1:T(8,128)S(1)}, f32[256,3,128]{2,0,1:T(8,128)}, u32[]{:S(2)}) %copy-start.1) | copy-done | bytes 393240
  2.3 0.0 copy-start.4
  2.3 0.9 copy-done.4
  3.2 7.2 %shard_map.112 = (f32[512,4,128]{2,1,0:T(4,128)}, s32[256]{0:T(256)S(1)}, f32[8,128]{1,0:T(8,128)S(1)}) custom-call(s32[256]{0:T(256)S(1)} %bitcast.21, s32[256]{0:T(256)S(1)} %copy-done.9, s32[256,128]{1,0:T(8,128)S(1)} %copy-done.4, f32[3,256,128]{2,1,0:T(8,128)S(1)} %bitcast.14), custom_call_target="tpu_custom_call" | custom-call | flops 7000000000 | bytes 21000000 | tf_op jit(solution)/shard_map/pallas_call | solution.py:357
  10.4 0.0 copy-start
  10.4 0.0 copy-start.3
  10.4 11.1 %all-to-all-start = ((f32[128,16,128]{2,1,0:T(8,128)}), f32[128,16,128]{2,1,0:T(8,128)S(1)}, u32[]{:S(2)}, u32[]{:S(2)}) async-start(f32[128,16,128]{2,1,0:T(8,128)} %bitcast.2), calls=%async_computation | async-start | bytes 2097152 | tf_op jit(solution)/shard_map/all_to_all | solution.py:365
  21.6 0.0 copy-start.10
  21.6 0.0 copy-done
  21.6 0.0 copy-done.3
  21.6 0.6 copy-done.10
  22.3 0.6 shard_map.113
  22.9 1.3 %collective-permute-start.2 = (f32[3,8,256]{2,1,0:T(8,128)S(1)}, f32[3,8,256]{2,1,0:T(8,128)S(1)}, u32[]{:S(2)}, u32[]{:S(2)}) collective-permute-start(f32[3,8,256]{2,1,0:T(8,128)S(1)} %get-tuple-element.24), channel_id=1, source_target_pairs={{0,1},{1,2},{2,3},{3,4},{4,5},{5,6},{6,7},{8,9},{9,10},{10,11},{11... | collective-permute-start | bytes 73736 | tf_op jit(solution)/shard_map/ppermute | solution.py:376
  24.2 1.3 %collective-permute-start.3 = (f32[3,8,256]{2,1,0:T(8,128)S(1)}, f32[3,8,256]{2,1,0:T(8,128)S(1)}, u32[]{:S(2)}, u32[]{:S(2)}) collective-permute-start(f32[3,8,256]{2,1,0:T(8,128)S(1)} %get-tuple-element.25), channel_id=1, source_target_pairs={{1,0},{2,1},{3,2},{4,3},{5,4},{6,5},{7,6},{9,8},{10,9},{11,10},{12... | collective-permute-start | bytes 73736 | tf_op jit(solution)/shard_map/ppermute | solution.py:377
  25.5 1.9 %collective-permute-start = (f32[144,128]{1,0:T(8,128)S(1)}, f32[144,128]{1,0:T(8,128)S(1)}, u32[]{:S(2)}, u32[]{:S(2)}) collective-permute-start(f32[144,128]{1,0:T(8,128)S(1)} %get-tuple-element.22), channel_id=1, source_target_pairs={{0,8},{8,16},{16,24},{24,32},{32,40},{40,48},{48,56},{56,64},{64,7... | collective-permute-start | bytes 221192 | tf_op jit(solution)/shard_map/ppermute | solution.py:374
  27.4 4.1 %collective-permute-start.1 = (f32[144,128]{1,0:T(8,128)S(1)}, f32[144,128]{1,0:T(8,128)S(1)}, u32[]{:S(2)}, u32[]{:S(2)}) collective-permute-start(f32[144,128]{1,0:T(8,128)S(1)} %get-tuple-element.23), channel_id=1, source_target_pairs={{8,0},{16,8},{24,16},{32,24},{40,32},{48,40},{56,48},{64,56},{72,6... | collective-permute-start | bytes 221192 | tf_op jit(solution)/shard_map/ppermute | solution.py:375
  31.5 0.1 add_convert_fusion.inside
  31.6 0.0 collective-permute-done.2.from_left
  31.6 0.0 collective-permute-done.3.from_right
  31.6 7.1 %collective-permute-done.from_low.low = f32[144,128]{1,0:T(8,128)S(1)} collective-permute-done((f32[144,128]{1,0:T(8,128)S(1)}, f32[144,128]{1,0:T(8,128)S(1)}, u32[]{:S(2)}, u32[]{:S(2)}) %collective-permute-start) | collective-permute-done | bytes 73760 | tf_op jit(solution)/shard_map/ppermute | solution.py:374
  38.7 0.0 collective-permute-done.1.from_high.high
  38.7 0.8 shard_map.114.spread
  39.5 1.5 %all-to-all-done = f32[128,16,128]{2,1,0:T(8,128)S(1)} async-done(((f32[128,16,128]{2,1,0:T(8,128)}), f32[128,16,128]{2,1,0:T(8,128)S(1)}, u32[]{:S(2)}, u32[]{:S(2)}) %all-to-all-start) | async-done | bytes 1048608 | tf_op jit(solution)/shard_map/all_to_all | solution.py:365
  41.0 3.2 %shard_map.115 = (f32[3,8,16,256]{3,2,1,0:T(8,128)}, f32[2048,128]{1,0:T(8,128)}, f32[8,128]{1,0:T(8,128)S(1)}) custom-call(f32[2048,128]{1,0:T(8,128)S(1)} %bitcast.11, f32[3,8,16,256]{3,2,1,0:T(8,128)S(1)} %copy-done, f32[3,8,16,256]{3,2,1,0:T(8,128)S(1)} %shard_map.114.spread), custom_call_target="tpu_custom_call" | custom-call | flops 4000000000 | bytes 12000000 | tf_op jit(solution)/shard_map/pallas_call | solution.py:390
  44.2 0.0 copy-start.6
  44.2 0.0 copy-start.7
  44.2 6.3 %all-to-all-start.1 = ((f32[128,16,128]{2,1,0:T(8,128)}), f32[128,16,128]{2,1,0:T(8,128)S(1)}, u32[]{:S(2)}, u32[]{:S(2)}) async-start(f32[128,16,128]{2,1,0:T(8,128)} %bitcast.7), calls=%async_computation.1 | async-start | bytes 2097152 | tf_op jit(solution)/shard_map/all_to_all | solution.py:398
  50.6 0.0 copy-done.6
  50.6 0.0 copy-done.7
  50.6 0.0 copy-start.2
  50.6 0.0 copy-start.5
  50.6 12.0 %shard_map.116.push = f32[2048,128]{1,0:T(8,128)S(1)} custom-call(s32[2,512]{1,0:T(2,128)S(1)} %copy-done.6, s32[2,512]{1,0:T(2,128)S(1)} %copy-done.7, f32[3,256,128]{2,1,0:T(8,128)S(1)} %bitcast.18, f32[144,128]{1,0:T(8,128)S(1)} %collective-permute-done.from_low.low, f32[144,128]{1,0:T(8,128)S(1)} %collective-permute-done.1.from_high.high, ...), custom_call_target="tpu_custom_call" | custom-call | flops 14000000000 | bytes 42000000 | tf_op jit(solution)/shard_map/pallas_call | solution.py:399
  62.6 7.1 %all-to-all-done.1 = f32[128,16,128]{2,1,0:T(8,128)S(1)} async-done(((f32[128,16,128]{2,1,0:T(8,128)}), f32[128,16,128]{2,1,0:T(8,128)S(1)}, u32[]{:S(2)}, u32[]{:S(2)}) %all-to-all-start.1) | async-done | bytes 1048608 | tf_op jit(solution)/shard_map/all_to_all | solution.py:398
  69.7 0.0 copy-done.2
  69.7 0.0 copy-done.5
  69.7 1.0 %shard_map.117 = (f32[48,128]{1,0:T(8,128)S(1)}, f32[48,128]{1,0:T(8,128)S(1)}) custom-call(s32[256]{0:T(256)S(1)} %get-tuple-element.27.slot, s32[32]{0:T(128)S(1)} %copy-done.10, f32[512,4,128]{2,1,0:T(4,128)S(1)} %bitcast.12, s32[256,128]{1,0:T(8,128)S(1)} %copy-done.5, f32[3,256,128]{2,1,0:T(8,128)S(1)} %bitcast.19, f32[3,256,128]{2,1,0:T(8,128)S(1)} %bitcast.15, ...), custom_call_target="tpu_custom_call" | custom-call | flops 2000000000 | bytes 6000000 | tf_op jit(solution)/shard_map/pallas_call | solution.py:408
  70.7 0.5 collective-permute-start.4
  71.1 4.9 %collective-permute-start.5 = (f32[48,128]{1,0:T(8,128)S(1)}, f32[48,128]{1,0:T(8,128)S(1)}, u32[]{:S(2)}, u32[]{:S(2)}) collective-permute-start(f32[48,128]{1,0:T(8,128)S(1)} %get-tuple-element.30.after), channel_id=1, source_target_pairs={{8,0},{16,8},{24,16},{32,24},{40,32},{48,40},{56,48},{64,56},{72,6... | collective-permute-start | bytes 73736 | tf_op jit(solution)/shard_map/ppermute | solution.py:417
  76.1 3.9 %shard_map.118 = (f32[2048,128]{1,0:T(8,128)S(1)}, f32[3,256,128]{2,1,0:T(8,128)S(1)}, f32[3,256,128]{2,1,0:T(8,128)S(1)}) custom-call(s32[256]{0:T(256)S(1)} %get-tuple-element.27.slot, f32[512,4,128]{2,1,0:T(4,128)S(1)} %bitcast.13, s32[256,128]{1,0:T(8,128)S(1)} %copy-done.5, f32[3,256,128]{2,1,0:T(8,128)S(1)} %bitcast.20, f32[3,256,128]{2,1,0:T(8,128)S(1)} %bitcast.16, ...), custom_call_target="tpu_custom_call" | custom-call | flops 6000000000 | bytes 18000000 | tf_op jit(solution)/shard_map/pallas_call | solution.py:418
  80.0 0.0 collective-permute-done.4.low
  80.1 0.0 collective-permute-done.5.high
  80.1 13.1 %shard_map.119 = (f32[3,256,128]{2,1,0:T(8,128)}, f32[3,256,128]{2,1,0:T(8,128)}) custom-call(s32[2,512]{1,0:T(2,128)S(1)} %copy-done.6, s32[2,512]{1,0:T(2,128)S(1)} %copy-done.7, f32[3,256,128]{2,1,0:T(8,128)S(1)} %get-tuple-element.31.pos, f32[3,256,128]{2,1,0:T(8,128)S(1)} %get-tuple-element.32.vel, f32[48,128]{1,0:T(8,128)S(1)} %collective-permute-done.4.low, ...), custom_call_target="tpu_custom_call" | custom-call | flops 15000000512 | bytes 45000000 | tf_op jit(solution)/shard_map/pallas_call | solution.py:426
Async XLA Ops:
  0.6 0.7 copy-start.9
  0.6 0.7 copy-start.8
  1.3 1.0 %copy-start.1 = (f32[256,3,128]{2,0,1:T(8,128)S(1)}, f32[256,3,128]{2,0,1:T(8,128)}, u32[]{:S(2)}) copy-start(f32[256,3,128]{2,0,1:T(8,128)} %param.11) | copy-start | bytes 1179652
  2.3 0.9 copy-start.4
  10.4 11.2 %copy-start = (f32[3,8,16,256]{3,2,1,0:T(8,128)S(1)}, f32[3,8,16,256]{3,2,1,0:T(8,128)}, u32[]{:S(2)}) copy-start(f32[3,8,16,256]{3,2,1,0:T(8,128)} %fv.5) | copy-start | bytes 1179652
  10.4 11.2 %copy-start.3 = (f32[256,3,128]{2,0,1:T(8,128)S(1)}, f32[256,3,128]{2,0,1:T(8,128)}, u32[]{:S(2)}) copy-start(f32[256,3,128]{2,0,1:T(8,128)} %param.10) | copy-start | bytes 1179652
  10.4 30.6 %all-to-all-start = ((f32[128,16,128]{2,1,0:T(8,128)}), f32[128,16,128]{2,1,0:T(8,128)S(1)}, u32[]{:S(2)}, u32[]{:S(2)}) async-start(f32[128,16,128]{2,1,0:T(8,128)} %bitcast.2), calls=%async_computation | async-start | bytes 2097152 | tf_op jit(solution)/shard_map/all_to_all | solution.py:365
  21.6 0.7 copy-start.10
  22.9 8.7 %collective-permute-start.2 = (f32[3,8,256]{2,1,0:T(8,128)S(1)}, f32[3,8,256]{2,1,0:T(8,128)S(1)}, u32[]{:S(2)}, u32[]{:S(2)}) collective-permute-start(f32[3,8,256]{2,1,0:T(8,128)S(1)} %get-tuple-element.24), channel_id=1, source_target_pairs={{0,1},{1,2},{2,3},{3,4},{4,5},{5,6},{6,7},{8,9},{9,10},{10,11},{11... | collective-permute-start | bytes 73736 | tf_op jit(solution)/shard_map/ppermute | solution.py:376
  24.2 7.4 %collective-permute-start.3 = (f32[3,8,256]{2,1,0:T(8,128)S(1)}, f32[3,8,256]{2,1,0:T(8,128)S(1)}, u32[]{:S(2)}, u32[]{:S(2)}) collective-permute-start(f32[3,8,256]{2,1,0:T(8,128)S(1)} %get-tuple-element.25), channel_id=1, source_target_pairs={{1,0},{2,1},{3,2},{4,3},{5,4},{6,5},{7,6},{9,8},{10,9},{11,10},{12... | collective-permute-start | bytes 73736 | tf_op jit(solution)/shard_map/ppermute | solution.py:377
  25.5 13.1 %collective-permute-start = (f32[144,128]{1,0:T(8,128)S(1)}, f32[144,128]{1,0:T(8,128)S(1)}, u32[]{:S(2)}, u32[]{:S(2)}) collective-permute-start(f32[144,128]{1,0:T(8,128)S(1)} %get-tuple-element.22), channel_id=1, source_target_pairs={{0,8},{8,16},{16,24},{24,32},{32,40},{40,48},{48,56},{56,64},{64,7... | collective-permute-start | bytes 221192 | tf_op jit(solution)/shard_map/ppermute | solution.py:374
  27.4 11.3 %collective-permute-start.1 = (f32[144,128]{1,0:T(8,128)S(1)}, f32[144,128]{1,0:T(8,128)S(1)}, u32[]{:S(2)}, u32[]{:S(2)}) collective-permute-start(f32[144,128]{1,0:T(8,128)S(1)} %get-tuple-element.23), channel_id=1, source_target_pairs={{8,0},{16,8},{24,16},{32,24},{40,32},{48,40},{56,48},{64,56},{72,6... | collective-permute-start | bytes 221192 | tf_op jit(solution)/shard_map/ppermute | solution.py:375
  44.2 6.3 %copy-start.6 = (s32[2,512]{1,0:T(2,128)S(1)}, s32[2,512]{1,0:T(2,128)}, u32[]{:S(2)}) copy-start(s32[2,512]{1,0:T(2,128)} %first.3) | copy-start | bytes 12292
  44.2 6.3 %copy-start.7 = (s32[2,512]{1,0:T(2,128)S(1)}, s32[2,512]{1,0:T(2,128)}, u32[]{:S(2)}) copy-start(s32[2,512]{1,0:T(2,128)} %second.3) | copy-start | bytes 12292
  44.2 25.5 %all-to-all-start.1 = ((f32[128,16,128]{2,1,0:T(8,128)}), f32[128,16,128]{2,1,0:T(8,128)S(1)}, u32[]{:S(2)}, u32[]{:S(2)}) async-start(f32[128,16,128]{2,1,0:T(8,128)} %bitcast.7), calls=%async_computation.1 | async-start | bytes 2097152 | tf_op jit(solution)/shard_map/all_to_all | solution.py:398
  50.6 19.1 %copy-start.2 = (f32[256,3,128]{2,0,1:T(8,128)S(1)}, f32[256,3,128]{2,0,1:T(8,128)}, u32[]{:S(2)}) copy-start(f32[256,3,128]{2,0,1:T(8,128)} %param.11) | copy-start | bytes 1179652
  50.6 19.1 %copy-start.5 = (s32[256,128]{1,0:T(8,128)S(1)}, s32[256,128]{1,0:T(8,128)}, u32[]{:S(2)}) copy-start(s32[256,128]{1,0:T(8,128)} %cell.5) | copy-start | bytes 393220
  70.7 9.4 %collective-permute-start.4 = (f32[48,128]{1,0:T(8,128)S(1)}, f32[48,128]{1,0:T(8,128)S(1)}, u32[]{:S(2)}, u32[]{:S(2)}) collective-permute-start(f32[48,128]{1,0:T(8,128)S(1)} %get-tuple-element.33), channel_id=1, source_target_pairs={{0,8},{8,16},{16,24},{24,32},{32,40},{40,48},{48,56},{56,64},{64,7... | collective-permute-start | bytes 73736 | tf_op jit(solution)/shard_map/ppermute | solution.py:416
  71.1 8.9 %collective-permute-start.5 = (f32[48,128]{1,0:T(8,128)S(1)}, f32[48,128]{1,0:T(8,128)S(1)}, u32[]{:S(2)}, u32[]{:S(2)}) collective-permute-start(f32[48,128]{1,0:T(8,128)S(1)} %get-tuple-element.30.after), channel_id=1, source_target_pairs={{8,0},{16,8},{24,16},{32,24},{40,32},{48,40},{56,48},{64,56},{72,6... | collective-permute-start | bytes 73736 | tf_op jit(solution)/shard_map/ppermute | solution.py:417

commit v4 on v3

--- a/solution.py
+++ b/solution.py
@@ -11,11 +11,12 @@
 BF16 = jnp.bfloat16
 PAIR_GROUP = 128
 BLOCK_GROUP = 32
+DEPOSIT_GROUP = 64
 CAP = 4
 EPS2 = 0.0025
 VMEM = pl.BlockSpec(memory_space=pltpu.VMEM)
 SMEM = pl.BlockSpec(memory_space=pltpu.SMEM)
-PARAMS = dict(vmem_limit_bytes=20 * 1024 * 1024)
+HBM = pl.BlockSpec(memory_space=pltpu.HBM)
 
 
 def split2(x):
@@ -32,27 +33,31 @@
     return lax.dot_general(a, b, (dims, ((), ())), preferred_element_type=F32)
 
 
-def pack_rows(halo, pos, out, first, half):
-    for j in range(16):
-        q = halo[half * 16 + j]
+def faces_kernel(fv, after, down_out, up_out, left_out, right_out):
+    for out, x in ((down_out, 0), (up_out, fv.shape[1] - 1)):
         for m in range(3):
-            out[pl.ds(first + m * 16 + j, 1), :] = pos[m, pl.ds(q, 1), :]
-
-
-def faces_kernel(halo, fv, pos, after, down_out, up_out, left_out, right_out):
-    sx = fv.shape[1]
-    for out, x, half in ((down_out, 0, 0), (up_out, sx - 1, 1)):
-        for m in range(3):
-            for h in range(2):
-                out[(m * 2 + h) * 16 : (m * 2 + h + 1) * 16, :] = fv[m, x, :, h * 128 : (h + 1) * 128]
-        pack_rows(halo, pos, out, 96, half)
+            out[m] = fv[m, x]
     for out, y in ((left_out, 0), (right_out, fv.shape[2] - 1)):
         for m in range(3):
-            out[m, :, :] = fv[m, :, y, :]
-
-
-def deposit_kernel(owner, local, cell, vel, out, slot_out, done, taken):
+            out[m] = fv[m, :, y, :]
+
+
+def send_kernel(halo, pos, after, down_out, up_out):
+    for half, out in ((0, down_out), (1, up_out)):
+        for j in range(16):
+            q = halo[half * 16 + j]
+            for m in range(3):
+                out[m * 16 + j : m * 16 + j + 1, :] = pos[m, pl.ds(q, 1), :]
+
+
+def deposit_kernel(owner_in, local_in, cell_in, vel_in, out, slot_out, done, taken, owner, local, cell, vel, sems):
     blocks = cell.shape[0]
+    copies = [
+        pltpu.make_async_copy(src, dst, sems.at[i])
+        for i, (src, dst) in enumerate(((vel_in, vel), (cell_in, cell), (owner_in, owner), (local_in, local)))
+    ]
+    for c in copies:
+        c.start()
     lanes = lax.broadcasted_iota(jnp.int32, (4, 128), 1)
     rows4 = lax.broadcasted_iota(jnp.int32, (4, 128), 0)
     mark = (lanes == 127) & (rows4 == 0)
@@ -65,20 +70,21 @@
 
     lax.fori_loop(0, taken.shape[0], clear, 0, unroll=8)
     r8 = lax.broadcasted_iota(jnp.int32, (8, 128), 0)
+    for c in copies:
+        c.wait()
 
     def group(g, c):
-        base = pl.multiple_of(g * BLOCK_GROUP, BLOCK_GROUP)
-        cells = cell[pl.ds(base, BLOCK_GROUP), :]
-        v = [vel[m, pl.ds(base, BLOCK_GROUP), :] for m in range(3)]
-        for k in range(BLOCK_GROUP):
+        base = pl.multiple_of(g * DEPOSIT_GROUP, DEPOSIT_GROUP)
+        cells = cell[pl.ds(base, DEPOSIT_GROUP), :]
+        v = [vel[m, pl.ds(base, DEPOSIT_GROUP), :] for m in range(3)]
+        for k in range(DEPOSIT_GROUP):
             q = base + k
-            hot = onehot_cells(cells[k : k + 1, :])
             rows = [jnp.broadcast_to(v[m][k : k + 1, :], (8, 128)) for m in range(3)]
             load = jnp.where(r8 == 1, rows[0], jnp.where(r8 == 2, rows[1], rows[2]))
             load = jnp.where(r8 == 0, 1.0, jnp.where(r8 < 4, load, 0.0))
             hi = load.astype(BF16).astype(F32)
             lhs = jnp.concatenate([hi, load - hi], axis=0).astype(BF16)
-            both = dot(lhs, hot, ((1,), (1,)))
+            both = dot(lhs, onehot_cells(cells[k : k + 1, :]), ((1,), (1,)))
             both = both[0:8] + both[8:16]
             tile = owner[q]
             rank = taken[tile]
@@ -89,7 +95,7 @@
             out[slot] = jnp.where(mark, ident, both[0:4])
         return c
 
-    lax.fori_loop(0, blocks // BLOCK_GROUP, group, 0)
+    lax.fori_loop(0, blocks // DEPOSIT_GROUP, group, 0)
 
 
 def swap_groups(v):
@@ -104,31 +110,49 @@
     return v
 
 
-def spread_kernel(inside, fv, from_low, from_high, from_left, from_right, out):
+def places(sx, sy):
+    return [
+        (bx * 2, slice(by * 4, by * 4 + 4), slice(h * 128, h * 128 + 128))
+        for bx in range(sx // 2)
+        for by in range(sy // 4)
+        for h in range(2)
+    ]
+
+
+def to_bricks(grid, m):
+    tiles = [jnp.concatenate([grid[m, x, y, z], grid[m, x + 1, y, z]], axis=0) for x, y, z in places(*grid.shape[1:3])]
+    return swap_groups(jnp.stack(tiles, axis=0)).reshape(len(tiles) * 8, 128)
+
+
+def old_kernel(fv, bricks):
+    for m in range(3):
+        bricks[m] = to_bricks(fv, m)
+
+
+def spread_kernel(fv, from_low, from_high, from_left, from_right, bricks, grid):
     sx, sy, sz = fv.shape[1:]
     yrow = lax.broadcasted_iota(jnp.int32, (sy, sz), 0)
     zlane = lax.broadcasted_iota(jnp.int32, (sy, sz), 1)
-    low_on = (inside[0]).astype(F32)
-    high_on = (inside[1]).astype(F32)
-    for m in range(3):
-        low = jnp.concatenate([from_low[(m * 2 + h) * 16 : (m * 2 + h + 1) * 16, :] for h in range(2)], axis=1) * low_on
-        high = jnp.concatenate([from_high[(m * 2 + h) * 16 : (m * 2 + h + 1) * 16, :] for h in range(2)], axis=1) * high_on
+    for m in range(3):
         for x in range(sx):
             f = fv[m, x]
-            beside = (fv[m, x + 1] if x < sx - 1 else high) + (fv[m, x - 1] if x > 0 else low)
+            high = fv[m, x + 1] if x < sx - 1 else from_high[m]
+            low = fv[m, x - 1] if x > 0 else from_low[m]
+            beside = high + low
             right = jnp.broadcast_to(from_right[m, x : x + 1, :], (sy, sz))
             left = jnp.broadcast_to(from_left[m, x : x + 1, :], (sy, sz))
             beside = beside + jnp.where(yrow == sy - 1, right, pltpu.roll(f, sy - 1, 0))
             beside = beside + jnp.where(yrow == 0, left, pltpu.roll(f, 1, 0))
             beside = beside + jnp.where(zlane == sz - 1, 0.0, pltpu.roll(f, sz - 1, 1))
             beside = beside + jnp.where(zlane == 0, 0.0, pltpu.roll(f, 1, 1))
-            out[m, x] = f + 0.1 * (beside - 6.0 * f)
-
-
-def fluid_kernel(recv, fv, spread, fluid, answer, done, grid):
-    sx, sy, sz = fv.shape[1:]
+            grid[m, x] = f + 0.1 * (beside - 6.0 * f)
+    for m in range(3):
+        bricks[m] = to_bricks(grid, m)
+
+
+def fluid_kernel(recv, old, spread, answer, new):
     slots = recv.shape[0] // 4
-    bricks = sx // 2 * (sy // 4) * (sz // 16)
+    bricks = old.shape[1]
     count = recv[pl.ds(0, slots, stride=4), :]
     lane = lax.broadcasted_iota(jnp.int32, (slots, 128), 1)
     ident = count[:, 127:128]
@@ -150,39 +174,17 @@
     voids = 1.0 - 0.6 * solid / (1.0 + solid)
     beta = (1.0 - voids) / (voids * voids)
     scale = 0.15 * beta
-    sources = [scale * momentum[m] for m in range(3)] + [scale * cnt]
-    for c in range(4):
-        moved = swap_groups(sources[c].reshape(bricks // 8, 8, 128))
-        for bx in range(sx // 2):
-            for by in range(sy // 4):
-                for h in range(2):
-                    v = moved[(bx * 4 + by) * 2 + h]
-                    for x in range(2):
-                        grid[c, bx * 2 + x, by * 4 : by * 4 + 4, h * 128 : h * 128 + 128] = v[x * 4 : x * 4 + 4, :]
-    for m in range(3):
-        for x in range(sx):
-            fluid[m, x] = spread[m, x] + (grid[m, x] - grid[3, x] * fv[m, x])
     table = []
     for m in range(3):
-        tiles = []
-        for bx in range(sx // 2):
-            for by in range(sy // 4):
-                for h in range(2):
-                    tiles.append(
-                        jnp.concatenate(
-                            [fluid[m, bx * 2 + x, by * 4 : by * 4 + 4, h * 128 : h * 128 + 128] for x in range(2)],
-                            axis=0,
-                        )
-                    )
-        v = swap_groups(jnp.stack(tiles, axis=0)).reshape(bricks, 128)
-        table += list(split2(v))
+        fluid = spread[m] + scale * (momentum[m] - cnt * old[m])
+        new[m] = fluid
+        table += list(split2(fluid))
     table += list(split2(beta))
     found = dot(by_slot, jnp.concatenate(table, axis=1))
     for c in range(4):
         answer[pl.ds(c, slots, stride=4), :] = (
             found[:, 2 * c * 128 : (2 * c + 1) * 128] + found[:, (2 * c + 1) * 128 : (2 * c + 2) * 128]
         )
-    done[...] = jnp.zeros(done.shape, F32)
 
 
 def feature_rows(x):
@@ -223,9 +225,9 @@
         return c
 
     lax.fori_loop(0, blocks // 8, own, 0, unroll=2)
-    for i, (ref, at) in enumerate((low, high)):
+    for i, ref in enumerate((low, high)):
         for g in range(2):
-            hi, lo, _, norm = feature_rows([ref[at + m * 16 + g * 8 : at + m * 16 + g * 8 + 8, :] for m in range(3)])
+            hi, lo, _, norm = feature_rows([ref[m * 16 + g * 8 : m * 16 + g * 8 + 8, :] for m in range(3)])
             n = split3(norm)
             put(feat_b, blocks + i * 16 + g * 8, hi + [one, n[0], n[1], n[2], one] + lo + [one, zero, zero, zero, zero])
     push[...] = jnp.zeros(push.shape, F32)
@@ -256,8 +258,13 @@
     lax.fori_loop(0, first.shape[1] // PAIR_GROUP, pairs, 0)
 
 
-def push_kernel(first, second, pos, low, high, after, push, feat_b, feat_a):
-    push_loop(0, first, second, pos, (low, 96), (high, 96), push, feat_b, feat_a)
+def push_kernel(first, second, pos, low, high, new, push, fluid, feat_b, feat_a):
+    for m in range(3):
+        moved = swap_groups(new[m].reshape(new.shape[1] // 8, 8, 128))
+        for i, (x, y, z) in enumerate(places(*fluid.shape[1:3])):
+            fluid[m, x, y, z] = moved[i, 0:4]
+            fluid[m, x + 1, y, z] = moved[i, 4:8]
+    push_loop(0, first, second, pos, low, high, push, feat_b, feat_a)
 
 
 def advance(pos, vel, push, flow, pos_out, vel_out):
@@ -315,18 +322,18 @@
 
 
 def last_kernel(first, second, pos, vel, low, high, flow, pos_out, vel_out, push, feat_b, feat_a):
-    push_loop(1, first, second, pos, (low, 0), (high, 0), push, feat_b, feat_a)
+    push_loop(1, first, second, pos, low, high, push, feat_b, feat_a)
     advance(pos, vel, push, flow, pos_out, vel_out)
 
 
-def call(kernel, in_specs, out_shape, out_specs, scratch=(), micros=1):
+def call(kernel, in_specs, out_shape, out_specs, scratch=(), micros=1, vmem=20 * 1024 * 1024):
     return pl.pallas_call(
         kernel,
         in_specs=in_specs,
         out_shape=out_shape,
         out_specs=out_specs,
         scratch_shapes=list(scratch),
-        compiler_params=pltpu.CompilerParams(**PARAMS),
+        compiler_params=pltpu.CompilerParams(vmem_limit_bytes=vmem),
         cost_estimate=pl.CostEstimate(flops=micros * 1_000_000_000, bytes_accessed=micros * 3_000_000, transcendentals=0),
     )
 
@@ -356,54 +363,71 @@
 
     send, slot, placed = call(
         deposit_kernel,
-        [SMEM, SMEM, VMEM, VMEM],
+        [HBM] * 4,
         [shape(slots, 4, 128), shape(blocks, dtype=jnp.int32), shape(8, 128)],
         [VMEM, SMEM, VMEM],
-        [pltpu.SMEM((tiles,), jnp.int32)],
+        [
+            pltpu.SMEM((tiles,), jnp.int32),
+            pltpu.SMEM((blocks,), jnp.int32),
+            pltpu.SMEM((blocks,), jnp.int32),
+            pltpu.VMEM((blocks, 128), jnp.int32),
+            pltpu.VMEM((3, blocks, 128), F32),
+            pltpu.SemaphoreType.DMA((4,)),
+        ],
         7,
+        63_000_000,
     )(brick_owner[:, 0], brick_local, cell_in_brick, vel)
     recv = lax.all_to_all(send.reshape(slots * 4, 128), ("gx", "gy"), split_axis=0, concat_axis=0, tiled=True)
+
     down, up, left, right = call(
         faces_kernel,
-        [SMEM, VMEM, VMEM, VMEM],
-        [shape(144, 128), shape(144, 128), shape(3, sx, sz), shape(3, sx, sz)],
+        [VMEM, VMEM],
+        [shape(3, sy, sz), shape(3, sy, sz), shape(3, sx, sz), shape(3, sx, sz)],
         [VMEM] * 4,
-    )(halo_list, fluid_vel, pos, placed)
+    )(fluid_vel, placed)
+    from_low = lax.ppermute(up, "gx", [(i, i + 1) for i in range(nx - 1)])
+    from_high = lax.ppermute(down, "gx", [(i + 1, i) for i in range(nx - 1)])
+    from_left = lax.ppermute(right, "gy", [(i, i + 1) for i in range(ny - 1)])
+    from_right = lax.ppermute(left, "gy", [(i + 1, i) for i in range(ny - 1)])
+    down, up = call(
+        send_kernel,
+        [SMEM, VMEM, VMEM],
+        [shape(48, 128), shape(48, 128)],
+        [VMEM] * 2,
+    )(halo_list, pos, left)
     fwd = [(i, (i + 1) % nx) for i in range(nx)]
     bwd = [((i + 1) % nx, i) for i in range(nx)]
-    from_low = lax.ppermute(up, "gx", fwd)
-    from_high = lax.ppermute(down, "gx", bwd)
-    from_left = lax.ppermute(right, "gy", [(i, i + 1) for i in range(ny - 1)])
-    from_right = lax.ppermute(left, "gy", [(i + 1, i) for i in range(ny - 1)])
-
-
-    pair_scratch = [pltpu.VMEM(((blocks + 32) * 16, 128), F32), pltpu.VMEM((blocks * 16, 128), F32)]
-
-    me = lax.axis_index("gx")
-    ends = jnp.stack([me > 0, me < nx - 1]).astype(jnp.int32)
+    low = lax.ppermute(up, "gx", fwd)
+    high = lax.ppermute(down, "gx", bwd)
+
+    bricks = sx // 2 * (sy // 4) * (sz // 16)
+    old = call(old_kernel, [VMEM], shape(3, bricks, 128), VMEM)(fluid_vel)
     spread = call(
         spread_kernel,
-        [SMEM] + [VMEM] * 5,
-        shape(3, sx, sy, sz),
+        [VMEM] * 5,
+        shape(3, bricks, 128),
         VMEM,
-    )(ends, fluid_vel, from_low, from_high, from_left, from_right)
-    fluid, answer, stepped = call(
+        [pltpu.VMEM((3, sx, sy, sz), F32)],
+        2,
+    )(fluid_vel, from_low, from_high, from_left, from_right)
+    answer, new = call(
         fluid_kernel,
         [VMEM] * 3,
-        [shape(3, sx, sy, sz), shape(slots * 4, 128), shape(8, 128)],
-        [VMEM] * 3,
-        [pltpu.VMEM((4, sx, sy, sz), F32)],
-        4,
-    )(recv, fluid_vel, spread)
+        [shape(slots * 4, 128), shape(3, bricks, 128)],
+        [VMEM] * 2,
+        (),
+        3,
+    )(recv, old, spread)
     back = lax.all_to_all(answer, ("gx", "gy"), split_axis=0, concat_axis=0, tiled=True).reshape(slots, 4, 128)
-    push = call(
+    pair_scratch = [pltpu.VMEM(((blocks + 32) * 16, 128), F32), pltpu.VMEM((blocks * 16, 128), F32)]
+    push, fluid = call(
         push_kernel,
         [SMEM, SMEM, VMEM, VMEM, VMEM, VMEM],
-        shape(blocks * 8, 128),
-        VMEM,
+        [shape(blocks * 8, 128), shape(3, sx, sy, sz)],
+        [VMEM, VMEM],
         pair_scratch,
         14,
-    )(pair_self, pair_other, pos, from_low, from_high, stepped)
+    )(pair_self, pair_other, pos, low, high, new)
 
     down, up = call(
         listed_kernel,

time: 93.6 us -> 93.9 us (level)
  starting transfers between devices: 31.5 us -> 41.2 us
  waiting for transfers between devices: 15.7 us -> 7.88 us
  local copies, waits for them, and re-layouts: 3.24 us -> 0.72 us
  Pallas kernels: 41.9 us -> 42.9 us
    ppermute x2, waiting for transfers between devices: 7.07 us -> 0.01 us  [the longest x1 0.01 us: per_device(): from_low = lax.ppermute(up, 'gx', [(i, i + 1) for i in range(nx - 1)])]
    ppermute x1 -> x2, starting transfers between devices: 4.95 us -> 10 us  [per_device(): high = lax.ppermute(down, 'gx', bwd)]
    all_to_all x1, starting transfers between devices: 6.31 us -> 9.99 us  [per_device(): lax.all_to_all(answer, ('gx', 'gy'), split_axis=0, concat_axis=0, tiled=T...]
    unnamed x22 -> x18, local copies, waits for them, and re-layouts: 3.24 us -> 0.72 us
    ppermute x1 -> x2, starting transfers between devices: 0.47 us -> 2.32 us  [per_device(): low = lax.ppermute(up, 'gx', fwd)]
    all_to_all x1, waiting for transfers between devices: 7.13 us -> 5.64 us  [per_device(): lax.all_to_all(answer, ('gx', 'gy'), split_axis=0, concat_axis=0, tiled=T...]
    ppermute x2, starting transfers between devices: 6 us -> 4.92 us  [the longest x1 3.63 us: per_device(): from_low = lax.ppermute(up, 'gx', [(i, i + 1) for i in range(nx - 1)])]
    pallas_call x5 -> x7, Pallas kernels: 23.8 us -> 24.8 us  [the longest x1 13.4 us: per_device(): call(push_kernel, [SMEM, SMEM, VMEM, VMEM, VMEM, VMEM], [shape(blocks * 8...]
  transfers between devices with their start and end apart: 8 -> 10, of which waited for: 3 -> 2; matrix products, arithmetic and copies ran while one was open for 0% -> 0% of each run, Pallas kernels for 19% -> 23%
where the time goes in v4:
time: 93.9 us; the launch traced here: 93.5 us
  Pallas kernels  42.9 us (46%)
  starting transfers between devices  41.2 us (44%)
  waiting for transfers between devices  7.88 us (8%)
    pallas_call x1, Pallas kernels, per_device(): call(push_kernel, [SMEM, SMEM, VMEM, VMEM, VMEM, VMEM], [shape(blocks * 8...  13.4 us
    pallas_call x1, Pallas kernels, per_device(): call(last_kernel, [SMEM, SMEM] + [VMEM] * 5, [shape(3, blocks, 128), shap...  13.1 us
    all_to_all x1, starting transfers between devices, per_device(): lax.all_to_all(send.reshape(slots * 4, 128), ('gx', 'gy'), split_axis=0,...  11.1 us
    ppermute x2, starting transfers between devices, per_device(): high = lax.ppermute(down, 'gx', bwd)  10 us
    all_to_all x1, starting transfers between devices, per_device(): lax.all_to_all(answer, ('gx', 'gy'), split_axis=0, concat_axis=0, tiled=T...  9.99 us
    pallas_call x1, Pallas kernels, per_device(): call(deposit_kernel, [HBM] * 4, [shape(slots, 4, 128), shape(blocks, dtyp...  6.93 us
    all_to_all x1, waiting for transfers between devices, per_device(): lax.all_to_all(answer, ('gx', 'gy'), split_axis=0, concat_axis=0, tiled=T...  5.64 us
    pallas_call x1, Pallas kernels, per_device(): call(pick_kernel, [SMEM] + [VMEM] * 6, [shape(blocks * 8, 128), shape(3,...  3.95 us
  transfers between devices with their start and end apart: 10, of which 2 were waited for; matrix products, arithmetic and copies ran while one was open for 0% of the time, Pallas kernels for 23%

profile of v4, /device:TPU:0, one launch (start us, length us, event | category | flops | bytes accessed | tf_op | source)
XLA Modules:
  0.0 93.5 jit_solution(12117371694113885696)
XLA Ops:
  0.6 6.9 %shard_map.112 = (f32[512,4,128]{2,1,0:T(4,128)}, s32[256]{0:T(256)}, f32[8,128]{1,0:T(8,128)}) custom-call(s32[256]{0:T(256)} %bitcast.20, s32[256]{0:T(256)} %local_in.1, s32[256,128]{1,0:T(8,128)} %cell.3, f32[3,256,128]{2,1,0:T(8,128)} %bitcast.16), custom_call_target="tpu_custom_call" | custom-call | flops 7000000000 | bytes 21000000 | tf_op jit(solution)/shard_map/pallas_call | solution.py:364
  7.6 0.0 copy-start
  7.6 0.0 copy-start.7
  7.6 11.1 %all-to-all-start = ((f32[128,16,128]{2,1,0:T(8,128)}), f32[128,16,128]{2,1,0:T(8,128)S(1)}, u32[]{:S(2)}, u32[]{:S(2)}) async-start(f32[128,16,128]{2,1,0:T(8,128)} %bitcast.19), calls=%async_computation | async-start | bytes 2097152 | tf_op jit(solution)/shard_map/all_to_all | solution.py:380
  18.7 0.0 copy-done
  18.8 0.0 copy-done.7
  18.8 0.0 copy-start.1
  18.8 1.5 %collective-permute-start.4 = (f32[3,8,256]{2,1,0:T(8,128)S(1)}, f32[3,8,256]{2,1,0:T(8,128)S(1)}, u32[]{:S(2)}, u32[]{:S(2)}) collective-permute-start(f32[3,8,256]{2,1,0:T(8,128)S(1)} %get-tuple-element.30), channel_id=1, source_target_pairs={{0,1},{1,2},{2,3},{3,4},{4,5},{5,6},{6,7},{8,9},{9,10},{10,11},{11... | collective-permute-start | bytes 73736 | tf_op jit(solution)/shard_map/ppermute | solution.py:390
  20.3 0.0 copy-start.6
  20.3 1.3 %collective-permute-start.5 = (f32[3,8,256]{2,1,0:T(8,128)S(1)}, f32[3,8,256]{2,1,0:T(8,128)S(1)}, u32[]{:S(2)}, u32[]{:S(2)}) collective-permute-start(f32[3,8,256]{2,1,0:T(8,128)S(1)} %get-tuple-element.24.after), channel_id=1, source_target_pairs={{1,0},{2,1},{3,2},{4,3},{5,4},{6,5},{7,6},{9,8},{10,9},{11,10},{12... | collective-permute-start | bytes 73736 | tf_op jit(solution)/shard_map/ppermute | solution.py:391
  21.6 0.0 copy-done.1
  21.6 0.0 copy-done.6
  21.6 0.6 shard_map.114
  22.2 1.9 %collective-permute-start = (f32[48,128]{1,0:T(8,128)S(1)}, f32[48,128]{1,0:T(8,128)S(1)}, u32[]{:S(2)}, u32[]{:S(2)}) collective-permute-start(f32[48,128]{1,0:T(8,128)S(1)} %get-tuple-element.25), channel_id=1, source_target_pairs={{0,8},{8,16},{16,24},{24,32},{32,40},{40,48},{48,56},{56,64},{64,7... | collective-permute-start | bytes 73736 | tf_op jit(solution)/shard_map/ppermute | solution.py:400
  24.1 3.6 %collective-permute-start.2 = (f32[3,16,256]{2,1,0:T(8,128)S(1)}, f32[3,16,256]{2,1,0:T(8,128)S(1)}, u32[]{:S(2)}, u32[]{:S(2)}) collective-permute-start(f32[3,16,256]{2,1,0:T(8,128)S(1)} %get-tuple-element.28), channel_id=1, source_target_pairs={{0,8},{8,16},{16,24},{24,32},{32,40},{40,48},{48,56},{56,64},{64,7... | collective-permute-start | bytes 147464 | tf_op jit(solution)/shard_map/ppermute | solution.py:388
  27.7 1.3 %collective-permute-start.3 = (f32[3,16,256]{2,1,0:T(8,128)S(1)}, f32[3,16,256]{2,1,0:T(8,128)S(1)}, u32[]{:S(2)}, u32[]{:S(2)}) collective-permute-start(f32[3,16,256]{2,1,0:T(8,128)S(1)} %get-tuple-element.29), channel_id=1, source_target_pairs={{8,0},{16,8},{24,16},{32,24},{40,32},{48,40},{56,48},{64,56},{72,6... | collective-permute-start | bytes 147464 | tf_op jit(solution)/shard_map/ppermute | solution.py:389
  29.0 0.8 shard_map.115.old
  29.8 0.0 collective-permute-done.4.from_left
  29.8 5.1 %collective-permute-start.1 = (f32[48,128]{1,0:T(8,128)S(1)}, f32[48,128]{1,0:T(8,128)S(1)}, u32[]{:S(2)}, u32[]{:S(2)}) collective-permute-start(f32[48,128]{1,0:T(8,128)S(1)} %get-tuple-element.26), channel_id=1, source_target_pairs={{8,0},{16,8},{24,16},{32,24},{40,32},{48,40},{56,48},{64,56},{72,6... | collective-permute-start | bytes 73736 | tf_op jit(solution)/shard_map/ppermute | solution.py:401
  34.9 0.0 collective-permute-done.5.from_right
  34.9 0.0 collective-permute-done.2.from_low
  34.9 0.0 collective-permute-done.3.from_high
  34.9 1.0 %shard_map.116.spread = f32[3,256,128]{2,1,0:T(8,128)S(1)} custom-call(f32[3,8,16,256]{3,2,1,0:T(8,128)S(1)} %copy-done, f32[3,16,256]{2,1,0:T(8,128)S(1)} %collective-permute-done.2.from_low, f32[3,16,256]{2,1,0:T(8,128)S(1)} %collective-permute-done.3.from_high, f32[3,8,256]{2,1,0:T(8,128)S(1)} %collective-permute-done.4.from_left, ...), custom_call_target="tpu_custom_call" | custom-call | flops 2000000000 | bytes 6000000 | tf_op jit(solution)/shard_map/pallas_call | solution.py:405
  35.9 2.2 %all-to-all-done = f32[128,16,128]{2,1,0:T(8,128)S(1)} async-done(((f32[128,16,128]{2,1,0:T(8,128)}), f32[128,16,128]{2,1,0:T(8,128)S(1)}, u32[]{:S(2)}, u32[]{:S(2)}) %all-to-all-start) | async-done | bytes 1048608 | tf_op jit(solution)/shard_map/all_to_all | solution.py:380
  38.2 2.0 %shard_map.117 = (f32[2048,128]{1,0:T(8,128)}, f32[3,256,128]{2,1,0:T(8,128)S(1)}) custom-call(f32[2048,128]{1,0:T(8,128)S(1)} %bitcast.9, f32[3,256,128]{2,1,0:T(8,128)S(1)} %shard_map.115.old, f32[3,256,128]{2,1,0:T(8,128)S(1)} %shard_map.116.spread), custom_call_target="tpu_custom_call" | custom-call | flops 3000000000 | bytes 9000000 | tf_op jit(solution)/shard_map/pallas_call | solution.py:413
  40.2 0.0 copy-start.4
  40.2 0.0 copy-start.5
  40.2 10.0 %all-to-all-start.1 = ((f32[128,16,128]{2,1,0:T(8,128)}), f32[128,16,128]{2,1,0:T(8,128)S(1)}, u32[]{:S(2)}, u32[]{:S(2)}) async-start(f32[128,16,128]{2,1,0:T(8,128)} %bitcast.5), calls=%async_computation.1 | async-start | bytes 2097152 | tf_op jit(solution)/shard_map/all_to_all | solution.py:421
  50.2 0.0 collective-permute-done.low
  50.2 0.0 collective-permute-done.1.high
  50.2 0.0 copy-done.4
  50.2 0.0 copy-done.5
  50.2 0.0 copy-start.2
  50.3 0.0 copy-start.3
  50.3 13.4 %shard_map.118 = (f32[2048,128]{1,0:T(8,128)S(1)}, f32[3,8,16,256]{3,2,1,0:T(8,128)}) custom-call(s32[2,512]{1,0:T(2,128)S(1)} %copy-done.4, s32[2,512]{1,0:T(2,128)S(1)} %copy-done.5, f32[3,256,128]{2,1,0:T(8,128)S(1)} %bitcast.13, f32[48,128]{1,0:T(8,128)S(1)} %collective-permute-done.low, f32[48,128]{1,0:T(8,128)S(1)} %collective-permute-done.1.high, ...), custom_call_target="tpu_custom_call" | custom-call | flops 14000000000 | bytes 42000000 | tf_op jit(solution)/shard_map/pallas_call | solution.py:423
  63.7 5.6 %all-to-all-done.1 = f32[128,16,128]{2,1,0:T(8,128)S(1)} async-done(((f32[128,16,128]{2,1,0:T(8,128)}), f32[128,16,128]{2,1,0:T(8,128)S(1)}, u32[]{:S(2)}, u32[]{:S(2)}) %all-to-all-start.1) | async-done | bytes 1048608 | tf_op jit(solution)/shard_map/all_to_all | solution.py:421
  69.3 0.0 copy-start.8
  69.3 0.0 copy-done.2
  69.4 0.0 copy-done.3
  69.4 0.7 copy-done.8
  70.0 1.0 %shard_map.119 = (f32[48,128]{1,0:T(8,128)S(1)}, f32[48,128]{1,0:T(8,128)S(1)}) custom-call(s32[256]{0:T(256)S(1)} %copy-done.8, s32[32]{0:T(128)S(1)} %copy-done.6, f32[512,4,128]{2,1,0:T(4,128)S(1)} %bitcast.10, s32[256,128]{1,0:T(8,128)S(1)} %copy-done.3, f32[3,256,128]{2,1,0:T(8,128)S(1)} %bitcast.14, f32[3,256,128]{2,1,0:T(8,128)S(1)} %bitcast.17, ...), custom_call_target="tpu_custom_call" | custom-call | flops 2000000000 | bytes 6000000 | tf_op jit(solution)/shard_map/pallas_call | solution.py:432
  71.0 0.5 collective-permute-start.6
  71.5 4.9 %collective-permute-start.7 = (f32[48,128]{1,0:T(8,128)S(1)}, f32[48,128]{1,0:T(8,128)S(1)}, u32[]{:S(2)}, u32[]{:S(2)}) collective-permute-start(f32[48,128]{1,0:T(8,128)S(1)} %get-tuple-element.36.after), channel_id=1, source_target_pairs={{8,0},{16,8},{24,16},{32,24},{40,32},{48,40},{56,48},{64,56},{72,6... | collective-permute-start | bytes 73736 | tf_op jit(solution)/shard_map/ppermute | solution.py:441
  76.4 3.9 %shard_map.120 = (f32[2048,128]{1,0:T(8,128)S(1)}, f32[3,256,128]{2,1,0:T(8,128)S(1)}, f32[3,256,128]{2,1,0:T(8,128)S(1)}) custom-call(s32[256]{0:T(256)S(1)} %copy-done.8, f32[512,4,128]{2,1,0:T(4,128)S(1)} %bitcast.11, s32[256,128]{1,0:T(8,128)S(1)} %copy-done.3, f32[3,256,128]{2,1,0:T(8,128)S(1)} %bitcast.15, f32[3,256,128]{2,1,0:T(8,128)S(1)} %bitcast.18, ...), custom_call_target="tpu_custom_call" | custom-call | flops 6000000000 | bytes 18000000 | tf_op jit(solution)/shard_map/pallas_call | solution.py:442
  80.4 0.0 collective-permute-done.6.low
  80.4 0.0 collective-permute-done.7.high
  80.4 13.1 %shard_map.121 = (f32[3,256,128]{2,1,0:T(8,128)}, f32[3,256,128]{2,1,0:T(8,128)}) custom-call(s32[2,512]{1,0:T(2,128)S(1)} %copy-done.4, s32[2,512]{1,0:T(2,128)S(1)} %copy-done.5, f32[3,256,128]{2,1,0:T(8,128)S(1)} %get-tuple-element.37.pos, f32[3,256,128]{2,1,0:T(8,128)S(1)} %get-tuple-element.38.vel, f32[48,128]{1,0:T(8,128)S(1)} %collective-permute-done.6.low, ...), custom_call_target="tpu_custom_call" | custom-call | flops 15000000512 | bytes 45000000 | tf_op jit(solution)/shard_map/pallas_call | solution.py:450
  (1 shorter events, 0.0 us)
Async XLA Ops:
  7.6 11.2 %copy-start = (f32[3,8,16,256]{3,2,1,0:T(8,128)S(1)}, f32[3,8,16,256]{3,2,1,0:T(8,128)}, u32[]{:S(2)}) copy-start(f32[3,8,16,256]{3,2,1,0:T(8,128)} %fv.5) | copy-start | bytes 1179652
  7.6 11.2 %copy-start.7 = (f32[8,128]{1,0:T(8,128)S(1)}, f32[8,128]{1,0:T(8,128)}, u32[]{:S(2)}) copy-start(f32[8,128]{1,0:T(8,128)} %get-tuple-element.23.after) | copy-start | bytes 12292
  7.6 30.6 %all-to-all-start = ((f32[128,16,128]{2,1,0:T(8,128)}), f32[128,16,128]{2,1,0:T(8,128)S(1)}, u32[]{:S(2)}, u32[]{:S(2)}) async-start(f32[128,16,128]{2,1,0:T(8,128)} %bitcast.19), calls=%async_computation | async-start | bytes 2097152 | tf_op jit(solution)/shard_map/all_to_all | solution.py:380
  18.8 2.9 %copy-start.1 = (f32[256,3,128]{2,0,1:T(8,128)S(1)}, f32[256,3,128]{2,0,1:T(8,128)}, u32[]{:S(2)}) copy-start(f32[256,3,128]{2,0,1:T(8,128)} %param.10) | copy-start | bytes 1179652
  18.8 11.0 %collective-permute-start.4 = (f32[3,8,256]{2,1,0:T(8,128)S(1)}, f32[3,8,256]{2,1,0:T(8,128)S(1)}, u32[]{:S(2)}, u32[]{:S(2)}) collective-permute-start(f32[3,8,256]{2,1,0:T(8,128)S(1)} %get-tuple-element.30), channel_id=1, source_target_pairs={{0,1},{1,2},{2,3},{3,4},{4,5},{5,6},{6,7},{8,9},{9,10},{10,11},{11... | collective-permute-start | bytes 73736 | tf_op jit(solution)/shard_map/ppermute | solution.py:390
  20.3 1.3 %copy-start.6 = (s32[32]{0:T(128)S(1)}, s32[32]{0:T(128)}, u32[]{:S(2)}) copy-start(s32[32]{0:T(128)} %halo.3) | copy-start | bytes 388
  20.3 14.6 %collective-permute-start.5 = (f32[3,8,256]{2,1,0:T(8,128)S(1)}, f32[3,8,256]{2,1,0:T(8,128)S(1)}, u32[]{:S(2)}, u32[]{:S(2)}) collective-permute-start(f32[3,8,256]{2,1,0:T(8,128)S(1)} %get-tuple-element.24.after), channel_id=1, source_target_pairs={{1,0},{2,1},{3,2},{4,3},{5,4},{6,5},{7,6},{9,8},{10,9},{11,10},{12... | collective-permute-start | bytes 73736 | tf_op jit(solution)/shard_map/ppermute | solution.py:391
  22.2 28.0 %collective-permute-start = (f32[48,128]{1,0:T(8,128)S(1)}, f32[48,128]{1,0:T(8,128)S(1)}, u32[]{:S(2)}, u32[]{:S(2)}) collective-permute-start(f32[48,128]{1,0:T(8,128)S(1)} %get-tuple-element.25), channel_id=1, source_target_pairs={{0,8},{8,16},{16,24},{24,32},{32,40},{40,48},{48,56},{56,64},{64,7... | collective-permute-start | bytes 73736 | tf_op jit(solution)/shard_map/ppermute | solution.py:400
  24.1 10.8 %collective-permute-start.2 = (f32[3,16,256]{2,1,0:T(8,128)S(1)}, f32[3,16,256]{2,1,0:T(8,128)S(1)}, u32[]{:S(2)}, u32[]{:S(2)}) collective-permute-start(f32[3,16,256]{2,1,0:T(8,128)S(1)} %get-tuple-element.28), channel_id=1, source_target_pairs={{0,8},{8,16},{16,24},{24,32},{32,40},{40,48},{48,56},{56,64},{64,7... | collective-permute-start | bytes 147464 | tf_op jit(solution)/shard_map/ppermute | solution.py:388
  27.7 7.2 %collective-permute-start.3 = (f32[3,16,256]{2,1,0:T(8,128)S(1)}, f32[3,16,256]{2,1,0:T(8,128)S(1)}, u32[]{:S(2)}, u32[]{:S(2)}) collective-permute-start(f32[3,16,256]{2,1,0:T(8,128)S(1)} %get-tuple-element.29), channel_id=1, source_target_pairs={{8,0},{16,8},{24,16},{32,24},{40,32},{48,40},{56,48},{64,56},{72,6... | collective-permute-start | bytes 147464 | tf_op jit(solution)/shard_map/ppermute | solution.py:389
  29.8 20.4 %collective-permute-start.1 = (f32[48,128]{1,0:T(8,128)S(1)}, f32[48,128]{1,0:T(8,128)S(1)}, u32[]{:S(2)}, u32[]{:S(2)}) collective-permute-start(f32[48,128]{1,0:T(8,128)S(1)} %get-tuple-element.26), channel_id=1, source_target_pairs={{8,0},{16,8},{24,16},{32,24},{40,32},{48,40},{56,48},{64,56},{72,6... | collective-permute-start | bytes 73736 | tf_op jit(solution)/shard_map/ppermute | solution.py:401
  40.2 10.0 %copy-start.4 = (s32[2,512]{1,0:T(2,128)S(1)}, s32[2,512]{1,0:T(2,128)}, u32[]{:S(2)}) copy-start(s32[2,512]{1,0:T(2,128)} %first.3) | copy-start | bytes 12292
  40.2 10.0 %copy-start.5 = (s32[2,512]{1,0:T(2,128)S(1)}, s32[2,512]{1,0:T(2,128)}, u32[]{:S(2)}) copy-start(s32[2,512]{1,0:T(2,128)} %second.3) | copy-start | bytes 12292
  40.2 29.1 %all-to-all-start.1 = ((f32[128,16,128]{2,1,0:T(8,128)}), f32[128,16,128]{2,1,0:T(8,128)S(1)}, u32[]{:S(2)}, u32[]{:S(2)}) async-start(f32[128,16,128]{2,1,0:T(8,128)} %bitcast.5), calls=%async_computation.1 | async-start | bytes 2097152 | tf_op jit(solution)/shard_map/all_to_all | solution.py:421
  50.2 19.1 %copy-start.2 = (f32[256,3,128]{2,0,1:T(8,128)S(1)}, f32[256,3,128]{2,0,1:T(8,128)}, u32[]{:S(2)}) copy-start(f32[256,3,128]{2,0,1:T(8,128)} %param.11) | copy-start | bytes 1179652
  50.3 19.1 %copy-start.3 = (s32[256,128]{1,0:T(8,128)S(1)}, s32[256,128]{1,0:T(8,128)}, u32[]{:S(2)}) copy-start(s32[256,128]{1,0:T(8,128)} %cell.3) | copy-start | bytes 393220
  69.3 0.7 copy-start.8
  71.0 9.4 %collective-permute-start.6 = (f32[48,128]{1,0:T(8,128)S(1)}, f32[48,128]{1,0:T(8,128)S(1)}, u32[]{:S(2)}, u32[]{:S(2)}) collective-permute-start(f32[48,128]{1,0:T(8,128)S(1)} %get-tuple-element.39), channel_id=1, source_target_pairs={{0,8},{8,16},{16,24},{24,32},{32,40},{40,48},{48,56},{56,64},{64,7... | collective-permute-start | bytes 73736 | tf_op jit(solution)/shard_map/ppermute | solution.py:440
  71.5 8.9 %collective-permute-start.7 = (f32[48,128]{1,0:T(8,128)S(1)}, f32[48,128]{1,0:T(8,128)S(1)}, u32[]{:S(2)}, u32[]{:S(2)}) collective-permute-start(f32[48,128]{1,0:T(8,128)S(1)} %get-tuple-element.36.after), channel_id=1, source_target_pairs={{8,0},{16,8},{24,16},{32,24},{40,32},{48,40},{56,48},{64,56},{72,6... | collective-permute-start | bytes 73736 | tf_op jit(solution)/shard_map/ppermute | solution.py:441

commit v5 on v4

--- a/solution.py
+++ b/solution.py
@@ -33,21 +33,32 @@
     return lax.dot_general(a, b, (dims, ((), ())), preferred_element_type=F32)
 
 
-def faces_kernel(fv, after, down_out, up_out, left_out, right_out):
-    for out, x in ((down_out, 0), (up_out, fv.shape[1] - 1)):
+def swaps(n, closed):
+    first = [(i, i ^ 1) for i in range(n)]
+    second = [(i, (i + 1 if i % 2 else i - 1) % n) for i in range(n)]
+    return first, (second if closed else second[1:-1])
+
+
+def put_listed(halo, half, pos, out, at):
+    for j in range(16):
+        q = halo[half * 16 + j]
         for m in range(3):
-            out[m] = fv[m, x]
-    for out, y in ((left_out, 0), (right_out, fv.shape[2] - 1)):
+            out[at + m * 16 + j : at + m * 16 + j + 1, :] = pos[m, pl.ds(q, 1), :]
+
+
+def faces_kernel(side, halo, fv, pos, after, first_x, second_x, first_y, second_y):
+    sx, sy, sz = fv.shape[1:]
+    for out, upper in ((first_x, 1 - side[0]), (second_x, side[0])):
+        x = upper * (sx - 1)
         for m in range(3):
-            out[m] = fv[m, :, y, :]
-
-
-def send_kernel(halo, pos, after, down_out, up_out):
-    for half, out in ((0, down_out), (1, up_out)):
-        for j in range(16):
-            q = halo[half * 16 + j]
-            for m in range(3):
-                out[m * 16 + j : m * 16 + j + 1, :] = pos[m, pl.ds(q, 1), :]
+            for h in range(2):
+                out[(m * 2 + h) * 16 : (m * 2 + h + 1) * 16, :] = fv[m, x, :, h * 128 : (h + 1) * 128]
+        put_listed(halo, upper, pos, out, 96)
+    odd = jnp.full((sx, sz), side[1], jnp.int32) == 1
+    for m in range(3):
+        begin, end = fv[m, :, 0, :], fv[m, :, sy - 1, :]
+        first_y[m] = jnp.where(odd, begin, end)
+        second_y[m] = jnp.where(odd, end, begin)
 
 
 def deposit_kernel(owner_in, local_in, cell_in, vel_in, out, slot_out, done, taken, owner, local, cell, vel, sems):
@@ -129,18 +140,29 @@
         bricks[m] = to_bricks(fv, m)
 
 
-def spread_kernel(fv, from_low, from_high, from_left, from_right, bricks, grid):
+def spread_kernel(side, fv, first_x, second_x, first_y, second_y, bricks, grid):
     sx, sy, sz = fv.shape[1:]
+    odd = side[0].astype(F32)
+    has_low, has_high = side[2].astype(F32), side[3].astype(F32)
+    odd_y = jnp.full((sx, sz), side[1], jnp.int32) == 1
     yrow = lax.broadcasted_iota(jnp.int32, (sy, sz), 0)
     zlane = lax.broadcasted_iota(jnp.int32, (sy, sz), 1)
     for m in range(3):
+        first, second = [
+            jnp.concatenate([ref[(m * 2 + h) * 16 : (m * 2 + h + 1) * 16, :] for h in range(2)], axis=1)
+            for ref in (first_x, second_x)
+        ]
+        from_low = (odd * has_low) * first + ((1.0 - odd) * has_low) * second
+        from_high = ((1.0 - odd) * has_high) * first + (odd * has_high) * second
+        lefts = jnp.where(odd_y, first_y[m], second_y[m])
+        rights = jnp.where(odd_y, second_y[m], first_y[m])
         for x in range(sx):
             f = fv[m, x]
-            high = fv[m, x + 1] if x < sx - 1 else from_high[m]
-            low = fv[m, x - 1] if x > 0 else from_low[m]
+            high = fv[m, x + 1] if x < sx - 1 else from_high
+            low = fv[m, x - 1] if x > 0 else from_low
             beside = high + low
-            right = jnp.broadcast_to(from_right[m, x : x + 1, :], (sy, sz))
-            left = jnp.broadcast_to(from_left[m, x : x + 1, :], (sy, sz))
+            right = jnp.broadcast_to(rights[x : x + 1, :], (sy, sz))
+            left = jnp.broadcast_to(lefts[x : x + 1, :], (sy, sz))
             beside = beside + jnp.where(yrow == sy - 1, right, pltpu.roll(f, sy - 1, 0))
             beside = beside + jnp.where(yrow == 0, left, pltpu.roll(f, 1, 0))
             beside = beside + jnp.where(zlane == sz - 1, 0.0, pltpu.roll(f, sz - 1, 1))
@@ -205,7 +227,7 @@
     return a, b, n - a - b
 
 
-def push_loop(step, first, second, pos, low, high, push, feat_b, feat_a):
+def push_loop(step, side, first, second, pos, listed, at, push, feat_b, feat_a):
     blocks = pos.shape[1]
     one = jnp.ones((8, 128), F32)
     zero = jnp.zeros((8, 128), F32)
@@ -225,11 +247,11 @@
         return c
 
     lax.fori_loop(0, blocks // 8, own, 0, unroll=2)
-    for i, ref in enumerate((low, high)):
+    for ref, upper in zip(listed, (1 - side[0], side[0])):
         for g in range(2):
-            hi, lo, _, norm = feature_rows([ref[m * 16 + g * 8 : m * 16 + g * 8 + 8, :] for m in range(3)])
+            hi, lo, _, norm = feature_rows([ref[at + m * 16 + g * 8 : at + m * 16 + g * 8 + 8, :] for m in range(3)])
             n = split3(norm)
-            put(feat_b, blocks + i * 16 + g * 8, hi + [one, n[0], n[1], n[2], one] + lo + [one, zero, zero, zero, zero])
+            put(feat_b, pl.multiple_of(blocks + upper * 16 + g * 8, 8), hi + [one, n[0], n[1], n[2], one] + lo + [one, zero, zero, zero, zero])
     push[...] = jnp.zeros(push.shape, F32)
     top = lax.broadcasted_iota(jnp.int32, (8, 128), 0) < 3
 
@@ -258,13 +280,18 @@
     lax.fori_loop(0, first.shape[1] // PAIR_GROUP, pairs, 0)
 
 
-def push_kernel(first, second, pos, low, high, new, push, fluid, feat_b, feat_a):
+def push_kernel(side, first, second, slot, pos, listed_a, listed_b, new, push, fluid, slot_out, feat_b, feat_a):
+    def hand_on(q, c):
+        slot_out[q] = slot[q]
+        return c
+
+    lax.fori_loop(0, slot.shape[0], hand_on, 0, unroll=8)
     for m in range(3):
         moved = swap_groups(new[m].reshape(new.shape[1] // 8, 8, 128))
         for i, (x, y, z) in enumerate(places(*fluid.shape[1:3])):
             fluid[m, x, y, z] = moved[i, 0:4]
             fluid[m, x + 1, y, z] = moved[i, 4:8]
-    push_loop(0, first, second, pos, low, high, push, feat_b, feat_a)
+    push_loop(0, side, first, second, pos, (listed_a, listed_b), 96, push, feat_b, feat_a)
 
 
 def advance(pos, vel, push, flow, pos_out, vel_out):
@@ -287,16 +314,16 @@
     return both[0:8] + both[8:16]
 
 
-def listed_kernel(slot, halo, back, cell, pos, vel, push, down_out, up_out):
+def listed_kernel(side, slot, halo, back, cell, pos, vel, push, first_out, second_out):
     r8 = lax.broadcasted_iota(jnp.int32, (8, 128), 0)
 
     def tile(ref, q):
         rows = [jnp.broadcast_to(ref[m, pl.ds(q, 1), :], (8, 128)) for m in range(3)]
         return jnp.where(r8 == 0, rows[0], jnp.where(r8 == 1, rows[1], rows[2]))
 
-    for half, out in ((0, down_out), (1, up_out)):
+    for out, upper in ((first_out, 1 - side[0]), (second_out, side[0])):
         for j in range(16):
-            q = halo[half * 16 + j]
+            q = halo[upper * 16 + j]
             flow = pick(onehot_cells(cell[pl.ds(q, 1), :]), back[slot[q]])
             v = tile(vel, q)
             rows = pl.ds(pl.multiple_of(q * 8, 8), 8)
@@ -321,8 +348,8 @@
     advance(pos, vel, push, flow, pos_out, vel_out)
 
 
-def last_kernel(first, second, pos, vel, low, high, flow, pos_out, vel_out, push, feat_b, feat_a):
-    push_loop(1, first, second, pos, low, high, push, feat_b, feat_a)
+def last_kernel(side, first, second, pos, vel, listed_a, listed_b, flow, pos_out, vel_out, push, feat_b, feat_a):
+    push_loop(1, side, first, second, pos, (listed_a, listed_b), 0, push, feat_b, feat_a)
     advance(pos, vel, push, flow, pos_out, vel_out)
 
 
@@ -379,37 +406,30 @@
     )(brick_owner[:, 0], brick_local, cell_in_brick, vel)
     recv = lax.all_to_all(send.reshape(slots * 4, 128), ("gx", "gy"), split_axis=0, concat_axis=0, tiled=True)
 
-    down, up, left, right = call(
+    me_x, me_y = lax.axis_index("gx"), lax.axis_index("gy")
+    side = jnp.stack([me_x % 2, me_y % 2, me_x > 0, me_x < nx - 1]).astype(jnp.int32)
+    first_x, second_x, first_y, second_y = call(
         faces_kernel,
-        [VMEM, VMEM],
-        [shape(3, sy, sz), shape(3, sy, sz), shape(3, sx, sz), shape(3, sx, sz)],
+        [SMEM, SMEM, VMEM, VMEM, VMEM],
+        [shape(144, 128), shape(144, 128), shape(3, sx, sz), shape(3, sx, sz)],
         [VMEM] * 4,
-    )(fluid_vel, placed)
-    from_low = lax.ppermute(up, "gx", [(i, i + 1) for i in range(nx - 1)])
-    from_high = lax.ppermute(down, "gx", [(i + 1, i) for i in range(nx - 1)])
-    from_left = lax.ppermute(right, "gy", [(i, i + 1) for i in range(ny - 1)])
-    from_right = lax.ppermute(left, "gy", [(i + 1, i) for i in range(ny - 1)])
-    down, up = call(
-        send_kernel,
-        [SMEM, VMEM, VMEM],
-        [shape(48, 128), shape(48, 128)],
-        [VMEM] * 2,
-    )(halo_list, pos, left)
-    fwd = [(i, (i + 1) % nx) for i in range(nx)]
-    bwd = [((i + 1) % nx, i) for i in range(nx)]
-    low = lax.ppermute(up, "gx", fwd)
-    high = lax.ppermute(down, "gx", bwd)
+    )(side, halo_list, fluid_vel, pos, placed)
+    perms_x, perms_y = swaps(nx, True), swaps(ny, False)
+    first_x = lax.ppermute(first_x, "gx", perms_x[0])
+    second_x = lax.ppermute(second_x, "gx", perms_x[1])
+    first_y = lax.ppermute(first_y, "gy", perms_y[0])
+    second_y = lax.ppermute(second_y, "gy", perms_y[1])
 
     bricks = sx // 2 * (sy // 4) * (sz // 16)
     old = call(old_kernel, [VMEM], shape(3, bricks, 128), VMEM)(fluid_vel)
     spread = call(
         spread_kernel,
-        [VMEM] * 5,
+        [SMEM] + [VMEM] * 5,
         shape(3, bricks, 128),
         VMEM,
         [pltpu.VMEM((3, sx, sy, sz), F32)],
         2,
-    )(fluid_vel, from_low, from_high, from_left, from_right)
+    )(side, fluid_vel, first_x, second_x, first_y, second_y)
     answer, new = call(
         fluid_kernel,
         [VMEM] * 3,
@@ -420,25 +440,25 @@
     )(recv, old, spread)
     back = lax.all_to_all(answer, ("gx", "gy"), split_axis=0, concat_axis=0, tiled=True).reshape(slots, 4, 128)
     pair_scratch = [pltpu.VMEM(((blocks + 32) * 16, 128), F32), pltpu.VMEM((blocks * 16, 128), F32)]
-    push, fluid = call(
+    push, fluid, slot = call(
         push_kernel,
-        [SMEM, SMEM, VMEM, VMEM, VMEM, VMEM],
-        [shape(blocks * 8, 128), shape(3, sx, sy, sz)],
-        [VMEM, VMEM],
+        [SMEM] * 4 + [VMEM] * 4,
+        [shape(blocks * 8, 128), shape(3, sx, sy, sz), shape(blocks, dtype=jnp.int32)],
+        [VMEM, VMEM, SMEM],
         pair_scratch,
         14,
-    )(pair_self, pair_other, pos, low, high, new)
-
-    down, up = call(
+    )(side, pair_self, pair_other, slot, pos, first_x, second_x, new)
+
+    first, second = call(
         listed_kernel,
-        [SMEM, SMEM] + [VMEM] * 5,
+        [SMEM] * 3 + [VMEM] * 5,
         [shape(48, 128), shape(48, 128)],
         [VMEM] * 2,
         (),
         2,
-    )(slot, halo_list, back, cell_in_brick, pos, vel, push)
-    low = lax.ppermute(up, "gx", fwd)
-    high = lax.ppermute(down, "gx", bwd)
+    )(side, slot, halo_list, back, cell_in_brick, pos, vel, push)
+    listed_a = lax.ppermute(first, "gx", perms_x[0])
+    listed_b = lax.ppermute(second, "gx", perms_x[1])
     flow, pos, vel = call(
         pick_kernel,
         [SMEM] + [VMEM] * 6,
@@ -446,15 +466,15 @@
         [VMEM] * 3,
         (),
         6,
-    )(slot, back, cell_in_brick, pos, vel, push, down)
+    )(slot, back, cell_in_brick, pos, vel, push, first)
     pos, vel = call(
         last_kernel,
-        [SMEM, SMEM] + [VMEM] * 5,
+        [SMEM] * 3 + [VMEM] * 5,
         [shape(3, blocks, 128), shape(3, blocks, 128)],
         [VMEM] * 2,
         [pltpu.VMEM((blocks * 8, 128), F32)] + pair_scratch,
         15,
-    )(pair_self, pair_other, pos, vel, low, high, flow)
+    )(side, pair_self, pair_other, pos, vel, listed_a, listed_b, flow)
     return fluid, jnp.transpose(pos, (1, 0, 2)), jnp.transpose(vel, (1, 0, 2))
 
 

time: 93.9 us -> 88.4 us (0.941)
  starting transfers between devices: 41.2 us -> 26.1 us
  waiting for transfers between devices: 7.88 us -> 14.1 us
  local copies, waits for them, and re-layouts: 0.72 us -> 3.07 us
  Pallas kernels: 42.9 us -> 43.9 us
    ppermute x8 -> x6, starting transfers between devices: 20 us -> 8.36 us  [the longest x1 4.65 us: per_device(): second_x = lax.ppermute(second_x, 'gx', perms_x[1])]
    ppermute x8 -> x6, waiting for transfers between devices: 0.02 us -> 9.89 us  [the longest x1 5.93 us: per_device(): first_x = lax.ppermute(first_x, 'gx', perms_x[0])]
    all_to_all x1, starting transfers between devices: 9.99 us -> 6.64 us  [per_device(): lax.all_to_all(answer, ('gx', 'gy'), split_axis=0, concat_axis=0, tiled=T...]
    unnamed x18 -> x22, local copies, waits for them, and re-layouts: 0.72 us -> 3.07 us
    all_to_all x1, waiting for transfers between devices: 5.64 us -> 3.58 us  [per_device(): lax.all_to_all(answer, ('gx', 'gy'), split_axis=0, concat_axis=0, tiled=T...]
    all_to_all x1, waiting for transfers between devices: 2.22 us -> 0.65 us  [per_device(): lax.all_to_all(send.reshape(slots * 4, 128), ('gx', 'gy'), split_axis=0,...]
    pallas_call x6 -> x5, Pallas kernels: 29.2 us -> 30.1 us  [the longest x1 13.9 us: per_device(): call(push_kernel, [SMEM] * 4 + [VMEM] * 4, [shape(blocks * 8, 128), shape...]
  transfers between devices with their start and end apart: 10 -> 8, of which waited for: 2 -> 5; matrix products, arithmetic and copies ran while one was open for 0% -> 0% of each run, Pallas kernels for 23% -> 24%
where the time goes in v5:
time: 88.4 us; the launch traced here: 88.1 us
  Pallas kernels  43.9 us (50%)
  starting transfers between devices  26.1 us (30%)
  waiting for transfers between devices  14.1 us (16%)
  local copies, waits for them, and re-layouts  3.07 us (3%)
    pallas_call x1, Pallas kernels, per_device(): call(push_kernel, [SMEM] * 4 + [VMEM] * 4, [shape(blocks * 8, 128), shape...  13.9 us
    pallas_call x1, Pallas kernels, per_device(): call(last_kernel, [SMEM] * 3 + [VMEM] * 5, [shape(3, blocks, 128), shape(...  13.1 us
    all_to_all x1, starting transfers between devices, per_device(): lax.all_to_all(send.reshape(slots * 4, 128), ('gx', 'gy'), split_axis=0,...  11.1 us
    pallas_call x1, Pallas kernels, per_device(): call(deposit_kernel, [HBM] * 4, [shape(slots, 4, 128), shape(blocks, dtyp...  6.93 us
    all_to_all x1, starting transfers between devices, per_device(): lax.all_to_all(answer, ('gx', 'gy'), split_axis=0, concat_axis=0, tiled=T...  6.64 us
    ppermute x1, waiting for transfers between devices, per_device(): first_x = lax.ppermute(first_x, 'gx', perms_x[0])  5.93 us
    ppermute x1, starting transfers between devices, per_device(): second_x = lax.ppermute(second_x, 'gx', perms_x[1])  4.65 us
    pallas_call x1, Pallas kernels, per_device(): call(pick_kernel, [SMEM] + [VMEM] * 6, [shape(blocks * 8, 128), shape(3,...  3.96 us
  transfers between devices with their start and end apart: 8, of which 5 were waited for; matrix products, arithmetic and copies ran while one was open for 0% of the time, Pallas kernels for 24%

profile of v5, /device:TPU:0, one launch (start us, length us, event | category | flops | bytes accessed | tf_op | source)
XLA Modules:
  0.0 88.1 jit_solution(6264035801069916792)
XLA Ops:
  0.6 6.9 %shard_map.112 = (f32[512,4,128]{2,1,0:T(4,128)}, s32[256]{0:T(256)}, f32[8,128]{1,0:T(8,128)}) custom-call(s32[256]{0:T(256)} %bitcast.24, s32[256]{0:T(256)} %local_in.1, s32[256,128]{1,0:T(8,128)} %cell.3, f32[3,256,128]{2,1,0:T(8,128)} %bitcast.16), custom_call_target="tpu_custom_call" | custom-call | flops 7000000000 | bytes 21000000 | tf_op jit(solution)/shard_map/pallas_call | solution.py:391
  7.6 0.0 copy-start
  7.6 0.0 copy-start.2
  7.6 11.1 %all-to-all-start = ((f32[128,16,128]{2,1,0:T(8,128)}), f32[128,16,128]{2,1,0:T(8,128)S(1)}, u32[]{:S(2)}, u32[]{:S(2)}) async-start(f32[128,16,128]{2,1,0:T(8,128)} %bitcast.23), calls=%async_computation | async-start | bytes 2097152 | tf_op jit(solution)/shard_map/all_to_all | solution.py:407
  18.8 0.0 copy-start.9
  18.8 0.1 pad_add_fusion.side
  18.9 0.0 copy-start.6
  18.9 0.0 copy-done
  18.9 0.0 copy-done.2
  18.9 0.6 copy-done.9
  19.5 0.1 copy-done.6
  19.5 0.6 shard_map.113
  20.1 0.1 collective-permute-start.2
  20.2 0.7 collective-permute-start.3
  20.9 1.3 %collective-permute-start = (f32[144,128]{1,0:T(8,128)S(1)}, f32[144,128]{1,0:T(8,128)S(1)}, u32[]{:S(2)}, u32[]{:S(2)}) collective-permute-start(f32[144,128]{1,0:T(8,128)S(1)} %get-tuple-element.24), channel_id=1, source_target_pairs={{0,8},{8,0},{16,24},{24,16},{32,40},{40,32},{48,56},{56,48},{64,72... | collective-permute-start | bytes 221192 | tf_op jit(solution)/shard_map/ppermute | solution.py:418
  22.2 4.6 %collective-permute-start.1 = (f32[144,128]{1,0:T(8,128)S(1)}, f32[144,128]{1,0:T(8,128)S(1)}, u32[]{:S(2)}, u32[]{:S(2)}) collective-permute-start(f32[144,128]{1,0:T(8,128)S(1)} %get-tuple-element.25), channel_id=1, source_target_pairs={{0,120},{8,16},{16,8},{24,32},{32,24},{40,48},{48,40},{56,64},{64,... | collective-permute-start | bytes 221192 | tf_op jit(solution)/shard_map/ppermute | solution.py:419
  26.8 0.8 shard_map.114.old
  27.6 0.0 collective-permute-done.2.first_y
  27.6 0.0 collective-permute-done.3.second_y
  27.7 5.9 %collective-permute-done.first_x.listed_a = f32[144,128]{1,0:T(8,128)S(1)} collective-permute-done((f32[144,128]{1,0:T(8,128)S(1)}, f32[144,128]{1,0:T(8,128)S(1)}, u32[]{:S(2)}, u32[]{:S(2)}) %collective-permute-start) | collective-permute-done | bytes 73760 | tf_op jit(solution)/shard_map/ppermute | solution.py:418
  33.6 2.4 %collective-permute-done.1.second_x.listed_b = f32[144,128]{1,0:T(8,128)S(1)} collective-permute-done((f32[144,128]{1,0:T(8,128)S(1)}, f32[144,128]{1,0:T(8,128)S(1)}, u32[]{:S(2)}, u32[]{:S(2)}) %collective-permute-start.1) | collective-permute-done | bytes 73760 | tf_op jit(solution)/shard_map/ppermute | solution.py:419
  35.9 1.6 %shard_map.115.spread = f32[3,256,128]{2,1,0:T(8,128)S(1)} custom-call(s32[4]{0:T(128)S(1)} %pad_add_fusion.side, f32[3,8,16,256]{3,2,1,0:T(8,128)S(1)} %copy-done, f32[144,128]{1,0:T(8,128)S(1)} %collective-permute-done.first_x.listed_a, f32[144,128]{1,0:T(8,128)S(1)} %collective-permute-done.1.second_x.listed_b, ...), custom_call_target="tpu_custom_call" | custom-call | flops 2000000000 | bytes 6000000 | tf_op jit(solution)/shard_map/pallas_call | solution.py:425
  37.5 0.6 all-to-all-done
  38.2 2.0 %shard_map.116 = (f32[2048,128]{1,0:T(8,128)}, f32[3,256,128]{2,1,0:T(8,128)S(1)}) custom-call(f32[2048,128]{1,0:T(8,128)S(1)} %bitcast.13, f32[3,256,128]{2,1,0:T(8,128)S(1)} %shard_map.114.old, f32[3,256,128]{2,1,0:T(8,128)S(1)} %shard_map.115.spread), custom_call_target="tpu_custom_call" | custom-call | flops 3000000000 | bytes 9000000 | tf_op jit(solution)/shard_map/pallas_call | solution.py:433
  40.2 0.0 copy-start.7
  40.2 0.0 copy-start.4
  40.2 0.0 copy-start.5
  40.2 0.7 copy-done.7
  40.9 6.6 %all-to-all-start.1 = ((f32[128,16,128]{2,1,0:T(8,128)}), f32[128,16,128]{2,1,0:T(8,128)S(1)}, u32[]{:S(2)}, u32[]{:S(2)}) async-start(f32[128,16,128]{2,1,0:T(8,128)} %bitcast.9), calls=%async_computation.1 | async-start | bytes 2097152 | tf_op jit(solution)/shard_map/all_to_all | solution.py:441
  47.6 0.0 copy-start.10
  47.6 0.0 copy-done.4
  47.6 0.0 copy-done.5
  47.6 0.7 copy-done.10
  48.3 0.0 copy-start.8
  48.3 1.0 %copy-done.8 = f32[3,256,128]{2,1,0:T(8,128)S(1)} copy-done((f32[3,256,128]{2,1,0:T(8,128)S(1)}, f32[3,256,128]{2,1,0:T(8,128)}, u32[]{:S(2)}) %copy-start.8) | copy-done | bytes 393240
  49.3 0.0 copy-start.1
  49.3 0.0 copy-start.3
  49.3 13.9 %shard_map.117 = (f32[2048,128]{1,0:T(8,128)S(1)}, f32[3,8,16,256]{3,2,1,0:T(8,128)}, s32[256]{0:T(256)S(1)}) custom-call(s32[4]{0:T(128)S(1)} %pad_add_fusion.side, s32[2,512]{1,0:T(2,128)S(1)} %copy-done.4, s32[2,512]{1,0:T(2,128)S(1)} %copy-done.5, s32[256]{0:T(256)S(1)} %copy-done.10, f32[3,256,128]{2,1,0:T(8,128)S(1)} %bitcast.20, ...), custom_call_target="tpu_custom_call" | custom-call | flops 14000000000 | bytes 42000000 | tf_op jit(solution)/shard_map/pallas_call | solution.py:443
  63.2 3.6 %all-to-all-done.1 = f32[128,16,128]{2,1,0:T(8,128)S(1)} async-done(((f32[128,16,128]{2,1,0:T(8,128)}), f32[128,16,128]{2,1,0:T(8,128)S(1)}, u32[]{:S(2)}, u32[]{:S(2)}) %all-to-all-start.1) | async-done | bytes 1048608 | tf_op jit(solution)/shard_map/all_to_all | solution.py:441
  66.7 0.0 copy-done.1
  66.7 0.0 copy-done.3
  66.7 1.0 %shard_map.118 = (f32[48,128]{1,0:T(8,128)S(1)}, f32[48,128]{1,0:T(8,128)S(1)}) custom-call(s32[4]{0:T(128)S(1)} %pad_add_fusion.side, s32[256]{0:T(256)S(1)} %get-tuple-element.31.slot, s32[32]{0:T(128)S(1)} %copy-done.6, f32[512,4,128]{2,1,0:T(4,128)S(1)} %bitcast.14, s32[256,128]{1,0:T(8,128)S(1)} %copy-done.3, f32[3,256,128]{2,1,0:T(8,128)S(1)} %bitcast.21, ...), custom_call_target="tpu_custom_call" | custom-call | flops 2000000000 | bytes 6000000 | tf_op jit(solution)/shard_map/pallas_call | solution.py:452
  67.7 1.7 %collective-permute-start.5 = (f32[48,128]{1,0:T(8,128)S(1)}, f32[48,128]{1,0:T(8,128)S(1)}, u32[]{:S(2)}, u32[]{:S(2)}) collective-permute-start(f32[48,128]{1,0:T(8,128)S(1)} %get-tuple-element.37), channel_id=1, source_target_pairs={{0,120},{8,16},{16,8},{24,32},{32,24},{40,48},{48,40},{56,64},{64,... | collective-permute-start | bytes 73736 | tf_op jit(solution)/shard_map/ppermute | solution.py:461
  69.4 0.0 collective-permute-start.4
  69.4 4.0 %shard_map.119 = (f32[2048,128]{1,0:T(8,128)S(1)}, f32[3,256,128]{2,1,0:T(8,128)S(1)}, f32[3,256,128]{2,1,0:T(8,128)S(1)}) custom-call(s32[256]{0:T(256)S(1)} %get-tuple-element.31.slot, f32[512,4,128]{2,1,0:T(4,128)S(1)} %bitcast.15, s32[256,128]{1,0:T(8,128)S(1)} %copy-done.3, f32[3,256,128]{2,1,0:T(8,128)S(1)} %bitcast.22, f32[3,256,128]{2,1,0:T(8,128)S(1)} %bitcast.18, ...), custom_call_target="tpu_custom_call" | custom-call | flops 6000000000 | bytes 18000000 | tf_op jit(solution)/shard_map/pallas_call | solution.py:462
  73.4 1.6 %collective-permute-done.5.listed_b = f32[48,128]{1,0:T(8,128)S(1)} collective-permute-done((f32[48,128]{1,0:T(8,128)S(1)}, f32[48,128]{1,0:T(8,128)S(1)}, u32[]{:S(2)}, u32[]{:S(2)}) %collective-permute-start.5) | collective-permute-done | bytes 24608 | tf_op jit(solution)/shard_map/ppermute | solution.py:461
  74.9 0.0 collective-permute-done.4.listed_a
  75.0 13.1 %shard_map.120 = (f32[3,256,128]{2,1,0:T(8,128)}, f32[3,256,128]{2,1,0:T(8,128)}) custom-call(s32[4]{0:T(128)S(1)} %pad_add_fusion.side, s32[2,512]{1,0:T(2,128)S(1)} %copy-done.4, s32[2,512]{1,0:T(2,128)S(1)} %copy-done.5, f32[3,256,128]{2,1,0:T(8,128)S(1)} %get-tuple-element.35.pos, f32[3,256,128]{2,1,0:T(8,128)S(1)} %get-tuple-element.36.vel, ...), custom_call_target="tpu_custom_call" | custom-call | flops 15000000512 | bytes 45000000 | tf_op jit(solution)/shard_map/pallas_call | solution.py:470
Async XLA Ops:
  7.6 11.3 %copy-start = (f32[3,8,16,256]{3,2,1,0:T(8,128)S(1)}, f32[3,8,16,256]{3,2,1,0:T(8,128)}, u32[]{:S(2)}) copy-start(f32[3,8,16,256]{3,2,1,0:T(8,128)} %fv.5) | copy-start | bytes 1179652
  7.6 11.3 %copy-start.2 = (f32[256,3,128]{2,0,1:T(8,128)S(1)}, f32[256,3,128]{2,0,1:T(8,128)}, u32[]{:S(2)}) copy-start(f32[256,3,128]{2,0,1:T(8,128)} %param.10) | copy-start | bytes 1179652
  7.6 30.6 %all-to-all-start = ((f32[128,16,128]{2,1,0:T(8,128)}), f32[128,16,128]{2,1,0:T(8,128)S(1)}, u32[]{:S(2)}, u32[]{:S(2)}) async-start(f32[128,16,128]{2,1,0:T(8,128)} %bitcast.23), calls=%async_computation | async-start | bytes 2097152 | tf_op jit(solution)/shard_map/all_to_all | solution.py:407
  18.8 0.7 copy-start.9
  18.9 0.7 copy-start.6
  20.1 7.5 %collective-permute-start.2 = (f32[3,8,256]{2,1,0:T(8,128)S(1)}, f32[3,8,256]{2,1,0:T(8,128)S(1)}, u32[]{:S(2)}, u32[]{:S(2)}) collective-permute-start(f32[3,8,256]{2,1,0:T(8,128)S(1)} %get-tuple-element.27), channel_id=1, source_target_pairs={{0,1},{1,0},{2,3},{3,2},{4,5},{5,4},{6,7},{7,6},{8,9},{9,8},{10,11... | collective-permute-start | bytes 73736 | tf_op jit(solution)/shard_map/ppermute | solution.py:420
  20.2 7.4 %collective-permute-start.3 = (f32[3,8,256]{2,1,0:T(8,128)S(1)}, f32[3,8,256]{2,1,0:T(8,128)S(1)}, u32[]{:S(2)}, u32[]{:S(2)}) collective-permute-start(f32[3,8,256]{2,1,0:T(8,128)S(1)} %get-tuple-element.28), channel_id=1, source_target_pairs={{1,2},{2,1},{3,4},{4,3},{5,6},{6,5},{9,10},{10,9},{11,12},{12,11},... | collective-permute-start | bytes 73736 | tf_op jit(solution)/shard_map/ppermute | solution.py:421
  20.9 12.7 %collective-permute-start = (f32[144,128]{1,0:T(8,128)S(1)}, f32[144,128]{1,0:T(8,128)S(1)}, u32[]{:S(2)}, u32[]{:S(2)}) collective-permute-start(f32[144,128]{1,0:T(8,128)S(1)} %get-tuple-element.24), channel_id=1, source_target_pairs={{0,8},{8,0},{16,24},{24,16},{32,40},{40,32},{48,56},{56,48},{64,72... | collective-permute-start | bytes 221192 | tf_op jit(solution)/shard_map/ppermute | solution.py:418
  22.2 13.8 %collective-permute-start.1 = (f32[144,128]{1,0:T(8,128)S(1)}, f32[144,128]{1,0:T(8,128)S(1)}, u32[]{:S(2)}, u32[]{:S(2)}) collective-permute-start(f32[144,128]{1,0:T(8,128)S(1)} %get-tuple-element.25), channel_id=1, source_target_pairs={{0,120},{8,16},{16,8},{24,32},{32,24},{40,48},{48,40},{56,64},{64,... | collective-permute-start | bytes 221192 | tf_op jit(solution)/shard_map/ppermute | solution.py:419
  40.2 0.7 copy-start.7
  40.2 7.4 %copy-start.4 = (s32[2,512]{1,0:T(2,128)S(1)}, s32[2,512]{1,0:T(2,128)}, u32[]{:S(2)}) copy-start(s32[2,512]{1,0:T(2,128)} %first.3) | copy-start | bytes 12292
  40.2 7.4 %copy-start.5 = (s32[2,512]{1,0:T(2,128)S(1)}, s32[2,512]{1,0:T(2,128)}, u32[]{:S(2)}) copy-start(s32[2,512]{1,0:T(2,128)} %second.3) | copy-start | bytes 12292
  40.9 25.8 %all-to-all-start.1 = ((f32[128,16,128]{2,1,0:T(8,128)}), f32[128,16,128]{2,1,0:T(8,128)S(1)}, u32[]{:S(2)}, u32[]{:S(2)}) async-start(f32[128,16,128]{2,1,0:T(8,128)} %bitcast.9), calls=%async_computation.1 | async-start | bytes 2097152 | tf_op jit(solution)/shard_map/all_to_all | solution.py:441
  47.6 0.7 copy-start.10
  48.3 1.0 %copy-start.8 = (f32[3,256,128]{2,1,0:T(8,128)S(1)}, f32[3,256,128]{2,1,0:T(8,128)}, u32[]{:S(2)}) copy-start(f32[3,256,128]{2,1,0:T(8,128)} %copy-done.7) | copy-start | bytes 1179652
  49.3 17.5 %copy-start.1 = (f32[256,3,128]{2,0,1:T(8,128)S(1)}, f32[256,3,128]{2,0,1:T(8,128)}, u32[]{:S(2)}) copy-start(f32[256,3,128]{2,0,1:T(8,128)} %param.11) | copy-start | bytes 1179652
  49.3 17.5 %copy-start.3 = (s32[256,128]{1,0:T(8,128)S(1)}, s32[256,128]{1,0:T(8,128)}, u32[]{:S(2)}) copy-start(s32[256,128]{1,0:T(8,128)} %cell.3) | copy-start | bytes 393220
  67.7 7.2 %collective-permute-start.5 = (f32[48,128]{1,0:T(8,128)S(1)}, f32[48,128]{1,0:T(8,128)S(1)}, u32[]{:S(2)}, u32[]{:S(2)}) collective-permute-start(f32[48,128]{1,0:T(8,128)S(1)} %get-tuple-element.37), channel_id=1, source_target_pairs={{0,120},{8,16},{16,8},{24,32},{32,24},{40,48},{48,40},{56,64},{64,... | collective-permute-start | bytes 73736 | tf_op jit(solution)/shard_map/ppermute | solution.py:461
  69.4 5.6 %collective-permute-start.4 = (f32[48,128]{1,0:T(8,128)S(1)}, f32[48,128]{1,0:T(8,128)S(1)}, u32[]{:S(2)}, u32[]{:S(2)}) collective-permute-start(f32[48,128]{1,0:T(8,128)S(1)} %get-tuple-element.34.after), channel_id=1, source_target_pairs={{0,8},{8,0},{16,24},{24,16},{32,40},{40,32},{48,56},{56,48},{64,72... | collective-permute-start | bytes 73736 | tf_op jit(solution)/shard_map/ppermute | solution.py:460

commit v6 on v5

--- a/solution.py
+++ b/solution.py
@@ -11,7 +11,7 @@
 BF16 = jnp.bfloat16
 PAIR_GROUP = 128
 BLOCK_GROUP = 32
-DEPOSIT_GROUP = 64
+DEPOSIT_GROUP = 128
 CAP = 4
 EPS2 = 0.0025
 VMEM = pl.BlockSpec(memory_space=pltpu.VMEM)
@@ -81,6 +81,7 @@
 
     lax.fori_loop(0, taken.shape[0], clear, 0, unroll=8)
     r8 = lax.broadcasted_iota(jnp.int32, (8, 128), 0)
+    lane16 = lax.broadcasted_iota(jnp.int32, (128, 128), 1) // 16
     for c in copies:
         c.wait()
 
@@ -88,22 +89,29 @@
         base = pl.multiple_of(g * DEPOSIT_GROUP, DEPOSIT_GROUP)
         cells = cell[pl.ds(base, DEPOSIT_GROUP), :]
         v = [vel[m, pl.ds(base, DEPOSIT_GROUP), :] for m in range(3)]
-        for k in range(DEPOSIT_GROUP):
-            q = base + k
-            rows = [jnp.broadcast_to(v[m][k : k + 1, :], (8, 128)) for m in range(3)]
-            load = jnp.where(r8 == 1, rows[0], jnp.where(r8 == 2, rows[1], rows[2]))
-            load = jnp.where(r8 == 0, 1.0, jnp.where(r8 < 4, load, 0.0))
-            hi = load.astype(BF16).astype(F32)
-            lhs = jnp.concatenate([hi, load - hi], axis=0).astype(BF16)
-            both = dot(lhs, onehot_cells(cells[k : k + 1, :]), ((1,), (1,)))
-            both = both[0:8] + both[8:16]
-            tile = owner[q]
-            rank = taken[tile]
-            taken[tile] = rank + 1
-            slot = tile * CAP + rank
-            slot_out[q] = slot
-            ident = jnp.full((4, 128), local[q], jnp.int32).astype(F32)
-            out[slot] = jnp.where(mark, ident, both[0:4])
+        for start in range(0, DEPOSIT_GROUP, 8):
+            loads, hots = [], []
+            for k in range(start, start + 8):
+                rows = [jnp.broadcast_to(v[m][k : k + 1, :], (8, 128)) for m in range(3)]
+                load = jnp.where(r8 == 1, rows[0], jnp.where(r8 == 2, rows[1], rows[2]))
+                load = jnp.where(r8 == 0, 1.0, jnp.where(r8 < 4, load, 0.0))
+                hi = load.astype(BF16).astype(F32)
+                loads += [hi, load - hi]
+                hots.append(onehot_cells(cells[k : k + 1, :]))
+            turned = jnp.concatenate(loads, axis=0).T
+            turned = turned.astype(BF16)
+            apart = [jnp.where(lane16 == k, turned, jnp.zeros_like(turned)) for k in range(8)]
+            found = dot(jnp.concatenate(hots, axis=1), jnp.concatenate(apart, axis=0)).T
+            for k in range(8):
+                q = base + start + k
+                both = found[k * 16 : k * 16 + 8] + found[k * 16 + 8 : k * 16 + 16]
+                tile = owner[q]
+                rank = taken[tile]
+                taken[tile] = rank + 1
+                slot = tile * CAP + rank
+                slot_out[q] = slot
+                ident = jnp.full((4, 128), local[q], jnp.int32).astype(F32)
+                out[slot] = jnp.where(mark, ident, both[0:4])
         return c
 
     lax.fori_loop(0, blocks // DEPOSIT_GROUP, group, 0)
@@ -172,7 +180,8 @@
         bricks[m] = to_bricks(grid, m)
 
 
-def fluid_kernel(recv, old, spread, answer, new):
+def fluid_kernel(recv, old, spread, answer, fluid, done):
+    done[...] = jnp.zeros(done.shape, F32)
     slots = recv.shape[0] // 4
     bricks = old.shape[1]
     count = recv[pl.ds(0, slots, stride=4), :]
@@ -198,9 +207,12 @@
     scale = 0.15 * beta
     table = []
     for m in range(3):
-        fluid = spread[m] + scale * (momentum[m] - cnt * old[m])
-        new[m] = fluid
-        table += list(split2(fluid))
+        new = spread[m] + scale * (momentum[m] - cnt * old[m])
+        table += list(split2(new))
+        moved = swap_groups(new.reshape(bricks // 8, 8, 128))
+        for i, (x, y, z) in enumerate(places(*fluid.shape[1:3])):
+            fluid[m, x, y, z] = moved[i, 0:4]
+            fluid[m, x + 1, y, z] = moved[i, 4:8]
     table += list(split2(beta))
     found = dot(by_slot, jnp.concatenate(table, axis=1))
     for c in range(4):
@@ -280,17 +292,12 @@
     lax.fori_loop(0, first.shape[1] // PAIR_GROUP, pairs, 0)
 
 
-def push_kernel(side, first, second, slot, pos, listed_a, listed_b, new, push, fluid, slot_out, feat_b, feat_a):
+def push_kernel(side, first, second, slot, pos, listed_a, listed_b, after, push, slot_out, feat_b, feat_a):
     def hand_on(q, c):
         slot_out[q] = slot[q]
         return c
 
     lax.fori_loop(0, slot.shape[0], hand_on, 0, unroll=8)
-    for m in range(3):
-        moved = swap_groups(new[m].reshape(new.shape[1] // 8, 8, 128))
-        for i, (x, y, z) in enumerate(places(*fluid.shape[1:3])):
-            fluid[m, x, y, z] = moved[i, 0:4]
-            fluid[m, x + 1, y, z] = moved[i, 4:8]
     push_loop(0, side, first, second, pos, (listed_a, listed_b), 96, push, feat_b, feat_a)
 
 
@@ -430,24 +437,24 @@
         [pltpu.VMEM((3, sx, sy, sz), F32)],
         2,
     )(side, fluid_vel, first_x, second_x, first_y, second_y)
-    answer, new = call(
+    answer, fluid, stepped = call(
         fluid_kernel,
         [VMEM] * 3,
-        [shape(slots * 4, 128), shape(3, bricks, 128)],
-        [VMEM] * 2,
+        [shape(slots * 4, 128), shape(3, sx, sy, sz), shape(8, 128)],
+        [VMEM] * 3,
         (),
         3,
     )(recv, old, spread)
     back = lax.all_to_all(answer, ("gx", "gy"), split_axis=0, concat_axis=0, tiled=True).reshape(slots, 4, 128)
     pair_scratch = [pltpu.VMEM(((blocks + 32) * 16, 128), F32), pltpu.VMEM((blocks * 16, 128), F32)]
-    push, fluid, slot = call(
+    push, slot = call(
         push_kernel,
         [SMEM] * 4 + [VMEM] * 4,
-        [shape(blocks * 8, 128), shape(3, sx, sy, sz), shape(blocks, dtype=jnp.int32)],
-        [VMEM, VMEM, SMEM],
+        [shape(blocks * 8, 128), shape(blocks, dtype=jnp.int32)],
+        [VMEM, SMEM],
         pair_scratch,
         14,
-    )(side, pair_self, pair_other, slot, pos, first_x, second_x, new)
+    )(side, pair_self, pair_other, slot, pos, first_x, second_x, stepped)
 
     first, second = call(
         listed_kernel,

time: 88.4 us -> 85.9 us (0.972)
  waiting for transfers between devices: 14.1 us -> 17 us
  Pallas kernels: 43.9 us -> 41.1 us
  local copies, waits for them, and re-layouts: 3.07 us -> 1.33 us
  starting transfers between devices: 26.1 us -> 25.2 us
    all_to_all x1, waiting for transfers between devices: 3.58 us -> 5.51 us  [per_device(): lax.all_to_all(answer, ('gx', 'gy'), split_axis=0, concat_axis=0, tiled=T...]
    pallas_call x1, Pallas kernels: 6.93 us -> 5.04 us  [per_device(): call(deposit_kernel, [HBM] * 4, [shape(slots, 4, 128), shape(blocks, dtyp...]
    unnamed x22 -> x18, local copies, waits for them, and re-layouts: 3.07 us -> 1.33 us
    ppermute x1, starting transfers between devices: 1.67 us -> 0.71 us  [per_device(): listed_b = lax.ppermute(second, 'gx', perms_x[1])]
    pallas_call x1, Pallas kernels: 13.9 us -> 12.9 us  [per_device(): call(push_kernel, [SMEM] * 4 + [VMEM] * 4, [shape(blocks * 8, 128), shape...]
    ppermute x1, waiting for transfers between devices: 1.59 us -> 2.51 us  [per_device(): listed_b = lax.ppermute(second, 'gx', perms_x[1])]
  transfers between devices with their start and end apart: 8 -> 8, of which waited for: 5 -> 5; matrix products, arithmetic and copies ran while one was open for 0% -> 0% of each run, Pallas kernels for 24% -> 23%
where the time goes in v6:
time: 85.9 us; the launch traced here: 85.5 us
  Pallas kernels  41.1 us (48%)
  starting transfers between devices  25.2 us (29%)
  waiting for transfers between devices  17 us (20%)
  local copies, waits for them, and re-layouts  1.33 us (2%)
    pallas_call x1, Pallas kernels, per_device(): call(last_kernel, [SMEM] * 3 + [VMEM] * 5, [shape(3, blocks, 128), shape(...  13.1 us
    pallas_call x1, Pallas kernels, per_device(): call(push_kernel, [SMEM] * 4 + [VMEM] * 4, [shape(blocks * 8, 128), shape...  12.9 us
    all_to_all x1, starting transfers between devices, per_device(): lax.all_to_all(send.reshape(slots * 4, 128), ('gx', 'gy'), split_axis=0,...  11.1 us
    all_to_all x1, starting transfers between devices, per_device(): lax.all_to_all(answer, ('gx', 'gy'), split_axis=0, concat_axis=0, tiled=T...  6.64 us
    ppermute x1, waiting for transfers between devices, per_device(): first_x = lax.ppermute(first_x, 'gx', perms_x[0])  5.93 us
    all_to_all x1, waiting for transfers between devices, per_device(): lax.all_to_all(answer, ('gx', 'gy'), split_axis=0, concat_axis=0, tiled=T...  5.51 us
    pallas_call x1, Pallas kernels, per_device(): call(deposit_kernel, [HBM] * 4, [shape(slots, 4, 128), shape(blocks, dtyp...  5.04 us
    ppermute x1, starting transfers between devices, per_device(): second_x = lax.ppermute(second_x, 'gx', perms_x[1])  4.65 us
  transfers between devices with their start and end apart: 8, of which 5 were waited for; matrix products, arithmetic and copies ran while one was open for 0% of the time, Pallas kernels for 23%

profile of v6, /device:TPU:0, one launch (start us, length us, event | category | flops | bytes accessed | tf_op | source)
XLA Modules:
  0.0 85.5 jit_solution(1474641663893806336)
XLA Ops:
  0.6 5.0 %shard_map.112 = (f32[512,4,128]{2,1,0:T(4,128)}, s32[256]{0:T(256)}, f32[8,128]{1,0:T(8,128)}) custom-call(s32[256]{0:T(256)} %bitcast.24, s32[256]{0:T(256)} %local_in.1, s32[256,128]{1,0:T(8,128)} %cell.3, f32[3,256,128]{2,1,0:T(8,128)} %bitcast.16), custom_call_target="tpu_custom_call" | custom-call | flops 7000000000 | bytes 21000000 | tf_op jit(solution)/shard_map/pallas_call | solution.py:398
  5.7 0.0 copy-start
  5.7 0.0 copy-start.2
  5.7 11.1 %all-to-all-start = ((f32[128,16,128]{2,1,0:T(8,128)}), f32[128,16,128]{2,1,0:T(8,128)S(1)}, u32[]{:S(2)}, u32[]{:S(2)}) async-start(f32[128,16,128]{2,1,0:T(8,128)} %bitcast.23), calls=%async_computation | async-start | bytes 2097152 | tf_op jit(solution)/shard_map/all_to_all | solution.py:414
  16.9 0.0 copy-start.7
  16.9 0.1 pad_add_fusion.side
  17.0 0.0 copy-start.6
  17.0 0.0 copy-done
  17.0 0.0 copy-done.2
  17.0 0.6 copy-done.7
  17.6 0.1 copy-done.6
  17.6 0.6 shard_map.114
  18.2 0.1 collective-permute-start.2
  18.3 0.7 collective-permute-start.3
  19.0 1.3 %collective-permute-start = (f32[144,128]{1,0:T(8,128)S(1)}, f32[144,128]{1,0:T(8,128)S(1)}, u32[]{:S(2)}, u32[]{:S(2)}) collective-permute-start(f32[144,128]{1,0:T(8,128)S(1)} %get-tuple-element.24), channel_id=1, source_target_pairs={{0,8},{8,0},{16,24},{24,16},{32,40},{40,32},{48,56},{56,48},{64,72... | collective-permute-start | bytes 221192 | tf_op jit(solution)/shard_map/ppermute | solution.py:425
  20.3 4.6 %collective-permute-start.1 = (f32[144,128]{1,0:T(8,128)S(1)}, f32[144,128]{1,0:T(8,128)S(1)}, u32[]{:S(2)}, u32[]{:S(2)}) collective-permute-start(f32[144,128]{1,0:T(8,128)S(1)} %get-tuple-element.25), channel_id=1, source_target_pairs={{0,120},{8,16},{16,8},{24,32},{32,24},{40,48},{48,40},{56,64},{64,... | collective-permute-start | bytes 221192 | tf_op jit(solution)/shard_map/ppermute | solution.py:426
  24.9 0.8 shard_map.113.old
  25.7 0.0 collective-permute-done.2.first_y
  25.8 0.0 collective-permute-done.3.second_y
  25.8 5.9 %collective-permute-done.first_x.listed_a = f32[144,128]{1,0:T(8,128)S(1)} collective-permute-done((f32[144,128]{1,0:T(8,128)S(1)}, f32[144,128]{1,0:T(8,128)S(1)}, u32[]{:S(2)}, u32[]{:S(2)}) %collective-permute-start) | collective-permute-done | bytes 73760 | tf_op jit(solution)/shard_map/ppermute | solution.py:425
  31.7 2.4 %collective-permute-done.1.second_x.listed_b = f32[144,128]{1,0:T(8,128)S(1)} collective-permute-done((f32[144,128]{1,0:T(8,128)S(1)}, f32[144,128]{1,0:T(8,128)S(1)}, u32[]{:S(2)}, u32[]{:S(2)}) %collective-permute-start.1) | collective-permute-done | bytes 73760 | tf_op jit(solution)/shard_map/ppermute | solution.py:426
  34.1 1.6 %shard_map.115.spread = f32[3,256,128]{2,1,0:T(8,128)S(1)} custom-call(s32[4]{0:T(128)S(1)} %pad_add_fusion.side, f32[3,8,16,256]{3,2,1,0:T(8,128)S(1)} %copy-done, f32[144,128]{1,0:T(8,128)S(1)} %collective-permute-done.first_x.listed_a, f32[144,128]{1,0:T(8,128)S(1)} %collective-permute-done.1.second_x.listed_b, ...), custom_call_target="tpu_custom_call" | custom-call | flops 2000000000 | bytes 6000000 | tf_op jit(solution)/shard_map/pallas_call | solution.py:432
  35.6 0.6 all-to-all-done
  36.3 2.1 %shard_map.116 = (f32[2048,128]{1,0:T(8,128)}, f32[3,8,16,256]{3,2,1,0:T(8,128)}, f32[8,128]{1,0:T(8,128)S(1)}) custom-call(f32[2048,128]{1,0:T(8,128)S(1)} %bitcast.13, f32[3,256,128]{2,1,0:T(8,128)S(1)} %shard_map.113.old, f32[3,256,128]{2,1,0:T(8,128)S(1)} %shard_map.115.spread), custom_call_target="tpu_custom_call" | custom-call | flops 3000000000 | bytes 9000000 | tf_op jit(solution)/shard_map/pallas_call | solution.py:440
  38.4 0.0 copy-start.4
  38.4 0.0 copy-start.5
  38.4 6.6 %all-to-all-start.1 = ((f32[128,16,128]{2,1,0:T(8,128)}), f32[128,16,128]{2,1,0:T(8,128)S(1)}, u32[]{:S(2)}, u32[]{:S(2)}) async-start(f32[128,16,128]{2,1,0:T(8,128)} %bitcast.9), calls=%async_computation.1 | async-start | bytes 2097152 | tf_op jit(solution)/shard_map/all_to_all | solution.py:448
  45.0 0.0 copy-start.8
  45.1 0.0 copy-done.4
  45.1 0.0 copy-done.5
  45.1 0.7 copy-done.8
  45.7 0.0 copy-start.1
  45.7 0.0 copy-start.3
  45.7 12.9 %shard_map.117 = (f32[2048,128]{1,0:T(8,128)S(1)}, s32[256]{0:T(256)S(1)}) custom-call(s32[4]{0:T(128)S(1)} %pad_add_fusion.side, s32[2,512]{1,0:T(2,128)S(1)} %copy-done.4, s32[2,512]{1,0:T(2,128)S(1)} %copy-done.5, s32[256]{0:T(256)S(1)} %copy-done.8, f32[3,256,128]{2,1,0:T(8,128)S(1)} %bitcast.20, f32[144,128]{1,0:T(8,128)S(1)} %collective-permute-done.first_x.listed_a, ...), custom_call_target="tpu_custom_call" | custom-call | flops 14000000000 | bytes 42000000 | tf_op jit(solution)/shard_map/pallas_call | solution.py:450
  58.7 5.5 %all-to-all-done.1 = f32[128,16,128]{2,1,0:T(8,128)S(1)} async-done(((f32[128,16,128]{2,1,0:T(8,128)}), f32[128,16,128]{2,1,0:T(8,128)S(1)}, u32[]{:S(2)}, u32[]{:S(2)}) %all-to-all-start.1) | async-done | bytes 1048608 | tf_op jit(solution)/shard_map/all_to_all | solution.py:448
  64.2 0.0 copy-done.1
  64.2 0.0 copy-done.3
  64.2 1.0 %shard_map.118 = (f32[48,128]{1,0:T(8,128)S(1)}, f32[48,128]{1,0:T(8,128)S(1)}) custom-call(s32[4]{0:T(128)S(1)} %pad_add_fusion.side, s32[256]{0:T(256)S(1)} %get-tuple-element.31.slot, s32[32]{0:T(128)S(1)} %copy-done.6, f32[512,4,128]{2,1,0:T(4,128)S(1)} %bitcast.14, s32[256,128]{1,0:T(8,128)S(1)} %copy-done.3, f32[3,256,128]{2,1,0:T(8,128)S(1)} %bitcast.21, ...), custom_call_target="tpu_custom_call" | custom-call | flops 2000000000 | bytes 6000000 | tf_op jit(solution)/shard_map/pallas_call | solution.py:459
  65.2 0.7 collective-permute-start.5
  65.9 0.0 collective-permute-start.4
  65.9 4.0 %shard_map.119 = (f32[2048,128]{1,0:T(8,128)S(1)}, f32[3,256,128]{2,1,0:T(8,128)S(1)}, f32[3,256,128]{2,1,0:T(8,128)S(1)}) custom-call(s32[256]{0:T(256)S(1)} %get-tuple-element.31.slot, f32[512,4,128]{2,1,0:T(4,128)S(1)} %bitcast.15, s32[256,128]{1,0:T(8,128)S(1)} %copy-done.3, f32[3,256,128]{2,1,0:T(8,128)S(1)} %bitcast.22, f32[3,256,128]{2,1,0:T(8,128)S(1)} %bitcast.18, ...), custom_call_target="tpu_custom_call" | custom-call | flops 6000000000 | bytes 18000000 | tf_op jit(solution)/shard_map/pallas_call | solution.py:469
  69.9 2.5 %collective-permute-done.5.listed_b = f32[48,128]{1,0:T(8,128)S(1)} collective-permute-done((f32[48,128]{1,0:T(8,128)S(1)}, f32[48,128]{1,0:T(8,128)S(1)}, u32[]{:S(2)}, u32[]{:S(2)}) %collective-permute-start.5) | collective-permute-done | bytes 24608 | tf_op jit(solution)/shard_map/ppermute | solution.py:468
  72.4 0.0 collective-permute-done.4.listed_a
  72.4 13.1 %shard_map.120 = (f32[3,256,128]{2,1,0:T(8,128)}, f32[3,256,128]{2,1,0:T(8,128)}) custom-call(s32[4]{0:T(128)S(1)} %pad_add_fusion.side, s32[2,512]{1,0:T(2,128)S(1)} %copy-done.4, s32[2,512]{1,0:T(2,128)S(1)} %copy-done.5, f32[3,256,128]{2,1,0:T(8,128)S(1)} %get-tuple-element.35.pos, f32[3,256,128]{2,1,0:T(8,128)S(1)} %get-tuple-element.36.vel, ...), custom_call_target="tpu_custom_call" | custom-call | flops 15000000512 | bytes 45000000 | tf_op jit(solution)/shard_map/pallas_call | solution.py:477
Async XLA Ops:
  5.7 11.3 %copy-start = (f32[3,8,16,256]{3,2,1,0:T(8,128)S(1)}, f32[3,8,16,256]{3,2,1,0:T(8,128)}, u32[]{:S(2)}) copy-start(f32[3,8,16,256]{3,2,1,0:T(8,128)} %fv.5) | copy-start | bytes 1179652
  5.7 11.3 %copy-start.2 = (f32[256,3,128]{2,0,1:T(8,128)S(1)}, f32[256,3,128]{2,0,1:T(8,128)}, u32[]{:S(2)}) copy-start(f32[256,3,128]{2,0,1:T(8,128)} %param.10) | copy-start | bytes 1179652
  5.7 30.6 %all-to-all-start = ((f32[128,16,128]{2,1,0:T(8,128)}), f32[128,16,128]{2,1,0:T(8,128)S(1)}, u32[]{:S(2)}, u32[]{:S(2)}) async-start(f32[128,16,128]{2,1,0:T(8,128)} %bitcast.23), calls=%async_computation | async-start | bytes 2097152 | tf_op jit(solution)/shard_map/all_to_all | solution.py:414
  16.9 0.7 copy-start.7
  17.0 0.7 copy-start.6
  18.2 7.5 %collective-permute-start.2 = (f32[3,8,256]{2,1,0:T(8,128)S(1)}, f32[3,8,256]{2,1,0:T(8,128)S(1)}, u32[]{:S(2)}, u32[]{:S(2)}) collective-permute-start(f32[3,8,256]{2,1,0:T(8,128)S(1)} %get-tuple-element.26), channel_id=1, source_target_pairs={{0,1},{1,0},{2,3},{3,2},{4,5},{5,4},{6,7},{7,6},{8,9},{9,8},{10,11... | collective-permute-start | bytes 73736 | tf_op jit(solution)/shard_map/ppermute | solution.py:427
  18.3 7.4 %collective-permute-start.3 = (f32[3,8,256]{2,1,0:T(8,128)S(1)}, f32[3,8,256]{2,1,0:T(8,128)S(1)}, u32[]{:S(2)}, u32[]{:S(2)}) collective-permute-start(f32[3,8,256]{2,1,0:T(8,128)S(1)} %get-tuple-element.27), channel_id=1, source_target_pairs={{1,2},{2,1},{3,4},{4,3},{5,6},{6,5},{9,10},{10,9},{11,12},{12,11},... | collective-permute-start | bytes 73736 | tf_op jit(solution)/shard_map/ppermute | solution.py:428
  19.0 12.7 %collective-permute-start = (f32[144,128]{1,0:T(8,128)S(1)}, f32[144,128]{1,0:T(8,128)S(1)}, u32[]{:S(2)}, u32[]{:S(2)}) collective-permute-start(f32[144,128]{1,0:T(8,128)S(1)} %get-tuple-element.24), channel_id=1, source_target_pairs={{0,8},{8,0},{16,24},{24,16},{32,40},{40,32},{48,56},{56,48},{64,72... | collective-permute-start | bytes 221192 | tf_op jit(solution)/shard_map/ppermute | solution.py:425
  20.3 13.8 %collective-permute-start.1 = (f32[144,128]{1,0:T(8,128)S(1)}, f32[144,128]{1,0:T(8,128)S(1)}, u32[]{:S(2)}, u32[]{:S(2)}) collective-permute-start(f32[144,128]{1,0:T(8,128)S(1)} %get-tuple-element.25), channel_id=1, source_target_pairs={{0,120},{8,16},{16,8},{24,32},{32,24},{40,48},{48,40},{56,64},{64,... | collective-permute-start | bytes 221192 | tf_op jit(solution)/shard_map/ppermute | solution.py:426
  38.4 6.7 %copy-start.4 = (s32[2,512]{1,0:T(2,128)S(1)}, s32[2,512]{1,0:T(2,128)}, u32[]{:S(2)}) copy-start(s32[2,512]{1,0:T(2,128)} %first.3) | copy-start | bytes 12292
  38.4 6.7 %copy-start.5 = (s32[2,512]{1,0:T(2,128)S(1)}, s32[2,512]{1,0:T(2,128)}, u32[]{:S(2)}) copy-start(s32[2,512]{1,0:T(2,128)} %second.3) | copy-start | bytes 12292
  38.4 25.8 %all-to-all-start.1 = ((f32[128,16,128]{2,1,0:T(8,128)}), f32[128,16,128]{2,1,0:T(8,128)S(1)}, u32[]{:S(2)}, u32[]{:S(2)}) async-start(f32[128,16,128]{2,1,0:T(8,128)} %bitcast.9), calls=%async_computation.1 | async-start | bytes 2097152 | tf_op jit(solution)/shard_map/all_to_all | solution.py:448
  45.0 0.7 copy-start.8
  45.7 18.5 %copy-start.1 = (f32[256,3,128]{2,0,1:T(8,128)S(1)}, f32[256,3,128]{2,0,1:T(8,128)}, u32[]{:S(2)}) copy-start(f32[256,3,128]{2,0,1:T(8,128)} %param.11) | copy-start | bytes 1179652
  45.7 18.5 %copy-start.3 = (s32[256,128]{1,0:T(8,128)S(1)}, s32[256,128]{1,0:T(8,128)}, u32[]{:S(2)}) copy-start(s32[256,128]{1,0:T(8,128)} %cell.3) | copy-start | bytes 393220
  65.2 7.2 %collective-permute-start.5 = (f32[48,128]{1,0:T(8,128)S(1)}, f32[48,128]{1,0:T(8,128)S(1)}, u32[]{:S(2)}, u32[]{:S(2)}) collective-permute-start(f32[48,128]{1,0:T(8,128)S(1)} %get-tuple-element.37), channel_id=1, source_target_pairs={{0,120},{8,16},{16,8},{24,32},{32,24},{40,48},{48,40},{56,64},{64,... | collective-permute-start | bytes 73736 | tf_op jit(solution)/shard_map/ppermute | solution.py:468
  65.9 6.5 %collective-permute-start.4 = (f32[48,128]{1,0:T(8,128)S(1)}, f32[48,128]{1,0:T(8,128)S(1)}, u32[]{:S(2)}, u32[]{:S(2)}) collective-permute-start(f32[48,128]{1,0:T(8,128)S(1)} %get-tuple-element.34.after), channel_id=1, source_target_pairs={{0,8},{8,0},{16,24},{24,16},{32,40},{40,32},{48,56},{56,48},{64,72... | collective-permute-start | bytes 73736 | tf_op jit(solution)/shard_map/ppermute | solution.py:467

commit v7 on v6

--- a/solution.py
+++ b/solution.py
@@ -9,8 +9,8 @@
 
 F32 = jnp.float32
 BF16 = jnp.bfloat16
-PAIR_GROUP = 128
-BLOCK_GROUP = 32
+PAIR_GROUP = 256
+BLOCK_GROUP = 128
 DEPOSIT_GROUP = 128
 CAP = 4
 EPS2 = 0.0025
@@ -143,7 +143,8 @@
     return swap_groups(jnp.stack(tiles, axis=0)).reshape(len(tiles) * 8, 128)
 
 
-def old_kernel(fv, bricks):
+def old_kernel(fv, sent, bricks, around):
+    around[...] = sent[96:144, :]
     for m in range(3):
         bricks[m] = to_bricks(fv, m)
 
@@ -151,7 +152,6 @@
 def spread_kernel(side, fv, first_x, second_x, first_y, second_y, bricks, grid):
     sx, sy, sz = fv.shape[1:]
     odd = side[0].astype(F32)
-    has_low, has_high = side[2].astype(F32), side[3].astype(F32)
     odd_y = jnp.full((sx, sz), side[1], jnp.int32) == 1
     yrow = lax.broadcasted_iota(jnp.int32, (sy, sz), 0)
     zlane = lax.broadcasted_iota(jnp.int32, (sy, sz), 1)
@@ -160,8 +160,8 @@
             jnp.concatenate([ref[(m * 2 + h) * 16 : (m * 2 + h + 1) * 16, :] for h in range(2)], axis=1)
             for ref in (first_x, second_x)
         ]
-        from_low = (odd * has_low) * first + ((1.0 - odd) * has_low) * second
-        from_high = ((1.0 - odd) * has_high) * first + (odd * has_high) * second
+        from_low = odd * first + (1.0 - odd) * second
+        from_high = (1.0 - odd) * first + odd * second
         lefts = jnp.where(odd_y, first_y[m], second_y[m])
         rights = jnp.where(odd_y, second_y[m], first_y[m])
         for x in range(sx):
@@ -239,7 +239,7 @@
     return a, b, n - a - b
 
 
-def push_loop(step, side, first, second, pos, listed, at, push, feat_b, feat_a):
+def push_loop(step, side, first, second, pos, listed, push, feat_b, feat_a):
     blocks = pos.shape[1]
     one = jnp.ones((8, 128), F32)
     zero = jnp.zeros((8, 128), F32)
@@ -259,9 +259,9 @@
         return c
 
     lax.fori_loop(0, blocks // 8, own, 0, unroll=2)
-    for ref, upper in zip(listed, (1 - side[0], side[0])):
+    for refs, upper in zip(listed, (1 - side[0], side[0])):
         for g in range(2):
-            hi, lo, _, norm = feature_rows([ref[at + m * 16 + g * 8 : at + m * 16 + g * 8 + 8, :] for m in range(3)])
+            hi, lo, _, norm = feature_rows([sum(ref[at + m * 16 + g * 8 : at + m * 16 + g * 8 + 8, :] for ref, at in refs) for m in range(3)])
             n = split3(norm)
             put(feat_b, pl.multiple_of(blocks + upper * 16 + g * 8, 8), hi + [one, n[0], n[1], n[2], one] + lo + [one, zero, zero, zero, zero])
     push[...] = jnp.zeros(push.shape, F32)
@@ -292,13 +292,14 @@
     lax.fori_loop(0, first.shape[1] // PAIR_GROUP, pairs, 0)
 
 
-def push_kernel(side, first, second, slot, pos, listed_a, listed_b, after, push, slot_out, feat_b, feat_a):
+def push_kernel(side, first, second, slot, pos, listed_a, listed_b, around, after, push, slot_out, feat_b, feat_a):
     def hand_on(q, c):
         slot_out[q] = slot[q]
         return c
 
     lax.fori_loop(0, slot.shape[0], hand_on, 0, unroll=8)
-    push_loop(0, side, first, second, pos, (listed_a, listed_b), 96, push, feat_b, feat_a)
+    listed = (((listed_a, 96),), ((listed_b, 96), (around, 0)))
+    push_loop(0, side, first, second, pos, listed, push, feat_b, feat_a)
 
 
 def advance(pos, vel, push, flow, pos_out, vel_out):
@@ -356,7 +357,7 @@
 
 
 def last_kernel(side, first, second, pos, vel, listed_a, listed_b, flow, pos_out, vel_out, push, feat_b, feat_a):
-    push_loop(1, side, first, second, pos, (listed_a, listed_b), 0, push, feat_b, feat_a)
+    push_loop(1, side, first, second, pos, (((listed_a, 0),), ((listed_b, 0),)), push, feat_b, feat_a)
     advance(pos, vel, push, flow, pos_out, vel_out)
 
 
@@ -414,21 +415,24 @@
     recv = lax.all_to_all(send.reshape(slots * 4, 128), ("gx", "gy"), split_axis=0, concat_axis=0, tiled=True)
 
     me_x, me_y = lax.axis_index("gx"), lax.axis_index("gy")
-    side = jnp.stack([me_x % 2, me_y % 2, me_x > 0, me_x < nx - 1]).astype(jnp.int32)
+    side = jnp.stack([me_x % 2, me_y % 2]).astype(jnp.int32)
     first_x, second_x, first_y, second_y = call(
         faces_kernel,
         [SMEM, SMEM, VMEM, VMEM, VMEM],
         [shape(144, 128), shape(144, 128), shape(3, sx, sz), shape(3, sx, sz)],
         [VMEM] * 4,
     )(side, halo_list, fluid_vel, pos, placed)
+    bricks = sx // 2 * (sy // 4) * (sz // 16)
+    old, around = call(
+        old_kernel, [VMEM, VMEM], [shape(3, bricks, 128), shape(48, 128)], [VMEM, VMEM]
+    )(fluid_vel, second_x)
     perms_x, perms_y = swaps(nx, True), swaps(ny, False)
     first_x = lax.ppermute(first_x, "gx", perms_x[0])
-    second_x = lax.ppermute(second_x, "gx", perms_x[1])
+    second_x = lax.ppermute(second_x, "gx", perms_x[1][1:-1])
+    around = lax.ppermute(around, "gx", [(0, nx - 1), (nx - 1, 0)])
     first_y = lax.ppermute(first_y, "gy", perms_y[0])
     second_y = lax.ppermute(second_y, "gy", perms_y[1])
 
-    bricks = sx // 2 * (sy // 4) * (sz // 16)
-    old = call(old_kernel, [VMEM], shape(3, bricks, 128), VMEM)(fluid_vel)
     spread = call(
         spread_kernel,
         [SMEM] + [VMEM] * 5,
@@ -449,12 +453,12 @@
     pair_scratch = [pltpu.VMEM(((blocks + 32) * 16, 128), F32), pltpu.VMEM((blocks * 16, 128), F32)]
     push, slot = call(
         push_kernel,
-        [SMEM] * 4 + [VMEM] * 4,
+        [SMEM] * 4 + [VMEM] * 5,
         [shape(blocks * 8, 128), shape(blocks, dtype=jnp.int32)],
         [VMEM, SMEM],
         pair_scratch,
         14,
-    )(side, pair_self, pair_other, slot, pos, first_x, second_x, stepped)
+    )(side, pair_self, pair_other, slot, pos, first_x, second_x, around, stepped)
 
     first, second = call(
         listed_kernel,

time: 85.9 us -> 85.5 us (level)
  starting transfers between devices: 25.2 us -> 27.9 us
  Pallas kernels: 41.1 us -> 39.1 us
  waiting for transfers between devices: 17 us -> 15.8 us
    ppermute x1, waiting for transfers between devices: 5.93 us -> 3.33 us  [per_device(): first_x = lax.ppermute(first_x, 'gx', perms_x[0])]
    ppermute x1 -> x2, starting transfers between devices: 4.65 us -> 7.21 us  [the longest x1 6.56 us: per_device(): around = lax.ppermute(around, 'gx', [(0, nx - 1), (nx - 1, 0)])]
    all_to_all x1, waiting for transfers between devices: 0.65 us -> 3.04 us  [per_device(): lax.all_to_all(send.reshape(slots * 4, 128), ('gx', 'gy'), split_axis=0,...]
    ppermute x1 -> x2, waiting for transfers between devices: 2.36 us -> 0.01 us  [the longest x1 0.01 us: per_device(): second_x = lax.ppermute(second_x, 'gx', perms_x[1][1:-1])]
  transfers between devices with their start and end apart: 8 -> 9, of which waited for: 5 -> 4; matrix products, arithmetic and copies ran while one was open for 0% -> 0% of each run, Pallas kernels for 23% -> 24%
where the time goes in v7:
time: 85.5 us; the launch traced here: 85.1 us
  Pallas kernels  39.1 us (46%)
  starting transfers between devices  27.9 us (33%)
  waiting for transfers between devices  15.8 us (18%)
  local copies, waits for them, and re-layouts  1.34 us (2%)
    pallas_call x1, Pallas kernels, per_device(): call(last_kernel, [SMEM] * 3 + [VMEM] * 5, [shape(3, blocks, 128), shape(...  12.5 us
    pallas_call x1, Pallas kernels, per_device(): call(push_kernel, [SMEM] * 4 + [VMEM] * 5, [shape(blocks * 8, 128), shape...  12.3 us
    all_to_all x1, starting transfers between devices, per_device(): lax.all_to_all(send.reshape(slots * 4, 128), ('gx', 'gy'), split_axis=0,...  11.1 us
    all_to_all x1, starting transfers between devices, per_device(): lax.all_to_all(answer, ('gx', 'gy'), split_axis=0, concat_axis=0, tiled=T...  6.64 us
    ppermute x1, starting transfers between devices, per_device(): around = lax.ppermute(around, 'gx', [(0, nx - 1), (nx - 1, 0)])  6.56 us
    all_to_all x1, waiting for transfers between devices, per_device(): lax.all_to_all(answer, ('gx', 'gy'), split_axis=0, concat_axis=0, tiled=T...  6.13 us
    pallas_call x1, Pallas kernels, per_device(): call(deposit_kernel, [HBM] * 4, [shape(slots, 4, 128), shape(blocks, dtyp...  5.05 us
    ppermute x1, waiting for transfers between devices, per_device(): first_x = lax.ppermute(first_x, 'gx', perms_x[0])  3.33 us
  transfers between devices with their start and end apart: 9, of which 4 were waited for; matrix products, arithmetic and copies ran while one was open for 0% of the time, Pallas kernels for 24%

profile of v7, /device:TPU:0, one launch (start us, length us, event | category | flops | bytes accessed | tf_op | source)
XLA Modules:
  0.0 85.1 jit_solution(5864582040903830535)
XLA Ops:
  0.6 5.0 %shard_map.112 = (f32[512,4,128]{2,1,0:T(4,128)}, s32[256]{0:T(256)}, f32[8,128]{1,0:T(8,128)}) custom-call(s32[256]{0:T(256)} %bitcast.22, s32[256]{0:T(256)} %local_in.1, s32[256,128]{1,0:T(8,128)} %cell.3, f32[3,256,128]{2,1,0:T(8,128)} %bitcast.14), custom_call_target="tpu_custom_call" | custom-call | flops 7000000000 | bytes 21000000 | tf_op jit(solution)/shard_map/pallas_call | solution.py:399
  5.7 0.0 copy-start
  5.7 0.0 copy-start.2
  5.7 11.1 %all-to-all-start = ((f32[128,16,128]{2,1,0:T(8,128)}), f32[128,16,128]{2,1,0:T(8,128)S(1)}, u32[]{:S(2)}, u32[]{:S(2)}) async-start(f32[128,16,128]{2,1,0:T(8,128)} %bitcast.21), calls=%async_computation | async-start | bytes 2097152 | tf_op jit(solution)/shard_map/all_to_all | solution.py:415
  16.9 0.0 copy-start.7
  16.9 0.1 pad_add_fusion.side
  17.0 0.0 copy-start.6
  17.0 0.0 copy-done
  17.0 0.0 copy-done.2
  17.0 0.6 copy-done.7
  17.6 0.1 copy-done.6
  17.6 0.6 shard_map.113
  18.2 0.1 collective-permute-start.2
  18.3 0.7 collective-permute-start.3
  19.0 1.3 %collective-permute-start = (f32[144,128]{1,0:T(8,128)S(1)}, f32[144,128]{1,0:T(8,128)S(1)}, u32[]{:S(2)}, u32[]{:S(2)}) collective-permute-start(f32[144,128]{1,0:T(8,128)S(1)} %get-tuple-element.28), channel_id=1, source_target_pairs={{0,8},{8,0},{16,24},{24,16},{32,40},{40,32},{48,56},{56,48},{64,72... | collective-permute-start | bytes 221192 | tf_op jit(solution)/shard_map/ppermute | solution.py:430
  20.3 0.7 collective-permute-start.1
  21.0 0.8 shard_map.114
  21.8 6.6 %collective-permute-start.4 = (f32[48,128]{1,0:T(8,128)S(1)}, f32[48,128]{1,0:T(8,128)S(1)}, u32[]{:S(2)}, u32[]{:S(2)}) collective-permute-start(f32[48,128]{1,0:T(8,128)S(1)} %get-tuple-element.33), channel_id=1, source_target_pairs={{0,120},{120,0},{1,121},{121,1},{2,122},{122,2},{3,123},{123,3},{4... | collective-permute-start | bytes 73736 | tf_op jit(solution)/shard_map/ppermute | solution.py:432
  28.3 0.0 collective-permute-done.2.first_y
  28.3 0.0 collective-permute-done.3.second_y
  28.3 3.3 %collective-permute-done.first_x.listed_a = f32[144,128]{1,0:T(8,128)S(1)} collective-permute-done((f32[144,128]{1,0:T(8,128)S(1)}, f32[144,128]{1,0:T(8,128)S(1)}, u32[]{:S(2)}, u32[]{:S(2)}) %collective-permute-start) | collective-permute-done | bytes 73760 | tf_op jit(solution)/shard_map/ppermute | solution.py:430
  31.7 0.0 collective-permute-done.1.second_x.listed_b
  31.7 1.6 %shard_map.115.spread = f32[3,256,128]{2,1,0:T(8,128)S(1)} custom-call(s32[2]{0:T(128)S(1)} %pad_add_fusion.side, f32[3,8,16,256]{3,2,1,0:T(8,128)S(1)} %copy-done, f32[144,128]{1,0:T(8,128)S(1)} %collective-permute-done.first_x.listed_a, f32[144,128]{1,0:T(8,128)S(1)} %collective-permute-done.1.second_x.listed_b, ...), custom_call_target="tpu_custom_call" | custom-call | flops 2000000000 | bytes 6000000 | tf_op jit(solution)/shard_map/pallas_call | solution.py:436
  33.2 3.0 %all-to-all-done = f32[128,16,128]{2,1,0:T(8,128)S(1)} async-done(((f32[128,16,128]{2,1,0:T(8,128)}), f32[128,16,128]{2,1,0:T(8,128)S(1)}, u32[]{:S(2)}, u32[]{:S(2)}) %all-to-all-start) | async-done | bytes 1048608 | tf_op jit(solution)/shard_map/all_to_all | solution.py:415
  36.3 2.1 %shard_map.116 = (f32[2048,128]{1,0:T(8,128)}, f32[3,8,16,256]{3,2,1,0:T(8,128)}, f32[8,128]{1,0:T(8,128)S(1)}) custom-call(f32[2048,128]{1,0:T(8,128)S(1)} %bitcast.11, f32[3,256,128]{2,1,0:T(8,128)S(1)} %get-tuple-element.27.old, f32[3,256,128]{2,1,0:T(8,128)S(1)} %shard_map.115.spread), custom_call_target="tpu_custom_call" | custom-call | flops 3000000000 | bytes 9000000 | tf_op jit(solution)/shard_map/pallas_call | solution.py:444
  38.4 0.0 copy-start.4
  38.4 0.0 copy-start.5
  38.4 6.6 %all-to-all-start.1 = ((f32[128,16,128]{2,1,0:T(8,128)}), f32[128,16,128]{2,1,0:T(8,128)S(1)}, u32[]{:S(2)}, u32[]{:S(2)}) async-start(f32[128,16,128]{2,1,0:T(8,128)} %bitcast.7), calls=%async_computation.1 | async-start | bytes 2097152 | tf_op jit(solution)/shard_map/all_to_all | solution.py:452
  45.0 0.0 collective-permute-done.4.around
  45.1 0.0 copy-start.8
  45.1 0.0 copy-done.4
  45.1 0.0 copy-done.5
  45.1 0.7 copy-done.8
  45.7 0.0 copy-start.1
  45.7 0.0 copy-start.3
  45.7 12.3 %shard_map.117 = (f32[2048,128]{1,0:T(8,128)S(1)}, s32[256]{0:T(256)S(1)}) custom-call(s32[2]{0:T(128)S(1)} %pad_add_fusion.side, s32[2,512]{1,0:T(2,128)S(1)} %copy-done.4, s32[2,512]{1,0:T(2,128)S(1)} %copy-done.5, s32[256]{0:T(256)S(1)} %copy-done.8, f32[3,256,128]{2,1,0:T(8,128)S(1)} %bitcast.18, f32[144,128]{1,0:T(8,128)S(1)} %collective-permute-done.first_x.listed_a, ...), custom_call_target="tpu_custom_call" | custom-call | flops 14000000000 | bytes 42000000 | tf_op jit(solution)/shard_map/pallas_call | solution.py:454
  58.1 6.1 %all-to-all-done.1 = f32[128,16,128]{2,1,0:T(8,128)S(1)} async-done(((f32[128,16,128]{2,1,0:T(8,128)}), f32[128,16,128]{2,1,0:T(8,128)S(1)}, u32[]{:S(2)}, u32[]{:S(2)}) %all-to-all-start.1) | async-done | bytes 1048608 | tf_op jit(solution)/shard_map/all_to_all | solution.py:452
  64.2 0.0 copy-done.1
  64.2 0.0 copy-done.3
  64.2 1.0 %shard_map.118 = (f32[48,128]{1,0:T(8,128)S(1)}, f32[48,128]{1,0:T(8,128)S(1)}) custom-call(s32[2]{0:T(128)S(1)} %pad_add_fusion.side, s32[256]{0:T(256)S(1)} %get-tuple-element.35.slot, s32[32]{0:T(128)S(1)} %copy-done.6, f32[512,4,128]{2,1,0:T(4,128)S(1)} %bitcast.12, s32[256,128]{1,0:T(8,128)S(1)} %copy-done.3, f32[3,256,128]{2,1,0:T(8,128)S(1)} %bitcast.19, ...), custom_call_target="tpu_custom_call" | custom-call | flops 2000000000 | bytes 6000000 | tf_op jit(solution)/shard_map/pallas_call | solution.py:463
  65.2 0.9 %collective-permute-start.6 = (f32[48,128]{1,0:T(8,128)S(1)}, f32[48,128]{1,0:T(8,128)S(1)}, u32[]{:S(2)}, u32[]{:S(2)}) collective-permute-start(f32[48,128]{1,0:T(8,128)S(1)} %get-tuple-element.41), channel_id=1, source_target_pairs={{0,120},{8,16},{16,8},{24,32},{32,24},{40,48},{48,40},{56,64},{64,... | collective-permute-start | bytes 73736 | tf_op jit(solution)/shard_map/ppermute | solution.py:472
  66.1 0.0 collective-permute-start.5
  66.1 3.2 %shard_map.119 = (f32[2048,128]{1,0:T(8,128)S(1)}, f32[3,256,128]{2,1,0:T(8,128)S(1)}, f32[3,256,128]{2,1,0:T(8,128)S(1)}) custom-call(s32[256]{0:T(256)S(1)} %get-tuple-element.35.slot, f32[512,4,128]{2,1,0:T(4,128)S(1)} %bitcast.13, s32[256,128]{1,0:T(8,128)S(1)} %copy-done.3, f32[3,256,128]{2,1,0:T(8,128)S(1)} %bitcast.20, f32[3,256,128]{2,1,0:T(8,128)S(1)} %bitcast.16, ...), custom_call_target="tpu_custom_call" | custom-call | flops 6000000000 | bytes 18000000 | tf_op jit(solution)/shard_map/pallas_call | solution.py:473
  69.3 3.3 %collective-permute-done.6.listed_b = f32[48,128]{1,0:T(8,128)S(1)} collective-permute-done((f32[48,128]{1,0:T(8,128)S(1)}, f32[48,128]{1,0:T(8,128)S(1)}, u32[]{:S(2)}, u32[]{:S(2)}) %collective-permute-start.6) | collective-permute-done | bytes 24608 | tf_op jit(solution)/shard_map/ppermute | solution.py:472
  72.6 0.0 collective-permute-done.5.listed_a
  72.6 12.5 %shard_map.120 = (f32[3,256,128]{2,1,0:T(8,128)}, f32[3,256,128]{2,1,0:T(8,128)}) custom-call(s32[2]{0:T(128)S(1)} %pad_add_fusion.side, s32[2,512]{1,0:T(2,128)S(1)} %copy-done.4, s32[2,512]{1,0:T(2,128)S(1)} %copy-done.5, f32[3,256,128]{2,1,0:T(8,128)S(1)} %get-tuple-element.39.pos, f32[3,256,128]{2,1,0:T(8,128)S(1)} %get-tuple-element.40.vel, ...), custom_call_target="tpu_custom_call" | custom-call | flops 15000000512 | bytes 45000000 | tf_op jit(solution)/shard_map/pallas_call | solution.py:481
Async XLA Ops:
  5.7 11.3 %copy-start = (f32[3,8,16,256]{3,2,1,0:T(8,128)S(1)}, f32[3,8,16,256]{3,2,1,0:T(8,128)}, u32[]{:S(2)}) copy-start(f32[3,8,16,256]{3,2,1,0:T(8,128)} %fv.5) | copy-start | bytes 1179652
  5.7 11.3 %copy-start.2 = (f32[256,3,128]{2,0,1:T(8,128)S(1)}, f32[256,3,128]{2,0,1:T(8,128)}, u32[]{:S(2)}) copy-start(f32[256,3,128]{2,0,1:T(8,128)} %param.10) | copy-start | bytes 1179652
  5.7 30.6 %all-to-all-start = ((f32[128,16,128]{2,1,0:T(8,128)}), f32[128,16,128]{2,1,0:T(8,128)S(1)}, u32[]{:S(2)}, u32[]{:S(2)}) async-start(f32[128,16,128]{2,1,0:T(8,128)} %bitcast.21), calls=%async_computation | async-start | bytes 2097152 | tf_op jit(solution)/shard_map/all_to_all | solution.py:415
  16.9 0.7 copy-start.7
  17.0 0.7 copy-start.6
  18.2 10.1 %collective-permute-start.2 = (f32[3,8,256]{2,1,0:T(8,128)S(1)}, f32[3,8,256]{2,1,0:T(8,128)S(1)}, u32[]{:S(2)}, u32[]{:S(2)}) collective-permute-start(f32[3,8,256]{2,1,0:T(8,128)S(1)} %get-tuple-element.29), channel_id=1, source_target_pairs={{0,1},{1,0},{2,3},{3,2},{4,5},{5,4},{6,7},{7,6},{8,9},{9,8},{10,11... | collective-permute-start | bytes 73736 | tf_op jit(solution)/shard_map/ppermute | solution.py:433
  18.3 10.0 %collective-permute-start.3 = (f32[3,8,256]{2,1,0:T(8,128)S(1)}, f32[3,8,256]{2,1,0:T(8,128)S(1)}, u32[]{:S(2)}, u32[]{:S(2)}) collective-permute-start(f32[3,8,256]{2,1,0:T(8,128)S(1)} %get-tuple-element.30), channel_id=1, source_target_pairs={{1,2},{2,1},{3,4},{4,3},{5,6},{6,5},{9,10},{10,9},{11,12},{12,11},... | collective-permute-start | bytes 73736 | tf_op jit(solution)/shard_map/ppermute | solution.py:434
  19.0 12.7 %collective-permute-start = (f32[144,128]{1,0:T(8,128)S(1)}, f32[144,128]{1,0:T(8,128)S(1)}, u32[]{:S(2)}, u32[]{:S(2)}) collective-permute-start(f32[144,128]{1,0:T(8,128)S(1)} %get-tuple-element.28), channel_id=1, source_target_pairs={{0,8},{8,0},{16,24},{24,16},{32,40},{40,32},{48,56},{56,48},{64,72... | collective-permute-start | bytes 221192 | tf_op jit(solution)/shard_map/ppermute | solution.py:430
  20.3 11.4 %collective-permute-start.1 = (f32[144,128]{1,0:T(8,128)S(1)}, f32[144,128]{1,0:T(8,128)S(1)}, u32[]{:S(2)}, u32[]{:S(2)}) collective-permute-start(f32[144,128]{1,0:T(8,128)S(1)} %get-tuple-element.26.sent), channel_id=1, source_target_pairs={{8,16},{16,8},{24,32},{32,24},{40,48},{48,40},{56,64},{64,56},{72,... | collective-permute-start | bytes 221192 | tf_op jit(solution)/shard_map/ppermute | solution.py:431
  21.8 23.3 %collective-permute-start.4 = (f32[48,128]{1,0:T(8,128)S(1)}, f32[48,128]{1,0:T(8,128)S(1)}, u32[]{:S(2)}, u32[]{:S(2)}) collective-permute-start(f32[48,128]{1,0:T(8,128)S(1)} %get-tuple-element.33), channel_id=1, source_target_pairs={{0,120},{120,0},{1,121},{121,1},{2,122},{122,2},{3,123},{123,3},{4... | collective-permute-start | bytes 73736 | tf_op jit(solution)/shard_map/ppermute | solution.py:432
  38.4 6.7 %copy-start.4 = (s32[2,512]{1,0:T(2,128)S(1)}, s32[2,512]{1,0:T(2,128)}, u32[]{:S(2)}) copy-start(s32[2,512]{1,0:T(2,128)} %first.3) | copy-start | bytes 12292
  38.4 6.7 %copy-start.5 = (s32[2,512]{1,0:T(2,128)S(1)}, s32[2,512]{1,0:T(2,128)}, u32[]{:S(2)}) copy-start(s32[2,512]{1,0:T(2,128)} %second.3) | copy-start | bytes 12292
  38.4 25.8 %all-to-all-start.1 = ((f32[128,16,128]{2,1,0:T(8,128)}), f32[128,16,128]{2,1,0:T(8,128)S(1)}, u32[]{:S(2)}, u32[]{:S(2)}) async-start(f32[128,16,128]{2,1,0:T(8,128)} %bitcast.7), calls=%async_computation.1 | async-start | bytes 2097152 | tf_op jit(solution)/shard_map/all_to_all | solution.py:452
  45.1 0.7 copy-start.8
  45.7 18.5 %copy-start.1 = (f32[256,3,128]{2,0,1:T(8,128)S(1)}, f32[256,3,128]{2,0,1:T(8,128)}, u32[]{:S(2)}) copy-start(f32[256,3,128]{2,0,1:T(8,128)} %param.11) | copy-start | bytes 1179652
  45.7 18.5 %copy-start.3 = (s32[256,128]{1,0:T(8,128)S(1)}, s32[256,128]{1,0:T(8,128)}, u32[]{:S(2)}) copy-start(s32[256,128]{1,0:T(8,128)} %cell.3) | copy-start | bytes 393220
  65.2 7.4 %collective-permute-start.6 = (f32[48,128]{1,0:T(8,128)S(1)}, f32[48,128]{1,0:T(8,128)S(1)}, u32[]{:S(2)}, u32[]{:S(2)}) collective-permute-start(f32[48,128]{1,0:T(8,128)S(1)} %get-tuple-element.41), channel_id=1, source_target_pairs={{0,120},{8,16},{16,8},{24,32},{32,24},{40,48},{48,40},{56,64},{64,... | collective-permute-start | bytes 73736 | tf_op jit(solution)/shard_map/ppermute | solution.py:472
  66.1 6.5 %collective-permute-start.5 = (f32[48,128]{1,0:T(8,128)S(1)}, f32[48,128]{1,0:T(8,128)S(1)}, u32[]{:S(2)}, u32[]{:S(2)}) collective-permute-start(f32[48,128]{1,0:T(8,128)S(1)} %get-tuple-element.38.after), channel_id=1, source_target_pairs={{0,8},{8,0},{16,24},{24,16},{32,40},{40,32},{48,56},{56,48},{64,72... | collective-permute-start | bytes 73736 | tf_op jit(solution)/shard_map/ppermute | solution.py:471

commit v8 on v7

--- a/solution.py
+++ b/solution.py
@@ -10,6 +10,7 @@
 F32 = jnp.float32
 BF16 = jnp.bfloat16
 PAIR_GROUP = 256
+ORDERED_GROUP = 128
 BLOCK_GROUP = 128
 DEPOSIT_GROUP = 128
 CAP = 4
@@ -149,7 +150,7 @@
         bricks[m] = to_bricks(fv, m)
 
 
-def spread_kernel(side, fv, first_x, second_x, first_y, second_y, bricks, grid):
+def spread_kernel(side, ordered, fv, first_x, second_x, first_y, second_y, bricks, grid):
     sx, sy, sz = fv.shape[1:]
     odd = side[0].astype(F32)
     odd_y = jnp.full((sx, sz), side[1], jnp.int32) == 1
@@ -239,7 +240,23 @@
     return a, b, n - a - b
 
 
-def push_loop(step, side, first, second, pos, listed, push, feat_b, feat_a):
+def order_kernel(first, second, after, ordered):
+    n = first.shape[1]
+    blocks = n // 2
+
+    def place(p, own):
+        b = second[1, p]
+        inside = (b < blocks).astype(jnp.int32)
+        at = jnp.where(inside == 1, own, n - 1 - p + own)
+        ordered[at] = first[1, p]
+        ordered[n + at] = b
+        return own + inside
+
+    own = lax.fori_loop(0, n, place, jnp.int32(0), unroll=8)
+    ordered[2 * n] = own // ORDERED_GROUP
+
+
+def features(side, pos, listed, feat_b, feat_a):
     blocks = pos.shape[1]
     one = jnp.ones((8, 128), F32)
     zero = jnp.zeros((8, 128), F32)
@@ -259,17 +276,19 @@
         return c
 
     lax.fori_loop(0, blocks // 8, own, 0, unroll=2)
-    for refs, upper in zip(listed, (1 - side[0], side[0])):
+    for i, refs in enumerate(listed):
+        upper = side[0] if i else 1 - side[0]
         for g in range(2):
             hi, lo, _, norm = feature_rows([sum(ref[at + m * 16 + g * 8 : at + m * 16 + g * 8 + 8, :] for ref, at in refs) for m in range(3)])
             n = split3(norm)
             put(feat_b, pl.multiple_of(blocks + upper * 16 + g * 8, 8), hi + [one, n[0], n[1], n[2], one] + lo + [one, zero, zero, zero, zero])
-    push[...] = jnp.zeros(push.shape, F32)
+
+
+def push_pairs(pair, begin, end, group, push, feat_b, feat_a):
     top = lax.broadcasted_iota(jnp.int32, (8, 128), 0) < 3
 
     def one_pair(p):
-        a = first[step, p]
-        b = second[step, p]
+        a, b = pair(p)
         fb = feat_b[pl.ds(pl.multiple_of(b * 16, 16), 16), :]
         fa = feat_a[pl.ds(pl.multiple_of(a * 16, 16), 16), :]
         x, y = fa[0:8], fa[8:16]
@@ -283,13 +302,13 @@
         return a, (-0.5) * (x + z) * total - (res[0:8] + res[8:16])
 
     def pairs(g, c):
-        done = [one_pair(g * PAIR_GROUP + k) for k in range(PAIR_GROUP)]
+        done = [one_pair(g * group + k) for k in range(group)]
         for a, f in done:
             rows = pl.ds(pl.multiple_of(a * 8, 8), 8)
             push[rows, :] = push[rows, :] + f
         return c
 
-    lax.fori_loop(0, first.shape[1] // PAIR_GROUP, pairs, 0)
+    lax.fori_loop(begin, end, pairs, 0)
 
 
 def push_kernel(side, first, second, slot, pos, listed_a, listed_b, around, after, push, slot_out, feat_b, feat_a):
@@ -299,7 +318,10 @@
 
     lax.fori_loop(0, slot.shape[0], hand_on, 0, unroll=8)
     listed = (((listed_a, 96),), ((listed_b, 96), (around, 0)))
-    push_loop(0, side, first, second, pos, listed, push, feat_b, feat_a)
+    features(side, pos, listed, feat_b, feat_a)
+    push[...] = jnp.zeros(push.shape, F32)
+    groups = first.shape[1] // PAIR_GROUP
+    push_pairs(lambda p: (first[0, p], second[0, p]), 0, groups, PAIR_GROUP, push, feat_b, feat_a)
 
 
 def advance(pos, vel, push, flow, pos_out, vel_out):
@@ -322,28 +344,7 @@
     return both[0:8] + both[8:16]
 
 
-def listed_kernel(side, slot, halo, back, cell, pos, vel, push, first_out, second_out):
-    r8 = lax.broadcasted_iota(jnp.int32, (8, 128), 0)
-
-    def tile(ref, q):
-        rows = [jnp.broadcast_to(ref[m, pl.ds(q, 1), :], (8, 128)) for m in range(3)]
-        return jnp.where(r8 == 0, rows[0], jnp.where(r8 == 1, rows[1], rows[2]))
-
-    for out, upper in ((first_out, 1 - side[0]), (second_out, side[0])):
-        for j in range(16):
-            q = halo[upper * 16 + j]
-            flow = pick(onehot_cells(cell[pl.ds(q, 1), :]), back[slot[q]])
-            v = tile(vel, q)
-            rows = pl.ds(pl.multiple_of(q * 8, 8), 8)
-            drift = 2.0 * jnp.broadcast_to(flow[3:4], (8, 128))
-            force = 2.5 * push[rows, :] + drift * (flow - v)
-            v = v + 0.1 * jnp.where(r8 == 2, force - 1.0, force)
-            x = tile(pos, q) + 0.1 * v
-            for m in range(3):
-                out[m * 16 + j : m * 16 + j + 1, :] = x[m : m + 1, :]
-
-
-def pick_kernel(slot, back, cell, pos, vel, push, after, flow, pos_out, vel_out):
+def pick_kernel(side, slot, halo, back, cell, pos, vel, push, flow, pos_out, vel_out, first_x, second_x):
     def group(g, c):
         base = pl.multiple_of(g * BLOCK_GROUP, BLOCK_GROUP)
         cells = cell[pl.ds(base, BLOCK_GROUP), :]
@@ -354,10 +355,23 @@
 
     lax.fori_loop(0, cell.shape[0] // BLOCK_GROUP, group, 0)
     advance(pos, vel, push, flow, pos_out, vel_out)
-
-
-def last_kernel(side, first, second, pos, vel, listed_a, listed_b, flow, pos_out, vel_out, push, feat_b, feat_a):
-    push_loop(1, side, first, second, pos, (((listed_a, 0),), ((listed_b, 0),)), push, feat_b, feat_a)
+    put_listed(halo, 1 - side[0], pos_out, first_x, 0)
+    put_listed(halo, side[0], pos_out, second_x, 0)
+
+
+def inner_kernel(ordered, pos, push, feat_b, feat_a):
+    n = pos.shape[1] * 2
+    features(None, pos, (), feat_b, feat_a)
+    push[...] = jnp.zeros(push.shape, F32)
+    push_pairs(lambda p: (ordered[p], ordered[n + p]), 0, ordered[2 * n], ORDERED_GROUP, push, feat_b, feat_a)
+
+
+def last_kernel(side, ordered, pos, vel, listed_a, listed_b, flow, inner, pos_out, vel_out, push, feat_b, feat_a):
+    n = pos.shape[1] * 2
+    features(side, pos, (((listed_a, 0),), ((listed_b, 0),)), feat_b, feat_a)
+    push[...] = inner[...]
+    groups = n // ORDERED_GROUP
+    push_pairs(lambda p: (ordered[p], ordered[n + p]), ordered[2 * n], groups, ORDERED_GROUP, push, feat_b, feat_a)
     advance(pos, vel, push, flow, pos_out, vel_out)
 
 
@@ -426,6 +440,14 @@
     old, around = call(
         old_kernel, [VMEM, VMEM], [shape(3, bricks, 128), shape(48, 128)], [VMEM, VMEM]
     )(fluid_vel, second_x)
+    ordered = call(
+        order_kernel,
+        [SMEM, SMEM, VMEM],
+        shape(2 * pair_self.shape[1] + 128, dtype=jnp.int32),
+        SMEM,
+        (),
+        2,
+    )(pair_self, pair_other, around)
     perms_x, perms_y = swaps(nx, True), swaps(ny, False)
     first_x = lax.ppermute(first_x, "gx", perms_x[0])
     second_x = lax.ppermute(second_x, "gx", perms_x[1][1:-1])
@@ -435,12 +457,12 @@
 
     spread = call(
         spread_kernel,
-        [SMEM] + [VMEM] * 5,
+        [SMEM] * 2 + [VMEM] * 5,
         shape(3, bricks, 128),
         VMEM,
         [pltpu.VMEM((3, sx, sy, sz), F32)],
         2,
-    )(side, fluid_vel, first_x, second_x, first_y, second_y)
+    )(side, ordered, fluid_vel, first_x, second_x, first_y, second_y)
     answer, fluid, stepped = call(
         fluid_kernel,
         [VMEM] * 3,
@@ -460,32 +482,32 @@
         14,
     )(side, pair_self, pair_other, slot, pos, first_x, second_x, around, stepped)
 
-    first, second = call(
-        listed_kernel,
+    flow, pos, vel, listed_a, listed_b = call(
+        pick_kernel,
         [SMEM] * 3 + [VMEM] * 5,
-        [shape(48, 128), shape(48, 128)],
-        [VMEM] * 2,
+        [shape(blocks * 8, 128), shape(3, blocks, 128), shape(3, blocks, 128), shape(48, 128), shape(48, 128)],
+        [VMEM] * 5,
         (),
-        2,
+        4,
     )(side, slot, halo_list, back, cell_in_brick, pos, vel, push)
-    listed_a = lax.ppermute(first, "gx", perms_x[0])
-    listed_b = lax.ppermute(second, "gx", perms_x[1])
-    flow, pos, vel = call(
-        pick_kernel,
-        [SMEM] + [VMEM] * 6,
-        [shape(blocks * 8, 128), shape(3, blocks, 128), shape(3, blocks, 128)],
-        [VMEM] * 3,
-        (),
-        6,
-    )(slot, back, cell_in_brick, pos, vel, push, first)
+    listed_a = lax.ppermute(listed_a, "gx", perms_x[0])
+    listed_b = lax.ppermute(listed_b, "gx", perms_x[1])
+    inner = call(
+        inner_kernel,
+        [SMEM, VMEM],
+        shape(blocks * 8, 128),
+        VMEM,
+        pair_scratch,
+        10,
+    )(ordered, pos)
     pos, vel = call(
         last_kernel,
-        [SMEM] * 3 + [VMEM] * 5,
+        [SMEM] * 2 + [VMEM] * 6,
         [shape(3, blocks, 128), shape(3, blocks, 128)],
         [VMEM] * 2,
         [pltpu.VMEM((blocks * 8, 128), F32)] + pair_scratch,
-        15,
-    )(side, pair_self, pair_other, pos, vel, listed_a, listed_b, flow)
+        5,
+    )(side, ordered, pos, vel, listed_a, listed_b, flow, inner)
     return fluid, jnp.transpose(pos, (1, 0, 2)), jnp.transpose(vel, (1, 0, 2))
 
 

time: 85.5 us -> 85.1 us (level)
  waiting for transfers between devices: 15.8 us -> 7.92 us
  Pallas kernels: 39.1 us -> 45.2 us
    pallas_call x4 -> x5, Pallas kernels: 18.3 us -> 24.3 us  [the longest x1 9.35 us: per_device(): call(inner_kernel, [SMEM, VMEM], shape(blocks * 8, 128), VMEM, pair_scrat...]
    ppermute x1, waiting for transfers between devices: 3.33 us -> 0.01 us  [per_device(): first_x = lax.ppermute(first_x, 'gx', perms_x[0])]
    ppermute x2, waiting for transfers between devices: 3.28 us -> 0.01 us  [the longest x1 0.01 us: per_device(): listed_a = lax.ppermute(listed_a, 'gx', perms_x[0])]
    all_to_all x1, waiting for transfers between devices: 3.04 us -> 1.96 us  [per_device(): lax.all_to_all(send.reshape(slots * 4, 128), ('gx', 'gy'), split_axis=0,...]
  transfers between devices with their start and end apart: 9 -> 9, of which waited for: 4 -> 2; matrix products, arithmetic and copies ran while one was open for 0% -> 0% of each run, Pallas kernels for 24% -> 37%
where the time goes in v8:
time: 85.1 us; the launch traced here: 84.1 us
  Pallas kernels  45.2 us (53%)
  starting transfers between devices  28.6 us (34%)
  waiting for transfers between devices  7.92 us (9%)
  local copies, waits for them, and re-layouts  1.36 us (2%)
  between operations  0.86 us (1%)
    pallas_call x1, Pallas kernels, per_device(): call(push_kernel, [SMEM] * 4 + [VMEM] * 5, [shape(blocks * 8, 128), shape...  12.3 us
    all_to_all x1, starting transfers between devices, per_device(): lax.all_to_all(send.reshape(slots * 4, 128), ('gx', 'gy'), split_axis=0,...  11.1 us
    pallas_call x1, Pallas kernels, per_device(): call(inner_kernel, [SMEM, VMEM], shape(blocks * 8, 128), VMEM, pair_scrat...  9.35 us
    all_to_all x1, starting transfers between devices, per_device(): lax.all_to_all(answer, ('gx', 'gy'), split_axis=0, concat_axis=0, tiled=T...  6.89 us
    ppermute x1, starting transfers between devices, per_device(): around = lax.ppermute(around, 'gx', [(0, nx - 1), (nx - 1, 0)])  6.56 us
    all_to_all x1, waiting for transfers between devices, per_device(): lax.all_to_all(answer, ('gx', 'gy'), split_axis=0, concat_axis=0, tiled=T...  5.95 us
    pallas_call x1, Pallas kernels, per_device(): call(last_kernel, [SMEM] * 2 + [VMEM] * 6, [shape(3, blocks, 128), shape(...  5.81 us
    pallas_call x1, Pallas kernels, per_device(): call(deposit_kernel, [HBM] * 4, [shape(slots, 4, 128), shape(blocks, dtyp...  5.05 us
  transfers between devices with their start and end apart: 9, of which 2 were waited for; matrix products, arithmetic and copies ran while one was open for 0% of the time, Pallas kernels for 37%

profile of v8, /device:TPU:0, one launch (start us, length us, event | category | flops | bytes accessed | tf_op | source)
XLA Modules:
  0.0 84.1 jit_solution(2230506325806012256)
XLA Ops:
  0.6 5.1 %shard_map.112 = (f32[512,4,128]{2,1,0:T(4,128)}, s32[256]{0:T(256)}, f32[8,128]{1,0:T(8,128)}) custom-call(s32[256]{0:T(256)} %bitcast.19, s32[256]{0:T(256)} %local_in.1, s32[256,128]{1,0:T(8,128)} %cell.1, f32[3,256,128]{2,1,0:T(8,128)} %bitcast.13), custom_call_target="tpu_custom_call" | custom-call | flops 7000000000 | bytes 21000000 | tf_op jit(solution)/shard_map/pallas_call | solution.py:413
  5.7 0.0 copy-start
  5.7 0.0 copy-start.2
  5.7 11.1 %all-to-all-start = ((f32[128,16,128]{2,1,0:T(8,128)}), f32[128,16,128]{2,1,0:T(8,128)S(1)}, u32[]{:S(2)}, u32[]{:S(2)}) async-start(f32[128,16,128]{2,1,0:T(8,128)} %bitcast.18), calls=%async_computation | async-start | bytes 2097152 | tf_op jit(solution)/shard_map/all_to_all | solution.py:429
  16.9 0.0 copy-start.7
  16.9 0.1 pad_add_fusion.side
  17.0 0.0 copy-start.6
  17.0 0.0 copy-done
  17.0 0.0 copy-done.2
  17.0 0.6 copy-done.7
  17.6 0.1 copy-done.6
  17.6 0.6 shard_map.113
  18.3 0.1 collective-permute-start.2
  18.3 0.7 collective-permute-start.3
  19.0 1.3 %collective-permute-start = (f32[144,128]{1,0:T(8,128)S(1)}, f32[144,128]{1,0:T(8,128)S(1)}, u32[]{:S(2)}, u32[]{:S(2)}) collective-permute-start(f32[144,128]{1,0:T(8,128)S(1)} %get-tuple-element.29), channel_id=1, source_target_pairs={{0,8},{8,0},{16,24},{24,16},{32,40},{40,32},{48,56},{56,48},{64,72... | collective-permute-start | bytes 221192 | tf_op jit(solution)/shard_map/ppermute | solution.py:452
  20.3 0.0 copy-start.4
  20.3 0.0 copy-start.5
  20.3 0.8 collective-permute-start.1
  21.1 0.8 shard_map.114
  21.9 6.6 %collective-permute-start.4 = (f32[48,128]{1,0:T(8,128)S(1)}, f32[48,128]{1,0:T(8,128)S(1)}, u32[]{:S(2)}, u32[]{:S(2)}) collective-permute-start(f32[48,128]{1,0:T(8,128)S(1)} %get-tuple-element.28.after), channel_id=1, source_target_pairs={{0,120},{120,0},{1,121},{121,1},{2,122},{122,2},{3,123},{123,3},{4... | collective-permute-start | bytes 73736 | tf_op jit(solution)/shard_map/ppermute | solution.py:454
  28.5 0.0 copy-done.4
  28.5 0.0 copy-done.5
  28.5 4.2 %shard_map.115.ordered = s32[1152]{0:T(1024)S(1)} custom-call(s32[2,512]{1,0:T(2,128)S(1)} %copy-done.4, s32[2,512]{1,0:T(2,128)S(1)} %copy-done.5, f32[48,128]{1,0:T(8,128)S(1)} %get-tuple-element.28.after), custom_call_target="tpu_custom_call" | custom-call | flops 2000000000 | bytes 6000000 | tf_op jit(solution)/shard_map/pallas_call | solution.py:443
  32.6 0.0 collective-permute-done.2.first_y
  32.7 0.0 collective-permute-done.3.second_y
  32.7 0.0 collective-permute-done.first_x.listed_a
  32.7 0.0 collective-permute-done.1.second_x.listed_b
  32.7 1.6 %shard_map.116.spread = f32[3,256,128]{2,1,0:T(8,128)S(1)} custom-call(s32[2]{0:T(128)S(1)} %pad_add_fusion.side, s32[1152]{0:T(1024)S(1)} %shard_map.115.ordered, f32[3,8,16,256]{3,2,1,0:T(8,128)S(1)} %copy-done, f32[144,128]{1,0:T(8,128)S(1)} %collective-permute-done.first_x.listed_a, f32[144,128]{1,0:T(8,128)S(1)} %collective-permute-done.1.second_x.listed_b, ...), custom_call_target="tpu_custom_call" | custom-call | flops 2000000000 | bytes 6000000 | tf_op jit(solution)/shard_map/pallas_call | solution.py:458
  34.3 2.0 %all-to-all-done = f32[128,16,128]{2,1,0:T(8,128)S(1)} async-done(((f32[128,16,128]{2,1,0:T(8,128)}), f32[128,16,128]{2,1,0:T(8,128)S(1)}, u32[]{:S(2)}, u32[]{:S(2)}) %all-to-all-start) | async-done | bytes 1048608 | tf_op jit(solution)/shard_map/all_to_all | solution.py:429
  36.3 2.1 %shard_map.117 = (f32[2048,128]{1,0:T(8,128)}, f32[3,8,16,256]{3,2,1,0:T(8,128)}, f32[8,128]{1,0:T(8,128)S(1)}) custom-call(f32[2048,128]{1,0:T(8,128)S(1)} %bitcast.11, f32[3,256,128]{2,1,0:T(8,128)S(1)} %get-tuple-element.27.old, f32[3,256,128]{2,1,0:T(8,128)S(1)} %shard_map.116.spread), custom_call_target="tpu_custom_call" | custom-call | flops 3000000000 | bytes 9000000 | tf_op jit(solution)/shard_map/pallas_call | solution.py:466
  38.4 6.9 %all-to-all-start.1 = ((f32[128,16,128]{2,1,0:T(8,128)}), f32[128,16,128]{2,1,0:T(8,128)S(1)}, u32[]{:S(2)}, u32[]{:S(2)}) async-start(f32[128,16,128]{2,1,0:T(8,128)} %bitcast.7), calls=%async_computation.1 | async-start | bytes 2097152 | tf_op jit(solution)/shard_map/all_to_all | solution.py:474
  45.3 0.0 collective-permute-done.4.around
  45.3 0.0 copy-start.8
  45.3 0.7 copy-done.8
  46.0 0.0 copy-start.1
  46.0 0.0 copy-start.3
  46.0 12.3 %shard_map.118 = (f32[2048,128]{1,0:T(8,128)S(1)}, s32[256]{0:T(256)S(1)}) custom-call(s32[2]{0:T(128)S(1)} %pad_add_fusion.side, s32[2,512]{1,0:T(2,128)S(1)} %copy-done.4, s32[2,512]{1,0:T(2,128)S(1)} %copy-done.5, s32[256]{0:T(256)S(1)} %copy-done.8, f32[3,256,128]{2,1,0:T(8,128)S(1)} %bitcast.16, f32[144,128]{1,0:T(8,128)S(1)} %collective-permute-done.first_x.listed_a, ...), custom_call_target="tpu_custom_call" | custom-call | flops 14000000000 | bytes 42000000 | tf_op jit(solution)/shard_map/pallas_call | solution.py:476
  58.3 5.9 %all-to-all-done.1 = f32[128,16,128]{2,1,0:T(8,128)S(1)} async-done(((f32[128,16,128]{2,1,0:T(8,128)}), f32[128,16,128]{2,1,0:T(8,128)S(1)}, u32[]{:S(2)}, u32[]{:S(2)}) %all-to-all-start.1) | async-done | bytes 1048608 | tf_op jit(solution)/shard_map/all_to_all | solution.py:474
  64.3 0.0 copy-done.1
  64.3 0.0 copy-done.3
  64.3 3.4 %shard_map.119 = (f32[2048,128]{1,0:T(8,128)S(1)}, f32[3,256,128]{2,1,0:T(8,128)S(1)}, f32[3,256,128]{2,1,0:T(8,128)S(1)}, f32[48,128]{1,0:T(8,128)S(1)}, f32[48,128]{1,0:T(8,128)S(1)}) custom-call(s32[2]{0:T(128)S(1)} %pad_add_fusion.side, s32[256]{0:T(256)S(1)} %get-tuple-element.35.slot, s32[32]{0:T(128)S(1)} %copy-done.6, f32[512,4,128]{2,1,0:T(4,128)S(1)} %bitcast.12, ...), custom_call_target="tpu_custom_call" | custom-call | flops 4000000000 | bytes 12000000 | tf_op jit(solution)/shard_map/pallas_call | solution.py:485
  67.7 0.5 collective-permute-start.5
  68.1 0.7 collective-permute-start.6
  68.9 9.3 %shard_map.120.inner = f32[2048,128]{1,0:T(8,128)S(1)} custom-call(s32[1152]{0:T(1024)S(1)} %shard_map.115.ordered, f32[3,256,128]{2,1,0:T(8,128)S(1)} %get-tuple-element.38.pos), custom_call_target="tpu_custom_call" | custom-call | flops 10000000000 | bytes 30000000 | tf_op jit(solution)/shard_map/pallas_call | solution.py:495
  78.2 0.0 collective-permute-done.5.listed_a
  78.3 0.0 collective-permute-done.6.listed_b
  78.3 5.8 %shard_map.121 = (f32[3,256,128]{2,1,0:T(8,128)}, f32[3,256,128]{2,1,0:T(8,128)}) custom-call(s32[2]{0:T(128)S(1)} %pad_add_fusion.side, s32[1152]{0:T(1024)S(1)} %shard_map.115.ordered, f32[3,256,128]{2,1,0:T(8,128)S(1)} %get-tuple-element.38.pos, f32[3,256,128]{2,1,0:T(8,128)S(1)} %get-tuple-element.39.vel, f32[48,128]{1,0:T(8,128)S(1)} %collective-permute-done.5.listed_a, ...), custom_call_target="tpu_custom_call" | custom-call | flops 5000000000 | bytes 15000000 | tf_op jit(solution)/shard_map/pallas_call | solution.py:503
Async XLA Ops:
  5.7 11.3 %copy-start = (f32[3,8,16,256]{3,2,1,0:T(8,128)S(1)}, f32[3,8,16,256]{3,2,1,0:T(8,128)}, u32[]{:S(2)}) copy-start(f32[3,8,16,256]{3,2,1,0:T(8,128)} %fv.5) | copy-start | bytes 1179652
  5.7 11.3 %copy-start.2 = (f32[256,3,128]{2,0,1:T(8,128)S(1)}, f32[256,3,128]{2,0,1:T(8,128)}, u32[]{:S(2)}) copy-start(f32[256,3,128]{2,0,1:T(8,128)} %param.10) | copy-start | bytes 1179652
  5.7 30.6 %all-to-all-start = ((f32[128,16,128]{2,1,0:T(8,128)}), f32[128,16,128]{2,1,0:T(8,128)S(1)}, u32[]{:S(2)}, u32[]{:S(2)}) async-start(f32[128,16,128]{2,1,0:T(8,128)} %bitcast.18), calls=%async_computation | async-start | bytes 2097152 | tf_op jit(solution)/shard_map/all_to_all | solution.py:429
  16.9 0.7 copy-start.7
  17.0 0.7 copy-start.6
  18.3 14.4 %collective-permute-start.2 = (f32[3,8,256]{2,1,0:T(8,128)S(1)}, f32[3,8,256]{2,1,0:T(8,128)S(1)}, u32[]{:S(2)}, u32[]{:S(2)}) collective-permute-start(f32[3,8,256]{2,1,0:T(8,128)S(1)} %get-tuple-element.30), channel_id=1, source_target_pairs={{0,1},{1,0},{2,3},{3,2},{4,5},{5,4},{6,7},{7,6},{8,9},{9,8},{10,11... | collective-permute-start | bytes 73736 | tf_op jit(solution)/shard_map/ppermute | solution.py:455
  18.3 14.3 %collective-permute-start.3 = (f32[3,8,256]{2,1,0:T(8,128)S(1)}, f32[3,8,256]{2,1,0:T(8,128)S(1)}, u32[]{:S(2)}, u32[]{:S(2)}) collective-permute-start(f32[3,8,256]{2,1,0:T(8,128)S(1)} %get-tuple-element.31), channel_id=1, source_target_pairs={{1,2},{2,1},{3,4},{4,3},{5,6},{6,5},{9,10},{10,9},{11,12},{12,11},... | collective-permute-start | bytes 73736 | tf_op jit(solution)/shard_map/ppermute | solution.py:456
  19.0 13.7 %collective-permute-start = (f32[144,128]{1,0:T(8,128)S(1)}, f32[144,128]{1,0:T(8,128)S(1)}, u32[]{:S(2)}, u32[]{:S(2)}) collective-permute-start(f32[144,128]{1,0:T(8,128)S(1)} %get-tuple-element.29), channel_id=1, source_target_pairs={{0,8},{8,0},{16,24},{24,16},{32,40},{40,32},{48,56},{56,48},{64,72... | collective-permute-start | bytes 221192 | tf_op jit(solution)/shard_map/ppermute | solution.py:452
  20.3 8.2 %copy-start.4 = (s32[2,512]{1,0:T(2,128)S(1)}, s32[2,512]{1,0:T(2,128)}, u32[]{:S(2)}) copy-start(s32[2,512]{1,0:T(2,128)} %first.3) | copy-start | bytes 12292
  20.3 8.2 %copy-start.5 = (s32[2,512]{1,0:T(2,128)S(1)}, s32[2,512]{1,0:T(2,128)}, u32[]{:S(2)}) copy-start(s32[2,512]{1,0:T(2,128)} %second.3) | copy-start | bytes 12292
  20.3 12.4 %collective-permute-start.1 = (f32[144,128]{1,0:T(8,128)S(1)}, f32[144,128]{1,0:T(8,128)S(1)}, u32[]{:S(2)}, u32[]{:S(2)}) collective-permute-start(f32[144,128]{1,0:T(8,128)S(1)} %get-tuple-element.26.sent), channel_id=1, source_target_pairs={{8,16},{16,8},{24,32},{32,24},{40,48},{48,40},{56,64},{64,56},{72,... | collective-permute-start | bytes 221192 | tf_op jit(solution)/shard_map/ppermute | solution.py:453
  21.9 23.4 %collective-permute-start.4 = (f32[48,128]{1,0:T(8,128)S(1)}, f32[48,128]{1,0:T(8,128)S(1)}, u32[]{:S(2)}, u32[]{:S(2)}) collective-permute-start(f32[48,128]{1,0:T(8,128)S(1)} %get-tuple-element.28.after), channel_id=1, source_target_pairs={{0,120},{120,0},{1,121},{121,1},{2,122},{122,2},{3,123},{123,3},{4... | collective-permute-start | bytes 73736 | tf_op jit(solution)/shard_map/ppermute | solution.py:454
  38.4 25.9 %all-to-all-start.1 = ((f32[128,16,128]{2,1,0:T(8,128)}), f32[128,16,128]{2,1,0:T(8,128)S(1)}, u32[]{:S(2)}, u32[]{:S(2)}) async-start(f32[128,16,128]{2,1,0:T(8,128)} %bitcast.7), calls=%async_computation.1 | async-start | bytes 2097152 | tf_op jit(solution)/shard_map/all_to_all | solution.py:474
  45.3 0.7 copy-start.8
  46.0 18.3 %copy-start.1 = (f32[256,3,128]{2,0,1:T(8,128)S(1)}, f32[256,3,128]{2,0,1:T(8,128)}, u32[]{:S(2)}) copy-start(f32[256,3,128]{2,0,1:T(8,128)} %param.11) | copy-start | bytes 1179652
  46.0 18.3 %copy-start.3 = (s32[256,128]{1,0:T(8,128)S(1)}, s32[256,128]{1,0:T(8,128)}, u32[]{:S(2)}) copy-start(s32[256,128]{1,0:T(8,128)} %cell.1) | copy-start | bytes 393220
  67.7 10.6 %collective-permute-start.5 = (f32[48,128]{1,0:T(8,128)S(1)}, f32[48,128]{1,0:T(8,128)S(1)}, u32[]{:S(2)}, u32[]{:S(2)}) collective-permute-start(f32[48,128]{1,0:T(8,128)S(1)} %get-tuple-element.40), channel_id=1, source_target_pairs={{0,8},{8,0},{16,24},{24,16},{32,40},{40,32},{48,56},{56,48},{64,72... | collective-permute-start | bytes 73736 | tf_op jit(solution)/shard_map/ppermute | solution.py:493
  68.1 10.1 %collective-permute-start.6 = (f32[48,128]{1,0:T(8,128)S(1)}, f32[48,128]{1,0:T(8,128)S(1)}, u32[]{:S(2)}, u32[]{:S(2)}) collective-permute-start(f32[48,128]{1,0:T(8,128)S(1)} %get-tuple-element.41), channel_id=1, source_target_pairs={{0,120},{8,16},{16,8},{24,32},{32,24},{40,48},{48,40},{56,64},{64,... | collective-permute-start | bytes 73736 | tf_op jit(solution)/shard_map/ppermute | solution.py:494

commit v9 on v8

--- a/solution.py
+++ b/solution.py
@@ -144,41 +144,60 @@
     return swap_groups(jnp.stack(tiles, axis=0)).reshape(len(tiles) * 8, 128)
 
 
-def old_kernel(fv, sent, bricks, around):
+def old_kernel(fv, sent, bricks, around, inner, grid):
     around[...] = sent[96:144, :]
-    for m in range(3):
-        bricks[m] = to_bricks(fv, m)
-
-
-def spread_kernel(side, ordered, fv, first_x, second_x, first_y, second_y, bricks, grid):
     sx, sy, sz = fv.shape[1:]
-    odd = side[0].astype(F32)
-    odd_y = jnp.full((sx, sz), side[1], jnp.int32) == 1
     yrow = lax.broadcasted_iota(jnp.int32, (sy, sz), 0)
     zlane = lax.broadcasted_iota(jnp.int32, (sy, sz), 1)
-    for m in range(3):
-        first, second = [
-            jnp.concatenate([ref[(m * 2 + h) * 16 : (m * 2 + h + 1) * 16, :] for h in range(2)], axis=1)
-            for ref in (first_x, second_x)
-        ]
-        from_low = odd * first + (1.0 - odd) * second
-        from_high = (1.0 - odd) * first + odd * second
-        lefts = jnp.where(odd_y, first_y[m], second_y[m])
-        rights = jnp.where(odd_y, second_y[m], first_y[m])
+    zero = jnp.zeros((sy, sz), F32)
+    for m in range(3):
+        bricks[m] = to_bricks(fv, m)
         for x in range(sx):
             f = fv[m, x]
-            high = fv[m, x + 1] if x < sx - 1 else from_high
-            low = fv[m, x - 1] if x > 0 else from_low
-            beside = high + low
-            right = jnp.broadcast_to(rights[x : x + 1, :], (sy, sz))
-            left = jnp.broadcast_to(lefts[x : x + 1, :], (sy, sz))
-            beside = beside + jnp.where(yrow == sy - 1, right, pltpu.roll(f, sy - 1, 0))
-            beside = beside + jnp.where(yrow == 0, left, pltpu.roll(f, 1, 0))
+            beside = (fv[m, x + 1] if x < sx - 1 else zero) + (fv[m, x - 1] if x > 0 else zero)
+            beside = beside + jnp.where(yrow == sy - 1, 0.0, pltpu.roll(f, sy - 1, 0))
+            beside = beside + jnp.where(yrow == 0, 0.0, pltpu.roll(f, 1, 0))
             beside = beside + jnp.where(zlane == sz - 1, 0.0, pltpu.roll(f, sz - 1, 1))
             beside = beside + jnp.where(zlane == 0, 0.0, pltpu.roll(f, 1, 1))
             grid[m, x] = f + 0.1 * (beside - 6.0 * f)
     for m in range(3):
-        bricks[m] = to_bricks(grid, m)
+        inner[m] = to_bricks(grid, m)
+
+
+def spread_kernel(side, inner, first_x, second_x, first_y, second_y, bricks):
+    sx, sz = first_y.shape[1:]
+    sy = 16
+    odd = side[0].astype(F32)
+    odd_y = jnp.full((sx, sz), side[1], jnp.int32) == 1
+    row4 = lax.broadcasted_iota(jnp.int32, (4, 128), 0)
+    zero = jnp.zeros((4, 128), F32)
+    for m in range(3):
+        lefts = 0.1 * jnp.where(odd_y, first_y[m], second_y[m])
+        rights = 0.1 * jnp.where(odd_y, second_y[m], first_y[m])
+        tiles, rows = [], []
+        for i, (x0, y, z) in enumerate(places(sx, sy)):
+            if 0 < x0 < sx - 2 and 0 < y.start < sy - 4:
+                bricks[m, i * 8 : i * 8 + 8] = inner[m, i * 8 : i * 8 + 8]
+                continue
+            halves = []
+            for x in (x0, x0 + 1):
+                part = zero
+                if x in (0, sx - 1):
+                    at = (m * 2 + z.start // 128) * 16
+                    first = first_x[at + y.start : at + y.stop, :]
+                    second = second_x[at + y.start : at + y.stop, :]
+                    keep = odd if x == 0 else 1.0 - odd
+                    part = 0.1 * (keep * first + (1.0 - keep) * second)
+                if y.start == 0:
+                    part = part + jnp.where(row4 == 0, jnp.broadcast_to(lefts[x : x + 1, z], (4, 128)), 0.0)
+                if y.stop == sy:
+                    part = part + jnp.where(row4 == 3, jnp.broadcast_to(rights[x : x + 1, z], (4, 128)), 0.0)
+                halves.append(part)
+            tiles.append(jnp.concatenate(halves, axis=0))
+            rows.append(i * 8)
+        moved = swap_groups(jnp.stack(tiles, axis=0))
+        for k, at in enumerate(rows):
+            bricks[m, at : at + 8] = inner[m, at : at + 8] + moved[k]
 
 
 def fluid_kernel(recv, old, spread, answer, fluid, done):
@@ -240,20 +259,14 @@
     return a, b, n - a - b
 
 
-def order_kernel(first, second, after, ordered):
+def order_pair(first, second, ordered, p, own):
     n = first.shape[1]
-    blocks = n // 2
-
-    def place(p, own):
-        b = second[1, p]
-        inside = (b < blocks).astype(jnp.int32)
-        at = jnp.where(inside == 1, own, n - 1 - p + own)
-        ordered[at] = first[1, p]
-        ordered[n + at] = b
-        return own + inside
-
-    own = lax.fori_loop(0, n, place, jnp.int32(0), unroll=8)
-    ordered[2 * n] = own // ORDERED_GROUP
+    b = second[1, p]
+    inside = (b < n // 2).astype(jnp.int32)
+    at = jnp.where(inside == 1, own, n - 1 - p + own)
+    ordered[at] = first[1, p]
+    ordered[n + at] = b
+    return own + inside
 
 
 def features(side, pos, listed, feat_b, feat_a):
@@ -284,7 +297,7 @@
             put(feat_b, pl.multiple_of(blocks + upper * 16 + g * 8, 8), hi + [one, n[0], n[1], n[2], one] + lo + [one, zero, zero, zero, zero])
 
 
-def push_pairs(pair, begin, end, group, push, feat_b, feat_a):
+def push_pairs(pair, begin, end, group, push, feat_b, feat_a, beside=lambda p, c: c):
     top = lax.broadcasted_iota(jnp.int32, (8, 128), 0) < 3
 
     def one_pair(p):
@@ -302,16 +315,19 @@
         return a, (-0.5) * (x + z) * total - (res[0:8] + res[8:16])
 
     def pairs(g, c):
-        done = [one_pair(g * group + k) for k in range(group)]
+        done = []
+        for k in range(group):
+            done.append(one_pair(g * group + k))
+            c = beside(g * group + k, c)
         for a, f in done:
             rows = pl.ds(pl.multiple_of(a * 8, 8), 8)
             push[rows, :] = push[rows, :] + f
         return c
 
-    lax.fori_loop(begin, end, pairs, 0)
-
-
-def push_kernel(side, first, second, slot, pos, listed_a, listed_b, around, after, push, slot_out, feat_b, feat_a):
+    return lax.fori_loop(begin, end, pairs, jnp.int32(0))
+
+
+def push_kernel(side, first, second, slot, pos, listed_a, listed_b, around, after, push, slot_out, ordered, feat_b, feat_a):
     def hand_on(q, c):
         slot_out[q] = slot[q]
         return c
@@ -321,7 +337,9 @@
     features(side, pos, listed, feat_b, feat_a)
     push[...] = jnp.zeros(push.shape, F32)
     groups = first.shape[1] // PAIR_GROUP
-    push_pairs(lambda p: (first[0, p], second[0, p]), 0, groups, PAIR_GROUP, push, feat_b, feat_a)
+    order = functools.partial(order_pair, first, second, ordered)
+    own = push_pairs(lambda p: (first[0, p], second[0, p]), 0, groups, PAIR_GROUP, push, feat_b, feat_a, order)
+    ordered[2 * first.shape[1]] = own // ORDERED_GROUP
 
 
 def advance(pos, vel, push, flow, pos_out, vel_out):
@@ -437,17 +455,14 @@
         [VMEM] * 4,
     )(side, halo_list, fluid_vel, pos, placed)
     bricks = sx // 2 * (sy // 4) * (sz // 16)
-    old, around = call(
-        old_kernel, [VMEM, VMEM], [shape(3, bricks, 128), shape(48, 128)], [VMEM, VMEM]
+    old, around, inner = call(
+        old_kernel,
+        [VMEM, VMEM],
+        [shape(3, bricks, 128), shape(48, 128), shape(3, bricks, 128)],
+        [VMEM] * 3,
+        [pltpu.VMEM((3, sx, sy, sz), F32)],
+        2,
     )(fluid_vel, second_x)
-    ordered = call(
-        order_kernel,
-        [SMEM, SMEM, VMEM],
-        shape(2 * pair_self.shape[1] + 128, dtype=jnp.int32),
-        SMEM,
-        (),
-        2,
-    )(pair_self, pair_other, around)
     perms_x, perms_y = swaps(nx, True), swaps(ny, False)
     first_x = lax.ppermute(first_x, "gx", perms_x[0])
     second_x = lax.ppermute(second_x, "gx", perms_x[1][1:-1])
@@ -457,12 +472,10 @@
 
     spread = call(
         spread_kernel,
-        [SMEM] * 2 + [VMEM] * 5,
+        [SMEM] + [VMEM] * 5,
         shape(3, bricks, 128),
         VMEM,
-        [pltpu.VMEM((3, sx, sy, sz), F32)],
-        2,
-    )(side, ordered, fluid_vel, first_x, second_x, first_y, second_y)
+    )(side, inner, first_x, second_x, first_y, second_y)
     answer, fluid, stepped = call(
         fluid_kernel,
         [VMEM] * 3,
@@ -473,11 +486,15 @@
     )(recv, old, spread)
     back = lax.all_to_all(answer, ("gx", "gy"), split_axis=0, concat_axis=0, tiled=True).reshape(slots, 4, 128)
     pair_scratch = [pltpu.VMEM(((blocks + 32) * 16, 128), F32), pltpu.VMEM((blocks * 16, 128), F32)]
-    push, slot = call(
+    push, slot, ordered = call(
         push_kernel,
         [SMEM] * 4 + [VMEM] * 5,
-        [shape(blocks * 8, 128), shape(blocks, dtype=jnp.int32)],
-        [VMEM, SMEM],
+        [
+            shape(blocks * 8, 128),
+            shape(blocks, dtype=jnp.int32),
+            shape(2 * pair_self.shape[1] + 128, dtype=jnp.int32),
+        ],
+        [VMEM, SMEM, SMEM],
         pair_scratch,
         14,
     )(side, pair_self, pair_other, slot, pos, first_x, second_x, around, stepped)

time: 85.1 us -> 84.8 us (level)
  waiting for transfers between devices: 7.92 us -> 11.6 us
  Pallas kernels: 45.2 us -> 41.8 us
    pallas_call x3 -> x2, Pallas kernels: 6.58 us -> 2.99 us  [the longest x1 1.73 us: per_device(): call(old_kernel, [VMEM, VMEM], [shape(3, bricks, 128), shape(48, 128), sh...]
    ppermute x1, waiting for transfers between devices: 0.01 us -> 2.39 us  [per_device(): first_x = lax.ppermute(first_x, 'gx', perms_x[0])]
    all_to_all x1, waiting for transfers between devices: 1.96 us -> 3.34 us  [per_device(): lax.all_to_all(send.reshape(slots * 4, 128), ('gx', 'gy'), split_axis=0,...]
  transfers between devices with their start and end apart: 9 -> 9, of which waited for: 2 -> 3; matrix products, arithmetic and copies ran while one was open for 0% -> 0% of each run, Pallas kernels for 37% -> 33%
where the time goes in v9:
time: 84.8 us; the launch traced here: 83.7 us
  Pallas kernels  41.8 us (49%)
  starting transfers between devices  28.1 us (33%)
  waiting for transfers between devices  11.6 us (14%)
  local copies, waits for them, and re-layouts  1.34 us (2%)
    pallas_call x1, Pallas kernels, per_device(): call(push_kernel, [SMEM] * 4 + [VMEM] * 5, [shape(blocks * 8, 128), shape...  12.5 us
    all_to_all x1, starting transfers between devices, per_device(): lax.all_to_all(send.reshape(slots * 4, 128), ('gx', 'gy'), split_axis=0,...  11.1 us
    pallas_call x1, Pallas kernels, per_device(): call(inner_kernel, [SMEM, VMEM], shape(blocks * 8, 128), VMEM, pair_scrat...  9.35 us
    ppermute x1, starting transfers between devices, per_device(): around = lax.ppermute(around, 'gx', [(0, nx - 1), (nx - 1, 0)])  6.56 us
    all_to_all x1, starting transfers between devices, per_device(): lax.all_to_all(answer, ('gx', 'gy'), split_axis=0, concat_axis=0, tiled=T...  6.52 us
    all_to_all x1, waiting for transfers between devices, per_device(): lax.all_to_all(answer, ('gx', 'gy'), split_axis=0, concat_axis=0, tiled=T...  5.81 us
    pallas_call x1, Pallas kernels, per_device(): call(last_kernel, [SMEM] * 2 + [VMEM] * 6, [shape(3, blocks, 128), shape(...  5.81 us
    pallas_call x1, Pallas kernels, per_device(): call(deposit_kernel, [HBM] * 4, [shape(slots, 4, 128), shape(blocks, dtyp...  5.05 us
  transfers between devices with their start and end apart: 9, of which 3 were waited for; matrix products, arithmetic and copies ran while one was open for 0% of the time, Pallas kernels for 33%

profile of v9, /device:TPU:0, one launch (start us, length us, event | category | flops | bytes accessed | tf_op | source)
XLA Modules:
  0.0 83.7 jit_solution(8195553526498952924)
XLA Ops:
  0.6 5.1 %shard_map.112 = (f32[512,4,128]{2,1,0:T(4,128)}, s32[256]{0:T(256)}, f32[8,128]{1,0:T(8,128)}) custom-call(s32[256]{0:T(256)} %bitcast.19, s32[256]{0:T(256)} %local_in.1, s32[256,128]{1,0:T(8,128)} %cell.1, f32[3,256,128]{2,1,0:T(8,128)} %bitcast.13), custom_call_target="tpu_custom_call" | custom-call | flops 7000000000 | bytes 21000000 | tf_op jit(solution)/shard_map/pallas_call | solution.py:431
  5.7 0.0 copy-start
  5.7 0.0 copy-start.2
  5.7 11.1 %all-to-all-start = ((f32[128,16,128]{2,1,0:T(8,128)}), f32[128,16,128]{2,1,0:T(8,128)S(1)}, u32[]{:S(2)}, u32[]{:S(2)}) async-start(f32[128,16,128]{2,1,0:T(8,128)} %bitcast.18), calls=%async_computation | async-start | bytes 2097152 | tf_op jit(solution)/shard_map/all_to_all | solution.py:447
  16.9 0.0 copy-start.7
  16.9 0.1 pad_add_fusion.side
  17.0 0.0 copy-start.6
  17.0 0.0 copy-done
  17.0 0.0 copy-done.2
  17.0 0.6 copy-done.7
  17.6 0.1 copy-done.6
  17.6 0.6 shard_map.113
  18.3 0.1 collective-permute-start.2
  18.3 0.7 collective-permute-start.3
  19.0 1.3 %collective-permute-start = (f32[144,128]{1,0:T(8,128)S(1)}, f32[144,128]{1,0:T(8,128)S(1)}, u32[]{:S(2)}, u32[]{:S(2)}) collective-permute-start(f32[144,128]{1,0:T(8,128)S(1)} %get-tuple-element.31), channel_id=1, source_target_pairs={{0,8},{8,0},{16,24},{24,16},{32,40},{40,32},{48,56},{56,48},{64,72... | collective-permute-start | bytes 221192 | tf_op jit(solution)/shard_map/ppermute | solution.py:467
  20.3 0.7 collective-permute-start.1
  21.0 1.7 %shard_map.114 = (f32[3,256,128]{2,1,0:T(8,128)S(1)}, f32[48,128]{1,0:T(8,128)S(1)}, f32[3,256,128]{2,1,0:T(8,128)S(1)}) custom-call(f32[3,8,16,256]{3,2,1,0:T(8,128)S(1)} %copy-done, f32[144,128]{1,0:T(8,128)S(1)} %get-tuple-element.28.sent), custom_call_target="tpu_custom_call" | custom-call | flops 2000000000 | bytes 6000000 | tf_op jit(solution)/shard_map/pallas_call | solution.py:458
  22.7 6.6 %collective-permute-start.4 = (f32[48,128]{1,0:T(8,128)S(1)}, f32[48,128]{1,0:T(8,128)S(1)}, u32[]{:S(2)}, u32[]{:S(2)}) collective-permute-start(f32[48,128]{1,0:T(8,128)S(1)} %get-tuple-element.36), channel_id=1, source_target_pairs={{0,120},{120,0},{1,121},{121,1},{2,122},{122,2},{3,123},{123,3},{4... | collective-permute-start | bytes 73736 | tf_op jit(solution)/shard_map/ppermute | solution.py:469
  29.3 0.0 collective-permute-done.2.first_y
  29.3 0.0 collective-permute-done.3.second_y
  29.3 2.4 %collective-permute-done.first_x.listed_a = f32[144,128]{1,0:T(8,128)S(1)} collective-permute-done((f32[144,128]{1,0:T(8,128)S(1)}, f32[144,128]{1,0:T(8,128)S(1)}, u32[]{:S(2)}, u32[]{:S(2)}) %collective-permute-start) | collective-permute-done | bytes 73760 | tf_op jit(solution)/shard_map/ppermute | solution.py:467
  31.7 0.0 collective-permute-done.1.second_x.listed_b
  31.7 1.3 %shard_map.115.spread = f32[3,256,128]{2,1,0:T(8,128)S(1)} custom-call(s32[2]{0:T(128)S(1)} %pad_add_fusion.side, f32[3,256,128]{2,1,0:T(8,128)S(1)} %get-tuple-element.30.inner, f32[144,128]{1,0:T(8,128)S(1)} %collective-permute-done.first_x.listed_a, f32[144,128]{1,0:T(8,128)S(1)} %collective-permute-done.1.second_x.listed_b, ...), custom_call_target="tpu_custom_call" | custom-call | flops 1000000000 | bytes 3000000 | tf_op jit(solution)/shard_map/pallas_call | solution.py:473
  32.9 3.3 %all-to-all-done = f32[128,16,128]{2,1,0:T(8,128)S(1)} async-done(((f32[128,16,128]{2,1,0:T(8,128)}), f32[128,16,128]{2,1,0:T(8,128)S(1)}, u32[]{:S(2)}, u32[]{:S(2)}) %all-to-all-start) | async-done | bytes 1048608 | tf_op jit(solution)/shard_map/all_to_all | solution.py:447
  36.3 2.1 %shard_map.116 = (f32[2048,128]{1,0:T(8,128)}, f32[3,8,16,256]{3,2,1,0:T(8,128)}, f32[8,128]{1,0:T(8,128)S(1)}) custom-call(f32[2048,128]{1,0:T(8,128)S(1)} %bitcast.11, f32[3,256,128]{2,1,0:T(8,128)S(1)} %get-tuple-element.29.old, f32[3,256,128]{2,1,0:T(8,128)S(1)} %shard_map.115.spread), custom_call_target="tpu_custom_call" | custom-call | flops 3000000000 | bytes 9000000 | tf_op jit(solution)/shard_map/pallas_call | solution.py:479
  38.4 0.0 copy-start.4
  38.4 0.0 copy-start.5
  38.4 6.5 %all-to-all-start.1 = ((f32[128,16,128]{2,1,0:T(8,128)}), f32[128,16,128]{2,1,0:T(8,128)S(1)}, u32[]{:S(2)}, u32[]{:S(2)}) async-start(f32[128,16,128]{2,1,0:T(8,128)} %bitcast.7), calls=%async_computation.1 | async-start | bytes 2097152 | tf_op jit(solution)/shard_map/all_to_all | solution.py:487
  44.9 0.0 collective-permute-done.4.around
  44.9 0.0 copy-start.8
  44.9 0.0 copy-done.4
  45.0 0.0 copy-done.5
  45.0 0.7 copy-done.8
  45.6 0.0 copy-start.1
  45.6 0.0 copy-start.3
  45.6 12.5 %shard_map.117 = (f32[2048,128]{1,0:T(8,128)S(1)}, s32[256]{0:T(256)S(1)}, s32[1152]{0:T(1024)S(1)}) custom-call(s32[2]{0:T(128)S(1)} %pad_add_fusion.side, s32[2,512]{1,0:T(2,128)S(1)} %copy-done.4, s32[2,512]{1,0:T(2,128)S(1)} %copy-done.5, s32[256]{0:T(256)S(1)} %copy-done.8, f32[3,256,128]{2,1,0:T(8,128)S(1)} %bitcast.16, ...), custom_call_target="tpu_custom_call" | custom-call | flops 14000000000 | bytes 42000000 | tf_op jit(solution)/shard_map/pallas_call | solution.py:489
  58.1 5.8 %all-to-all-done.1 = f32[128,16,128]{2,1,0:T(8,128)S(1)} async-done(((f32[128,16,128]{2,1,0:T(8,128)}), f32[128,16,128]{2,1,0:T(8,128)S(1)}, u32[]{:S(2)}, u32[]{:S(2)}) %all-to-all-start.1) | async-done | bytes 1048608 | tf_op jit(solution)/shard_map/all_to_all | solution.py:487
  63.9 0.0 copy-done.1
  63.9 0.0 copy-done.3
  63.9 3.4 %shard_map.118 = (f32[2048,128]{1,0:T(8,128)S(1)}, f32[3,256,128]{2,1,0:T(8,128)S(1)}, f32[3,256,128]{2,1,0:T(8,128)S(1)}, f32[48,128]{1,0:T(8,128)S(1)}, f32[48,128]{1,0:T(8,128)S(1)}) custom-call(s32[2]{0:T(128)S(1)} %pad_add_fusion.side, s32[256]{0:T(256)S(1)} %get-tuple-element.39.slot, s32[32]{0:T(128)S(1)} %copy-done.6, f32[512,4,128]{2,1,0:T(4,128)S(1)} %bitcast.12, ...), custom_call_target="tpu_custom_call" | custom-call | flops 4000000000 | bytes 12000000 | tf_op jit(solution)/shard_map/pallas_call | solution.py:502
  67.3 0.5 collective-permute-start.5
  67.8 0.7 collective-permute-start.6
  68.5 9.3 %shard_map.119.inner = f32[2048,128]{1,0:T(8,128)S(1)} custom-call(s32[1152]{0:T(1024)S(1)} %get-tuple-element.38.ordered, f32[3,256,128]{2,1,0:T(8,128)S(1)} %get-tuple-element.42.pos), custom_call_target="tpu_custom_call" | custom-call | flops 10000000000 | bytes 30000000 | tf_op jit(solution)/shard_map/pallas_call | solution.py:512
  77.9 0.0 collective-permute-done.5.listed_a
  77.9 0.0 collective-permute-done.6.listed_b
  77.9 5.8 %shard_map.120 = (f32[3,256,128]{2,1,0:T(8,128)}, f32[3,256,128]{2,1,0:T(8,128)}) custom-call(s32[2]{0:T(128)S(1)} %pad_add_fusion.side, s32[1152]{0:T(1024)S(1)} %get-tuple-element.38.ordered, f32[3,256,128]{2,1,0:T(8,128)S(1)} %get-tuple-element.42.pos, f32[3,256,128]{2,1,0:T(8,128)S(1)} %get-tuple-element.43.vel, ...), custom_call_target="tpu_custom_call" | custom-call | flops 5000000000 | bytes 15000000 | tf_op jit(solution)/shard_map/pallas_call | solution.py:520
Async XLA Ops:
  5.7 11.3 %copy-start = (f32[3,8,16,256]{3,2,1,0:T(8,128)S(1)}, f32[3,8,16,256]{3,2,1,0:T(8,128)}, u32[]{:S(2)}) copy-start(f32[3,8,16,256]{3,2,1,0:T(8,128)} %fv.3) | copy-start | bytes 1179652
  5.7 11.3 %copy-start.2 = (f32[256,3,128]{2,0,1:T(8,128)S(1)}, f32[256,3,128]{2,0,1:T(8,128)}, u32[]{:S(2)}) copy-start(f32[256,3,128]{2,0,1:T(8,128)} %param.10) | copy-start | bytes 1179652
  5.7 30.6 %all-to-all-start = ((f32[128,16,128]{2,1,0:T(8,128)}), f32[128,16,128]{2,1,0:T(8,128)S(1)}, u32[]{:S(2)}, u32[]{:S(2)}) async-start(f32[128,16,128]{2,1,0:T(8,128)} %bitcast.18), calls=%async_computation | async-start | bytes 2097152 | tf_op jit(solution)/shard_map/all_to_all | solution.py:447
  16.9 0.7 copy-start.7
  17.0 0.7 copy-start.6
  18.3 11.0 %collective-permute-start.2 = (f32[3,8,256]{2,1,0:T(8,128)S(1)}, f32[3,8,256]{2,1,0:T(8,128)S(1)}, u32[]{:S(2)}, u32[]{:S(2)}) collective-permute-start(f32[3,8,256]{2,1,0:T(8,128)S(1)} %get-tuple-element.32), channel_id=1, source_target_pairs={{0,1},{1,0},{2,3},{3,2},{4,5},{5,4},{6,7},{7,6},{8,9},{9,8},{10,11... | collective-permute-start | bytes 73736 | tf_op jit(solution)/shard_map/ppermute | solution.py:470
  18.3 10.9 %collective-permute-start.3 = (f32[3,8,256]{2,1,0:T(8,128)S(1)}, f32[3,8,256]{2,1,0:T(8,128)S(1)}, u32[]{:S(2)}, u32[]{:S(2)}) collective-permute-start(f32[3,8,256]{2,1,0:T(8,128)S(1)} %get-tuple-element.33), channel_id=1, source_target_pairs={{1,2},{2,1},{3,4},{4,3},{5,6},{6,5},{9,10},{10,9},{11,12},{12,11},... | collective-permute-start | bytes 73736 | tf_op jit(solution)/shard_map/ppermute | solution.py:471
  19.0 12.7 %collective-permute-start = (f32[144,128]{1,0:T(8,128)S(1)}, f32[144,128]{1,0:T(8,128)S(1)}, u32[]{:S(2)}, u32[]{:S(2)}) collective-permute-start(f32[144,128]{1,0:T(8,128)S(1)} %get-tuple-element.31), channel_id=1, source_target_pairs={{0,8},{8,0},{16,24},{24,16},{32,40},{40,32},{48,56},{56,48},{64,72... | collective-permute-start | bytes 221192 | tf_op jit(solution)/shard_map/ppermute | solution.py:467
  20.3 11.4 %collective-permute-start.1 = (f32[144,128]{1,0:T(8,128)S(1)}, f32[144,128]{1,0:T(8,128)S(1)}, u32[]{:S(2)}, u32[]{:S(2)}) collective-permute-start(f32[144,128]{1,0:T(8,128)S(1)} %get-tuple-element.28.sent), channel_id=1, source_target_pairs={{8,16},{16,8},{24,32},{32,24},{40,48},{48,40},{56,64},{64,56},{72,... | collective-permute-start | bytes 221192 | tf_op jit(solution)/shard_map/ppermute | solution.py:468
  22.7 22.2 %collective-permute-start.4 = (f32[48,128]{1,0:T(8,128)S(1)}, f32[48,128]{1,0:T(8,128)S(1)}, u32[]{:S(2)}, u32[]{:S(2)}) collective-permute-start(f32[48,128]{1,0:T(8,128)S(1)} %get-tuple-element.36), channel_id=1, source_target_pairs={{0,120},{120,0},{1,121},{121,1},{2,122},{122,2},{3,123},{123,3},{4... | collective-permute-start | bytes 73736 | tf_op jit(solution)/shard_map/ppermute | solution.py:469
  38.4 6.6 %copy-start.4 = (s32[2,512]{1,0:T(2,128)S(1)}, s32[2,512]{1,0:T(2,128)}, u32[]{:S(2)}) copy-start(s32[2,512]{1,0:T(2,128)} %first.1) | copy-start | bytes 12292
  38.4 6.6 %copy-start.5 = (s32[2,512]{1,0:T(2,128)S(1)}, s32[2,512]{1,0:T(2,128)}, u32[]{:S(2)}) copy-start(s32[2,512]{1,0:T(2,128)} %second.1) | copy-start | bytes 12292
  38.4 25.5 %all-to-all-start.1 = ((f32[128,16,128]{2,1,0:T(8,128)}), f32[128,16,128]{2,1,0:T(8,128)S(1)}, u32[]{:S(2)}, u32[]{:S(2)}) async-start(f32[128,16,128]{2,1,0:T(8,128)} %bitcast.7), calls=%async_computation.1 | async-start | bytes 2097152 | tf_op jit(solution)/shard_map/all_to_all | solution.py:487
  44.9 0.7 copy-start.8
  45.6 18.3 %copy-start.1 = (f32[256,3,128]{2,0,1:T(8,128)S(1)}, f32[256,3,128]{2,0,1:T(8,128)}, u32[]{:S(2)}) copy-start(f32[256,3,128]{2,0,1:T(8,128)} %param.11) | copy-start | bytes 1179652
  45.6 18.3 %copy-start.3 = (s32[256,128]{1,0:T(8,128)S(1)}, s32[256,128]{1,0:T(8,128)}, u32[]{:S(2)}) copy-start(s32[256,128]{1,0:T(8,128)} %cell.1) | copy-start | bytes 393220
  67.3 10.6 %collective-permute-start.5 = (f32[48,128]{1,0:T(8,128)S(1)}, f32[48,128]{1,0:T(8,128)S(1)}, u32[]{:S(2)}, u32[]{:S(2)}) collective-permute-start(f32[48,128]{1,0:T(8,128)S(1)} %get-tuple-element.44), channel_id=1, source_target_pairs={{0,8},{8,0},{16,24},{24,16},{32,40},{40,32},{48,56},{56,48},{64,72... | collective-permute-start | bytes 73736 | tf_op jit(solution)/shard_map/ppermute | solution.py:510
  67.8 10.1 %collective-permute-start.6 = (f32[48,128]{1,0:T(8,128)S(1)}, f32[48,128]{1,0:T(8,128)S(1)}, u32[]{:S(2)}, u32[]{:S(2)}) collective-permute-start(f32[48,128]{1,0:T(8,128)S(1)} %get-tuple-element.45), channel_id=1, source_target_pairs={{0,120},{8,16},{16,8},{24,32},{32,24},{40,48},{48,40},{56,64},{64,... | collective-permute-start | bytes 73736 | tf_op jit(solution)/shard_map/ppermute | solution.py:511

commit v10 on v9

--- a/solution.py
+++ b/solution.py
@@ -10,7 +10,8 @@
 F32 = jnp.float32
 BF16 = jnp.bfloat16
 PAIR_GROUP = 256
-ORDERED_GROUP = 128
+INNER_GROUP = 384
+LAST_GROUP = 128
 BLOCK_GROUP = 128
 DEPOSIT_GROUP = 128
 CAP = 4
@@ -339,15 +340,14 @@
     groups = first.shape[1] // PAIR_GROUP
     order = functools.partial(order_pair, first, second, ordered)
     own = push_pairs(lambda p: (first[0, p], second[0, p]), 0, groups, PAIR_GROUP, push, feat_b, feat_a, order)
-    ordered[2 * first.shape[1]] = own // ORDERED_GROUP
-
-
-def advance(pos, vel, push, flow, pos_out, vel_out):
+    ordered[2 * first.shape[1]] = own // INNER_GROUP
+
+
+def advance(pos, vel, push, air, pos_out, vel_out):
     blocks = pos.shape[1]
-    drift = 2.0 * flow[pl.ds(3, blocks, stride=8), :]
     for m in range(3):
         v = vel[m]
-        force = 2.5 * push[pl.ds(m, blocks, stride=8), :] + drift * (flow[pl.ds(m, blocks, stride=8), :] - v)
+        force = 2.5 * push[pl.ds(m, blocks, stride=8), :] + air[3] * (air[m] - v)
         if m == 2:
             force = force - 1.0
         v = v + 0.1 * force
@@ -362,7 +362,7 @@
     return both[0:8] + both[8:16]
 
 
-def pick_kernel(side, slot, halo, back, cell, pos, vel, push, flow, pos_out, vel_out, first_x, second_x):
+def pick_kernel(side, slot, halo, back, cell, pos, vel, push, air, pos_out, vel_out, first_x, second_x, flow):
     def group(g, c):
         base = pl.multiple_of(g * BLOCK_GROUP, BLOCK_GROUP)
         cells = cell[pl.ds(base, BLOCK_GROUP), :]
@@ -372,7 +372,10 @@
         return c
 
     lax.fori_loop(0, cell.shape[0] // BLOCK_GROUP, group, 0)
-    advance(pos, vel, push, flow, pos_out, vel_out)
+    for m in range(3):
+        air[m] = flow[pl.ds(m, cell.shape[0], stride=8), :]
+    air[3] = 2.0 * flow[pl.ds(3, cell.shape[0], stride=8), :]
+    advance(pos, vel, push, air, pos_out, vel_out)
     put_listed(halo, 1 - side[0], pos_out, first_x, 0)
     put_listed(halo, side[0], pos_out, second_x, 0)
 
@@ -381,16 +384,16 @@
     n = pos.shape[1] * 2
     features(None, pos, (), feat_b, feat_a)
     push[...] = jnp.zeros(push.shape, F32)
-    push_pairs(lambda p: (ordered[p], ordered[n + p]), 0, ordered[2 * n], ORDERED_GROUP, push, feat_b, feat_a)
-
-
-def last_kernel(side, ordered, pos, vel, listed_a, listed_b, flow, inner, pos_out, vel_out, push, feat_b, feat_a):
+    push_pairs(lambda p: (ordered[p], ordered[n + p]), 0, ordered[2 * n], INNER_GROUP, push, feat_b, feat_a)
+
+
+def last_kernel(side, ordered, pos, vel, listed_a, listed_b, air, inner, pos_out, vel_out, push, feat_b, feat_a):
     n = pos.shape[1] * 2
     features(side, pos, (((listed_a, 0),), ((listed_b, 0),)), feat_b, feat_a)
     push[...] = inner[...]
-    groups = n // ORDERED_GROUP
-    push_pairs(lambda p: (ordered[p], ordered[n + p]), ordered[2 * n], groups, ORDERED_GROUP, push, feat_b, feat_a)
-    advance(pos, vel, push, flow, pos_out, vel_out)
+    begin = ordered[2 * n] * (INNER_GROUP // LAST_GROUP)
+    push_pairs(lambda p: (ordered[p], ordered[n + p]), begin, n // LAST_GROUP, LAST_GROUP, push, feat_b, feat_a)
+    advance(pos, vel, push, air, pos_out, vel_out)
 
 
 def call(kernel, in_specs, out_shape, out_specs, scratch=(), micros=1, vmem=20 * 1024 * 1024):
@@ -499,12 +502,12 @@
         14,
     )(side, pair_self, pair_other, slot, pos, first_x, second_x, around, stepped)
 
-    flow, pos, vel, listed_a, listed_b = call(
+    air, pos, vel, listed_a, listed_b = call(
         pick_kernel,
         [SMEM] * 3 + [VMEM] * 5,
-        [shape(blocks * 8, 128), shape(3, blocks, 128), shape(3, blocks, 128), shape(48, 128), shape(48, 128)],
+        [shape(4, blocks, 128), shape(3, blocks, 128), shape(3, blocks, 128), shape(48, 128), shape(48, 128)],
         [VMEM] * 5,
-        (),
+        [pltpu.VMEM((blocks * 8, 128), F32)],
         4,
     )(side, slot, halo_list, back, cell_in_brick, pos, vel, push)
     listed_a = lax.ppermute(listed_a, "gx", perms_x[0])
@@ -524,7 +527,7 @@
         [VMEM] * 2,
         [pltpu.VMEM((blocks * 8, 128), F32)] + pair_scratch,
         5,
-    )(side, ordered, pos, vel, listed_a, listed_b, flow, inner)
+    )(side, ordered, pos, vel, listed_a, listed_b, air, inner)
     return fluid, jnp.transpose(pos, (1, 0, 2)), jnp.transpose(vel, (1, 0, 2))
 
 

time: 84.8 us -> 84.1 us (level)
  no operation moved by 1% of the time
where the time goes in v10:
time: 84.1 us; the launch traced here: 83 us
  Pallas kernels  41.1 us (49%)
  starting transfers between devices  28.1 us (33%)
  waiting for transfers between devices  11.6 us (14%)
  local copies, waits for them, and re-layouts  1.34 us (2%)
    pallas_call x1, Pallas kernels, per_device(): call(push_kernel, [SMEM] * 4 + [VMEM] * 5, [shape(blocks * 8, 128), shape...  12.5 us
    all_to_all x1, starting transfers between devices, per_device(): lax.all_to_all(send.reshape(slots * 4, 128), ('gx', 'gy'), split_axis=0,...  11.1 us
    pallas_call x1, Pallas kernels, per_device(): call(inner_kernel, [SMEM, VMEM], shape(blocks * 8, 128), VMEM, pair_scrat...  8.94 us
    ppermute x1, starting transfers between devices, per_device(): around = lax.ppermute(around, 'gx', [(0, nx - 1), (nx - 1, 0)])  6.56 us
    all_to_all x1, starting transfers between devices, per_device(): lax.all_to_all(answer, ('gx', 'gy'), split_axis=0, concat_axis=0, tiled=T...  6.52 us
    all_to_all x1, waiting for transfers between devices, per_device(): lax.all_to_all(answer, ('gx', 'gy'), split_axis=0, concat_axis=0, tiled=T...  5.81 us
    pallas_call x1, Pallas kernels, per_device(): call(last_kernel, [SMEM] * 2 + [VMEM] * 6, [shape(3, blocks, 128), shape(...  5.5 us
    pallas_call x1, Pallas kernels, per_device(): call(deposit_kernel, [HBM] * 4, [shape(slots, 4, 128), shape(blocks, dtyp...  5.05 us
  transfers between devices with their start and end apart: 9, of which 3 were waited for; matrix products, arithmetic and copies ran while one was open for 0% of the time, Pallas kernels for 33%

profile of v10, /device:TPU:0, one launch (start us, length us, event | category | flops | bytes accessed | tf_op | source)
XLA Modules:
  0.0 83.0 jit_solution(7438018774817357571)
XLA Ops:
  0.6 5.1 %shard_map.112 = (f32[512,4,128]{2,1,0:T(4,128)}, s32[256]{0:T(256)}, f32[8,128]{1,0:T(8,128)}) custom-call(s32[256]{0:T(256)} %bitcast.19, s32[256]{0:T(256)} %local_in.1, s32[256,128]{1,0:T(8,128)} %cell.1, f32[3,256,128]{2,1,0:T(8,128)} %bitcast.13), custom_call_target="tpu_custom_call" | custom-call | flops 7000000000 | bytes 21000000 | tf_op jit(solution)/shard_map/pallas_call | solution.py:434
  5.7 0.0 copy-start
  5.7 0.0 copy-start.2
  5.7 11.1 %all-to-all-start = ((f32[128,16,128]{2,1,0:T(8,128)}), f32[128,16,128]{2,1,0:T(8,128)S(1)}, u32[]{:S(2)}, u32[]{:S(2)}) async-start(f32[128,16,128]{2,1,0:T(8,128)} %bitcast.18), calls=%async_computation | async-start | bytes 2097152 | tf_op jit(solution)/shard_map/all_to_all | solution.py:450
  16.9 0.0 copy-start.7
  16.9 0.1 pad_add_fusion.side
  17.0 0.0 copy-start.6
  17.0 0.0 copy-done
  17.0 0.0 copy-done.2
  17.0 0.6 copy-done.7
  17.6 0.1 copy-done.6
  17.6 0.6 shard_map.113
  18.3 0.1 collective-permute-start.2
  18.3 0.7 collective-permute-start.3
  19.0 1.3 %collective-permute-start = (f32[144,128]{1,0:T(8,128)S(1)}, f32[144,128]{1,0:T(8,128)S(1)}, u32[]{:S(2)}, u32[]{:S(2)}) collective-permute-start(f32[144,128]{1,0:T(8,128)S(1)} %get-tuple-element.31), channel_id=1, source_target_pairs={{0,8},{8,0},{16,24},{24,16},{32,40},{40,32},{48,56},{56,48},{64,72... | collective-permute-start | bytes 221192 | tf_op jit(solution)/shard_map/ppermute | solution.py:470
  20.3 0.7 collective-permute-start.1
  21.0 1.7 %shard_map.114 = (f32[3,256,128]{2,1,0:T(8,128)S(1)}, f32[48,128]{1,0:T(8,128)S(1)}, f32[3,256,128]{2,1,0:T(8,128)S(1)}) custom-call(f32[3,8,16,256]{3,2,1,0:T(8,128)S(1)} %copy-done, f32[144,128]{1,0:T(8,128)S(1)} %get-tuple-element.28.sent), custom_call_target="tpu_custom_call" | custom-call | flops 2000000000 | bytes 6000000 | tf_op jit(solution)/shard_map/pallas_call | solution.py:461
  22.7 6.6 %collective-permute-start.4 = (f32[48,128]{1,0:T(8,128)S(1)}, f32[48,128]{1,0:T(8,128)S(1)}, u32[]{:S(2)}, u32[]{:S(2)}) collective-permute-start(f32[48,128]{1,0:T(8,128)S(1)} %get-tuple-element.36), channel_id=1, source_target_pairs={{0,120},{120,0},{1,121},{121,1},{2,122},{122,2},{3,123},{123,3},{4... | collective-permute-start | bytes 73736 | tf_op jit(solution)/shard_map/ppermute | solution.py:472
  29.3 0.0 collective-permute-done.2.first_y
  29.3 0.0 collective-permute-done.3.second_y
  29.3 2.4 %collective-permute-done.first_x.listed_a = f32[144,128]{1,0:T(8,128)S(1)} collective-permute-done((f32[144,128]{1,0:T(8,128)S(1)}, f32[144,128]{1,0:T(8,128)S(1)}, u32[]{:S(2)}, u32[]{:S(2)}) %collective-permute-start) | collective-permute-done | bytes 73760 | tf_op jit(solution)/shard_map/ppermute | solution.py:470
  31.7 0.0 collective-permute-done.1.second_x.listed_b
  31.7 1.3 %shard_map.115.spread = f32[3,256,128]{2,1,0:T(8,128)S(1)} custom-call(s32[2]{0:T(128)S(1)} %pad_add_fusion.side, f32[3,256,128]{2,1,0:T(8,128)S(1)} %get-tuple-element.30.inner, f32[144,128]{1,0:T(8,128)S(1)} %collective-permute-done.first_x.listed_a, f32[144,128]{1,0:T(8,128)S(1)} %collective-permute-done.1.second_x.listed_b, ...), custom_call_target="tpu_custom_call" | custom-call | flops 1000000000 | bytes 3000000 | tf_op jit(solution)/shard_map/pallas_call | solution.py:476
  32.9 3.3 %all-to-all-done = f32[128,16,128]{2,1,0:T(8,128)S(1)} async-done(((f32[128,16,128]{2,1,0:T(8,128)}), f32[128,16,128]{2,1,0:T(8,128)S(1)}, u32[]{:S(2)}, u32[]{:S(2)}) %all-to-all-start) | async-done | bytes 1048608 | tf_op jit(solution)/shard_map/all_to_all | solution.py:450
  36.3 2.1 %shard_map.116 = (f32[2048,128]{1,0:T(8,128)}, f32[3,8,16,256]{3,2,1,0:T(8,128)}, f32[8,128]{1,0:T(8,128)S(1)}) custom-call(f32[2048,128]{1,0:T(8,128)S(1)} %bitcast.11, f32[3,256,128]{2,1,0:T(8,128)S(1)} %get-tuple-element.29.old, f32[3,256,128]{2,1,0:T(8,128)S(1)} %shard_map.115.spread), custom_call_target="tpu_custom_call" | custom-call | flops 3000000000 | bytes 9000000 | tf_op jit(solution)/shard_map/pallas_call | solution.py:482
  38.4 0.0 copy-start.4
  38.4 0.0 copy-start.5
  38.4 6.5 %all-to-all-start.1 = ((f32[128,16,128]{2,1,0:T(8,128)}), f32[128,16,128]{2,1,0:T(8,128)S(1)}, u32[]{:S(2)}, u32[]{:S(2)}) async-start(f32[128,16,128]{2,1,0:T(8,128)} %bitcast.7), calls=%async_computation.1 | async-start | bytes 2097152 | tf_op jit(solution)/shard_map/all_to_all | solution.py:490
  44.9 0.0 collective-permute-done.4.around
  44.9 0.0 copy-start.8
  44.9 0.0 copy-done.4
  45.0 0.0 copy-done.5
  45.0 0.7 copy-done.8
  45.6 0.0 copy-start.1
  45.6 0.0 copy-start.3
  45.6 12.5 %shard_map.117 = (f32[2048,128]{1,0:T(8,128)S(1)}, s32[256]{0:T(256)S(1)}, s32[1152]{0:T(1024)S(1)}) custom-call(s32[2]{0:T(128)S(1)} %pad_add_fusion.side, s32[2,512]{1,0:T(2,128)S(1)} %copy-done.4, s32[2,512]{1,0:T(2,128)S(1)} %copy-done.5, s32[256]{0:T(256)S(1)} %copy-done.8, f32[3,256,128]{2,1,0:T(8,128)S(1)} %bitcast.16, ...), custom_call_target="tpu_custom_call" | custom-call | flops 14000000000 | bytes 42000000 | tf_op jit(solution)/shard_map/pallas_call | solution.py:492
  58.1 5.8 %all-to-all-done.1 = f32[128,16,128]{2,1,0:T(8,128)S(1)} async-done(((f32[128,16,128]{2,1,0:T(8,128)}), f32[128,16,128]{2,1,0:T(8,128)S(1)}, u32[]{:S(2)}, u32[]{:S(2)}) %all-to-all-start.1) | async-done | bytes 1048608 | tf_op jit(solution)/shard_map/all_to_all | solution.py:490
  63.9 0.0 copy-done.1
  63.9 0.0 copy-done.3
  63.9 3.4 %shard_map.118 = (f32[4,256,128]{2,1,0:T(8,128)S(1)}, f32[3,256,128]{2,1,0:T(8,128)S(1)}, f32[3,256,128]{2,1,0:T(8,128)S(1)}, f32[48,128]{1,0:T(8,128)S(1)}, f32[48,128]{1,0:T(8,128)S(1)}) custom-call(s32[2]{0:T(128)S(1)} %pad_add_fusion.side, s32[256]{0:T(256)S(1)} %get-tuple-element.39.slot, s32[32]{0:T(128)S(1)} %copy-done.6, ...), custom_call_target="tpu_custom_call" | custom-call | flops 4000000000 | bytes 12000000 | tf_op jit(solution)/shard_map/pallas_call | solution.py:505
  67.3 0.5 collective-permute-start.5
  67.8 0.7 collective-permute-start.6
  68.5 8.9 %shard_map.119.inner = f32[2048,128]{1,0:T(8,128)S(1)} custom-call(s32[1152]{0:T(1024)S(1)} %get-tuple-element.38.ordered, f32[3,256,128]{2,1,0:T(8,128)S(1)} %get-tuple-element.42.pos), custom_call_target="tpu_custom_call" | custom-call | flops 10000000000 | bytes 30000000 | tf_op jit(solution)/shard_map/pallas_call | solution.py:515
  77.5 0.0 collective-permute-done.5.listed_a
  77.5 0.0 collective-permute-done.6.listed_b
  77.5 5.5 %shard_map.120 = (f32[3,256,128]{2,1,0:T(8,128)}, f32[3,256,128]{2,1,0:T(8,128)}) custom-call(s32[2]{0:T(128)S(1)} %pad_add_fusion.side, s32[1152]{0:T(1024)S(1)} %get-tuple-element.38.ordered, f32[3,256,128]{2,1,0:T(8,128)S(1)} %get-tuple-element.42.pos, f32[3,256,128]{2,1,0:T(8,128)S(1)} %get-tuple-element.43.vel, ...), custom_call_target="tpu_custom_call" | custom-call | flops 5000000000 | bytes 15000000 | tf_op jit(solution)/shard_map/pallas_call | solution.py:523
Async XLA Ops:
  5.7 11.3 %copy-start = (f32[3,8,16,256]{3,2,1,0:T(8,128)S(1)}, f32[3,8,16,256]{3,2,1,0:T(8,128)}, u32[]{:S(2)}) copy-start(f32[3,8,16,256]{3,2,1,0:T(8,128)} %fv.3) | copy-start | bytes 1179652
  5.7 11.3 %copy-start.2 = (f32[256,3,128]{2,0,1:T(8,128)S(1)}, f32[256,3,128]{2,0,1:T(8,128)}, u32[]{:S(2)}) copy-start(f32[256,3,128]{2,0,1:T(8,128)} %param.10) | copy-start | bytes 1179652
  5.7 30.6 %all-to-all-start = ((f32[128,16,128]{2,1,0:T(8,128)}), f32[128,16,128]{2,1,0:T(8,128)S(1)}, u32[]{:S(2)}, u32[]{:S(2)}) async-start(f32[128,16,128]{2,1,0:T(8,128)} %bitcast.18), calls=%async_computation | async-start | bytes 2097152 | tf_op jit(solution)/shard_map/all_to_all | solution.py:450
  16.9 0.7 copy-start.7
  17.0 0.7 copy-start.6
  18.3 11.0 %collective-permute-start.2 = (f32[3,8,256]{2,1,0:T(8,128)S(1)}, f32[3,8,256]{2,1,0:T(8,128)S(1)}, u32[]{:S(2)}, u32[]{:S(2)}) collective-permute-start(f32[3,8,256]{2,1,0:T(8,128)S(1)} %get-tuple-element.32), channel_id=1, source_target_pairs={{0,1},{1,0},{2,3},{3,2},{4,5},{5,4},{6,7},{7,6},{8,9},{9,8},{10,11... | collective-permute-start | bytes 73736 | tf_op jit(solution)/shard_map/ppermute | solution.py:473
  18.3 10.9 %collective-permute-start.3 = (f32[3,8,256]{2,1,0:T(8,128)S(1)}, f32[3,8,256]{2,1,0:T(8,128)S(1)}, u32[]{:S(2)}, u32[]{:S(2)}) collective-permute-start(f32[3,8,256]{2,1,0:T(8,128)S(1)} %get-tuple-element.33), channel_id=1, source_target_pairs={{1,2},{2,1},{3,4},{4,3},{5,6},{6,5},{9,10},{10,9},{11,12},{12,11},... | collective-permute-start | bytes 73736 | tf_op jit(solution)/shard_map/ppermute | solution.py:474
  19.0 12.7 %collective-permute-start = (f32[144,128]{1,0:T(8,128)S(1)}, f32[144,128]{1,0:T(8,128)S(1)}, u32[]{:S(2)}, u32[]{:S(2)}) collective-permute-start(f32[144,128]{1,0:T(8,128)S(1)} %get-tuple-element.31), channel_id=1, source_target_pairs={{0,8},{8,0},{16,24},{24,16},{32,40},{40,32},{48,56},{56,48},{64,72... | collective-permute-start | bytes 221192 | tf_op jit(solution)/shard_map/ppermute | solution.py:470
  20.3 11.4 %collective-permute-start.1 = (f32[144,128]{1,0:T(8,128)S(1)}, f32[144,128]{1,0:T(8,128)S(1)}, u32[]{:S(2)}, u32[]{:S(2)}) collective-permute-start(f32[144,128]{1,0:T(8,128)S(1)} %get-tuple-element.28.sent), channel_id=1, source_target_pairs={{8,16},{16,8},{24,32},{32,24},{40,48},{48,40},{56,64},{64,56},{72,... | collective-permute-start | bytes 221192 | tf_op jit(solution)/shard_map/ppermute | solution.py:471
  22.7 22.2 %collective-permute-start.4 = (f32[48,128]{1,0:T(8,128)S(1)}, f32[48,128]{1,0:T(8,128)S(1)}, u32[]{:S(2)}, u32[]{:S(2)}) collective-permute-start(f32[48,128]{1,0:T(8,128)S(1)} %get-tuple-element.36), channel_id=1, source_target_pairs={{0,120},{120,0},{1,121},{121,1},{2,122},{122,2},{3,123},{123,3},{4... | collective-permute-start | bytes 73736 | tf_op jit(solution)/shard_map/ppermute | solution.py:472
  38.4 6.6 %copy-start.4 = (s32[2,512]{1,0:T(2,128)S(1)}, s32[2,512]{1,0:T(2,128)}, u32[]{:S(2)}) copy-start(s32[2,512]{1,0:T(2,128)} %first.1) | copy-start | bytes 12292
  38.4 6.6 %copy-start.5 = (s32[2,512]{1,0:T(2,128)S(1)}, s32[2,512]{1,0:T(2,128)}, u32[]{:S(2)}) copy-start(s32[2,512]{1,0:T(2,128)} %second.1) | copy-start | bytes 12292
  38.4 25.5 %all-to-all-start.1 = ((f32[128,16,128]{2,1,0:T(8,128)}), f32[128,16,128]{2,1,0:T(8,128)S(1)}, u32[]{:S(2)}, u32[]{:S(2)}) async-start(f32[128,16,128]{2,1,0:T(8,128)} %bitcast.7), calls=%async_computation.1 | async-start | bytes 2097152 | tf_op jit(solution)/shard_map/all_to_all | solution.py:490
  44.9 0.7 copy-start.8
  45.6 18.3 %copy-start.1 = (f32[256,3,128]{2,0,1:T(8,128)S(1)}, f32[256,3,128]{2,0,1:T(8,128)}, u32[]{:S(2)}) copy-start(f32[256,3,128]{2,0,1:T(8,128)} %param.11) | copy-start | bytes 1179652
  45.6 18.3 %copy-start.3 = (s32[256,128]{1,0:T(8,128)S(1)}, s32[256,128]{1,0:T(8,128)}, u32[]{:S(2)}) copy-start(s32[256,128]{1,0:T(8,128)} %cell.1) | copy-start | bytes 393220
  67.3 10.2 %collective-permute-start.5 = (f32[48,128]{1,0:T(8,128)S(1)}, f32[48,128]{1,0:T(8,128)S(1)}, u32[]{:S(2)}, u32[]{:S(2)}) collective-permute-start(f32[48,128]{1,0:T(8,128)S(1)} %get-tuple-element.44), channel_id=1, source_target_pairs={{0,8},{8,0},{16,24},{24,16},{32,40},{40,32},{48,56},{56,48},{64,72... | collective-permute-start | bytes 73736 | tf_op jit(solution)/shard_map/ppermute | solution.py:513
  67.8 9.7 %collective-permute-start.6 = (f32[48,128]{1,0:T(8,128)S(1)}, f32[48,128]{1,0:T(8,128)S(1)}, u32[]{:S(2)}, u32[]{:S(2)}) collective-permute-start(f32[48,128]{1,0:T(8,128)S(1)} %get-tuple-element.45), channel_id=1, source_target_pairs={{0,120},{8,16},{16,8},{24,32},{32,24},{40,48},{48,40},{56,64},{64,... | collective-permute-start | bytes 73736 | tf_op jit(solution)/shard_map/ppermute | solution.py:514

commit v11 on v10

--- a/solution.py
+++ b/solution.py
@@ -12,7 +12,7 @@
 PAIR_GROUP = 256
 INNER_GROUP = 384
 LAST_GROUP = 128
-BLOCK_GROUP = 128
+BLOCK_GROUP = 256
 DEPOSIT_GROUP = 128
 CAP = 4
 EPS2 = 0.0025
@@ -65,11 +65,18 @@
 
 def deposit_kernel(owner_in, local_in, cell_in, vel_in, out, slot_out, done, taken, owner, local, cell, vel, sems):
     blocks = cell.shape[0]
-    copies = [
-        pltpu.make_async_copy(src, dst, sems.at[i])
-        for i, (src, dst) in enumerate(((vel_in, vel), (cell_in, cell), (owner_in, owner), (local_in, local)))
-    ]
-    for c in copies:
+    groups = blocks // DEPOSIT_GROUP
+    lists = [pltpu.make_async_copy(owner_in, owner, sems.at[0]), pltpu.make_async_copy(local_in, local, sems.at[1])]
+    parts = []
+    for g in range(groups):
+        some = pl.ds(g * DEPOSIT_GROUP, DEPOSIT_GROUP)
+        parts.append(
+            [
+                pltpu.make_async_copy(cell_in.at[some, :], cell.at[some, :], sems.at[2 + 2 * g]),
+                pltpu.make_async_copy(vel_in.at[:, some, :], vel.at[:, some, :], sems.at[3 + 2 * g]),
+            ]
+        )
+    for c in lists + sum(parts, []):
         c.start()
     lanes = lax.broadcasted_iota(jnp.int32, (4, 128), 1)
     rows4 = lax.broadcasted_iota(jnp.int32, (4, 128), 0)
@@ -84,11 +91,12 @@
     lax.fori_loop(0, taken.shape[0], clear, 0, unroll=8)
     r8 = lax.broadcasted_iota(jnp.int32, (8, 128), 0)
     lane16 = lax.broadcasted_iota(jnp.int32, (128, 128), 1) // 16
-    for c in copies:
+    for c in lists:
         c.wait()
-
-    def group(g, c):
-        base = pl.multiple_of(g * DEPOSIT_GROUP, DEPOSIT_GROUP)
+    for g in range(groups):
+        for c in parts[g]:
+            c.wait()
+        base = g * DEPOSIT_GROUP
         cells = cell[pl.ds(base, DEPOSIT_GROUP), :]
         v = [vel[m, pl.ds(base, DEPOSIT_GROUP), :] for m in range(3)]
         for start in range(0, DEPOSIT_GROUP, 8):
@@ -114,9 +122,6 @@
                 slot_out[q] = slot
                 ident = jnp.full((4, 128), local[q], jnp.int32).astype(F32)
                 out[slot] = jnp.where(mark, ident, both[0:4])
-        return c
-
-    lax.fori_loop(0, blocks // DEPOSIT_GROUP, group, 0)
 
 
 def swap_groups(v):
@@ -442,7 +447,7 @@
             pltpu.SMEM((blocks,), jnp.int32),
             pltpu.VMEM((blocks, 128), jnp.int32),
             pltpu.VMEM((3, blocks, 128), F32),
-            pltpu.SemaphoreType.DMA((4,)),
+            pltpu.SemaphoreType.DMA((2 + 2 * blocks // DEPOSIT_GROUP,)),
         ],
         7,
         63_000_000,

time: 84.1 us -> 83.9 us (level)
  no operation moved by 1% of the time
where the time goes in v11:
time: 83.9 us; the launch traced here: 82.8 us
  Pallas kernels  40.8 us (49%)
  starting transfers between devices  28.1 us (33%)
  waiting for transfers between devices  11.6 us (14%)
  local copies, waits for them, and re-layouts  1.34 us (2%)
  between operations  0.84 us (1%)
    pallas_call x1, Pallas kernels, per_device(): call(push_kernel, [SMEM] * 4 + [VMEM] * 5, [shape(blocks * 8, 128), shape...  12.5 us
    all_to_all x1, starting transfers between devices, per_device(): lax.all_to_all(send.reshape(slots * 4, 128), ('gx', 'gy'), split_axis=0,...  11.2 us
    pallas_call x1, Pallas kernels, per_device(): call(inner_kernel, [SMEM, VMEM], shape(blocks * 8, 128), VMEM, pair_scrat...  8.95 us
    ppermute x1, starting transfers between devices, per_device(): around = lax.ppermute(around, 'gx', [(0, nx - 1), (nx - 1, 0)])  6.56 us
    all_to_all x1, starting transfers between devices, per_device(): lax.all_to_all(answer, ('gx', 'gy'), split_axis=0, concat_axis=0, tiled=T...  6.51 us
    all_to_all x1, waiting for transfers between devices, per_device(): lax.all_to_all(answer, ('gx', 'gy'), split_axis=0, concat_axis=0, tiled=T...  5.81 us
    pallas_call x1, Pallas kernels, per_device(): call(last_kernel, [SMEM] * 2 + [VMEM] * 6, [shape(3, blocks, 128), shape(...  5.5 us
    pallas_call x1, Pallas kernels, per_device(): call(deposit_kernel, [HBM] * 4, [shape(slots, 4, 128), shape(blocks, dtyp...  5.19 us
  transfers between devices with their start and end apart: 9, of which 3 were waited for; matrix products, arithmetic and copies ran while one was open for 0% of the time, Pallas kernels for 33%

profile of v11, /device:TPU:0, one launch (start us, length us, event | category | flops | bytes accessed | tf_op | source)
XLA Modules:
  0.0 82.8 jit_solution(11581378775079241204)
XLA Ops:
  0.6 5.2 %shard_map.112 = (f32[512,4,128]{2,1,0:T(4,128)}, s32[256]{0:T(256)}, f32[8,128]{1,0:T(8,128)}) custom-call(s32[256]{0:T(256)} %bitcast.19, s32[256]{0:T(256)} %local_in.1, s32[256,128]{1,0:T(8,128)} %cell.1, f32[3,256,128]{2,1,0:T(8,128)} %bitcast.13), custom_call_target="tpu_custom_call" | custom-call | flops 7000000000 | bytes 21000000 | tf_op jit(solution)/shard_map/pallas_call | solution.py:439
  5.8 0.0 copy-start
  5.8 0.0 copy-start.2
  5.9 11.2 %all-to-all-start = ((f32[128,16,128]{2,1,0:T(8,128)}), f32[128,16,128]{2,1,0:T(8,128)S(1)}, u32[]{:S(2)}, u32[]{:S(2)}) async-start(f32[128,16,128]{2,1,0:T(8,128)} %bitcast.18), calls=%async_computation | async-start | bytes 2097152 | tf_op jit(solution)/shard_map/all_to_all | solution.py:455
  17.0 0.0 copy-start.7
  17.1 0.1 pad_add_fusion.side
  17.1 0.0 copy-start.6
  17.1 0.0 copy-done
  17.1 0.0 copy-done.2
  17.1 0.6 copy-done.7
  17.7 0.1 copy-done.6
  17.8 0.6 shard_map.113
  18.4 0.1 collective-permute-start.2
  18.5 0.7 collective-permute-start.3
  19.2 1.3 %collective-permute-start = (f32[144,128]{1,0:T(8,128)S(1)}, f32[144,128]{1,0:T(8,128)S(1)}, u32[]{:S(2)}, u32[]{:S(2)}) collective-permute-start(f32[144,128]{1,0:T(8,128)S(1)} %get-tuple-element.31), channel_id=1, source_target_pairs={{0,8},{8,0},{16,24},{24,16},{32,40},{40,32},{48,56},{56,48},{64,72... | collective-permute-start | bytes 221192 | tf_op jit(solution)/shard_map/ppermute | solution.py:475
  20.5 0.7 collective-permute-start.1
  21.1 1.7 %shard_map.114 = (f32[3,256,128]{2,1,0:T(8,128)S(1)}, f32[48,128]{1,0:T(8,128)S(1)}, f32[3,256,128]{2,1,0:T(8,128)S(1)}) custom-call(f32[3,8,16,256]{3,2,1,0:T(8,128)S(1)} %copy-done, f32[144,128]{1,0:T(8,128)S(1)} %get-tuple-element.28.sent), custom_call_target="tpu_custom_call" | custom-call | flops 2000000000 | bytes 6000000 | tf_op jit(solution)/shard_map/pallas_call | solution.py:466
  22.9 6.6 %collective-permute-start.4 = (f32[48,128]{1,0:T(8,128)S(1)}, f32[48,128]{1,0:T(8,128)S(1)}, u32[]{:S(2)}, u32[]{:S(2)}) collective-permute-start(f32[48,128]{1,0:T(8,128)S(1)} %get-tuple-element.36), channel_id=1, source_target_pairs={{0,120},{120,0},{1,121},{121,1},{2,122},{122,2},{3,123},{123,3},{4... | collective-permute-start | bytes 73736 | tf_op jit(solution)/shard_map/ppermute | solution.py:477
  29.4 0.0 collective-permute-done.2.first_y
  29.4 0.0 collective-permute-done.3.second_y
  29.4 2.4 %collective-permute-done.first_x.listed_a = f32[144,128]{1,0:T(8,128)S(1)} collective-permute-done((f32[144,128]{1,0:T(8,128)S(1)}, f32[144,128]{1,0:T(8,128)S(1)}, u32[]{:S(2)}, u32[]{:S(2)}) %collective-permute-start) | collective-permute-done | bytes 73760 | tf_op jit(solution)/shard_map/ppermute | solution.py:475
  31.8 0.0 collective-permute-done.1.second_x.listed_b
  31.8 1.3 %shard_map.115.spread = f32[3,256,128]{2,1,0:T(8,128)S(1)} custom-call(s32[2]{0:T(128)S(1)} %pad_add_fusion.side, f32[3,256,128]{2,1,0:T(8,128)S(1)} %get-tuple-element.30.inner, f32[144,128]{1,0:T(8,128)S(1)} %collective-permute-done.first_x.listed_a, f32[144,128]{1,0:T(8,128)S(1)} %collective-permute-done.1.second_x.listed_b, ...), custom_call_target="tpu_custom_call" | custom-call | flops 1000000000 | bytes 3000000 | tf_op jit(solution)/shard_map/pallas_call | solution.py:481
  33.1 3.3 %all-to-all-done = f32[128,16,128]{2,1,0:T(8,128)S(1)} async-done(((f32[128,16,128]{2,1,0:T(8,128)}), f32[128,16,128]{2,1,0:T(8,128)S(1)}, u32[]{:S(2)}, u32[]{:S(2)}) %all-to-all-start) | async-done | bytes 1048608 | tf_op jit(solution)/shard_map/all_to_all | solution.py:455
  36.4 2.1 %shard_map.116 = (f32[2048,128]{1,0:T(8,128)}, f32[3,8,16,256]{3,2,1,0:T(8,128)}, f32[8,128]{1,0:T(8,128)S(1)}) custom-call(f32[2048,128]{1,0:T(8,128)S(1)} %bitcast.11, f32[3,256,128]{2,1,0:T(8,128)S(1)} %get-tuple-element.29.old, f32[3,256,128]{2,1,0:T(8,128)S(1)} %shard_map.115.spread), custom_call_target="tpu_custom_call" | custom-call | flops 3000000000 | bytes 9000000 | tf_op jit(solution)/shard_map/pallas_call | solution.py:487
  38.6 0.0 copy-start.4
  38.6 0.0 copy-start.5
  38.6 6.5 %all-to-all-start.1 = ((f32[128,16,128]{2,1,0:T(8,128)}), f32[128,16,128]{2,1,0:T(8,128)S(1)}, u32[]{:S(2)}, u32[]{:S(2)}) async-start(f32[128,16,128]{2,1,0:T(8,128)} %bitcast.7), calls=%async_computation.1 | async-start | bytes 2097152 | tf_op jit(solution)/shard_map/all_to_all | solution.py:495
  45.1 0.0 collective-permute-done.4.around
  45.1 0.0 copy-start.8
  45.1 0.0 copy-done.4
  45.1 0.0 copy-done.5
  45.1 0.7 copy-done.8
  45.8 0.0 copy-start.1
  45.8 0.0 copy-start.3
  45.8 12.5 %shard_map.117 = (f32[2048,128]{1,0:T(8,128)S(1)}, s32[256]{0:T(256)S(1)}, s32[1152]{0:T(1024)S(1)}) custom-call(s32[2]{0:T(128)S(1)} %pad_add_fusion.side, s32[2,512]{1,0:T(2,128)S(1)} %copy-done.4, s32[2,512]{1,0:T(2,128)S(1)} %copy-done.5, s32[256]{0:T(256)S(1)} %copy-done.8, f32[3,256,128]{2,1,0:T(8,128)S(1)} %bitcast.16, ...), custom_call_target="tpu_custom_call" | custom-call | flops 14000000000 | bytes 42000000 | tf_op jit(solution)/shard_map/pallas_call | solution.py:497
  58.2 5.8 %all-to-all-done.1 = f32[128,16,128]{2,1,0:T(8,128)S(1)} async-done(((f32[128,16,128]{2,1,0:T(8,128)}), f32[128,16,128]{2,1,0:T(8,128)S(1)}, u32[]{:S(2)}, u32[]{:S(2)}) %all-to-all-start.1) | async-done | bytes 1048608 | tf_op jit(solution)/shard_map/all_to_all | solution.py:495
  64.0 0.0 copy-done.1
  64.0 0.0 copy-done.3
  64.1 3.0 %shard_map.118 = (f32[4,256,128]{2,1,0:T(8,128)S(1)}, f32[3,256,128]{2,1,0:T(8,128)S(1)}, f32[3,256,128]{2,1,0:T(8,128)S(1)}, f32[48,128]{1,0:T(8,128)S(1)}, f32[48,128]{1,0:T(8,128)S(1)}) custom-call(s32[2]{0:T(128)S(1)} %pad_add_fusion.side, s32[256]{0:T(256)S(1)} %get-tuple-element.39.slot, s32[32]{0:T(128)S(1)} %copy-done.6, ...), custom_call_target="tpu_custom_call" | custom-call | flops 4000000000 | bytes 12000000 | tf_op jit(solution)/shard_map/pallas_call | solution.py:510
  67.1 0.5 collective-permute-start.5
  67.5 0.7 collective-permute-start.6
  68.3 8.9 %shard_map.119.inner = f32[2048,128]{1,0:T(8,128)S(1)} custom-call(s32[1152]{0:T(1024)S(1)} %get-tuple-element.38.ordered, f32[3,256,128]{2,1,0:T(8,128)S(1)} %get-tuple-element.42.pos), custom_call_target="tpu_custom_call" | custom-call | flops 10000000000 | bytes 30000000 | tf_op jit(solution)/shard_map/pallas_call | solution.py:520
  77.2 0.0 collective-permute-done.5.listed_a
  77.2 0.0 collective-permute-done.6.listed_b
  77.3 5.5 %shard_map.120 = (f32[3,256,128]{2,1,0:T(8,128)}, f32[3,256,128]{2,1,0:T(8,128)}) custom-call(s32[2]{0:T(128)S(1)} %pad_add_fusion.side, s32[1152]{0:T(1024)S(1)} %get-tuple-element.38.ordered, f32[3,256,128]{2,1,0:T(8,128)S(1)} %get-tuple-element.42.pos, f32[3,256,128]{2,1,0:T(8,128)S(1)} %get-tuple-element.43.vel, ...), custom_call_target="tpu_custom_call" | custom-call | flops 5000000000 | bytes 15000000 | tf_op jit(solution)/shard_map/pallas_call | solution.py:528
Async XLA Ops:
  5.8 11.3 %copy-start = (f32[3,8,16,256]{3,2,1,0:T(8,128)S(1)}, f32[3,8,16,256]{3,2,1,0:T(8,128)}, u32[]{:S(2)}) copy-start(f32[3,8,16,256]{3,2,1,0:T(8,128)} %fv.3) | copy-start | bytes 1179652
  5.8 11.3 %copy-start.2 = (f32[256,3,128]{2,0,1:T(8,128)S(1)}, f32[256,3,128]{2,0,1:T(8,128)}, u32[]{:S(2)}) copy-start(f32[256,3,128]{2,0,1:T(8,128)} %param.10) | copy-start | bytes 1179652
  5.9 30.6 %all-to-all-start = ((f32[128,16,128]{2,1,0:T(8,128)}), f32[128,16,128]{2,1,0:T(8,128)S(1)}, u32[]{:S(2)}, u32[]{:S(2)}) async-start(f32[128,16,128]{2,1,0:T(8,128)} %bitcast.18), calls=%async_computation | async-start | bytes 2097152 | tf_op jit(solution)/shard_map/all_to_all | solution.py:455
  17.0 0.7 copy-start.7
  17.1 0.7 copy-start.6
  18.4 11.0 %collective-permute-start.2 = (f32[3,8,256]{2,1,0:T(8,128)S(1)}, f32[3,8,256]{2,1,0:T(8,128)S(1)}, u32[]{:S(2)}, u32[]{:S(2)}) collective-permute-start(f32[3,8,256]{2,1,0:T(8,128)S(1)} %get-tuple-element.32), channel_id=1, source_target_pairs={{0,1},{1,0},{2,3},{3,2},{4,5},{5,4},{6,7},{7,6},{8,9},{9,8},{10,11... | collective-permute-start | bytes 73736 | tf_op jit(solution)/shard_map/ppermute | solution.py:478
  18.5 10.9 %collective-permute-start.3 = (f32[3,8,256]{2,1,0:T(8,128)S(1)}, f32[3,8,256]{2,1,0:T(8,128)S(1)}, u32[]{:S(2)}, u32[]{:S(2)}) collective-permute-start(f32[3,8,256]{2,1,0:T(8,128)S(1)} %get-tuple-element.33), channel_id=1, source_target_pairs={{1,2},{2,1},{3,4},{4,3},{5,6},{6,5},{9,10},{10,9},{11,12},{12,11},... | collective-permute-start | bytes 73736 | tf_op jit(solution)/shard_map/ppermute | solution.py:479
  19.2 12.7 %collective-permute-start = (f32[144,128]{1,0:T(8,128)S(1)}, f32[144,128]{1,0:T(8,128)S(1)}, u32[]{:S(2)}, u32[]{:S(2)}) collective-permute-start(f32[144,128]{1,0:T(8,128)S(1)} %get-tuple-element.31), channel_id=1, source_target_pairs={{0,8},{8,0},{16,24},{24,16},{32,40},{40,32},{48,56},{56,48},{64,72... | collective-permute-start | bytes 221192 | tf_op jit(solution)/shard_map/ppermute | solution.py:475
  20.5 11.4 %collective-permute-start.1 = (f32[144,128]{1,0:T(8,128)S(1)}, f32[144,128]{1,0:T(8,128)S(1)}, u32[]{:S(2)}, u32[]{:S(2)}) collective-permute-start(f32[144,128]{1,0:T(8,128)S(1)} %get-tuple-element.28.sent), channel_id=1, source_target_pairs={{8,16},{16,8},{24,32},{32,24},{40,48},{48,40},{56,64},{64,56},{72,... | collective-permute-start | bytes 221192 | tf_op jit(solution)/shard_map/ppermute | solution.py:476
  22.9 22.2 %collective-permute-start.4 = (f32[48,128]{1,0:T(8,128)S(1)}, f32[48,128]{1,0:T(8,128)S(1)}, u32[]{:S(2)}, u32[]{:S(2)}) collective-permute-start(f32[48,128]{1,0:T(8,128)S(1)} %get-tuple-element.36), channel_id=1, source_target_pairs={{0,120},{120,0},{1,121},{121,1},{2,122},{122,2},{3,123},{123,3},{4... | collective-permute-start | bytes 73736 | tf_op jit(solution)/shard_map/ppermute | solution.py:477
  38.6 6.5 %copy-start.4 = (s32[2,512]{1,0:T(2,128)S(1)}, s32[2,512]{1,0:T(2,128)}, u32[]{:S(2)}) copy-start(s32[2,512]{1,0:T(2,128)} %first.1) | copy-start | bytes 12292
  38.6 6.6 %copy-start.5 = (s32[2,512]{1,0:T(2,128)S(1)}, s32[2,512]{1,0:T(2,128)}, u32[]{:S(2)}) copy-start(s32[2,512]{1,0:T(2,128)} %second.1) | copy-start | bytes 12292
  38.6 25.5 %all-to-all-start.1 = ((f32[128,16,128]{2,1,0:T(8,128)}), f32[128,16,128]{2,1,0:T(8,128)S(1)}, u32[]{:S(2)}, u32[]{:S(2)}) async-start(f32[128,16,128]{2,1,0:T(8,128)} %bitcast.7), calls=%async_computation.1 | async-start | bytes 2097152 | tf_op jit(solution)/shard_map/all_to_all | solution.py:495
  45.1 0.7 copy-start.8
  45.8 18.3 %copy-start.1 = (f32[256,3,128]{2,0,1:T(8,128)S(1)}, f32[256,3,128]{2,0,1:T(8,128)}, u32[]{:S(2)}) copy-start(f32[256,3,128]{2,0,1:T(8,128)} %param.11) | copy-start | bytes 1179652
  45.8 18.3 %copy-start.3 = (s32[256,128]{1,0:T(8,128)S(1)}, s32[256,128]{1,0:T(8,128)}, u32[]{:S(2)}) copy-start(s32[256,128]{1,0:T(8,128)} %cell.1) | copy-start | bytes 393220
  67.1 10.2 %collective-permute-start.5 = (f32[48,128]{1,0:T(8,128)S(1)}, f32[48,128]{1,0:T(8,128)S(1)}, u32[]{:S(2)}, u32[]{:S(2)}) collective-permute-start(f32[48,128]{1,0:T(8,128)S(1)} %get-tuple-element.44), channel_id=1, source_target_pairs={{0,8},{8,0},{16,24},{24,16},{32,40},{40,32},{48,56},{56,48},{64,72... | collective-permute-start | bytes 73736 | tf_op jit(solution)/shard_map/ppermute | solution.py:518
  67.5 9.7 %collective-permute-start.6 = (f32[48,128]{1,0:T(8,128)S(1)}, f32[48,128]{1,0:T(8,128)S(1)}, u32[]{:S(2)}, u32[]{:S(2)}) collective-permute-start(f32[48,128]{1,0:T(8,128)S(1)} %get-tuple-element.45), channel_id=1, source_target_pairs={{0,120},{8,16},{16,8},{24,32},{32,24},{40,48},{48,40},{56,64},{64,... | collective-permute-start | bytes 73736 | tf_op jit(solution)/shard_map/ppermute | solution.py:519

commit v12 on v10

--- a/solution.py
+++ b/solution.py
@@ -12,7 +12,7 @@
 PAIR_GROUP = 256
 INNER_GROUP = 384
 LAST_GROUP = 128
-BLOCK_GROUP = 128
+BLOCK_GROUP = 256
 DEPOSIT_GROUP = 128
 CAP = 4
 EPS2 = 0.0025

time: 84.1 us -> 83.7 us (level)
  no operation moved by 1% of the time
where the time goes in v12:
time: 83.7 us; the launch traced here: 82.6 us
  Pallas kernels  40.7 us (49%)
  starting transfers between devices  28.1 us (34%)
  waiting for transfers between devices  11.6 us (14%)
  local copies, waits for them, and re-layouts  1.34 us (2%)
  between operations  0.84 us (1%)
    pallas_call x1, Pallas kernels, per_device(): call(push_kernel, [SMEM] * 4 + [VMEM] * 5, [shape(blocks * 8, 128), shape...  12.5 us
    all_to_all x1, starting transfers between devices, per_device(): lax.all_to_all(send.reshape(slots * 4, 128), ('gx', 'gy'), split_axis=0,...  11.1 us
    pallas_call x1, Pallas kernels, per_device(): call(inner_kernel, [SMEM, VMEM], shape(blocks * 8, 128), VMEM, pair_scrat...  8.94 us
    ppermute x1, starting transfers between devices, per_device(): around = lax.ppermute(around, 'gx', [(0, nx - 1), (nx - 1, 0)])  6.56 us
    all_to_all x1, starting transfers between devices, per_device(): lax.all_to_all(answer, ('gx', 'gy'), split_axis=0, concat_axis=0, tiled=T...  6.52 us
    all_to_all x1, waiting for transfers between devices, per_device(): lax.all_to_all(answer, ('gx', 'gy'), split_axis=0, concat_axis=0, tiled=T...  5.81 us
    pallas_call x1, Pallas kernels, per_device(): call(last_kernel, [SMEM] * 2 + [VMEM] * 6, [shape(3, blocks, 128), shape(...  5.5 us
    pallas_call x1, Pallas kernels, per_device(): call(deposit_kernel, [HBM] * 4, [shape(slots, 4, 128), shape(blocks, dtyp...  5.05 us
  transfers between devices with their start and end apart: 9, of which 3 were waited for; matrix products, arithmetic and copies ran while one was open for 0% of the time, Pallas kernels for 33%

profile of v12, /device:TPU:0, one launch (start us, length us, event | category | flops | bytes accessed | tf_op | source)
XLA Modules:
  0.0 82.6 jit_solution(18264756269814881048)
XLA Ops:
  0.6 5.1 %shard_map.112 = (f32[512,4,128]{2,1,0:T(4,128)}, s32[256]{0:T(256)}, f32[8,128]{1,0:T(8,128)}) custom-call(s32[256]{0:T(256)} %bitcast.19, s32[256]{0:T(256)} %local_in.1, s32[256,128]{1,0:T(8,128)} %cell.1, f32[3,256,128]{2,1,0:T(8,128)} %bitcast.13), custom_call_target="tpu_custom_call" | custom-call | flops 7000000000 | bytes 21000000 | tf_op jit(solution)/shard_map/pallas_call | solution.py:434
  5.7 0.0 copy-start
  5.7 0.0 copy-start.2
  5.7 11.1 %all-to-all-start = ((f32[128,16,128]{2,1,0:T(8,128)}), f32[128,16,128]{2,1,0:T(8,128)S(1)}, u32[]{:S(2)}, u32[]{:S(2)}) async-start(f32[128,16,128]{2,1,0:T(8,128)} %bitcast.18), calls=%async_computation | async-start | bytes 2097152 | tf_op jit(solution)/shard_map/all_to_all | solution.py:450
  16.9 0.0 copy-start.7
  16.9 0.1 pad_add_fusion.side
  17.0 0.0 copy-start.6
  17.0 0.0 copy-done
  17.0 0.0 copy-done.2
  17.0 0.6 copy-done.7
  17.6 0.1 copy-done.6
  17.6 0.6 shard_map.113
  18.3 0.1 collective-permute-start.2
  18.3 0.7 collective-permute-start.3
  19.0 1.3 %collective-permute-start = (f32[144,128]{1,0:T(8,128)S(1)}, f32[144,128]{1,0:T(8,128)S(1)}, u32[]{:S(2)}, u32[]{:S(2)}) collective-permute-start(f32[144,128]{1,0:T(8,128)S(1)} %get-tuple-element.31), channel_id=1, source_target_pairs={{0,8},{8,0},{16,24},{24,16},{32,40},{40,32},{48,56},{56,48},{64,72... | collective-permute-start | bytes 221192 | tf_op jit(solution)/shard_map/ppermute | solution.py:470
  20.3 0.7 collective-permute-start.1
  21.0 1.7 %shard_map.114 = (f32[3,256,128]{2,1,0:T(8,128)S(1)}, f32[48,128]{1,0:T(8,128)S(1)}, f32[3,256,128]{2,1,0:T(8,128)S(1)}) custom-call(f32[3,8,16,256]{3,2,1,0:T(8,128)S(1)} %copy-done, f32[144,128]{1,0:T(8,128)S(1)} %get-tuple-element.28.sent), custom_call_target="tpu_custom_call" | custom-call | flops 2000000000 | bytes 6000000 | tf_op jit(solution)/shard_map/pallas_call | solution.py:461
  22.7 6.6 %collective-permute-start.4 = (f32[48,128]{1,0:T(8,128)S(1)}, f32[48,128]{1,0:T(8,128)S(1)}, u32[]{:S(2)}, u32[]{:S(2)}) collective-permute-start(f32[48,128]{1,0:T(8,128)S(1)} %get-tuple-element.36), channel_id=1, source_target_pairs={{0,120},{120,0},{1,121},{121,1},{2,122},{122,2},{3,123},{123,3},{4... | collective-permute-start | bytes 73736 | tf_op jit(solution)/shard_map/ppermute | solution.py:472
  29.3 0.0 collective-permute-done.2.first_y
  29.3 0.0 collective-permute-done.3.second_y
  29.3 2.4 %collective-permute-done.first_x.listed_a = f32[144,128]{1,0:T(8,128)S(1)} collective-permute-done((f32[144,128]{1,0:T(8,128)S(1)}, f32[144,128]{1,0:T(8,128)S(1)}, u32[]{:S(2)}, u32[]{:S(2)}) %collective-permute-start) | collective-permute-done | bytes 73760 | tf_op jit(solution)/shard_map/ppermute | solution.py:470
  31.7 0.0 collective-permute-done.1.second_x.listed_b
  31.7 1.3 %shard_map.115.spread = f32[3,256,128]{2,1,0:T(8,128)S(1)} custom-call(s32[2]{0:T(128)S(1)} %pad_add_fusion.side, f32[3,256,128]{2,1,0:T(8,128)S(1)} %get-tuple-element.30.inner, f32[144,128]{1,0:T(8,128)S(1)} %collective-permute-done.first_x.listed_a, f32[144,128]{1,0:T(8,128)S(1)} %collective-permute-done.1.second_x.listed_b, ...), custom_call_target="tpu_custom_call" | custom-call | flops 1000000000 | bytes 3000000 | tf_op jit(solution)/shard_map/pallas_call | solution.py:476
  32.9 3.3 %all-to-all-done = f32[128,16,128]{2,1,0:T(8,128)S(1)} async-done(((f32[128,16,128]{2,1,0:T(8,128)}), f32[128,16,128]{2,1,0:T(8,128)S(1)}, u32[]{:S(2)}, u32[]{:S(2)}) %all-to-all-start) | async-done | bytes 1048608 | tf_op jit(solution)/shard_map/all_to_all | solution.py:450
  36.3 2.1 %shard_map.116 = (f32[2048,128]{1,0:T(8,128)}, f32[3,8,16,256]{3,2,1,0:T(8,128)}, f32[8,128]{1,0:T(8,128)S(1)}) custom-call(f32[2048,128]{1,0:T(8,128)S(1)} %bitcast.11, f32[3,256,128]{2,1,0:T(8,128)S(1)} %get-tuple-element.29.old, f32[3,256,128]{2,1,0:T(8,128)S(1)} %shard_map.115.spread), custom_call_target="tpu_custom_call" | custom-call | flops 3000000000 | bytes 9000000 | tf_op jit(solution)/shard_map/pallas_call | solution.py:482
  38.4 0.0 copy-start.4
  38.4 0.0 copy-start.5
  38.4 6.5 %all-to-all-start.1 = ((f32[128,16,128]{2,1,0:T(8,128)}), f32[128,16,128]{2,1,0:T(8,128)S(1)}, u32[]{:S(2)}, u32[]{:S(2)}) async-start(f32[128,16,128]{2,1,0:T(8,128)} %bitcast.7), calls=%async_computation.1 | async-start | bytes 2097152 | tf_op jit(solution)/shard_map/all_to_all | solution.py:490
  44.9 0.0 collective-permute-done.4.around
  44.9 0.0 copy-start.8
  44.9 0.0 copy-done.4
  45.0 0.0 copy-done.5
  45.0 0.7 copy-done.8
  45.6 0.0 copy-start.1
  45.6 0.0 copy-start.3
  45.6 12.5 %shard_map.117 = (f32[2048,128]{1,0:T(8,128)S(1)}, s32[256]{0:T(256)S(1)}, s32[1152]{0:T(1024)S(1)}) custom-call(s32[2]{0:T(128)S(1)} %pad_add_fusion.side, s32[2,512]{1,0:T(2,128)S(1)} %copy-done.4, s32[2,512]{1,0:T(2,128)S(1)} %copy-done.5, s32[256]{0:T(256)S(1)} %copy-done.8, f32[3,256,128]{2,1,0:T(8,128)S(1)} %bitcast.16, ...), custom_call_target="tpu_custom_call" | custom-call | flops 14000000000 | bytes 42000000 | tf_op jit(solution)/shard_map/pallas_call | solution.py:492
  58.1 5.8 %all-to-all-done.1 = f32[128,16,128]{2,1,0:T(8,128)S(1)} async-done(((f32[128,16,128]{2,1,0:T(8,128)}), f32[128,16,128]{2,1,0:T(8,128)S(1)}, u32[]{:S(2)}, u32[]{:S(2)}) %all-to-all-start.1) | async-done | bytes 1048608 | tf_op jit(solution)/shard_map/all_to_all | solution.py:490
  63.9 0.0 copy-done.1
  63.9 0.0 copy-done.3
  63.9 3.0 %shard_map.118 = (f32[4,256,128]{2,1,0:T(8,128)S(1)}, f32[3,256,128]{2,1,0:T(8,128)S(1)}, f32[3,256,128]{2,1,0:T(8,128)S(1)}, f32[48,128]{1,0:T(8,128)S(1)}, f32[48,128]{1,0:T(8,128)S(1)}) custom-call(s32[2]{0:T(128)S(1)} %pad_add_fusion.side, s32[256]{0:T(256)S(1)} %get-tuple-element.39.slot, s32[32]{0:T(128)S(1)} %copy-done.6, ...), custom_call_target="tpu_custom_call" | custom-call | flops 4000000000 | bytes 12000000 | tf_op jit(solution)/shard_map/pallas_call | solution.py:505
  66.9 0.5 collective-permute-start.5
  67.4 0.7 collective-permute-start.6
  68.1 8.9 %shard_map.119.inner = f32[2048,128]{1,0:T(8,128)S(1)} custom-call(s32[1152]{0:T(1024)S(1)} %get-tuple-element.38.ordered, f32[3,256,128]{2,1,0:T(8,128)S(1)} %get-tuple-element.42.pos), custom_call_target="tpu_custom_call" | custom-call | flops 10000000000 | bytes 30000000 | tf_op jit(solution)/shard_map/pallas_call | solution.py:515
  77.1 0.0 collective-permute-done.5.listed_a
  77.1 0.0 collective-permute-done.6.listed_b
  77.1 5.5 %shard_map.120 = (f32[3,256,128]{2,1,0:T(8,128)}, f32[3,256,128]{2,1,0:T(8,128)}) custom-call(s32[2]{0:T(128)S(1)} %pad_add_fusion.side, s32[1152]{0:T(1024)S(1)} %get-tuple-element.38.ordered, f32[3,256,128]{2,1,0:T(8,128)S(1)} %get-tuple-element.42.pos, f32[3,256,128]{2,1,0:T(8,128)S(1)} %get-tuple-element.43.vel, ...), custom_call_target="tpu_custom_call" | custom-call | flops 5000000000 | bytes 15000000 | tf_op jit(solution)/shard_map/pallas_call | solution.py:523
Async XLA Ops:
  5.7 11.3 %copy-start = (f32[3,8,16,256]{3,2,1,0:T(8,128)S(1)}, f32[3,8,16,256]{3,2,1,0:T(8,128)}, u32[]{:S(2)}) copy-start(f32[3,8,16,256]{3,2,1,0:T(8,128)} %fv.3) | copy-start | bytes 1179652
  5.7 11.3 %copy-start.2 = (f32[256,3,128]{2,0,1:T(8,128)S(1)}, f32[256,3,128]{2,0,1:T(8,128)}, u32[]{:S(2)}) copy-start(f32[256,3,128]{2,0,1:T(8,128)} %param.10) | copy-start | bytes 1179652
  5.7 30.6 %all-to-all-start = ((f32[128,16,128]{2,1,0:T(8,128)}), f32[128,16,128]{2,1,0:T(8,128)S(1)}, u32[]{:S(2)}, u32[]{:S(2)}) async-start(f32[128,16,128]{2,1,0:T(8,128)} %bitcast.18), calls=%async_computation | async-start | bytes 2097152 | tf_op jit(solution)/shard_map/all_to_all | solution.py:450
  16.9 0.7 copy-start.7
  17.0 0.7 copy-start.6
  18.3 11.0 %collective-permute-start.2 = (f32[3,8,256]{2,1,0:T(8,128)S(1)}, f32[3,8,256]{2,1,0:T(8,128)S(1)}, u32[]{:S(2)}, u32[]{:S(2)}) collective-permute-start(f32[3,8,256]{2,1,0:T(8,128)S(1)} %get-tuple-element.32), channel_id=1, source_target_pairs={{0,1},{1,0},{2,3},{3,2},{4,5},{5,4},{6,7},{7,6},{8,9},{9,8},{10,11... | collective-permute-start | bytes 73736 | tf_op jit(solution)/shard_map/ppermute | solution.py:473
  18.3 10.9 %collective-permute-start.3 = (f32[3,8,256]{2,1,0:T(8,128)S(1)}, f32[3,8,256]{2,1,0:T(8,128)S(1)}, u32[]{:S(2)}, u32[]{:S(2)}) collective-permute-start(f32[3,8,256]{2,1,0:T(8,128)S(1)} %get-tuple-element.33), channel_id=1, source_target_pairs={{1,2},{2,1},{3,4},{4,3},{5,6},{6,5},{9,10},{10,9},{11,12},{12,11},... | collective-permute-start | bytes 73736 | tf_op jit(solution)/shard_map/ppermute | solution.py:474
  19.0 12.7 %collective-permute-start = (f32[144,128]{1,0:T(8,128)S(1)}, f32[144,128]{1,0:T(8,128)S(1)}, u32[]{:S(2)}, u32[]{:S(2)}) collective-permute-start(f32[144,128]{1,0:T(8,128)S(1)} %get-tuple-element.31), channel_id=1, source_target_pairs={{0,8},{8,0},{16,24},{24,16},{32,40},{40,32},{48,56},{56,48},{64,72... | collective-permute-start | bytes 221192 | tf_op jit(solution)/shard_map/ppermute | solution.py:470
  20.3 11.4 %collective-permute-start.1 = (f32[144,128]{1,0:T(8,128)S(1)}, f32[144,128]{1,0:T(8,128)S(1)}, u32[]{:S(2)}, u32[]{:S(2)}) collective-permute-start(f32[144,128]{1,0:T(8,128)S(1)} %get-tuple-element.28.sent), channel_id=1, source_target_pairs={{8,16},{16,8},{24,32},{32,24},{40,48},{48,40},{56,64},{64,56},{72,... | collective-permute-start | bytes 221192 | tf_op jit(solution)/shard_map/ppermute | solution.py:471
  22.7 22.2 %collective-permute-start.4 = (f32[48,128]{1,0:T(8,128)S(1)}, f32[48,128]{1,0:T(8,128)S(1)}, u32[]{:S(2)}, u32[]{:S(2)}) collective-permute-start(f32[48,128]{1,0:T(8,128)S(1)} %get-tuple-element.36), channel_id=1, source_target_pairs={{0,120},{120,0},{1,121},{121,1},{2,122},{122,2},{3,123},{123,3},{4... | collective-permute-start | bytes 73736 | tf_op jit(solution)/shard_map/ppermute | solution.py:472
  38.4 6.6 %copy-start.4 = (s32[2,512]{1,0:T(2,128)S(1)}, s32[2,512]{1,0:T(2,128)}, u32[]{:S(2)}) copy-start(s32[2,512]{1,0:T(2,128)} %first.1) | copy-start | bytes 12292
  38.4 6.6 %copy-start.5 = (s32[2,512]{1,0:T(2,128)S(1)}, s32[2,512]{1,0:T(2,128)}, u32[]{:S(2)}) copy-start(s32[2,512]{1,0:T(2,128)} %second.1) | copy-start | bytes 12292
  38.4 25.5 %all-to-all-start.1 = ((f32[128,16,128]{2,1,0:T(8,128)}), f32[128,16,128]{2,1,0:T(8,128)S(1)}, u32[]{:S(2)}, u32[]{:S(2)}) async-start(f32[128,16,128]{2,1,0:T(8,128)} %bitcast.7), calls=%async_computation.1 | async-start | bytes 2097152 | tf_op jit(solution)/shard_map/all_to_all | solution.py:490
  44.9 0.7 copy-start.8
  45.6 18.3 %copy-start.1 = (f32[256,3,128]{2,0,1:T(8,128)S(1)}, f32[256,3,128]{2,0,1:T(8,128)}, u32[]{:S(2)}) copy-start(f32[256,3,128]{2,0,1:T(8,128)} %param.11) | copy-start | bytes 1179652
  45.6 18.3 %copy-start.3 = (s32[256,128]{1,0:T(8,128)S(1)}, s32[256,128]{1,0:T(8,128)}, u32[]{:S(2)}) copy-start(s32[256,128]{1,0:T(8,128)} %cell.1) | copy-start | bytes 393220
  66.9 10.2 %collective-permute-start.5 = (f32[48,128]{1,0:T(8,128)S(1)}, f32[48,128]{1,0:T(8,128)S(1)}, u32[]{:S(2)}, u32[]{:S(2)}) collective-permute-start(f32[48,128]{1,0:T(8,128)S(1)} %get-tuple-element.44), channel_id=1, source_target_pairs={{0,8},{8,0},{16,24},{24,16},{32,40},{40,32},{48,56},{56,48},{64,72... | collective-permute-start | bytes 73736 | tf_op jit(solution)/shard_map/ppermute | solution.py:513
  67.4 9.7 %collective-permute-start.6 = (f32[48,128]{1,0:T(8,128)S(1)}, f32[48,128]{1,0:T(8,128)S(1)}, u32[]{:S(2)}, u32[]{:S(2)}) collective-permute-start(f32[48,128]{1,0:T(8,128)S(1)} %get-tuple-element.45), channel_id=1, source_target_pairs={{0,120},{8,16},{16,8},{24,32},{32,24},{40,48},{48,40},{56,64},{64,... | collective-permute-start | bytes 73736 | tf_op jit(solution)/shard_map/ppermute | solution.py:514
